TPU v7x, 256 devices: a whole 4x4x8 slice. The times are simulated.
256 devices in a mesh: seq: 64 (over x, z, core), vocab: 4 (over y).
Axes of the slice: x: 4, y: 4, z: 8, core: 2. Of those that a mesh axis runs over, the one named last changes fastest.
Arguments:
- hidden: bfloat16 [4096, 4096], P('seq'), may hold values from -12 to 12
- head_weight: bfloat16 [4096, 126464], P(None, ('seq', 'vocab')), may hold values from -3 to 3
- teacher: bfloat16 [512, 126464], P(None, ('seq', 'vocab')), may hold values from -320 to 320
- positions: int32 [64, 8], P('seq'), may hold values from 0 to 63, as said below
- counts: int32 [64], P('seq'), may hold values from 1 to 8, 256 in all
Outputs:
- grad_hidden: bfloat16 [512, 4096], P(('seq', 'vocab'))
- grad_head: bfloat16 [4096, 126464], P(None, ('seq', 'vocab'))
Inputs may be any that keep to these rules, and one draw needn't show every extreme that they name: Each row holds 8 distinct token positions within its seq shard's block of 64 tokens; the first counts[s] of row s are its masked tokens. The counts sum to exactly 256.
All inputs are finite; a program needn't handle non-finite values. No bound on the sum of `counts` on one device may be relied on, other than what follows from the above.
Results may differ from a plain program's by a relative error of at most 0.012.
Values may be sent and summed in bfloat16 or wider, within the bound.
No kernel may reach another device: no remote copies, remote signals or barrier semaphores. Data moves between devices by JAX's collectives and lax.ppermute only.
A program may use at most 64 MiB of HBM per device.

v0:
```python
import jax
import jax.numpy as jnp
from jax import lax
from jax.sharding import PartitionSpec as P

SPAN = 1


loss_scale = 1024.0


def per_device(hidden, head_weight, teacher, positions, counts):
    capacity = positions.shape[1]
    seq_devices = lax.axis_size("seq")
    picked = jnp.take(hidden, positions[0], axis=0)
    gathered, all_counts = (
        lax.all_gather(picked, "seq", axis=0, tiled=True),
        lax.all_gather(counts, "seq", axis=0, tiled=True),
    )
    slot_rank = jnp.arange(capacity, dtype=jnp.int32)[None, :]
    validity = (slot_rank < all_counts[:, None]).reshape(-1)
    seq_count = jnp.sum(all_counts.reshape(seq_devices // SPAN, SPAN), axis=1).astype(jnp.int32)
    per_slot = jnp.repeat(seq_count, SPAN * capacity)
    weight = jnp.where(validity, loss_scale / per_slot.astype(jnp.float32), 0.0)
    student = jnp.dot(gathered, head_weight, preferred_element_type=jnp.float32)
    teacher_full = teacher.astype(jnp.float32)
    top_student, top_teacher = lax.pmax(
        (jnp.max(student, axis=1), jnp.max(teacher_full, axis=1)), ("seq", "vocab")
    )
    total_student, total_teacher = lax.psum(
        (
            jnp.sum(jnp.exp(student - top_student[:, None]), axis=1),
            jnp.sum(jnp.exp(teacher_full - top_teacher[:, None]), axis=1),
        ),
        ("seq", "vocab"),
    )
    prob_student = jnp.exp(student - top_student[:, None]) / total_student[:, None]
    prob_teacher = jnp.exp(teacher_full - top_teacher[:, None]) / total_teacher[:, None]
    grad_logits = (weight[:, None] * (prob_student - prob_teacher)).astype(jnp.bfloat16)
    grad_head = lax.dot_general(
        gathered, grad_logits, (((0,), (0,)), ((), ())), preferred_element_type=jnp.float32
    ).astype(jnp.bfloat16)
    row_sum = lax.psum_scatter(
        lax.dot_general(
            grad_logits, head_weight, (((1,), (1,)), ((), ())), preferred_element_type=jnp.float32
        ),
        ("seq", "vocab"),
        scatter_dimension=0,
        tiled=True,
    )
    return (row_sum.astype(jnp.bfloat16), grad_head)


def solution(mesh):
    return jax.shard_map(
        per_device,
        mesh=mesh,
        in_specs=(
            P("seq", None),
            P(None, ("seq", "vocab")),
            P(None, ("seq", "vocab")),
            P("seq", None),
            P("seq"),
        ),
        out_specs=(P(("seq", "vocab"), None), P(None, ("seq", "vocab"))),
        check_vma=False,
    )
```

profile of v0, /device:TPU:1, one launch (start us, length us, event | category | flops | bytes accessed | tf_op | source)
XLA Modules:
  0.0 412.5 jit_solution(2432597508514380009)
XLA Ops:
  7.2 0.0 copy-start
  7.2 0.0 all-gather.2.cloned.1.call-start
  7.2 0.7 fusion.3
  7.9 0.7 compare_and_fusion
  8.6 0.0 copy-done
  8.6 0.6 gather_fusion
  9.2 0.7 broadcast_select_fusion
  9.9 0.0 all-gather.2.cloned.1.call-update
  10.6 1.3 dynamic-slice
  11.9 0.8 dynamic-update-slice
  12.6 20.7 %all-reduce = s32[64]{0:T(128)S(1)} all-reduce(s32[64]{0:T(128)S(1)} %dynamic-update-slice), channel_id=1, replica_groups=mesh['seq'=64,'vocab'=4] {'seq'}, use_global_device_ids=true, to_apply=%add | all-reduce | flops 64 | bytes 512
  33.4 0.1 fusion.2
  33.4 0.1 select_n.32
  33.5 1.1 reduce_max.24
  34.7 0.0 copy-start.1
  34.7 59.9 %all-gather.2.cloned.1.call-done = bf16[512,4096]{1,0:T(8,128)(2,1)} async-done(((bf16[8,4096]{1,0:T(8,128)(2,1)}), bf16[512,4096]{1,0:T(8,128)(2,1)}) %all-gather.2.cloned.1.call-update) | async-done | bytes 4194320 | tf_op jit(solution)/shard_map/all_gather | solution.py:17
  94.6 5.7 %fusion.5 = (f32[512]{0:T(512)S(1)}, f32[512,494]{0,1:T(8,128)S(1)}) fusion(bf16[512,4096]{1,0:T(8,128)(2,1)} %all-gather.2.cloned.1.call-done, bf16[4096,494]{0,1:T(8,128)(2,1)} %param.6), kind=kOutput, calls=%fused_computation.18 | convolution fusion | flops 2072238592 | bytes 9254912 | tf_op jit(solution)/shard_map/dot_general | solution.py:25
  100.3 75.0 %all-reduce.3 = (f32[512]{0:T(512)S(1)}, f32[512]{0:T(512)S(1)}) all-reduce(bf16[512]{0:T(512)(128)(2,1)S(1)} %reduce_max.24, f32[512]{0:T(512)S(1)} %get-tuple-element.6), channel_id=1, replica_groups=mesh['seq'=64,'vocab'=4] {'seq','vocab'}, use_global_device_ids=true, to_apply=%region_5.6 | all-reduce | flops 1024 | bytes 7168 | tf_op jit(solution)/shard_map/pmax | solution.py:27
  175.4 0.0 copy-done.1
  175.4 0.3 fusion
  175.7 73.1 %all-reduce.2 = (f32[512]{0:T(512)S(1)}, f32[512]{0:T(512)S(1)}) all-reduce(f32[512]{0:T(512)S(1)} %get-tuple-element.8, f32[512]{0:T(512)S(1)} %get-tuple-element.9), channel_id=1, replica_groups=mesh['seq'=64,'vocab'=4] {'seq','vocab'}, use_global_device_ids=true, to_apply=%region_7.8 | all-reduce | flops 1024 | bytes 8192 | tf_op jit(solution)/shard_map/psum | solution.py:30
  248.8 7.9 %fusion.4 = f32[512,4096]{1,0:T(8,128)} fusion(bf16[4096,494]{0,1:T(8,128)(2,1)} %param.6, bf16[512,494]{0,1:T(8,128)(2,1)S(1)} %copy-done.1, f32[512,494]{0,1:T(8,128)S(1)} %get-tuple-element.7, f32[512]{0:T(512)S(1)} %get-tuple-element.2, f32[512]{0:T(512)S(1)} %get-tuple-element.4, f32[512]{0:T(512)S(1)} %get-tuple-element.3, ...), kind=kOutput, calls=%fused_computation.17 | convolution fusion | flops 2074009600 | bytes 13963264 | tf_op jit(solution)/shard_map/dot_general | solution.py:44
  256.7 141.0 %all-reduce.5 = bf16[512,4096]{1,0:T(8,128)(2,1)} all-reduce(f32[512,4096]{1,0:T(8,128)} %fusion.4), channel_id=2, replica_groups=mesh['seq'=64,'vocab'=4] {'seq','vocab'}, use_global_device_ids=true, to_apply=%region_8.9.clone | all-reduce | flops 2097152 | bytes 12582912
  397.7 1.5 dynamic-slice_convert_fusion
  399.2 6.5 %convolution_convert_fusion = bf16[4096,494]{0,1:T(8,128)(2,1)} fusion(bf16[512,4096]{1,0:T(8,128)(2,1)} %all-gather.2.cloned.1.call-done, bf16[512,494]{0,1:T(8,128)(2,1)S(1)} %copy-done.1, f32[512,494]{0,1:T(8,128)S(1)} %get-tuple-element.7, f32[512]{0:T(512)S(1)} %get-tuple-element.2, f32[512]{0:T(512)S(1)} %get-tuple-element.4, ...), kind=kOutput, calls=%fused_computation.1 | convolution fusion | flops 2076033024 | bytes 9768960 | tf_op jit(solution)/shard_map/dot_general | solution.py:40
  (3 shorter events, 0.0 us)
Async XLA Ops:
  7.2 1.4 copy-start
  7.2 87.4 %all-gather.2.cloned.1.call-start = ((), (), s32[]{:S(2)}) async-start(), calls=%async_computation | async-start | bytes 4259840 | tf_op jit(solution)/shard_map/all_gather | solution.py:17
  34.7 140.7 %copy-start.1 = (bf16[512,494]{0,1:T(8,128)(2,1)S(1)}, bf16[512,494]{0,1:T(8,128)(2,1)}, u32[]{:S(2)}) copy-start(bf16[512,494]{0,1:T(8,128)(2,1)} %param.7) | copy-start | bytes 1517572
Sparse Core Ops, SparseCore 0:
  11.4 83.1 all-gather.1
where the time goes:
time: 413 us
  blocking collectives  310 us (75%)
  waiting for transfers between devices  59.9 us (15%)
  matrix products  20.2 us (5%)
  between operations  14.7 us (4%)
  local copies, waits for them, and re-layouts  4.18 us (1%)
    unnamed x2, blocking collectives  162 us
    pmax x1, blocking collectives, per_device(): lax.pmax((jnp.max(student, axis=1), jnp.max(teacher_full, axis=1)), ('seq...  75 us
    psum x1, blocking collectives, per_device(): lax.psum((jnp.sum(jnp.exp(student - top_student[:, None]), axis=1), jnp.s...  73.1 us
    all_gather x1, waiting for transfers between devices, per_device(): lax.all_gather(picked, 'seq', axis=0, tiled=True)  59.9 us
  transfers between devices with their start and end apart: 1, of which 1 were waited for; matrix products, arithmetic and copies ran while one was open for 1% of the time, Pallas kernels for 0%

commit v1 on v0

v1 whole, which is shorter than its diff:
```python
import jax
import jax.numpy as jnp
from jax import lax
from jax.experimental import pallas as pl
from jax.experimental.pallas import tpu as pltpu
from jax.sharding import Mesh, PartitionSpec as P

LOSS_SCALE = 1024.0
MASKED = 256
MARK = 64.0
INTERPRET = False

SEQ = ("x", "z", "core")
ALL = ("x", "z", "core", "y")
CHIPS = ("x", "z", "y")
NX, NZ, NCORE, NY = 4, 8, 2, 4
BLOCKS = NCORE * NY
F32, BF16 = jnp.float32, jnp.bfloat16
NT = (((1,), (1,)), ((), ()))
TN = (((0,), (0,)), ((), ()))
VMEM = pl.BlockSpec(memory_space=pltpu.VMEM)
SMEM = pl.BlockSpec(memory_space=pltpu.SMEM)


def call(body, out, *args, specs=None, flops=0, scratch=()):
    leaves = jax.tree.leaves((args, out))
    nbytes = sum(x.size * x.dtype.itemsize for x in leaves)
    return pl.pallas_call(
        body,
        out_shape=out,
        in_specs=specs or [VMEM] * len(args),
        out_specs=jax.tree.map(lambda _: VMEM, out),
        scratch_shapes=list(scratch),
        cost_estimate=pl.CostEstimate(flops=flops, bytes_accessed=nbytes, transcendentals=0),
        compiler_params=pltpu.CompilerParams(vmem_limit_bytes=40 * 2**20),
        interpret=INTERPRET,
    )(*args)


def shape(dims, dtype):
    return jax.ShapeDtypeStruct(dims, dtype)


def block_of(y, core):
    return y * NCORE + core


def columns(block, width):
    return pl.ds(pl.multiple_of(block * width, width), width)


def pick_body(positions, counts, hidden, out):
    tokens, depth = hidden.shape
    shards, capacity, width = out.shape
    y = lax.axis_index("y")
    row = lax.broadcasted_iota(jnp.int32, (2 * capacity, tokens), 0)
    column = lax.broadcasted_iota(jnp.int32, (2 * capacity, tokens), 1)
    hot = jnp.zeros((2 * capacity, tokens), F32)
    for k in range(capacity):
        hot = jnp.where((row == k) & (column == positions[0, k]), 1.0, hot)
    mine = hidden[:, columns(y, NCORE * width)]
    rows = jnp.dot(hot.astype(BF16), mine, preferred_element_type=F32)[:capacity]
    rank = lax.broadcasted_iota(jnp.int32, rows.shape, 0)
    rows = jnp.where(rank < counts[0], rows, MARK).astype(BF16)
    for s in range(shards):
        core = s % NCORE
        out[s] = rows[:, core * width : (core + 1) * width]


def compact_body(rows, picked, chosen, count):
    slots = rows.shape[0]
    capacity = 8
    valid = (rows[:, 0:128].astype(F32)[:, 0:1] < MARK / 2).astype(F32)
    a = lax.broadcasted_iota(jnp.int32, (slots, slots), 0)
    b = lax.broadcasted_iota(jnp.int32, (slots, slots), 1)
    spread = jnp.broadcast_to(valid, (slots, slots))
    rank = jnp.sum(jnp.where(a < b, spread, 0.0), axis=0, keepdims=True)
    mine = jnp.sum(jnp.where(a == b, spread, 0.0), axis=0, keepdims=True)
    total = jnp.sum(jnp.where(a // capacity == b // capacity, spread, 0.0), axis=0, keepdims=True)
    place = jnp.where(mine > 0.5, rank, -1.0).astype(jnp.int32)
    target = lax.broadcasted_iota(jnp.int32, (MASKED, slots), 0)
    hot = (target == place).astype(F32).astype(BF16)
    chosen[...] = hot
    picked[...] = jnp.dot(hot, rows[...], preferred_element_type=F32).astype(BF16)
    totals = jnp.broadcast_to(total, (8, slots)).astype(BF16)
    count[...] = lax.dot_general(totals, hot, NT, preferred_element_type=F32)


def logsumexp(x):
    top = jnp.max(x, axis=0, keepdims=True)
    return top + jnp.log(jnp.sum(jnp.exp(x - top), axis=0, keepdims=True))


def teacher_body(teacher, chosen, out, lse):
    rows = lax.dot_general(teacher[...], chosen[...], NT, preferred_element_type=F32)
    out[...] = rows.astype(BF16)
    lse[...] = jnp.broadcast_to(logsumexp(rows), lse.shape)


def student_body(*refs):
    blocks, (weight, lse_teacher, out, stats) = refs[:BLOCKS], refs[BLOCKS:]
    width = blocks[0].shape[1]
    y, core = lax.axis_index("y"), lax.axis_index("core")
    total = jnp.zeros(out.shape, F32)
    for i, block in enumerate(blocks):
        owner = block_of(lax.rem(y - i // NCORE + NY, NY), core if i % NCORE == 0 else 1 - core)
        total += lax.dot_general(
            weight[:, columns(owner, width)], block[...], NT, preferred_element_type=F32
        )
    out[...] = total
    both = jnp.concatenate([logsumexp(total), lse_teacher[0:1, :]], axis=0)
    stats[...] = jnp.broadcast_to(both[None], stats.shape)


def combine_body(stats, out):
    x = stats[...]
    top = jnp.max(x, axis=0)
    out[...] = top + jnp.log(jnp.sum(jnp.exp(x - top[None]), axis=0))


def logits_body(student, teacher, mine, other, count, weight, grad_logits, *parts):
    width = parts[0].shape[1]
    y, core = lax.axis_index("y"), lax.axis_index("core")
    top = jnp.maximum(mine[...], other[...])
    lse = top + jnp.log(jnp.exp(mine[...] - top) + jnp.exp(other[...] - top))
    scale = LOSS_SCALE / count[0:1, :]
    prob_student = jnp.exp(student[...] - lse[0:1, :])
    prob_teacher = jnp.exp(teacher[...].astype(F32) - lse[1:2, :])
    grad = (scale * (prob_student - prob_teacher)).astype(BF16)
    grad_logits[...] = grad
    for i, part in enumerate(parts):
        owner = block_of(lax.rem(y + i // NCORE, NY), core if i % NCORE == 0 else 1 - core)
        part[...] = lax.dot_general(
            grad, weight[:, columns(owner, width)], TN, preferred_element_type=F32
        ).astype(BF16)


def head_body(*refs):
    blocks, (grad_logits, out) = refs[:BLOCKS], refs[BLOCKS:]
    width = blocks[0].shape[1]
    y, core = lax.axis_index("y"), lax.axis_index("core")
    for i, block in enumerate(blocks):
        owner = block_of(lax.rem(y - i // NCORE + NY, NY), core if i % NCORE == 0 else 1 - core)
        out[:, columns(owner, width)] = jnp.dot(
            grad_logits[...], block[...], preferred_element_type=F32
        ).astype(BF16)


def spread_body(a, b, c, d, chosen, out):
    total = a[...].astype(F32) + b[...].astype(F32) + c[...].astype(F32) + d[...].astype(F32)
    out[...] = lax.dot_general(
        chosen[...], total.astype(BF16), TN, preferred_element_type=F32
    ).astype(BF16)


def swap_core(x):
    return lax.ppermute(x, "core", [(0, 1), (1, 0)])


def shift_y(x, k):
    return lax.ppermute(x, "y", [(i, (i + k) % NY) for i in range(NY)])


def per_device(hidden, head_weight, teacher, positions, counts):
    tokens, depth = hidden.shape
    capacity = positions.shape[1]
    shards = NX * NZ * NCORE
    slots = shards * capacity
    vocab = head_weight.shape[1]
    width = depth // BLOCKS
    weight_t, teacher_t = head_weight.T, teacher.T

    send = call(
        pick_body, shape((shards, capacity, width), BF16), positions, counts, hidden,
        specs=[SMEM, SMEM, VMEM],
    )
    rows = lax.all_to_all(send, SEQ, 0, 0, tiled=True).reshape(slots, width)
    mine, chosen, count = call(
        compact_body,
        (shape((MASKED, width), BF16), shape((MASKED, slots), BF16), shape((8, MASKED), F32)),
        rows, flops=2 * MASKED * slots * width,
    )
    blocks = []
    for k in range(NY):
        block = mine if k == 0 else shift_y(mine, k)
        blocks += [block, swap_core(block)]
    teacher_rows, lse_teacher = call(
        teacher_body, (shape((vocab, MASKED), BF16), shape((8, MASKED), F32)),
        teacher_t, chosen, flops=2 * vocab * slots * MASKED,
    )
    student, stats = call(
        student_body,
        (shape((vocab, MASKED), F32), shape((NX * NZ * NY, 2, MASKED), F32)),
        *blocks, weight_t, lse_teacher, flops=2 * vocab * depth * MASKED,
    )
    stats = lax.all_to_all(stats, CHIPS, 0, 0, tiled=True)
    half = call(combine_body, shape((2, MASKED), F32), stats)
    grad_logits, *parts = call(
        logits_body,
        (shape((vocab, MASKED), BF16),) + (shape((MASKED, width), BF16),) * BLOCKS,
        student, teacher_rows, half, swap_core(half), count, weight_t,
        flops=2 * vocab * depth * MASKED,
    )
    grad_head = call(
        head_body, shape((vocab, depth), BF16), *blocks, grad_logits,
        flops=2 * vocab * depth * MASKED,
    )
    sums = []
    for k in range(NY):
        both = parts[2 * k].astype(F32) + swap_core(parts[2 * k + 1]).astype(F32)
        sums.append(both.astype(BF16) if k == 0 else shift_y(both.astype(BF16), k))
    partial = call(
        spread_body, shape((slots, width), BF16), *sums, chosen,
        flops=2 * MASKED * slots * width,
    )
    own = slots // (shards * NY)
    partial = lax.all_to_all(partial.reshape(shards * NY, own, width), ALL, 0, 0, tiled=True)
    total = partial.reshape(NX * NZ, NCORE, NY, own, width).astype(F32).sum(axis=0)
    grad_hidden = total.transpose(2, 1, 0, 3).reshape(own, depth).astype(BF16)
    return grad_hidden, grad_head.T


def solution(mesh):
    fine = Mesh(mesh.devices.reshape(NX, NZ, NCORE, NY), ALL)
    return jax.shard_map(
        per_device,
        mesh=fine,
        in_specs=(P(SEQ, None), P(None, ALL), P(None, ALL), P(SEQ, None), P(SEQ)),
        out_specs=(P(ALL, None), P(None, ALL)),
        check_vma=False,
    )
```

time: 413 us -> 131 us (0.32)
  blocking collectives: 310 us -> 50.2 us
  starting transfers between devices: 0.04 us -> 20.7 us
  matrix products: 20.2 us -> 0 us
  waiting for transfers between devices: 59.9 us -> 42.8 us
  between operations: 14.7 us -> 1.41 us
  Pallas kernels: 0 us -> 8.32 us
    unnamed x2 -> x0, blocking collectives: 162 us -> none
    pmax x1 -> x0, blocking collectives: 75 us -> none  [per_device(): lax.pmax((jnp.max(student, axis=1), jnp.max(teacher_full, axis=1)), ('seq...]
    psum x1 -> x0, blocking collectives: 73.1 us -> none  [per_device(): lax.psum((jnp.sum(jnp.exp(student - top_student[:, None]), axis=1), jnp.s...]
    all_gather x1 -> x0, waiting for transfers between devices: 59.9 us -> none  [per_device(): lax.all_gather(picked, 'seq', axis=0, tiled=True)]
    all_to_all x0 -> x2, blocking collectives: none -> 50.2 us  [the longest x1 30.1 us: per_device(): rows = lax.all_to_all(send, SEQ, 0, 0, tiled=True).reshape(slots, width)]
    ppermute x0 -> x15, waiting for transfers between devices: none -> 24.8 us  [the longest x6 23.3 us: shift_y(): return lax.ppermute(x, 'y', [(i, (i + k) % NY) for i in range(NY)])]
    dot_general x3 -> x0, matrix products: 20.2 us -> none  [the longest x1 7.9 us: per_device(): lax.dot_general(grad_logits, head_weight, (((1,), (1,)), ((), ())), prefe...]
    all_to_all x0 -> x1, waiting for transfers between devices: none -> 18 us  [per_device(): lax.all_to_all(partial.reshape(shards * NY, own, width), ALL, 0, 0, tiled...]
  transfers between devices with their start and end apart: 1 -> 16, of which waited for: 1 -> 8; matrix products, arithmetic and copies ran while one was open for 1% -> 0% of each run, Pallas kernels for 0% -> 3%
where the time goes in v1:
time: 131 us
  blocking collectives  50.2 us (38%)
  waiting for transfers between devices  42.8 us (33%)
  starting transfers between devices  20.7 us (16%)
  Pallas kernels  8.32 us (6%)
  local copies, waits for them, and re-layouts  6.51 us (5%)
  between operations  1.41 us (1%)
    all_to_all x1, blocking collectives, per_device(): rows = lax.all_to_all(send, SEQ, 0, 0, tiled=True).reshape(slots, width)  30.1 us
    ppermute x6, waiting for transfers between devices, shift_y(): return lax.ppermute(x, 'y', [(i, (i + k) % NY) for i in range(NY)])  23.3 us
    all_to_all x1, blocking collectives, per_device(): stats = lax.all_to_all(stats, CHIPS, 0, 0, tiled=True)  20.1 us
    all_to_all x1, waiting for transfers between devices, per_device(): lax.all_to_all(partial.reshape(shards * NY, own, width), ALL, 0, 0, tiled...  18 us
    pallas_call x8, Pallas kernels, call(): pl.pallas_call(body, out_shape=out, in_specs=specs or [VMEM] * len(args),...  8.32 us
    all_to_all x1, starting transfers between devices, per_device(): lax.all_to_all(partial.reshape(shards * NY, own, width), ALL, 0, 0, tiled...  7.23 us
    ppermute x6, starting transfers between devices, shift_y(): return lax.ppermute(x, 'y', [(i, (i + k) % NY) for i in range(NY)])  6.89 us
    ppermute x9, starting transfers between devices, swap_core(): return lax.ppermute(x, 'core', [(0, 1), (1, 0)])  6.56 us
  transfers between devices with their start and end apart: 16, of which 8 were waited for; matrix products, arithmetic and copies ran while one was open for 0% of the time, Pallas kernels for 3%

profile of v1, /device:TPU:1, one launch (start us, length us, event | category | flops | bytes accessed | tf_op | source)
XLA Modules:
  0.0 130.6 jit_solution(10108536890727854717)
XLA Ops:
  1.3 1.0 copy-done.2
  2.3 0.7 copy-done.4
  3.0 0.7 shard_map.68
  3.7 30.1 %all_to_all.15 = bf16[64,8,512]{2,1,0:T(8,128)(2,1)S(1)} all-to-all(bf16[64,8,512]{2,1,0:T(8,128)(2,1)S(1)} %shard_map.68), channel_id=1, replica_groups=mesh['x'=4,'z'=8,'core'=2,'y'=4] {'x','z','core'}, dimensions={0} | all-to-all | bytes 1048576 | tf_op jit(solution)/shard_map/all_to_all | solution.py:177
  33.8 0.5 shard_map.69
  34.3 2.8 %collective-permute-start.5 = (bf16[256,512]{1,0:T(8,128)(2,1)S(1)}, bf16[256,512]{1,0:T(8,128)(2,1)S(1)}, u32[]{:S(2)}, u32[]{:S(2)}) collective-permute-start(bf16[256,512]{1,0:T(8,128)(2,1)S(1)} %get-tuple-element.18.refs_0_), channel_id=1, source_target_pairs={{0,3},{1,0},{2,1},{3,2},{4,7},{5,4},{6,5},{7,6},{8,11},{9,8},{10,9... | collective-permute-start | bytes 786440 | tf_op jit(solution)/shard_map/ppermute | solution.py:161
  37.5 0.7 collective-permute-start.1
  38.2 1.2 collective-permute-start
  39.3 8.6 %collective-permute-done.5.refs_6_ = bf16[256,512]{1,0:T(8,128)(2,1)S(1)} collective-permute-done((bf16[256,512]{1,0:T(8,128)(2,1)S(1)}, bf16[256,512]{1,0:T(8,128)(2,1)S(1)}, u32[]{:S(2)}, u32[]{:S(2)}) %collective-permute-start.5) | collective-permute-done | bytes 262176 | tf_op jit(solution)/shard_map/ppermute | solution.py:161
  48.0 1.3 collective-permute-start.6
  49.3 3.2 %collective-permute-done.1.refs_2_ = bf16[256,512]{1,0:T(8,128)(2,1)S(1)} collective-permute-done((bf16[256,512]{1,0:T(8,128)(2,1)S(1)}, bf16[256,512]{1,0:T(8,128)(2,1)S(1)}, u32[]{:S(2)}, u32[]{:S(2)}) %collective-permute-start.1) | collective-permute-done | bytes 262176 | tf_op jit(solution)/shard_map/ppermute | solution.py:161
  52.5 0.5 collective-permute-start.2
  53.0 1.0 copy-done.3
  54.0 0.4 shard_map.70
  54.5 2.1 %copy-done = bf16[4096,494]{0,1:T(8,128)(2,1)S(1)} copy-done((bf16[4096,494]{0,1:T(8,128)(2,1)S(1)}, bf16[4096,494]{0,1:T(8,128)(2,1)}, u32[]{:S(2)}) %copy-start) | copy-done | bytes 4046872
  56.7 1.4 %shard_map.71 = (f32[494,256]{1,0:T(8,128)S(1)}, f32[128,2,256]{2,1,0:T(2,128)S(1)}) custom-call(bf16[256,512]{1,0:T(8,128)(2,1)S(1)} %get-tuple-element.18.refs_0_, bf16[256,512]{1,0:T(8,128)(2,1)S(1)} %collective-permute-done.refs_1_, bf16[256,512]{1,0:T(8,128)(2,1)S(1)} %collective-permute-done.1.refs_2_, ...), custom_call_target="tpu_custom_call" | custom-call | flops 1035993088 | bytes 6920192 | tf_op jit(solution)/shard_map/pallas_call | solution.py:28
  58.1 20.1 %all_to_all.16.stats = f32[128,2,256]{2,1,0:T(2,128)S(1)} all-to-all(f32[128,2,256]{2,1,0:T(2,128)S(1)} %get-tuple-element.23), channel_id=1, replica_groups=mesh['x'=4,'z'=8,'core'=2,'y'=4] {'x','z','y'}, dimensions={0} | all-to-all | bytes 524288 | tf_op jit(solution)/shard_map/all_to_all | solution.py:196
  78.4 2.4 %collective-permute-start.7 = (f32[2,256]{1,0:T(2,128)S(1)}, f32[2,256]{1,0:T(2,128)S(1)}, u32[]{:S(2)}, u32[]{:S(2)}) collective-permute-start(f32[2,256]{1,0:T(2,128)S(1)} %shard_map.72.mine), channel_id=1, source_target_pairs={{0,4},{4,0},{1,5},{5,1},{2,6},{6,2},{3,7},{7,3},{8,12},{12,8},{9,1... | collective-permute-start | bytes 6152 | tf_op jit(solution)/shard_map/ppermute | solution.py:157
  80.8 0.8 collective-permute-done.7.other
  81.7 1.4 %shard_map.73 = (bf16[494,256]{1,0:T(8,128)(2,1)S(1)}, bf16[256,512]{1,0:T(8,128)(2,1)S(1)}, bf16[256,512]{1,0:T(8,128)(2,1)S(1)}, bf16[256,512]{1,0:T(8,128)(2,...) custom-call(f32[494,256]{1,0:T(8,128)S(1)} %get-tuple-element.21.stu, ...), custom_call_target="tpu_custom_call" | custom-call | flops 1035993088 | bytes 7168000 | tf_op jit(solution)/shard_map/pallas_call | solution.py:28
  83.1 0.4 collective-permute-start.9
  84.3 0.4 collective-permute-done.9
  85.1 1.4 %collective-permute-start.12 = (bf16[256,512]{1,0:T(8,128)(2,1)S(1)}, bf16[256,512]{1,0:T(8,128)(2,1)S(1)}, u32[]{:S(2)}, u32[]{:S(2)}) collective-permute-start(bf16[256,512]{1,0:T(8,128)(2,1)S(1)} %add_convert_fusion.1), channel_id=1, source_target_pairs={{0,2},{1,3},{2,0},{3,1},{4,6},{5,7},{6,4},{7,5},{8,10},{9,11},{10,... | collective-permute-start | bytes 786440 | tf_op jit(solution)/shard_map/ppermute | solution.py:161
  86.6 1.5 %collective-permute-start.14 = (bf16[256,512]{1,0:T(8,128)(2,1)S(1)}, bf16[256,512]{1,0:T(8,128)(2,1)S(1)}, u32[]{:S(2)}, u32[]{:S(2)}) collective-permute-start(bf16[256,512]{1,0:T(8,128)(2,1)S(1)} %add_convert_fusion), channel_id=1, source_target_pairs={{0,3},{1,0},{2,1},{3,2},{4,7},{5,4},{6,5},{7,6},{8,11},{9,8},{10,9... | collective-permute-start | bytes 786440 | tf_op jit(solution)/shard_map/ppermute | solution.py:161
  88.2 11.0 %collective-permute-done.10.b = bf16[256,512]{1,0:T(8,128)(2,1)S(1)} collective-permute-done((bf16[256,512]{1,0:T(8,128)(2,1)S(1)}, bf16[256,512]{1,0:T(8,128)(2,1)S(1)}, u32[]{:S(2)}, u32[]{:S(2)}) %collective-permute-start.10) | collective-permute-done | bytes 262176 | tf_op jit(solution)/shard_map/ppermute | solution.py:161
  99.2 0.4 collective-permute-done.14.d
  100.1 1.0 reshape.16
  101.1 7.2 %all-to-all-start.2 = ((bf16[256,2,512]{2,1,0:T(2,128)(2,1)}), bf16[256,2,512]{2,1,0:T(2,128)(2,1)S(1)}, u32[]{:S(2)}, u32[]{:S(2)}) async-start(bf16[256,2,512]{2,1,0:T(2,128)(2,1)} %reshape.16), calls=%async_computation.2 | async-start | bytes 1048576 | tf_op jit(solution)/shard_map/all_to_all | solution.py:217
  108.3 3.2 %shard_map.75 = bf16[494,4096]{1,0:T(8,128)(2,1)} custom-call(bf16[256,512]{1,0:T(8,128)(2,1)S(1)} %get-tuple-element.18.refs_0_, bf16[256,512]{1,0:T(8,128)(2,1)S(1)} %collective-permute-done.refs_1_, bf16[256,512]{1,0:T(8,128)(2,1)S(1)} %collective-permute-done.1.refs_2_, bf16[256,512]{1,0:T(8,128)(2,1)S(1)} %collective-permute-done.2.refs_3_, ...), custom_call_target="tpu_custom_call" | custom-call | flops 1035993088 | bytes 6396928 | tf_op jit(solution)/shard_map/pallas_call | solution.py:28
  111.5 18.0 %all-to-all-done.2 = bf16[256,2,512]{2,1,0:T(2,128)(2,1)S(1)} async-done(((bf16[256,2,512]{2,1,0:T(2,128)(2,1)}), bf16[256,2,512]{2,1,0:T(2,128)(2,1)S(1)}, u32[]{:S(2)}, u32[]{:S(2)}) %all-to-all-start.2) | async-done | bytes 524320 | tf_op jit(solution)/shard_map/all_to_all | solution.py:217
  129.6 0.4 reduce
  130.0 0.6 convert_element_type.67
  (28 shorter events, 2.4 us)
Async XLA Ops:
  1.3 1.0 copy-start.2
  2.3 0.7 copy-start.4
  34.3 13.7 %collective-permute-start.5 = (bf16[256,512]{1,0:T(8,128)(2,1)S(1)}, bf16[256,512]{1,0:T(8,128)(2,1)S(1)}, u32[]{:S(2)}, u32[]{:S(2)}) collective-permute-start(bf16[256,512]{1,0:T(8,128)(2,1)S(1)} %get-tuple-element.18.refs_0_), channel_id=1, source_target_pairs={{0,3},{1,0},{2,1},{3,2},{4,7},{5,4},{6,5},{7,6},{8,11},{9,8},{10,9... | collective-permute-start | bytes 786440 | tf_op jit(solution)/shard_map/ppermute | solution.py:161
  37.1 12.1 %collective-permute-start.3 = (bf16[256,512]{1,0:T(8,128)(2,1)S(1)}, bf16[256,512]{1,0:T(8,128)(2,1)S(1)}, u32[]{:S(2)}, u32[]{:S(2)}) collective-permute-start(bf16[256,512]{1,0:T(8,128)(2,1)S(1)} %get-tuple-element.18.refs_0_), channel_id=1, source_target_pairs={{0,2},{1,3},{2,0},{3,1},{4,6},{5,7},{6,4},{7,5},{8,10},{9,11},{10,... | collective-permute-start | bytes 786440 | tf_op jit(solution)/shard_map/ppermute | solution.py:161
  37.5 15.0 %collective-permute-start.1 = (bf16[256,512]{1,0:T(8,128)(2,1)S(1)}, bf16[256,512]{1,0:T(8,128)(2,1)S(1)}, u32[]{:S(2)}, u32[]{:S(2)}) collective-permute-start(bf16[256,512]{1,0:T(8,128)(2,1)S(1)} %get-tuple-element.18.refs_0_), channel_id=1, source_target_pairs={{0,1},{1,2},{2,3},{3,0},{4,5},{5,6},{6,7},{7,4},{8,9},{9,10},{10,1... | collective-permute-start | bytes 786440 | tf_op jit(solution)/shard_map/ppermute | solution.py:161
  38.2 16.3 %collective-permute-start = (bf16[256,512]{1,0:T(8,128)(2,1)S(1)}, bf16[256,512]{1,0:T(8,128)(2,1)S(1)}, u32[]{:S(2)}, u32[]{:S(2)}) collective-permute-start(bf16[256,512]{1,0:T(8,128)(2,1)S(1)} %get-tuple-element.18.refs_0_), channel_id=1, source_target_pairs={{0,4},{4,0},{1,5},{5,1},{2,6},{6,2},{3,7},{7,3},{8,12},{12,8},{9,1... | collective-permute-start | bytes 786440 | tf_op jit(solution)/shard_map/ppermute | solution.py:157
  48.0 6.5 %collective-permute-start.6 = (bf16[256,512]{1,0:T(8,128)(2,1)S(1)}, bf16[256,512]{1,0:T(8,128)(2,1)S(1)}, u32[]{:S(2)}, u32[]{:S(2)}) collective-permute-start(bf16[256,512]{1,0:T(8,128)(2,1)S(1)} %collective-permute-done.5.refs_6_), channel_id=1, source_target_pairs={{0,4},{4,0},{1,5},{5,1},{2,6},{6,2},{3,7},{7,3},{8,12},{12,8},{9,1... | collective-permute-start | bytes 786440 | tf_op jit(solution)/shard_map/ppermute | solution.py:157
  49.3 5.2 %collective-permute-start.4 = (bf16[256,512]{1,0:T(8,128)(2,1)S(1)}, bf16[256,512]{1,0:T(8,128)(2,1)S(1)}, u32[]{:S(2)}, u32[]{:S(2)}) collective-permute-start(bf16[256,512]{1,0:T(8,128)(2,1)S(1)} %collective-permute-done.3.refs_4_), channel_id=1, source_target_pairs={{0,4},{4,0},{1,5},{5,1},{2,6},{6,2},{3,7},{7,3},{8,12},{12,8},{9,1... | collective-permute-start | bytes 786440 | tf_op jit(solution)/shard_map/ppermute | solution.py:157
  52.5 2.0 %collective-permute-start.2 = (bf16[256,512]{1,0:T(8,128)(2,1)S(1)}, bf16[256,512]{1,0:T(8,128)(2,1)S(1)}, u32[]{:S(2)}, u32[]{:S(2)}) collective-permute-start(bf16[256,512]{1,0:T(8,128)(2,1)S(1)} %collective-permute-done.1.refs_2_), channel_id=1, source_target_pairs={{0,4},{4,0},{1,5},{5,1},{2,6},{6,2},{3,7},{7,3},{8,12},{12,8},{9,1... | collective-permute-start | bytes 786440 | tf_op jit(solution)/shard_map/ppermute | solution.py:157
  53.0 1.0 copy-start.3
  54.5 2.2 %copy-start = (bf16[4096,494]{0,1:T(8,128)(2,1)S(1)}, bf16[4096,494]{0,1:T(8,128)(2,1)}, u32[]{:S(2)}) copy-start(bf16[4096,494]{0,1:T(8,128)(2,1)} %param.6) | copy-start | bytes 12140548
  56.7 25.0 %copy-start.1 = (bf16[4096,494]{0,1:T(8,128)(2,1)S(1)}, bf16[4096,494]{0,1:T(8,128)(2,1)}, u32[]{:S(2)}) copy-start(bf16[4096,494]{0,1:T(8,128)(2,1)} %param.6) | copy-start | bytes 12140548
  78.4 3.2 %collective-permute-start.7 = (f32[2,256]{1,0:T(2,128)S(1)}, f32[2,256]{1,0:T(2,128)S(1)}, u32[]{:S(2)}, u32[]{:S(2)}) collective-permute-start(f32[2,256]{1,0:T(2,128)S(1)} %shard_map.72.mine), channel_id=1, source_target_pairs={{0,4},{4,0},{1,5},{5,1},{2,6},{6,2},{3,7},{7,3},{8,12},{12,8},{9,1... | collective-permute-start | bytes 6152 | tf_op jit(solution)/shard_map/ppermute | solution.py:157
  83.1 1.6 %collective-permute-start.9 = (bf16[256,512]{1,0:T(8,128)(2,1)S(1)}, bf16[256,512]{1,0:T(8,128)(2,1)S(1)}, u32[]{:S(2)}, u32[]{:S(2)}) collective-permute-start(bf16[256,512]{1,0:T(8,128)(2,1)S(1)} %get-tuple-element.28), channel_id=1, source_target_pairs={{0,4},{4,0},{1,5},{5,1},{2,6},{6,2},{3,7},{7,3},{8,12},{12,8},{9,1... | collective-permute-start | bytes 786440 | tf_op jit(solution)/shard_map/ppermute | solution.py:157
  83.5 1.6 %collective-permute-start.11 = (bf16[256,512]{1,0:T(8,128)(2,1)S(1)}, bf16[256,512]{1,0:T(8,128)(2,1)S(1)}, u32[]{:S(2)}, u32[]{:S(2)}) collective-permute-start(bf16[256,512]{1,0:T(8,128)(2,1)S(1)} %get-tuple-element.30), channel_id=1, source_target_pairs={{0,4},{4,0},{1,5},{5,1},{2,6},{6,2},{3,7},{7,3},{8,12},{12,8},{9,1... | collective-permute-start | bytes 786440 | tf_op jit(solution)/shard_map/ppermute | solution.py:157
  83.8 4.3 %collective-permute-start.8 = (bf16[256,512]{1,0:T(8,128)(2,1)S(1)}, bf16[256,512]{1,0:T(8,128)(2,1)S(1)}, u32[]{:S(2)}, u32[]{:S(2)}) collective-permute-start(bf16[256,512]{1,0:T(8,128)(2,1)S(1)} %get-tuple-element.26), channel_id=1, source_target_pairs={{0,4},{4,0},{1,5},{5,1},{2,6},{6,2},{3,7},{7,3},{8,12},{12,8},{9,1... | collective-permute-start | bytes 786440 | tf_op jit(solution)/shard_map/ppermute | solution.py:157
  84.0 2.6 %collective-permute-start.13 = (bf16[256,512]{1,0:T(8,128)(2,1)S(1)}, bf16[256,512]{1,0:T(8,128)(2,1)S(1)}, u32[]{:S(2)}, u32[]{:S(2)}) collective-permute-start(bf16[256,512]{1,0:T(8,128)(2,1)S(1)} %get-tuple-element.32), channel_id=1, source_target_pairs={{0,4},{4,0},{1,5},{5,1},{2,6},{6,2},{3,7},{7,3},{8,12},{12,8},{9,1... | collective-permute-start | bytes 786440 | tf_op jit(solution)/shard_map/ppermute | solution.py:157
  84.8 14.5 %collective-permute-start.10 = (bf16[256,512]{1,0:T(8,128)(2,1)S(1)}, bf16[256,512]{1,0:T(8,128)(2,1)S(1)}, u32[]{:S(2)}, u32[]{:S(2)}) collective-permute-start(bf16[256,512]{1,0:T(8,128)(2,1)S(1)} %add_convert_fusion.2), channel_id=1, source_target_pairs={{0,1},{1,2},{2,3},{3,0},{4,5},{5,6},{6,7},{7,4},{8,9},{9,10},{10,1... | collective-permute-start | bytes 786440 | tf_op jit(solution)/shard_map/ppermute | solution.py:161
  85.1 14.1 %collective-permute-start.12 = (bf16[256,512]{1,0:T(8,128)(2,1)S(1)}, bf16[256,512]{1,0:T(8,128)(2,1)S(1)}, u32[]{:S(2)}, u32[]{:S(2)}) collective-permute-start(bf16[256,512]{1,0:T(8,128)(2,1)S(1)} %add_convert_fusion.1), channel_id=1, source_target_pairs={{0,2},{1,3},{2,0},{3,1},{4,6},{5,7},{6,4},{7,5},{8,10},{9,11},{10,... | collective-permute-start | bytes 786440 | tf_op jit(solution)/shard_map/ppermute | solution.py:161
  86.6 13.1 %collective-permute-start.14 = (bf16[256,512]{1,0:T(8,128)(2,1)S(1)}, bf16[256,512]{1,0:T(8,128)(2,1)S(1)}, u32[]{:S(2)}, u32[]{:S(2)}) collective-permute-start(bf16[256,512]{1,0:T(8,128)(2,1)S(1)} %add_convert_fusion), channel_id=1, source_target_pairs={{0,3},{1,0},{2,1},{3,2},{4,7},{5,4},{6,5},{7,6},{8,11},{9,8},{10,9... | collective-permute-start | bytes 786440 | tf_op jit(solution)/shard_map/ppermute | solution.py:161
  101.1 28.5 %all-to-all-start.2 = ((bf16[256,2,512]{2,1,0:T(2,128)(2,1)}), bf16[256,2,512]{2,1,0:T(2,128)(2,1)S(1)}, u32[]{:S(2)}, u32[]{:S(2)}) async-start(bf16[256,2,512]{2,1,0:T(2,128)(2,1)} %reshape.16), calls=%async_computation.2 | async-start | bytes 1048576 | tf_op jit(solution)/shard_map/all_to_all | solution.py:217

commit v2 on v1

v2 whole, which is shorter than its diff:
```python
import jax
import jax.numpy as jnp
from jax import lax
from jax.experimental import pallas as pl
from jax.experimental.pallas import tpu as pltpu
from jax.sharding import Mesh, PartitionSpec as P

LOSS_SCALE = 1024.0
MASKED = 256
MARK = 64.0

SEQ = ("x", "z", "core")
ALL = ("x", "z", "core", "y")
CHIPS = ("x", "z", "y")
PLANE = ("x", "y")
NX, NZ, NCORE, NY = 4, 8, 2, 4
BLOCKS = NX * NY
F32, BF16 = jnp.float32, jnp.bfloat16
NT = (((1,), (1,)), ((), ()))
TN = (((0,), (0,)), ((), ()))
VMEM = pl.BlockSpec(memory_space=pltpu.VMEM)
HBM = pl.BlockSpec(memory_space=pltpu.HBM)
DMA = pltpu.SemaphoreType.DMA


def call(body, out, *args, specs=None, flops=0, scratch=()):
    leaves = jax.tree.leaves((args, out))
    nbytes = sum(x.size * x.dtype.itemsize for x in leaves)
    return pl.pallas_call(
        body,
        out_shape=out,
        in_specs=specs or [VMEM] * len(args),
        out_specs=jax.tree.map(lambda _: VMEM, out),
        scratch_shapes=list(scratch),
        cost_estimate=pl.CostEstimate(flops=flops, bytes_accessed=nbytes, transcendentals=0),
        compiler_params=pltpu.CompilerParams(vmem_limit_bytes=32 * 2**20),
    )(*args)


def shape(dims, dtype):
    return jax.ShapeDtypeStruct(dims, dtype)


def columns(block, width):
    return pl.ds(pl.multiple_of(block * width, width), width)


def pick_body(positions_hbm, counts_hbm, hidden, out, positions, counts, mine, sems):
    shards, capacity, width = out.shape
    tokens = hidden.shape[0]
    pair = NCORE * width
    y = lax.axis_index("y")
    copies = [
        pltpu.make_async_copy(positions_hbm, positions, sems.at[0]),
        pltpu.make_async_copy(counts_hbm, counts, sems.at[1]),
    ]
    for x in range(NX):
        copies.append(
            pltpu.make_async_copy(
                hidden.at[:, columns(x * NY + y, pair)],
                mine.at[:, x * pair : (x + 1) * pair],
                sems.at[2 + x],
            )
        )
    for copy in copies:
        copy.start()
    for copy in copies:
        copy.wait()
    row = lax.broadcasted_iota(jnp.int32, (2 * capacity, tokens), 0)
    column = lax.broadcasted_iota(jnp.int32, (2 * capacity, tokens), 1)
    hot = jnp.zeros((2 * capacity, tokens), F32)
    for k in range(capacity):
        hot = jnp.where((row == k) & (column == positions[0, k]), 1.0, hot)
    rows = jnp.dot(hot.astype(BF16), mine[...], preferred_element_type=F32)[:capacity]
    rank = lax.broadcasted_iota(jnp.int32, rows.shape, 0)
    rows = jnp.where(rank < counts[0], rows, MARK).astype(BF16)
    for s in range(shards):
        start = s // (NZ * NCORE) * pair + s % NCORE * width
        out[s] = rows[:, start : start + width]


def compact_body(rows, picked, chosen, count):
    slots = rows.shape[0]
    capacity = 8
    valid = (rows[...].astype(F32)[:, 0:1] < MARK / 2).astype(F32)
    a = lax.broadcasted_iota(jnp.int32, (slots, slots), 0)
    b = lax.broadcasted_iota(jnp.int32, (slots, slots), 1)
    spread = jnp.broadcast_to(valid, (slots, slots))
    rank = jnp.sum(jnp.where(a < b, spread, 0.0), axis=0, keepdims=True)
    mine = jnp.sum(jnp.where(a == b, spread, 0.0), axis=0, keepdims=True)
    total = jnp.sum(jnp.where(a // capacity == b // capacity, spread, 0.0), axis=0, keepdims=True)
    place = jnp.where(mine > 0.5, rank, -1.0).astype(jnp.int32)
    target = lax.broadcasted_iota(jnp.int32, (MASKED, slots), 0)
    hot = (target == place).astype(F32).astype(BF16)
    chosen[...] = hot
    mine = jnp.dot(hot, rows[...], preferred_element_type=F32).astype(BF16)
    for i in range(picked.shape[0]):
        picked[i] = mine
    totals = jnp.broadcast_to(total, (8, slots)).astype(BF16)
    count[...] = lax.dot_general(totals, hot, NT, preferred_element_type=F32)


def logsumexp(x):
    top = jnp.max(x, axis=0, keepdims=True)
    return top + jnp.log(jnp.sum(jnp.exp(x - top), axis=0, keepdims=True))


def stage_body(teacher_hbm, weight_hbm, chosen, out, lse, ours, theirs, back, teacher, sems):
    width = ours.shape[1] // BLOCKS
    core = lax.axis_index("core")
    move_teacher = pltpu.make_async_copy(teacher_hbm, teacher, sems.at[0])
    copies = []
    for which, (target, side) in enumerate(((ours, core), (theirs, 1 - core))):
        for b in range(BLOCKS):
            copies.append(
                pltpu.make_async_copy(
                    weight_hbm.at[:, columns(b * NCORE + side, width)],
                    target.at[:, b * width : (b + 1) * width],
                    sems.at[1 + which * BLOCKS + b],
                )
            )
    move_teacher.start()
    for copy in copies:
        copy.start()
    sent, masked = back.shape
    slots = chosen.shape[1]
    row = lax.broadcasted_iota(jnp.int32, (sent, slots), 0)
    chip, q = row // 4, row % 4
    slot = chip // NY * 16 + q // 2 * 8 + chip % NY * 2 + q % 2
    column = lax.broadcasted_iota(jnp.int32, (sent, slots), 1)
    pick = (column == slot).astype(F32).astype(BF16)
    back[...] = lax.dot_general(pick, chosen[...], NT, preferred_element_type=F32).astype(BF16)
    move_teacher.wait()
    rows = lax.dot_general(teacher[...], chosen[...], NT, preferred_element_type=F32)
    out[...] = rows.astype(BF16)
    lse[...] = jnp.broadcast_to(logsumexp(rows), lse.shape)
    for copy in copies:
        copy.wait()


def lay_out(blocks, flat):
    width = blocks.shape[2]
    for b in range(blocks.shape[0]):
        flat[:, b * width : (b + 1) * width] = blocks[b]


def student_ours_body(blocks, weight, total, flat):
    lay_out(blocks, flat)
    total[...] = lax.dot_general(weight[...], flat[...], NT, preferred_element_type=F32)


def student_theirs_body(blocks, weight, first, lse_teacher, out, stats, flat):
    lay_out(blocks, flat)
    total = first[...] + lax.dot_general(weight[...], flat[...], NT, preferred_element_type=F32)
    out[...] = total
    both = jnp.concatenate([logsumexp(total), lse_teacher[0:1, :]], axis=0)
    stats[...] = jnp.broadcast_to(both[None], stats.shape)


def combine_body(stats, out):
    x = stats[...]
    top = jnp.max(x, axis=0)
    out[...] = top + jnp.log(jnp.sum(jnp.exp(x - top[None]), axis=0))


def products(grad, weight, parts):
    width = parts.shape[2]
    for b in range(0, parts.shape[0], 2):
        both = lax.dot_general(
            grad, weight[:, b * width : (b + 2) * width], TN, preferred_element_type=F32
        ).astype(parts.dtype)
        parts[b] = both[:, :width]
        parts[b + 1] = both[:, width:]


def logits_body(student, teacher, mine, other, count, weight, grad_logits, parts):
    top = jnp.maximum(mine[...], other[...])
    lse = top + jnp.log(jnp.exp(mine[...] - top) + jnp.exp(other[...] - top))
    scale = LOSS_SCALE / count[0:1, :]
    prob_student = jnp.exp(student[...] - lse[0:1, :])
    prob_teacher = jnp.exp(teacher[...].astype(F32) - lse[1:2, :])
    grad = (scale * (prob_student - prob_teacher)).astype(BF16)
    grad_logits[...] = grad
    products(grad, weight, parts)


def products_body(grad_logits, weight, parts):
    products(grad_logits[...], weight, parts)


def head_body(ours, theirs, grad_logits, out):
    core = lax.axis_index("core")
    width = ours.shape[1] // BLOCKS
    for flat, side in ((ours, core), (theirs, 1 - core)):
        for b in range(0, BLOCKS, 2):
            both = jnp.dot(
                grad_logits[...], flat[:, b * width : (b + 2) * width], preferred_element_type=F32
            ).astype(BF16)
            out[:, columns(b * NCORE + side, width)] = both[:, :width]
            out[:, columns((b + 1) * NCORE + side, width)] = both[:, width:]


def spread_body(parts, back, out):
    total = parts[0].astype(F32)
    for i in range(1, parts.shape[0]):
        total += parts[i].astype(F32)
    rows = jnp.dot(back[...], total.astype(BF16), preferred_element_type=F32)
    out[...] = rows.astype(BF16)


def collect_body(parts, mine, other):
    chips, rows, width = parts.shape
    total = jnp.sum(parts[...].astype(F32).reshape(NX, NZ, NY, rows, width), axis=1)
    total = total.reshape(NX * NY, rows, width)
    low, high = total[:, : rows // 2], total[:, rows // 2 :]
    first = lax.axis_index("core") == 0
    mine[...] = jnp.where(first, low, high)
    other[...] = jnp.where(first, high, low)


def finish_body(mine, other, out, whole):
    blocks, rows, width = mine.shape
    first = lax.axis_index("core") == 0
    by_core = (
        jnp.where(first, mine[...], other[...]), jnp.where(first, other[...], mine[...]),
    )
    for b in range(blocks):
        for core in range(NCORE):
            start = (b * NCORE + core) * width
            whole[:, start : start + width] = by_core[core][b]
    out[...] = whole[...].astype(BF16)


def swap_core(x):
    return lax.ppermute(x, "core", [(0, 1), (1, 0)])


def per_device(hidden, head_weight, teacher, positions, counts):
    tokens, depth = hidden.shape
    capacity = positions.shape[1]
    shards = NX * NZ * NCORE
    slots = shards * capacity
    vocab = head_weight.shape[1]
    width = depth // (BLOCKS * NCORE)
    share = depth // NCORE
    own = capacity // NY
    chips = NX * NZ * NY
    products_flops = vocab * depth * MASKED
    parts_shape = shape((BLOCKS, MASKED, width), BF16)

    send = call(
        pick_body, shape((shards, capacity, width), BF16), positions, counts, hidden,
        specs=[HBM] * 3,
        scratch=[
            pltpu.SMEM(positions.shape, jnp.int32), pltpu.SMEM(counts.shape, jnp.int32),
            pltpu.VMEM((tokens, NX * NCORE * width), BF16), DMA((2 + NX,)),
        ],
    )
    rows = lax.all_to_all(send, SEQ, 0, 0, tiled=True).reshape(slots, width)
    picked, chosen, count = call(
        compact_body,
        (parts_shape, shape((MASKED, slots), BF16), shape((8, MASKED), F32)),
        rows, flops=2 * MASKED * slots * width,
    )
    blocks = lax.all_to_all(picked, PLANE, 0, 0, tiled=True)
    staged = call(
        stage_body,
        (
            shape((vocab, MASKED), BF16), shape((8, MASKED), F32),
            shape((vocab, share), BF16), shape((vocab, share), BF16),
            shape((slots, MASKED), BF16),
        ),
        teacher.T, head_weight.T, chosen, specs=[HBM, HBM, VMEM],
        scratch=[pltpu.VMEM((vocab, slots), BF16), DMA((1 + 2 * BLOCKS,))],
        flops=2 * vocab * slots * MASKED + 2 * slots * slots * MASKED,
    )
    blocks, staged = lax.optimization_barrier((blocks, staged))
    teacher_rows, lse_teacher, weight_ours, weight_theirs, back = staged
    total, flat_ours = call(
        student_ours_body,
        (shape((vocab, MASKED), F32), shape((MASKED, share), BF16)),
        blocks, weight_ours, flops=products_flops,
    )
    student, stats, flat_theirs = call(
        student_theirs_body,
        (
            shape((vocab, MASKED), F32), shape((chips, 2, MASKED), F32),
            shape((MASKED, share), BF16),
        ),
        swap_core(blocks), weight_theirs, total, lse_teacher, flops=products_flops,
    )
    stats = lax.all_to_all(stats, CHIPS, 0, 0, tiled=True)
    half = call(combine_body, shape((2, MASKED), F32), stats)
    grad_logits, parts_theirs = call(
        logits_body, (shape((vocab, MASKED), BF16), parts_shape),
        student, teacher_rows, half, swap_core(half), count, weight_theirs, flops=products_flops,
    )
    parts_ours = call(
        products_body, shape(parts_shape.shape, F32), grad_logits, weight_ours,
        flops=products_flops,
    )
    parts = (parts_ours + swap_core(parts_theirs).astype(F32)).astype(BF16)
    parts = lax.all_to_all(parts, PLANE, 0, 0, tiled=True)
    grad_head = call(
        head_body, shape((vocab, depth), BF16), flat_ours, flat_theirs, grad_logits,
        flops=2 * products_flops,
    )
    parts, grad_head = lax.optimization_barrier((parts, grad_head))
    partial = call(
        spread_body, shape((slots, width), BF16), parts, back, flops=2 * MASKED * slots * width,
    )
    partial = lax.all_to_all(
        partial.reshape(chips, NCORE * own, width), CHIPS, 0, 0, tiled=True
    )
    mine, other = call(collect_body, (shape((BLOCKS, own, width), F32),) * 2, partial)
    grad_hidden = call(
        finish_body, shape((own, depth), BF16), mine, swap_core(other),
        scratch=[pltpu.VMEM((own, depth), F32)],
    )
    return grad_hidden, grad_head.T


def solution(mesh):
    fine = Mesh(mesh.devices.reshape(NX, NZ, NCORE, NY), ALL)
    return jax.shard_map(
        per_device,
        mesh=fine,
        in_specs=(P(SEQ, None), P(None, ALL), P(None, ALL), P(SEQ, None), P(SEQ)),
        out_specs=(P(ALL, None), P(None, ALL)),
        check_vma=False,
    )
```

time: 131 us -> 129 us (0.985)
  waiting for transfers between devices: 42.8 us -> 22.4 us
  blocking collectives: 50.2 us -> 60.5 us
  Pallas kernels: 8.32 us -> 13 us
  local copies, waits for them, and re-layouts: 6.51 us -> 11.1 us
  starting transfers between devices: 20.7 us -> 18.8 us
    ppermute x6 -> x0, waiting for transfers between devices: 23.3 us -> none  [shift_y(): return lax.ppermute(x, 'y', [(i, (i + k) % NY) for i in range(NY)])]
    all_to_all x0 -> x1, blocking collectives: none -> 18 us  [per_device(): lax.all_to_all(partial.reshape(chips, NCORE * own, width), CHIPS, 0, 0, t...]
    all_to_all x1, blocking collectives: 30.1 us -> 23.1 us  [per_device(): rows = lax.all_to_all(send, SEQ, 0, 0, tiled=True).reshape(slots, width)]
    ppermute x6 -> x0, starting transfers between devices: 6.89 us -> none  [shift_y(): return lax.ppermute(x, 'y', [(i, (i + k) % NY) for i in range(NY)])]
    unnamed x10 -> x26, local copies, waits for them, and re-layouts: 4.87 us -> 11.1 us
    pallas_call x8 -> x12, Pallas kernels: 8.32 us -> 13 us  [call(): pl.pallas_call(body, out_shape=out, in_specs=specs or [VMEM] * len(args),...]
    ppermute x9 -> x4, starting transfers between devices: 6.56 us -> 9.19 us  [swap_core(): return lax.ppermute(x, 'core', [(0, 1), (1, 0)])]
    all_to_all x1 -> x2, starting transfers between devices: 7.23 us -> 9.58 us  [the longest x1 5.61 us: per_device(): blocks = lax.all_to_all(picked, PLANE, 0, 0, tiled=True)]
  transfers between devices with their start and end apart: 16 -> 6, of which waited for: 8 -> 5; matrix products, arithmetic and copies ran while one was open for 0% -> 0% of each run, Pallas kernels for 3% -> 6%
where the time goes in v2:
time: 129 us; the launch traced here: 128 us
  blocking collectives  60.5 us (47%)
  waiting for transfers between devices  22.4 us (17%)
  starting transfers between devices  18.8 us (15%)
  Pallas kernels  13 us (10%)
  local copies, waits for them, and re-layouts  11.1 us (9%)
  between operations  1.42 us (1%)
    all_to_all x1, blocking collectives, per_device(): rows = lax.all_to_all(send, SEQ, 0, 0, tiled=True).reshape(slots, width)  23.1 us
    all_to_all x1, blocking collectives, per_device(): stats = lax.all_to_all(stats, CHIPS, 0, 0, tiled=True)  19.3 us
    all_to_all x1, blocking collectives, per_device(): lax.all_to_all(partial.reshape(chips, NCORE * own, width), CHIPS, 0, 0, t...  18 us
    pallas_call x12, Pallas kernels, call(): pl.pallas_call(body, out_shape=out, in_specs=specs or [VMEM] * len(args),...  13 us
    all_to_all x1, waiting for transfers between devices, per_device(): parts = lax.all_to_all(parts, PLANE, 0, 0, tiled=True)  12.9 us
    unnamed x26, local copies, waits for them, and re-layouts  11.1 us
    ppermute x4, starting transfers between devices, swap_core(): return lax.ppermute(x, 'core', [(0, 1), (1, 0)])  9.19 us
    all_to_all x1, waiting for transfers between devices, per_device(): blocks = lax.all_to_all(picked, PLANE, 0, 0, tiled=True)  6.24 us
  transfers between devices with their start and end apart: 6, of which 5 were waited for; matrix products, arithmetic and copies ran while one was open for 0% of the time, Pallas kernels for 6%

profile of v2, /device:TPU:1, one launch (start us, length us, event | category | flops | bytes accessed | tf_op | source)
XLA Modules:
  0.0 128.3 jit_solution(11835178561635715439)
XLA Ops:
  1.3 1.0 copy-done.6
  2.3 0.7 copy-done.12
  3.0 0.7 shard_map.68
  3.7 23.1 %all_to_all.25 = bf16[64,8,128]{2,1,0:T(8,128)(2,1)S(1)} all-to-all(bf16[64,8,128]{2,1,0:T(8,128)(2,1)S(1)} %shard_map.68), channel_id=1, replica_groups=mesh['x'=4,'z'=8,'core'=2,'y'=4] {'x','z','core'}, dimensions={0} | all-to-all | bytes 262144 | tf_op jit(solution)/shard_map/all_to_all | solution.py:259
  26.9 1.5 %shard_map.69 = (bf16[16,256,128]{2,1,0:T(8,128)(2,1)}, bf16[256,512]{1,0:T(8,128)(2,1)S(1)}, f32[8,256]{1,0:T(8,128)S(1)}) custom-call(bf16[512,128]{1,0:T(8,128)(2,1)S(1)} %bitcast.6), custom_call_target="tpu_custom_call" | custom-call | flops 33554432 | bytes 1449984 | tf_op jit(solution)/shard_map/pallas_call | solution.py:29
  28.4 5.6 %all-to-all-start.1 = ((bf16[16,256,128]{2,1,0:T(8,128)(2,1)}), bf16[16,256,128]{2,1,0:T(8,128)(2,1)S(1)}, u32[]{:S(2)}, u32[]{:S(2)}) async-start(bf16[16,256,128]{2,1,0:T(8,128)(2,1)} %get-tuple-element.27), calls=%async_computation.1 | async-start | bytes 2097152 | tf_op jit(solution)/shard_map/all_to_all | solution.py:265
  34.0 2.1 %copy-done.3 = bf16[4096,494]{0,1:T(8,128)(2,1)S(1)} copy-done((bf16[4096,494]{0,1:T(8,128)(2,1)S(1)}, bf16[4096,494]{0,1:T(8,128)(2,1)}, u32[]{:S(2)}) %copy-start.3) | copy-done | bytes 4046872
  36.2 1.0 copy-done.7
  37.2 2.9 %shard_map.70 = (bf16[494,256]{1,0:T(8,128)(2,1)S(1)}, f32[8,256]{1,0:T(8,128)S(1)}, bf16[494,2048]{1,0:T(8,128)(2,1)S(1)}, bf16[494,2048]{1,0:T(8,128)(2,1)S(1)}, bf16[512,256]{1,0:T(8,128)(2,1)S(1)}) custom-call(bf16[494,512]{1,0:T(8,128)(2,1)S(1)} %bitcast.8, bf16[494,4096]{1,0:T(8,128)(2,1)S(1)} %bitcast.5, bf16[256,512]{1,0:T(8,128)(2,1)S(1)} %get-tuple-element.28.chosen), custom_call_target="tpu_custom_call" | custom-call | flops 263716864 | bytes 9384960 | tf_op jit(solution)/shard_map/pallas_call | solution.py:29
  40.1 1.3 %copy-done = bf16[494,2048]{1,0:T(8,128)(2,1)} copy-done((bf16[494,2048]{1,0:T(8,128)(2,1)}, bf16[494,2048]{1,0:T(8,128)(2,1)S(1)}, u32[]{:S(2)}) %copy-start) | copy-done | bytes 2023448
  41.4 0.7 copy-done.8
  42.1 0.7 copy-done.10
  42.8 6.2 %all-to-all-done.1.blocks = bf16[16,256,128]{2,1,0:T(8,128)(2,1)S(1)} async-done(((bf16[16,256,128]{2,1,0:T(8,128)(2,1)}), bf16[16,256,128]{2,1,0:T(8,128)(2,1)S(1)}, u32[]{:S(2)}, u32[]{:S(2)}) %all-to-all-start.1) | async-done | bytes 1048608 | tf_op jit(solution)/shard_map/all_to_all | solution.py:265
  49.0 3.7 %collective-permute-start = (bf16[16,256,128]{2,1,0:T(8,128)(2,1)S(1)}, bf16[16,256,128]{2,1,0:T(8,128)(2,1)S(1)}, u32[]{:S(2)}, u32[]{:S(2)}) collective-permute-start(bf16[16,256,128]{2,1,0:T(8,128)(2,1)S(1)} %all-to-all-done.1.blocks), channel_id=1, source_target_pairs={{0,4},{4,0},{1,5},{5,1},{2,6},{6,2},{3,7},{7,3},{8,12},{12,8},{9,1... | collective-permute-start | bytes 3145736 | tf_op jit(solution)/shard_map/ppermute | solution.py:235
  52.8 1.6 %copy-done.1 = bf16[494,2048]{1,0:T(8,128)(2,1)S(1)} copy-done((bf16[494,2048]{1,0:T(8,128)(2,1)S(1)}, bf16[494,2048]{1,0:T(8,128)(2,1)}, u32[]{:S(2)}) %copy-start.1) | copy-done | bytes 2023448
  54.3 0.8 shard_map.71
  55.1 1.0 copy-done.4
  56.1 1.0 shard_map.72
  57.2 19.3 %all_to_all.26.stats = f32[128,2,256]{2,1,0:T(2,128)S(1)} all-to-all(f32[128,2,256]{2,1,0:T(2,128)S(1)} %get-tuple-element.41), channel_id=1, replica_groups=mesh['x'=4,'z'=8,'core'=2,'y'=4] {'x','z','y'}, dimensions={0} | all-to-all | bytes 524288 | tf_op jit(solution)/shard_map/all_to_all | solution.py:292
  76.7 2.1 %collective-permute-start.1 = (f32[2,256]{1,0:T(2,128)S(1)}, f32[2,256]{1,0:T(2,128)S(1)}, u32[]{:S(2)}, u32[]{:S(2)}) collective-permute-start(f32[2,256]{1,0:T(2,128)S(1)} %shard_map.73.mine), channel_id=1, source_target_pairs={{0,4},{4,0},{1,5},{5,1},{2,6},{6,2},{3,7},{7,3},{8,12},{12,8},{9,1... | collective-permute-start | bytes 6152 | tf_op jit(solution)/shard_map/ppermute | solution.py:235
  78.8 0.8 collective-permute-done.1.other
  79.7 0.9 shard_map.74
  80.9 0.7 shard_map.75
  81.7 1.6 %collective-permute-done.2 = bf16[16,256,128]{2,1,0:T(8,128)(2,1)S(1)} collective-permute-done((bf16[16,256,128]{2,1,0:T(8,128)(2,1)S(1)}, bf16[16,256,128]{2,1,0:T(8,128)(2,1)S(1)}, u32[]{:S(2)}, u32[]{:S(2)}) %collective-permute-start.2) | collective-permute-done | bytes 1048608 | tf_op jit(solution)/shard_map/ppermute | solution.py:235
  83.3 1.2 add_convert_fusion
  84.5 4.0 %all-to-all-start.3 = ((bf16[16,256,128]{2,1,0:T(8,128)(2,1)}), bf16[16,256,128]{2,1,0:T(8,128)(2,1)S(1)}, u32[]{:S(2)}, u32[]{:S(2)}) async-start(bf16[16,256,128]{2,1,0:T(8,128)(2,1)} %add_convert_fusion), calls=%async_computation.3 | async-start | bytes 2097152 | tf_op jit(solution)/shard_map/all_to_all | solution.py:303
  88.5 3.2 %shard_map.76 = bf16[494,4096]{1,0:T(8,128)(2,1)} custom-call(bf16[256,2048]{1,0:T(8,128)(2,1)S(1)} %copy-done.5, bf16[256,2048]{1,0:T(8,128)(2,1)S(1)} %get-tuple-element.46.theirs, bf16[494,256]{1,0:T(8,128)(2,1)S(1)} %get-tuple-element.43.grad_logits), custom_call_target="tpu_custom_call" | custom-call | flops 1035993088 | bytes 6396928 | tf_op jit(solution)/shard_map/pallas_call | solution.py:29
  91.7 12.9 %all-to-all-done.3.parts = bf16[16,256,128]{2,1,0:T(8,128)(2,1)S(1)} async-done(((bf16[16,256,128]{2,1,0:T(8,128)(2,1)}), bf16[16,256,128]{2,1,0:T(8,128)(2,1)S(1)}, u32[]{:S(2)}, u32[]{:S(2)}) %all-to-all-start.3) | async-done | bytes 1048608 | tf_op jit(solution)/shard_map/all_to_all | solution.py:303
  104.5 0.9 copy-done.9
  105.8 18.0 %all_to_all.27.parts = bf16[128,4,128]{2,1,0:T(4,128)(2,1)S(1)} all-to-all(bf16[128,4,128]{2,1,0:T(4,128)(2,1)S(1)} %bitcast.7), channel_id=1, replica_groups=mesh['x'=4,'z'=8,'core'=2,'y'=4] {'x','z','y'}, dimensions={0} | all-to-all | bytes 262144 | tf_op jit(solution)/shard_map/all_to_all | solution.py:312
  123.9 2.9 %collective-permute-start.3 = (f32[16,2,128]{2,1,0:T(2,128)S(1)}, f32[16,2,128]{2,1,0:T(2,128)S(1)}, u32[]{:S(2)}, u32[]{:S(2)}) collective-permute-start(f32[16,2,128]{2,1,0:T(2,128)S(1)} %get-tuple-element.50), channel_id=1, source_target_pairs={{0,4},{4,0},{1,5},{5,1},{2,6},{6,2},{3,7},{7,3},{8,12},{12,8},{9,1... | collective-permute-start | bytes 49160 | tf_op jit(solution)/shard_map/ppermute | solution.py:235
  126.8 0.8 collective-permute-done.3.other
  (22 shorter events, 1.7 us)
Async XLA Ops:
  1.3 1.0 copy-start.6
  2.3 0.7 copy-start.12
  28.4 20.6 %all-to-all-start.1 = ((bf16[16,256,128]{2,1,0:T(8,128)(2,1)}), bf16[16,256,128]{2,1,0:T(8,128)(2,1)S(1)}, u32[]{:S(2)}, u32[]{:S(2)}) async-start(bf16[16,256,128]{2,1,0:T(8,128)(2,1)} %get-tuple-element.27), calls=%async_computation.1 | async-start | bytes 2097152 | tf_op jit(solution)/shard_map/all_to_all | solution.py:265
  34.0 2.2 %copy-start.3 = (bf16[4096,494]{0,1:T(8,128)(2,1)S(1)}, bf16[4096,494]{0,1:T(8,128)(2,1)}, u32[]{:S(2)}) copy-start(bf16[4096,494]{0,1:T(8,128)(2,1)} %param.6) | copy-start | bytes 12140548
  36.2 1.0 copy-start.7
  40.1 1.3 %copy-start = (bf16[494,2048]{1,0:T(8,128)(2,1)}, bf16[494,2048]{1,0:T(8,128)(2,1)S(1)}, u32[]{:S(2)}) copy-start(bf16[494,2048]{1,0:T(8,128)(2,1)S(1)} %get-tuple-element.36.weight) | copy-start | bytes 6070276
  41.4 0.7 copy-start.8
  42.1 0.7 copy-start.10
  49.0 7.1 %collective-permute-start = (bf16[16,256,128]{2,1,0:T(8,128)(2,1)S(1)}, bf16[16,256,128]{2,1,0:T(8,128)(2,1)S(1)}, u32[]{:S(2)}, u32[]{:S(2)}) collective-permute-start(bf16[16,256,128]{2,1,0:T(8,128)(2,1)S(1)} %all-to-all-done.1.blocks), channel_id=1, source_target_pairs={{0,4},{4,0},{1,5},{5,1},{2,6},{6,2},{3,7},{7,3},{8,12},{12,8},{9,1... | collective-permute-start | bytes 3145736 | tf_op jit(solution)/shard_map/ppermute | solution.py:235
  52.8 1.6 %copy-start.1 = (bf16[494,2048]{1,0:T(8,128)(2,1)S(1)}, bf16[494,2048]{1,0:T(8,128)(2,1)}, u32[]{:S(2)}) copy-start(bf16[494,2048]{1,0:T(8,128)(2,1)} %copy-done) | copy-start | bytes 6070276
  55.1 1.0 copy-start.4
  56.1 23.5 %copy-start.11 = (bf16[494,256]{1,0:T(8,128)(2,1)S(1)}, bf16[494,256]{1,0:T(8,128)(2,1)}, u32[]{:S(2)}) copy-start(bf16[494,256]{1,0:T(8,128)(2,1)} %copy-done.10) | copy-start | bytes 758788
  57.1 23.8 %copy-start.2 = (bf16[494,2048]{1,0:T(8,128)(2,1)S(1)}, bf16[494,2048]{1,0:T(8,128)(2,1)}, u32[]{:S(2)}) copy-start(bf16[494,2048]{1,0:T(8,128)(2,1)} %copy-done) | copy-start | bytes 6070276
  76.7 2.9 %collective-permute-start.1 = (f32[2,256]{1,0:T(2,128)S(1)}, f32[2,256]{1,0:T(2,128)S(1)}, u32[]{:S(2)}, u32[]{:S(2)}) collective-permute-start(f32[2,256]{1,0:T(2,128)S(1)} %shard_map.73.mine), channel_id=1, source_target_pairs={{0,4},{4,0},{1,5},{5,1},{2,6},{6,2},{3,7},{7,3},{8,12},{12,8},{9,1... | collective-permute-start | bytes 6152 | tf_op jit(solution)/shard_map/ppermute | solution.py:235
  80.5 2.7 %collective-permute-start.2 = (bf16[16,256,128]{2,1,0:T(8,128)(2,1)S(1)}, bf16[16,256,128]{2,1,0:T(8,128)(2,1)S(1)}, u32[]{:S(2)}, u32[]{:S(2)}) collective-permute-start(bf16[16,256,128]{2,1,0:T(8,128)(2,1)S(1)} %get-tuple-element.44), channel_id=1, source_target_pairs={{0,4},{4,0},{1,5},{5,1},{2,6},{6,2},{3,7},{7,3},{8,12},{12,8},{9,1... | collective-permute-start | bytes 3145736 | tf_op jit(solution)/shard_map/ppermute | solution.py:235
  84.5 4.0 %copy-start.5 = (bf16[256,2048]{1,0:T(8,128)(2,1)S(1)}, bf16[256,2048]{1,0:T(8,128)(2,1)}, u32[]{:S(2)}) copy-start(bf16[256,2048]{1,0:T(8,128)(2,1)} %copy-done.4) | copy-start | bytes 3145732
  84.5 20.0 %all-to-all-start.3 = ((bf16[16,256,128]{2,1,0:T(8,128)(2,1)}), bf16[16,256,128]{2,1,0:T(8,128)(2,1)S(1)}, u32[]{:S(2)}, u32[]{:S(2)}) async-start(bf16[16,256,128]{2,1,0:T(8,128)(2,1)} %add_convert_fusion), calls=%async_computation.3 | async-start | bytes 2097152 | tf_op jit(solution)/shard_map/all_to_all | solution.py:303
  104.5 1.0 copy-start.9
  123.9 3.8 %collective-permute-start.3 = (f32[16,2,128]{2,1,0:T(2,128)S(1)}, f32[16,2,128]{2,1,0:T(2,128)S(1)}, u32[]{:S(2)}, u32[]{:S(2)}) collective-permute-start(f32[16,2,128]{2,1,0:T(2,128)S(1)} %get-tuple-element.50), channel_id=1, source_target_pairs={{0,4},{4,0},{1,5},{5,1},{2,6},{6,2},{3,7},{7,3},{8,12},{12,8},{9,1... | collective-permute-start | bytes 49160 | tf_op jit(solution)/shard_map/ppermute | solution.py:235

commit v3 on v2

--- a/solution.py
+++ b/solution.py
@@ -21,19 +21,20 @@
 VMEM = pl.BlockSpec(memory_space=pltpu.VMEM)
 HBM = pl.BlockSpec(memory_space=pltpu.HBM)
 DMA = pltpu.SemaphoreType.DMA
-
-
-def call(body, out, *args, specs=None, flops=0, scratch=()):
+LIMIT, WIDE_LIMIT = 32, 60
+
+
+def call(body, out, *args, specs=None, outs=VMEM, flops=0, scratch=(), limit=LIMIT):
     leaves = jax.tree.leaves((args, out))
     nbytes = sum(x.size * x.dtype.itemsize for x in leaves)
     return pl.pallas_call(
         body,
         out_shape=out,
         in_specs=specs or [VMEM] * len(args),
-        out_specs=jax.tree.map(lambda _: VMEM, out),
+        out_specs=jax.tree.map(lambda _: outs, out),
         scratch_shapes=list(scratch),
         cost_estimate=pl.CostEstimate(flops=flops, bytes_accessed=nbytes, transcendentals=0),
-        compiler_params=pltpu.CompilerParams(vmem_limit_bytes=32 * 2**20),
+        compiler_params=pltpu.CompilerParams(vmem_limit_bytes=limit * 2**20),
     )(*args)
 
 
@@ -105,23 +106,9 @@
     return top + jnp.log(jnp.sum(jnp.exp(x - top), axis=0, keepdims=True))
 
 
-def stage_body(teacher_hbm, weight_hbm, chosen, out, lse, ours, theirs, back, teacher, sems):
-    width = ours.shape[1] // BLOCKS
-    core = lax.axis_index("core")
-    move_teacher = pltpu.make_async_copy(teacher_hbm, teacher, sems.at[0])
-    copies = []
-    for which, (target, side) in enumerate(((ours, core), (theirs, 1 - core))):
-        for b in range(BLOCKS):
-            copies.append(
-                pltpu.make_async_copy(
-                    weight_hbm.at[:, columns(b * NCORE + side, width)],
-                    target.at[:, b * width : (b + 1) * width],
-                    sems.at[1 + which * BLOCKS + b],
-                )
-            )
-    move_teacher.start()
-    for copy in copies:
-        copy.start()
+def teacher_body(teacher_hbm, chosen, out, lse, back, teacher, sem):
+    move = pltpu.make_async_copy(teacher_hbm, teacher, sem)
+    move.start()
     sent, masked = back.shape
     slots = chosen.shape[1]
     row = lax.broadcasted_iota(jnp.int32, (sent, slots), 0)
@@ -130,12 +117,25 @@
     column = lax.broadcasted_iota(jnp.int32, (sent, slots), 1)
     pick = (column == slot).astype(F32).astype(BF16)
     back[...] = lax.dot_general(pick, chosen[...], NT, preferred_element_type=F32).astype(BF16)
-    move_teacher.wait()
+    move.wait()
     rows = lax.dot_general(teacher[...], chosen[...], NT, preferred_element_type=F32)
     out[...] = rows.astype(BF16)
     lse[...] = jnp.broadcast_to(logsumexp(rows), lse.shape)
-    for copy in copies:
-        copy.wait()
+
+
+def load_blocks(weight_hbm, target, side, sems):
+    width = target.shape[1] // BLOCKS
+    copies = [
+        pltpu.make_async_copy(
+            weight_hbm.at[:, columns(b * NCORE + side, width)],
+            target.at[:, b * width : (b + 1) * width],
+            sems.at[b],
+        )
+        for b in range(BLOCKS)
+    ]
+    for copy in copies:
+        copy.start()
+    return copies
 
 
 def lay_out(blocks, flat):
@@ -144,9 +144,16 @@
         flat[:, b * width : (b + 1) * width] = blocks[b]
 
 
-def student_ours_body(blocks, weight, total, flat):
+def student_ours_body(blocks, weight_hbm, total, theirs, ours, flat, sems, their_sems):
+    core = lax.axis_index("core")
+    copies = load_blocks(weight_hbm, ours, core, sems)
+    later = load_blocks(weight_hbm, theirs, 1 - core, their_sems)
     lay_out(blocks, flat)
-    total[...] = lax.dot_general(weight[...], flat[...], NT, preferred_element_type=F32)
+    for copy in copies:
+        copy.wait()
+    total[...] = lax.dot_general(ours[...], flat[...], NT, preferred_element_type=F32)
+    for copy in later:
+        copy.wait()
 
 
 def student_theirs_body(blocks, weight, first, lse_teacher, out, stats, flat):
@@ -163,9 +170,11 @@
     out[...] = top + jnp.log(jnp.sum(jnp.exp(x - top[None]), axis=0))
 
 
-def products(grad, weight, parts):
+def products(grad, copies, weight, parts):
     width = parts.shape[2]
     for b in range(0, parts.shape[0], 2):
+        copies[b].wait()
+        copies[b + 1].wait()
         both = lax.dot_general(
             grad, weight[:, b * width : (b + 2) * width], TN, preferred_element_type=F32
         ).astype(parts.dtype)
@@ -173,7 +182,8 @@
         parts[b + 1] = both[:, width:]
 
 
-def logits_body(student, teacher, mine, other, count, weight, grad_logits, parts):
+def logits_body(student, teacher, mine, other, count, weight_hbm, grad_logits, parts, weight, sems):
+    copies = load_blocks(weight_hbm, weight, 1 - lax.axis_index("core"), sems)
     top = jnp.maximum(mine[...], other[...])
     lse = top + jnp.log(jnp.exp(mine[...] - top) + jnp.exp(other[...] - top))
     scale = LOSS_SCALE / count[0:1, :]
@@ -181,23 +191,33 @@
     prob_teacher = jnp.exp(teacher[...].astype(F32) - lse[1:2, :])
     grad = (scale * (prob_student - prob_teacher)).astype(BF16)
     grad_logits[...] = grad
-    products(grad, weight, parts)
-
-
-def products_body(grad_logits, weight, parts):
-    products(grad_logits[...], weight, parts)
-
-
-def head_body(ours, theirs, grad_logits, out):
+    products(grad, copies, weight, parts)
+
+
+def products_body(grad_logits, weight_hbm, parts, weight, sems):
+    copies = load_blocks(weight_hbm, weight, lax.axis_index("core"), sems)
+    products(grad_logits[...], copies, weight, parts)
+
+
+def head_body(ours, theirs, grad_logits, out_hbm, flat_ours, flat_theirs, out, sems):
     core = lax.axis_index("core")
-    width = ours.shape[1] // BLOCKS
-    for flat, side in ((ours, core), (theirs, 1 - core)):
-        for b in range(0, BLOCKS, 2):
+    width = ours.shape[2]
+    lay_out(ours, flat_ours)
+    lay_out(theirs, flat_theirs)
+    copies = []
+    for b in range(0, BLOCKS, 2):
+        for flat, side in ((flat_ours, core), (flat_theirs, 1 - core)):
             both = jnp.dot(
                 grad_logits[...], flat[:, b * width : (b + 2) * width], preferred_element_type=F32
             ).astype(BF16)
             out[:, columns(b * NCORE + side, width)] = both[:, :width]
             out[:, columns((b + 1) * NCORE + side, width)] = both[:, width:]
+        span = slice(b * NCORE * width, (b + 2) * NCORE * width)
+        copy = pltpu.make_async_copy(out.at[:, span], out_hbm.at[:, span], sems.at[b])
+        copy.start()
+        copies.append(copy)
+    for copy in copies:
+        copy.wait()
 
 
 def spread_body(parts, back, out):
@@ -255,6 +275,7 @@
             pltpu.SMEM(positions.shape, jnp.int32), pltpu.SMEM(counts.shape, jnp.int32),
             pltpu.VMEM((tokens, NX * NCORE * width), BF16), DMA((2 + NX,)),
         ],
+        limit=WIDE_LIMIT,
     )
     rows = lax.all_to_all(send, SEQ, 0, 0, tiled=True).reshape(slots, width)
     picked, chosen, count = call(
@@ -263,49 +284,54 @@
         rows, flops=2 * MASKED * slots * width,
     )
     blocks = lax.all_to_all(picked, PLANE, 0, 0, tiled=True)
+    swapped = swap_core(blocks)
+    blocks, chosen = lax.optimization_barrier((blocks, chosen))
     staged = call(
-        stage_body,
+        teacher_body,
         (
-            shape((vocab, MASKED), BF16), shape((8, MASKED), F32),
-            shape((vocab, share), BF16), shape((vocab, share), BF16),
-            shape((slots, MASKED), BF16),
+            shape((vocab, MASKED), BF16), shape((8, MASKED), F32), shape((slots, MASKED), BF16),
         ),
-        teacher.T, head_weight.T, chosen, specs=[HBM, HBM, VMEM],
-        scratch=[pltpu.VMEM((vocab, slots), BF16), DMA((1 + 2 * BLOCKS,))],
+        teacher.T, chosen, specs=[HBM, VMEM],
+        scratch=[pltpu.VMEM((vocab, slots), BF16), DMA(())],
         flops=2 * vocab * slots * MASKED + 2 * slots * slots * MASKED,
     )
-    blocks, staged = lax.optimization_barrier((blocks, staged))
-    teacher_rows, lse_teacher, weight_ours, weight_theirs, back = staged
-    total, flat_ours = call(
+    weight = head_weight.T
+    some_weight, flat = pltpu.VMEM((vocab, share), BF16), pltpu.VMEM((MASKED, share), BF16)
+    total, weight_theirs = call(
         student_ours_body,
-        (shape((vocab, MASKED), F32), shape((MASKED, share), BF16)),
-        blocks, weight_ours, flops=products_flops,
-    )
-    student, stats, flat_theirs = call(
+        (shape((vocab, MASKED), F32), shape((vocab, share), BF16)),
+        blocks, weight, specs=[VMEM, HBM],
+        scratch=[some_weight, flat, DMA((BLOCKS,)), DMA((BLOCKS,))],
+        flops=products_flops,
+    )
+    swapped, staged, total = lax.optimization_barrier((swapped, staged, total))
+    teacher_rows, lse_teacher, back = staged
+    student, stats = call(
         student_theirs_body,
-        (
-            shape((vocab, MASKED), F32), shape((chips, 2, MASKED), F32),
-            shape((MASKED, share), BF16),
-        ),
-        swap_core(blocks), weight_theirs, total, lse_teacher, flops=products_flops,
+        (shape((vocab, MASKED), F32), shape((chips, 2, MASKED), F32)),
+        swapped, weight_theirs, total, lse_teacher, scratch=[flat], flops=products_flops,
     )
     stats = lax.all_to_all(stats, CHIPS, 0, 0, tiled=True)
     half = call(combine_body, shape((2, MASKED), F32), stats)
     grad_logits, parts_theirs = call(
         logits_body, (shape((vocab, MASKED), BF16), parts_shape),
-        student, teacher_rows, half, swap_core(half), count, weight_theirs, flops=products_flops,
+        student, teacher_rows, half, swap_core(half), count, weight, specs=[VMEM] * 5 + [HBM],
+        scratch=[some_weight, DMA((BLOCKS,))], flops=products_flops,
     )
     parts_ours = call(
-        products_body, shape(parts_shape.shape, F32), grad_logits, weight_ours,
-        flops=products_flops,
-    )
-    parts = (parts_ours + swap_core(parts_theirs).astype(F32)).astype(BF16)
+        products_body, shape(parts_shape.shape, F32), grad_logits, weight, specs=[VMEM, HBM],
+        scratch=[some_weight, DMA((BLOCKS,))], flops=products_flops,
+    )
+    grad_head = call(
+        head_body, shape((vocab, depth), BF16), blocks, swapped, grad_logits,
+        outs=HBM, scratch=[flat, flat, pltpu.VMEM((vocab, depth), BF16), DMA((BLOCKS,))],
+        flops=2 * products_flops,
+    )
+    parts_theirs, parts_ours, grad_head = lax.optimization_barrier(
+        (swap_core(parts_theirs), parts_ours, grad_head)
+    )
+    parts = (parts_ours + parts_theirs.astype(F32)).astype(BF16)
     parts = lax.all_to_all(parts, PLANE, 0, 0, tiled=True)
-    grad_head = call(
-        head_body, shape((vocab, depth), BF16), flat_ours, flat_theirs, grad_logits,
-        flops=2 * products_flops,
-    )
-    parts, grad_head = lax.optimization_barrier((parts, grad_head))
     partial = call(
         spread_body, shape((slots, width), BF16), parts, back, flops=2 * MASKED * slots * width,
     )

time: 129 us -> 130 us (level)
  blocking collectives: 60.5 us -> 100 us
  waiting for transfers between devices: 22.4 us -> 1.66 us
  starting transfers between devices: 18.8 us -> 7.67 us
  local copies, waits for them, and re-layouts: 11.1 us -> 1.04 us
  Pallas kernels: 13 us -> 17.2 us
    all_to_all x0 -> x2, blocking collectives: none -> 40.3 us  [the longest x1 21.4 us: per_device(): blocks = lax.all_to_all(picked, PLANE, 0, 0, tiled=True)]
    all_to_all x2 -> x0, waiting for transfers between devices: 19.1 us -> none  [the longest x1 12.9 us: per_device(): parts = lax.all_to_all(parts, PLANE, 0, 0, tiled=True)]
    unnamed x26 -> x4, local copies, waits for them, and re-layouts: 11.1 us -> 1.04 us
    all_to_all x2 -> x0, starting transfers between devices: 9.58 us -> none  [the longest x1 5.61 us: per_device(): blocks = lax.all_to_all(picked, PLANE, 0, 0, tiled=True)]
    pallas_call x12, Pallas kernels: 13 us -> 17.2 us  [call(): pl.pallas_call(body, out_shape=out, in_specs=specs or [VMEM] * len(args),...]
    ppermute x4, waiting for transfers between devices: 3.24 us -> 1.66 us  [swap_core(): return lax.ppermute(x, 'core', [(0, 1), (1, 0)])]
    ppermute x4, starting transfers between devices: 9.19 us -> 7.67 us  [swap_core(): return lax.ppermute(x, 'core', [(0, 1), (1, 0)])]
  transfers between devices with their start and end apart: 6 -> 4, of which waited for: 5 -> 2; matrix products, arithmetic and copies ran while one was open for 0% -> 0% of each run, Pallas kernels for 6% -> 7%
where the time goes in v3:
time: 130 us
  blocking collectives  100 us (77%)
  Pallas kernels  17.2 us (13%)
  starting transfers between devices  7.67 us (6%)
  waiting for transfers between devices  1.66 us (1%)
  between operations  1.55 us (1%)
    all_to_all x1, blocking collectives, per_device(): rows = lax.all_to_all(send, SEQ, 0, 0, tiled=True).reshape(slots, width)  23.4 us
    all_to_all x1, blocking collectives, per_device(): blocks = lax.all_to_all(picked, PLANE, 0, 0, tiled=True)  21.4 us
    all_to_all x1, blocking collectives, per_device(): stats = lax.all_to_all(stats, CHIPS, 0, 0, tiled=True)  19.2 us
    all_to_all x1, blocking collectives, per_device(): parts = lax.all_to_all(parts, PLANE, 0, 0, tiled=True)  19 us
    all_to_all x1, blocking collectives, per_device(): lax.all_to_all(partial.reshape(chips, NCORE * own, width), CHIPS, 0, 0, t...  17.5 us
    pallas_call x12, Pallas kernels, call(): pl.pallas_call(body, out_shape=out, in_specs=specs or [VMEM] * len(args),...  17.2 us
    ppermute x4, starting transfers between devices, swap_core(): return lax.ppermute(x, 'core', [(0, 1), (1, 0)])  7.67 us
  transfers between devices with their start and end apart: 4, of which 2 were waited for; matrix products, arithmetic and copies ran while one was open for 0% of the time, Pallas kernels for 7%

profile of v3, /device:TPU:1, one launch (start us, length us, event | category | flops | bytes accessed | tf_op | source)
XLA Modules:
  0.0 129.9 jit_solution(8647061315997507549)
XLA Ops:
  0.6 0.0 copy-start
  1.4 1.8 %shard_map.68 = bf16[64,8,128]{2,1,0:T(8,128)(2,1)} custom-call(s32[1,8]{1,0:T(1,128)} %positions_hbm.1, s32[1]{0:T(128)S(6)} %copy.7.counts_hbm, bf16[64,4096]{1,0:T(8,128)(2,1)} %hidden.1), custom_call_target="tpu_custom_call" | custom-call | bytes 655396 | tf_op jit(solution)/shard_map/pallas_call | solution.py:30
  3.3 23.4 %all_to_all.25 = bf16[64,8,128]{2,1,0:T(8,128)(2,1)S(1)} all-to-all(bf16[64,8,128]{2,1,0:T(8,128)(2,1)} %shard_map.68), channel_id=1, replica_groups=mesh['x'=4,'z'=8,'core'=2,'y'=4] {'x','z','core'}, dimensions={0} | all-to-all | bytes 262144 | tf_op jit(solution)/shard_map/all_to_all | solution.py:280
  26.6 0.5 shard_map.69
  27.1 21.4 %all_to_all.26.blocks.ours = bf16[16,256,128]{2,1,0:T(8,128)(2,1)S(1)} all-to-all(bf16[16,256,128]{2,1,0:T(8,128)(2,1)S(1)} %get-tuple-element.26), channel_id=1, replica_groups=mesh['x'=4,'z'=8,'core'=2,'y'=4] {'x','y'}, dimensions={0} | all-to-all | bytes 2097152 | tf_op jit(solution)/shard_map/all_to_all | solution.py:286
  48.5 2.1 %collective-permute-start = (bf16[16,256,128]{2,1,0:T(8,128)(2,1)S(1)}, bf16[16,256,128]{2,1,0:T(8,128)(2,1)S(1)}, u32[]{:S(2)}, u32[]{:S(2)}) collective-permute-start(bf16[16,256,128]{2,1,0:T(8,128)(2,1)S(1)} %all_to_all.26.blocks.ours), channel_id=1, source_target_pairs={{0,4},{4,0},{1,5},{5,1},{2,6},{6,2},{3,7},{7,3},{8,12},{12,8},{9,1... | collective-permute-start | bytes 3145736 | tf_op jit(solution)/shard_map/ppermute | solution.py:255
  50.6 0.0 copy-start.1
  50.6 1.0 copy-done.1
  51.6 1.4 %shard_map.70 = (bf16[494,256]{1,0:T(8,128)(2,1)S(1)}, f32[8,256]{1,0:T(8,128)S(1)}, bf16[512,256]{1,0:T(8,128)(2,1)S(1)}) custom-call(bf16[494,512]{1,0:T(8,128)(2,1)S(1)} %bitcast.10, bf16[256,512]{1,0:T(8,128)(2,1)S(1)} %get-tuple-element.28.chosen), custom_call_target="tpu_custom_call" | custom-call | flops 263716864 | bytes 1291264 | tf_op jit(solution)/shard_map/pallas_call | solution.py:30
  53.0 0.0 copy-done
  53.0 2.5 %shard_map.71 = (f32[494,256]{1,0:T(8,128)S(1)}, bf16[494,2048]{1,0:T(8,128)(2,1)S(1)}) custom-call(bf16[16,256,128]{2,1,0:T(8,128)(2,1)S(1)} %all_to_all.26.blocks.ours, bf16[494,4096]{1,0:T(8,128)(2,1)S(1)} %bitcast.5), custom_call_target="tpu_custom_call" | custom-call | flops 517996544 | bytes 7624704 | tf_op jit(solution)/shard_map/pallas_call | solution.py:30
  55.6 0.0 collective-permute-done.blocks.theirs
  55.6 1.0 shard_map.72
  56.5 19.2 %all_to_all.27.stats = f32[128,2,256]{2,1,0:T(2,128)S(1)} all-to-all(f32[128,2,256]{2,1,0:T(2,128)S(1)} %get-tuple-element.40), channel_id=1, replica_groups=mesh['x'=4,'z'=8,'core'=2,'y'=4] {'x','z','y'}, dimensions={0} | all-to-all | bytes 524288 | tf_op jit(solution)/shard_map/all_to_all | solution.py:314
  75.8 0.2 shard_map.73.mine
  76.0 2.2 %collective-permute-start.1 = (f32[2,256]{1,0:T(2,128)S(1)}, f32[2,256]{1,0:T(2,128)S(1)}, u32[]{:S(2)}, u32[]{:S(2)}) collective-permute-start(f32[2,256]{1,0:T(2,128)S(1)} %shard_map.73.mine), channel_id=1, source_target_pairs={{0,4},{4,0},{1,5},{5,1},{2,6},{6,2},{3,7},{7,3},{8,12},{12,8},{9,1... | collective-permute-start | bytes 6152 | tf_op jit(solution)/shard_map/ppermute | solution.py:255
  78.2 0.8 collective-permute-done.1.other
  79.0 3.2 %shard_map.74 = (bf16[494,256]{1,0:T(8,128)(2,1)S(1)}, bf16[16,256,128]{2,1,0:T(8,128)(2,1)S(1)}) custom-call(f32[494,256]{1,0:T(8,128)S(1)} %get-tuple-element.38.student, bf16[494,256]{1,0:T(8,128)(2,1)S(1)} %get-tuple-element.39.teacher, f32[2,256]{1,0:T(2,128)S(1)} %shard_map.73.mine, f32[2,256]{1,0:T(2,128)S(1)} %collective-permute-done.1.other, ...), custom_call_target="tpu_custom_call" | custom-call | flops 517996544 | bytes 6119424 | tf_op jit(solution)/shard_map/pallas_call | solution.py:30
  82.2 0.6 collective-permute-start.2
  82.8 3.1 %shard_map.75 = f32[16,256,128]{2,1,0:T(8,128)S(1)} custom-call(bf16[494,256]{1,0:T(8,128)(2,1)S(1)} %get-tuple-element.43.grad_logits, bf16[494,4096]{1,0:T(8,128)(2,1)S(1)} %bitcast.7), custom_call_target="tpu_custom_call" | custom-call | flops 517996544 | bytes 6396928 | tf_op jit(solution)/shard_map/pallas_call | solution.py:30
  85.9 2.5 %shard_map.76 = bf16[494,4096]{1,0:T(8,128)(2,1)} custom-call(bf16[16,256,128]{2,1,0:T(8,128)(2,1)S(1)} %all_to_all.26.blocks.ours, bf16[16,256,128]{2,1,0:T(8,128)(2,1)S(1)} %collective-permute-done.blocks.theirs, bf16[494,256]{1,0:T(8,128)(2,1)S(1)} %get-tuple-element.43.grad_logits), custom_call_target="tpu_custom_call" | custom-call | flops 1035993088 | bytes 6396928 | tf_op jit(solution)/shard_map/pallas_call | solution.py:30
  88.4 0.0 collective-permute-done.2
  88.4 0.3 add_convert_fusion
  88.7 19.0 %all_to_all.28.parts = bf16[16,256,128]{2,1,0:T(8,128)(2,1)S(1)} all-to-all(bf16[16,256,128]{2,1,0:T(8,128)(2,1)S(1)} %add_convert_fusion), channel_id=1, replica_groups=mesh['x'=4,'z'=8,'core'=2,'y'=4] {'x','y'}, dimensions={0} | all-to-all | bytes 2097152 | tf_op jit(solution)/shard_map/all_to_all | solution.py:334
  107.7 0.3 shard_map.77
  108.0 17.5 %all_to_all.29.parts = bf16[128,4,128]{2,1,0:T(4,128)(2,1)S(1)} all-to-all(bf16[128,4,128]{2,1,0:T(4,128)(2,1)S(1)} %bitcast.9), channel_id=1, replica_groups=mesh['x'=4,'z'=8,'core'=2,'y'=4] {'x','z','y'}, dimensions={0} | all-to-all | bytes 262144 | tf_op jit(solution)/shard_map/all_to_all | solution.py:338
  125.5 0.1 shard_map.78
  125.6 2.8 %collective-permute-start.3 = (f32[16,2,128]{2,1,0:T(2,128)S(1)}, f32[16,2,128]{2,1,0:T(2,128)S(1)}, u32[]{:S(2)}, u32[]{:S(2)}) collective-permute-start(f32[16,2,128]{2,1,0:T(2,128)S(1)} %get-tuple-element.48), channel_id=1, source_target_pairs={{0,4},{4,0},{1,5},{5,1},{2,6},{6,2},{3,7},{7,3},{8,12},{12,8},{9,1... | collective-permute-start | bytes 49160 | tf_op jit(solution)/shard_map/ppermute | solution.py:255
  128.4 0.8 collective-permute-done.3.other
  129.2 0.6 shard_map.79
Async XLA Ops:
  0.6 52.4 %copy-start = (bf16[4096,494]{0,1:T(8,128)(2,1)S(1)}, bf16[4096,494]{0,1:T(8,128)(2,1)}, u32[]{:S(2)}) copy-start(bf16[4096,494]{0,1:T(8,128)(2,1)} %param.6) | copy-start | bytes 12140548
  48.5 7.1 %collective-permute-start = (bf16[16,256,128]{2,1,0:T(8,128)(2,1)S(1)}, bf16[16,256,128]{2,1,0:T(8,128)(2,1)S(1)}, u32[]{:S(2)}, u32[]{:S(2)}) collective-permute-start(bf16[16,256,128]{2,1,0:T(8,128)(2,1)S(1)} %all_to_all.26.blocks.ours), channel_id=1, source_target_pairs={{0,4},{4,0},{1,5},{5,1},{2,6},{6,2},{3,7},{7,3},{8,12},{12,8},{9,1... | collective-permute-start | bytes 3145736 | tf_op jit(solution)/shard_map/ppermute | solution.py:255
  50.6 1.0 copy-start.1
  76.0 3.0 %collective-permute-start.1 = (f32[2,256]{1,0:T(2,128)S(1)}, f32[2,256]{1,0:T(2,128)S(1)}, u32[]{:S(2)}, u32[]{:S(2)}) collective-permute-start(f32[2,256]{1,0:T(2,128)S(1)} %shard_map.73.mine), channel_id=1, source_target_pairs={{0,4},{4,0},{1,5},{5,1},{2,6},{6,2},{3,7},{7,3},{8,12},{12,8},{9,1... | collective-permute-start | bytes 6152 | tf_op jit(solution)/shard_map/ppermute | solution.py:255
  82.2 6.2 %collective-permute-start.2 = (bf16[16,256,128]{2,1,0:T(8,128)(2,1)S(1)}, bf16[16,256,128]{2,1,0:T(8,128)(2,1)S(1)}, u32[]{:S(2)}, u32[]{:S(2)}) collective-permute-start(bf16[16,256,128]{2,1,0:T(8,128)(2,1)S(1)} %get-tuple-element.42), channel_id=1, source_target_pairs={{0,4},{4,0},{1,5},{5,1},{2,6},{6,2},{3,7},{7,3},{8,12},{12,8},{9,1... | collective-permute-start | bytes 3145736 | tf_op jit(solution)/shard_map/ppermute | solution.py:255
  125.6 3.6 %collective-permute-start.3 = (f32[16,2,128]{2,1,0:T(2,128)S(1)}, f32[16,2,128]{2,1,0:T(2,128)S(1)}, u32[]{:S(2)}, u32[]{:S(2)}) collective-permute-start(f32[16,2,128]{2,1,0:T(2,128)S(1)} %get-tuple-element.48), channel_id=1, source_target_pairs={{0,4},{4,0},{1,5},{5,1},{2,6},{6,2},{3,7},{7,3},{8,12},{12,8},{9,1... | collective-permute-start | bytes 49160 | tf_op jit(solution)/shard_map/ppermute | solution.py:255

commit v4 on v3

v4 whole, which is shorter than its diff:
```python
import jax
import jax.numpy as jnp
from jax import lax
from jax.experimental import pallas as pl
from jax.experimental.pallas import tpu as pltpu
from jax.sharding import Mesh, PartitionSpec as P

LOSS_SCALE = 1024.0
MASKED = 256
MARK = 64.0

SEQ = ("x", "z", "core")
ALL = ("x", "z", "core", "y")
CHIPS = ("x", "z", "y")
PLANE = ("x", "y")
NX, NZ, NCORE, NY = 4, 8, 2, 4
BLOCKS = NX * NY
F32, BF16 = jnp.float32, jnp.bfloat16
NT = (((1,), (1,)), ((), ()))
TN = (((0,), (0,)), ((), ()))
VMEM = pl.BlockSpec(memory_space=pltpu.VMEM)
HBM = pl.BlockSpec(memory_space=pltpu.HBM)
DMA = pltpu.SemaphoreType.DMA
LIMIT, PICK_LIMIT = 32 << 20, 62717952


def call(body, out, *args, specs=None, outs=VMEM, flops=0, scratch=(), limit=LIMIT):
    leaves = jax.tree.leaves((args, out))
    nbytes = sum(x.size * x.dtype.itemsize for x in leaves)
    return pl.pallas_call(
        body,
        out_shape=out,
        in_specs=specs or [VMEM] * len(args),
        out_specs=jax.tree.map(lambda _: outs, out),
        scratch_shapes=list(scratch),
        cost_estimate=pl.CostEstimate(flops=flops, bytes_accessed=nbytes, transcendentals=0),
        compiler_params=pltpu.CompilerParams(vmem_limit_bytes=limit),
    )(*args)


def shape(dims, dtype):
    return jax.ShapeDtypeStruct(dims, dtype)


def columns(block, width):
    return pl.ds(pl.multiple_of(block * width, width), width)


def part_of(y, core):
    return y * NCORE + core


def pick_body(positions_hbm, counts_hbm, hidden, out, positions, counts, mine, sems):
    shards, capacity, width = out.shape
    tokens = hidden.shape[0]
    y = lax.axis_index("y")
    copies = [
        pltpu.make_async_copy(positions_hbm, positions, sems.at[0]),
        pltpu.make_async_copy(counts_hbm, counts, sems.at[1]),
        pltpu.make_async_copy(hidden.at[:, columns(y, mine.shape[1])], mine, sems.at[2]),
    ]
    for copy in copies:
        copy.start()
    for copy in copies:
        copy.wait()
    row = lax.broadcasted_iota(jnp.int32, (2 * capacity, tokens), 0)
    column = lax.broadcasted_iota(jnp.int32, (2 * capacity, tokens), 1)
    hot = jnp.zeros((2 * capacity, tokens), F32)
    for k in range(capacity):
        hot = jnp.where((row == k) & (column == positions[0, k]), 1.0, hot)
    rows = jnp.dot(hot.astype(BF16), mine[...], preferred_element_type=F32)[:capacity]
    rank = lax.broadcasted_iota(jnp.int32, rows.shape, 0)
    rows = jnp.where(rank < counts[0, 0], rows, MARK).astype(BF16)
    for s in range(shards):
        start = (s % NCORE * NX + s // (NZ * NCORE)) * width
        out[s] = rows[:, start : start + width]


def compact_body(rows, picked, chosen, count):
    slots = rows.shape[0]
    capacity = 8
    valid = (rows[...].astype(F32)[:, 0:1] < MARK / 2).astype(F32)
    a = lax.broadcasted_iota(jnp.int32, (slots, slots), 0)
    b = lax.broadcasted_iota(jnp.int32, (slots, slots), 1)
    spread = jnp.broadcast_to(valid, (slots, slots))
    rank = jnp.sum(jnp.where(a < b, spread, 0.0), axis=0, keepdims=True)
    mine = jnp.sum(jnp.where(a == b, spread, 0.0), axis=0, keepdims=True)
    total = jnp.sum(jnp.where(a // capacity == b // capacity, spread, 0.0), axis=0, keepdims=True)
    place = jnp.where(mine > 0.5, rank, -1.0).astype(jnp.int32)
    target = lax.broadcasted_iota(jnp.int32, (MASKED, slots), 0)
    hot = (target == place).astype(F32).astype(BF16)
    chosen[...] = hot
    mine = jnp.dot(hot, rows[...], preferred_element_type=F32).astype(BF16)
    for i in range(picked.shape[0]):
        picked[i] = mine
    totals = jnp.broadcast_to(total, (8, slots)).astype(BF16)
    count[...] = lax.dot_general(totals, hot, NT, preferred_element_type=F32)


def logsumexp(x):
    top = jnp.max(x, axis=0, keepdims=True)
    return top + jnp.log(jnp.sum(jnp.exp(x - top), axis=0, keepdims=True))


def teacher_body(teacher_hbm, chosen, out, lse, back, teacher, sem):
    move = pltpu.make_async_copy(teacher_hbm, teacher, sem)
    move.start()
    halves, sent, masked = back.shape
    slots = chosen.shape[1]
    row = lax.broadcasted_iota(jnp.int32, (sent, slots), 0)
    chip, q = row // 8, row % 8
    slot = chip // NY * 16 + q // 4 * 8 + chip % NY * 2 + q // 2 % 2
    column = lax.broadcasted_iota(jnp.int32, (sent, slots), 1)
    pick = (column == slot).astype(F32).astype(BF16)
    placed = lax.dot_general(pick, chosen[...], NT, preferred_element_type=F32)
    odd = lax.broadcasted_iota(jnp.int32, (sent, masked), 0) % 2
    for h in range(halves):
        back[h] = jnp.where(odd == h, placed, 0.0).astype(BF16)
    move.wait()
    rows = lax.dot_general(teacher[...], chosen[...], NT, preferred_element_type=F32)
    out[...] = rows.astype(BF16)
    lse[...] = jnp.broadcast_to(logsumexp(rows), lse.shape)


def lay_out(blocks, flat):
    width = blocks.shape[2]
    for x in range(NX):
        for y in range(NY):
            start = (y * NX + x) * width
            flat[:, start : start + width] = blocks[x * NY + y]


def student_part(blocks, weight, side, flat):
    lay_out(blocks, flat)
    width = flat.shape[1] // NY
    total = jnp.zeros((weight.shape[0], MASKED), F32)
    for y in range(NY):
        total += lax.dot_general(
            weight[:, columns(part_of(y, side), width)], flat[:, y * width : (y + 1) * width],
            NT, preferred_element_type=F32,
        )
    return total


def student_ours_body(blocks, weight, total, flat):
    total[...] = student_part(blocks, weight, lax.axis_index("core"), flat)


def student_theirs_body(blocks, weight, first, lse_teacher, out, stats, flat):
    total = first[...] + student_part(blocks, weight, 1 - lax.axis_index("core"), flat)
    out[...] = total
    both = jnp.concatenate([logsumexp(total), lse_teacher[0:1, :]], axis=0)
    stats[...] = jnp.broadcast_to(both[None], stats.shape)


def combine_body(stats, out):
    x = stats[...]
    top = jnp.max(x, axis=0)
    out[...] = top + jnp.log(jnp.sum(jnp.exp(x - top[None]), axis=0))


def products(grad, weight, side, parts):
    y = lax.axis_index("y")
    for k, part in enumerate(parts):
        owner = part_of(lax.rem(y + k, NY), side)
        part[...] = lax.dot_general(
            grad, weight[:, columns(owner, part.shape[1])], TN, preferred_element_type=F32
        ).astype(part.dtype)


def logits_body(student, teacher, mine, other, count, weight, grad_logits, *parts):
    top = jnp.maximum(mine[...], other[...])
    lse = top + jnp.log(jnp.exp(mine[...] - top) + jnp.exp(other[...] - top))
    scale = LOSS_SCALE / count[0:1, :]
    prob_student = jnp.exp(student[...] - lse[0:1, :])
    prob_teacher = jnp.exp(teacher[...].astype(F32) - lse[1:2, :])
    grad = (scale * (prob_student - prob_teacher)).astype(BF16)
    grad_logits[...] = grad
    products(grad, weight, 1 - lax.axis_index("core"), parts)


def products_body(grad_logits, weight, *parts):
    products(grad_logits[...], weight, lax.axis_index("core"), parts)


def head_body(ours, theirs, grad_logits, out_hbm, flat_ours, flat_theirs, out, sems):
    core = lax.axis_index("core")
    width = flat_ours.shape[1] // NY
    lay_out(ours, flat_ours)
    lay_out(theirs, flat_theirs)
    copies = []
    for y in range(NY):
        for flat, side in ((flat_ours, core), (flat_theirs, 1 - core)):
            out[:, columns(part_of(y, side), width)] = jnp.dot(
                grad_logits[...], flat[:, y * width : (y + 1) * width], preferred_element_type=F32
            ).astype(BF16)
        span = slice(y * NCORE * width, (y + 1) * NCORE * width)
        copy = pltpu.make_async_copy(out.at[:, span], out_hbm.at[:, span], sems.at[y])
        copy.start()
        copies.append(copy)
    for copy in copies:
        copy.wait()


def spread_body(a, b, c, d, back, out):
    total = a[...].astype(F32) + b[...].astype(F32) + c[...].astype(F32) + d[...].astype(F32)
    total = total.astype(BF16)
    half = out.shape[1]
    out[...] = (
        jnp.dot(back[0], total[:, :half], preferred_element_type=F32)
        + jnp.dot(back[1], total[:, half:], preferred_element_type=F32)
    ).astype(BF16)


def collect_body(parts, mine, other):
    chips, rows, half = parts.shape
    total = jnp.sum(parts[...].astype(F32).reshape(NX * NZ, NY, rows, half), axis=0)
    low, high = total[:, : rows // 2], total[:, rows // 2 :]
    first = lax.axis_index("core") == 0
    mine[...] = jnp.where(first, low, high)
    other[...] = jnp.where(first, high, low)


def finish_body(mine, other, out, whole):
    half = mine.shape[2]
    first = lax.axis_index("core") == 0
    by_core = (
        jnp.where(first, mine[...], other[...]), jnp.where(first, other[...], mine[...]),
    )
    for i in range(out.shape[0]):
        for y in range(NY):
            for core in range(NCORE):
                for h in range(2):
                    start = (part_of(y, core) * 2 + h) * half
                    row = 2 * i + h
                    whole[i : i + 1, start : start + half] = by_core[core][y, row : row + 1]
    out[...] = whole[...].astype(BF16)


def swap_core(x):
    return lax.ppermute(x, "core", [(0, 1), (1, 0)])


def shift_y(x, k):
    return lax.ppermute(x, "y", [(i, (i + k) % NY) for i in range(NY)])


def per_device(hidden, head_weight, teacher, positions, counts):
    tokens, depth = hidden.shape
    capacity = positions.shape[1]
    shards = NX * NZ * NCORE
    slots = shards * capacity
    vocab = head_weight.shape[1]
    part = depth // (NY * NCORE)
    width = part // NX
    own = capacity // NY
    chips = NX * NZ * NY
    weight = head_weight.T
    half_flops = vocab * depth * MASKED
    logits_shape = shape((vocab, MASKED), F32)
    flat = pltpu.VMEM((MASKED, depth // NCORE), BF16)

    send = call(
        pick_body, shape((shards, capacity, width), BF16),
        positions, counts.reshape(1, 1), hidden, specs=[HBM] * 3,
        scratch=[
            pltpu.SMEM(positions.shape, jnp.int32), pltpu.SMEM((1, 1), jnp.int32),
            pltpu.VMEM((tokens, depth // NY), BF16), DMA((3,)),
        ],
        limit=PICK_LIMIT,
    )
    rows = lax.all_to_all(send, SEQ, 0, 0, tiled=True).reshape(slots, width)
    picked, chosen, count = call(
        compact_body,
        (
            shape((BLOCKS, MASKED, width), BF16), shape((MASKED, slots), BF16),
            shape((8, MASKED), F32),
        ),
        rows, flops=2 * MASKED * slots * width,
    )
    blocks = lax.all_to_all(picked, PLANE, 0, 0, tiled=True)
    swapped = swap_core(blocks)
    blocks, chosen = lax.optimization_barrier((blocks, chosen))
    staged = call(
        teacher_body,
        (
            shape((vocab, MASKED), BF16), shape((8, MASKED), F32),
            shape((2, 2 * slots, MASKED), BF16),
        ),
        teacher.T, chosen, specs=[HBM, VMEM],
        scratch=[pltpu.VMEM((vocab, slots), BF16), DMA(())],
        flops=2 * vocab * slots * MASKED + 4 * slots * slots * MASKED,
    )
    total = call(
        student_ours_body, logits_shape, blocks, weight, scratch=[flat], flops=half_flops
    )
    swapped, staged, total = lax.optimization_barrier((swapped, staged, total))
    teacher_rows, lse_teacher, back = staged
    student, stats = call(
        student_theirs_body, (logits_shape, shape((chips, 2, MASKED), F32)),
        swapped, weight, total, lse_teacher, scratch=[flat], flops=half_flops,
    )
    stats = lax.all_to_all(stats, CHIPS, 0, 0, tiled=True)
    lse = call(combine_body, shape((2, MASKED), F32), stats)
    grad_logits, *theirs = call(
        logits_body,
        (shape((vocab, MASKED), BF16),) + (shape((MASKED, part), BF16),) * NY,
        student, teacher_rows, lse, swap_core(lse), count, weight, flops=half_flops,
    )
    ours = call(
        products_body, (shape((MASKED, part), F32),) * NY, grad_logits, weight, flops=half_flops
    )
    sums = [(a + swap_core(b).astype(F32)).astype(BF16) for a, b in zip(ours, theirs)]
    sums = sums[:1] + [shift_y(sums[k], k) for k in range(1, NY)]
    grad_head = call(
        head_body, shape((vocab, depth), BF16), blocks, swapped, grad_logits, outs=HBM,
        scratch=[flat, flat, pltpu.VMEM((vocab, depth), BF16), DMA((NY,))],
        flops=2 * half_flops,
    )
    sums[1], grad_head = lax.optimization_barrier((sums[1], grad_head))
    partial = call(
        spread_body, shape((2 * slots, part // 2), BF16), *sums, back,
        flops=4 * MASKED * slots * part,
    )
    partial = lax.all_to_all(partial.reshape(chips, 8, part // 2), CHIPS, 0, 0, tiled=True)
    mine, other = call(collect_body, (shape((NY, 4, part // 2), F32),) * 2, partial)
    grad_hidden = call(
        finish_body, shape((own, depth), BF16), mine, swap_core(other),
        scratch=[pltpu.VMEM((own, depth), F32)],
    )
    return grad_hidden, grad_head.T


def solution(mesh):
    fine = Mesh(mesh.devices.reshape(NX, NZ, NCORE, NY), ALL)
    return jax.shard_map(
        per_device,
        mesh=fine,
        in_specs=(P(SEQ, None), P(None, ALL), P(None, ALL), P(SEQ, None), P(SEQ)),
        out_specs=(P(ALL, None), P(None, ALL)),
        check_vma=False,
    )
```

time: 130 us -> 126 us (0.969)
  blocking collectives: 100 us -> 89 us
  waiting for transfers between devices: 1.66 us -> 10.7 us
  Pallas kernels: 17.2 us -> 11.6 us
  starting transfers between devices: 7.67 us -> 12 us
    all_to_all x2 -> x1, blocking collectives: 36.5 us -> 25.1 us  [per_device(): lax.all_to_all(partial.reshape(chips, 8, part // 2), CHIPS, 0, 0, tiled=T...]
    ppermute x0 -> x3, waiting for transfers between devices: none -> 8.92 us  [shift_y(): return lax.ppermute(x, 'y', [(i, (i + k) % NY) for i in range(NY)])]
    pallas_call x12, Pallas kernels: 17.2 us -> 11.6 us  [call(): pl.pallas_call(body, out_shape=out, in_specs=specs or [VMEM] * len(args),...]
    ppermute x0 -> x3, starting transfers between devices: none -> 3.37 us  [shift_y(): return lax.ppermute(x, 'y', [(i, (i + k) % NY) for i in range(NY)])]
    ppermute x4 -> x7, starting transfers between devices: 7.67 us -> 8.6 us  [swap_core(): return lax.ppermute(x, 'core', [(0, 1), (1, 0)])]
  transfers between devices with their start and end apart: 4 -> 10, of which waited for: 2 -> 5; matrix products, arithmetic and copies ran while one was open for 0% -> 0% of each run, Pallas kernels for 7% -> 5%
where the time goes in v4:
time: 126 us
  blocking collectives  89 us (71%)
  starting transfers between devices  12 us (10%)
  Pallas kernels  11.6 us (9%)
  waiting for transfers between devices  10.7 us (8%)
  between operations  1.57 us (1%)
    all_to_all x1, blocking collectives, per_device(): lax.all_to_all(partial.reshape(chips, 8, part // 2), CHIPS, 0, 0, tiled=T...  25.1 us
    all_to_all x1, blocking collectives, per_device(): rows = lax.all_to_all(send, SEQ, 0, 0, tiled=True).reshape(slots, width)  23.4 us
    all_to_all x1, blocking collectives, per_device(): blocks = lax.all_to_all(picked, PLANE, 0, 0, tiled=True)  21.4 us
    all_to_all x1, blocking collectives, per_device(): stats = lax.all_to_all(stats, CHIPS, 0, 0, tiled=True)  19.2 us
    pallas_call x12, Pallas kernels, call(): pl.pallas_call(body, out_shape=out, in_specs=specs or [VMEM] * len(args),...  11.6 us
    ppermute x3, waiting for transfers between devices, shift_y(): return lax.ppermute(x, 'y', [(i, (i + k) % NY) for i in range(NY)])  8.92 us
    ppermute x7, starting transfers between devices, swap_core(): return lax.ppermute(x, 'core', [(0, 1), (1, 0)])  8.6 us
    ppermute x3, starting transfers between devices, shift_y(): return lax.ppermute(x, 'y', [(i, (i + k) % NY) for i in range(NY)])  3.37 us
  transfers between devices with their start and end apart: 10, of which 5 were waited for; matrix products, arithmetic and copies ran while one was open for 0% of the time, Pallas kernels for 5%

profile of v4, /device:TPU:1, one launch (start us, length us, event | category | flops | bytes accessed | tf_op | source)
XLA Modules:
  0.0 126.2 jit_solution(6751533834984137940)
XLA Ops:
  1.4 1.9 %shard_map.68 = bf16[64,8,128]{2,1,0:T(8,128)(2,1)} custom-call(s32[1,8]{1,0:T(1,128)} %positions_hbm.1, s32[1,1]{1,0:T(1,128)} %bitcast.6.counts_hbm, bf16[64,4096]{1,0:T(8,128)(2,1)} %hidden.1), custom_call_target="tpu_custom_call" | custom-call | bytes 655396 | tf_op jit(solution)/shard_map/pallas_call | solution.py:30
  3.4 23.4 %all_to_all.20 = bf16[64,8,128]{2,1,0:T(8,128)(2,1)S(1)} all-to-all(bf16[64,8,128]{2,1,0:T(8,128)(2,1)} %shard_map.68), channel_id=1, replica_groups=mesh['x'=4,'z'=8,'core'=2,'y'=4] {'x','z','core'}, dimensions={0} | all-to-all | bytes 262144 | tf_op jit(solution)/shard_map/all_to_all | solution.py:272
  26.7 0.5 shard_map.69
  27.2 21.4 %all_to_all.21.blocks.ours = bf16[16,256,128]{2,1,0:T(8,128)(2,1)S(1)} all-to-all(bf16[16,256,128]{2,1,0:T(8,128)(2,1)S(1)} %get-tuple-element.30), channel_id=1, replica_groups=mesh['x'=4,'z'=8,'core'=2,'y'=4] {'x','y'}, dimensions={0} | all-to-all | bytes 2097152 | tf_op jit(solution)/shard_map/all_to_all | solution.py:281
  48.6 2.1 %collective-permute-start = (bf16[16,256,128]{2,1,0:T(8,128)(2,1)S(1)}, bf16[16,256,128]{2,1,0:T(8,128)(2,1)S(1)}, u32[]{:S(2)}, u32[]{:S(2)}) collective-permute-start(bf16[16,256,128]{2,1,0:T(8,128)(2,1)S(1)} %all_to_all.21.blocks.ours), channel_id=1, source_target_pairs={{0,4},{4,0},{1,5},{5,1},{2,6},{6,2},{3,7},{7,3},{8,12},{12,8},{9,1... | collective-permute-start | bytes 3145736 | tf_op jit(solution)/shard_map/ppermute | solution.py:241
  50.7 1.0 copy-done.1
  51.7 1.9 %shard_map.70 = (bf16[494,256]{1,0:T(8,128)(2,1)S(1)}, f32[8,256]{1,0:T(8,128)S(1)}, bf16[2,1024,256]{2,1,0:T(8,128)(2,1)S(1)}) custom-call(bf16[494,512]{1,0:T(8,128)(2,1)S(1)} %bitcast.13, bf16[256,512]{1,0:T(8,128)(2,1)S(1)} %get-tuple-element.32.chosen), custom_call_target="tpu_custom_call" | custom-call | flops 397934592 | bytes 2077696 | tf_op jit(solution)/shard_map/pallas_call | solution.py:30
  53.6 0.8 shard_map.71.first
  54.4 1.0 shard_map.72
  55.4 19.2 %all_to_all.22.stats = f32[128,2,256]{2,1,0:T(2,128)S(1)} all-to-all(f32[128,2,256]{2,1,0:T(2,128)S(1)} %get-tuple-element.42), channel_id=1, replica_groups=mesh['x'=4,'z'=8,'core'=2,'y'=4] {'x','z','y'}, dimensions={0} | all-to-all | bytes 524288 | tf_op jit(solution)/shard_map/all_to_all | solution.py:303
  74.6 0.2 shard_map.73.mine
  74.9 2.1 %collective-permute-start.1 = (f32[2,256]{1,0:T(2,128)S(1)}, f32[2,256]{1,0:T(2,128)S(1)}, u32[]{:S(2)}, u32[]{:S(2)}) collective-permute-start(f32[2,256]{1,0:T(2,128)S(1)} %shard_map.73.mine), channel_id=1, source_target_pairs={{0,4},{4,0},{1,5},{5,1},{2,6},{6,2},{3,7},{7,3},{8,12},{12,8},{9,1... | collective-permute-start | bytes 6152 | tf_op jit(solution)/shard_map/ppermute | solution.py:241
  77.0 0.8 collective-permute-done.1.other
  77.8 0.8 shard_map.74
  78.6 0.4 collective-permute-start.3
  79.1 0.2 collective-permute-start.2
  79.2 0.3 collective-permute-start.5
  79.6 0.2 collective-permute-start.7
  79.7 0.7 shard_map.75
  80.6 0.4 collective-permute-start.4
  80.9 0.1 collective-permute-done.5
  81.1 1.5 %collective-permute-start.6 = (bf16[256,512]{1,0:T(8,128)(2,1)S(1)}, bf16[256,512]{1,0:T(8,128)(2,1)S(1)}, u32[]{:S(2)}, u32[]{:S(2)}) collective-permute-start(bf16[256,512]{1,0:T(8,128)(2,1)S(1)} %add_convert_fusion.1), channel_id=1, source_target_pairs={{0,2},{1,3},{2,0},{3,1},{4,6},{5,7},{6,4},{7,5},{8,10},{9,11},{10,... | collective-permute-start | bytes 786440 | tf_op jit(solution)/shard_map/ppermute | solution.py:245
  82.7 1.5 %collective-permute-start.8 = (bf16[256,512]{1,0:T(8,128)(2,1)S(1)}, bf16[256,512]{1,0:T(8,128)(2,1)S(1)}, u32[]{:S(2)}, u32[]{:S(2)}) collective-permute-start(bf16[256,512]{1,0:T(8,128)(2,1)S(1)} %add_convert_fusion), channel_id=1, source_target_pairs={{0,3},{1,0},{2,1},{3,2},{4,7},{5,4},{6,5},{7,6},{8,11},{9,8},{10,9... | collective-permute-start | bytes 786440 | tf_op jit(solution)/shard_map/ppermute | solution.py:245
  84.2 2.5 %shard_map.76 = bf16[494,4096]{1,0:T(8,128)(2,1)} custom-call(bf16[16,256,128]{2,1,0:T(8,128)(2,1)S(1)} %all_to_all.21.blocks.ours, bf16[16,256,128]{2,1,0:T(8,128)(2,1)S(1)} %collective-permute-done.blocks.theirs, bf16[494,256]{1,0:T(8,128)(2,1)S(1)} %get-tuple-element.44.grad_logits), custom_call_target="tpu_custom_call" | custom-call | flops 1035993088 | bytes 6396928 | tf_op jit(solution)/shard_map/pallas_call | solution.py:30
  86.8 8.5 %collective-permute-done.4.b = bf16[256,512]{1,0:T(8,128)(2,1)S(1)} collective-permute-done((bf16[256,512]{1,0:T(8,128)(2,1)S(1)}, bf16[256,512]{1,0:T(8,128)(2,1)S(1)}, u32[]{:S(2)}, u32[]{:S(2)}) %collective-permute-start.4) | collective-permute-done | bytes 262176 | tf_op jit(solution)/shard_map/ppermute | solution.py:245
  95.2 0.5 collective-permute-done.8.d
  95.7 0.5 shard_map.77
  96.2 25.1 %all_to_all.23.parts = bf16[128,8,256]{2,1,0:T(8,128)(2,1)S(1)} all-to-all(bf16[128,8,256]{2,1,0:T(8,128)(2,1)S(1)} %bitcast.11), channel_id=1, replica_groups=mesh['x'=4,'z'=8,'core'=2,'y'=4] {'x','z','y'}, dimensions={0} | all-to-all | bytes 1048576 | tf_op jit(solution)/shard_map/all_to_all | solution.py:325
  121.3 0.1 shard_map.78
  121.4 3.3 %collective-permute-start.9 = (f32[4,4,256]{2,1,0:T(4,128)S(1)}, f32[4,4,256]{2,1,0:T(4,128)S(1)}, u32[]{:S(2)}, u32[]{:S(2)}) collective-permute-start(f32[4,4,256]{2,1,0:T(4,128)S(1)} %get-tuple-element.56), channel_id=1, source_target_pairs={{0,4},{4,0},{1,5},{5,1},{2,6},{6,2},{3,7},{7,3},{8,12},{12,8},{9,1... | collective-permute-start | bytes 49160 | tf_op jit(solution)/shard_map/ppermute | solution.py:241
  124.7 0.8 collective-permute-done.9.other
  125.5 0.6 shard_map.79
  (12 shorter events, 0.3 us)
Async XLA Ops:
  0.6 53.0 %copy-start = (bf16[4096,494]{0,1:T(8,128)(2,1)S(1)}, bf16[4096,494]{0,1:T(8,128)(2,1)}, u32[]{:S(2)}) copy-start(bf16[4096,494]{0,1:T(8,128)(2,1)} %param.6) | copy-start | bytes 12140548
  48.6 5.9 %collective-permute-start = (bf16[16,256,128]{2,1,0:T(8,128)(2,1)S(1)}, bf16[16,256,128]{2,1,0:T(8,128)(2,1)S(1)}, u32[]{:S(2)}, u32[]{:S(2)}) collective-permute-start(bf16[16,256,128]{2,1,0:T(8,128)(2,1)S(1)} %all_to_all.21.blocks.ours), channel_id=1, source_target_pairs={{0,4},{4,0},{1,5},{5,1},{2,6},{6,2},{3,7},{7,3},{8,12},{12,8},{9,1... | collective-permute-start | bytes 3145736 | tf_op jit(solution)/shard_map/ppermute | solution.py:241
  50.7 1.0 copy-start.1
  74.9 2.9 %collective-permute-start.1 = (f32[2,256]{1,0:T(2,128)S(1)}, f32[2,256]{1,0:T(2,128)S(1)}, u32[]{:S(2)}, u32[]{:S(2)}) collective-permute-start(f32[2,256]{1,0:T(2,128)S(1)} %shard_map.73.mine), channel_id=1, source_target_pairs={{0,4},{4,0},{1,5},{5,1},{2,6},{6,2},{3,7},{7,3},{8,12},{12,8},{9,1... | collective-permute-start | bytes 6152 | tf_op jit(solution)/shard_map/ppermute | solution.py:241
  78.6 1.9 %collective-permute-start.3 = (bf16[256,512]{1,0:T(8,128)(2,1)S(1)}, bf16[256,512]{1,0:T(8,128)(2,1)S(1)}, u32[]{:S(2)}, u32[]{:S(2)}) collective-permute-start(bf16[256,512]{1,0:T(8,128)(2,1)S(1)} %get-tuple-element.48), channel_id=1, source_target_pairs={{0,4},{4,0},{1,5},{5,1},{2,6},{6,2},{3,7},{7,3},{8,12},{12,8},{9,1... | collective-permute-start | bytes 786440 | tf_op jit(solution)/shard_map/ppermute | solution.py:241
  79.1 7.6 %collective-permute-start.2 = (bf16[256,512]{1,0:T(8,128)(2,1)S(1)}, bf16[256,512]{1,0:T(8,128)(2,1)S(1)}, u32[]{:S(2)}, u32[]{:S(2)}) collective-permute-start(bf16[256,512]{1,0:T(8,128)(2,1)S(1)} %get-tuple-element.46), channel_id=1, source_target_pairs={{0,4},{4,0},{1,5},{5,1},{2,6},{6,2},{3,7},{7,3},{8,12},{12,8},{9,1... | collective-permute-start | bytes 786440 | tf_op jit(solution)/shard_map/ppermute | solution.py:241
  79.2 1.8 %collective-permute-start.5 = (bf16[256,512]{1,0:T(8,128)(2,1)S(1)}, bf16[256,512]{1,0:T(8,128)(2,1)S(1)}, u32[]{:S(2)}, u32[]{:S(2)}) collective-permute-start(bf16[256,512]{1,0:T(8,128)(2,1)S(1)} %get-tuple-element.51), channel_id=1, source_target_pairs={{0,4},{4,0},{1,5},{5,1},{2,6},{6,2},{3,7},{7,3},{8,12},{12,8},{9,1... | collective-permute-start | bytes 786440 | tf_op jit(solution)/shard_map/ppermute | solution.py:241
  79.6 3.1 %collective-permute-start.7 = (bf16[256,512]{1,0:T(8,128)(2,1)S(1)}, bf16[256,512]{1,0:T(8,128)(2,1)S(1)}, u32[]{:S(2)}, u32[]{:S(2)}) collective-permute-start(bf16[256,512]{1,0:T(8,128)(2,1)S(1)} %get-tuple-element.53), channel_id=1, source_target_pairs={{0,4},{4,0},{1,5},{5,1},{2,6},{6,2},{3,7},{7,3},{8,12},{12,8},{9,1... | collective-permute-start | bytes 786440 | tf_op jit(solution)/shard_map/ppermute | solution.py:241
  80.6 14.7 %collective-permute-start.4 = (bf16[256,512]{1,0:T(8,128)(2,1)S(1)}, bf16[256,512]{1,0:T(8,128)(2,1)S(1)}, u32[]{:S(2)}, u32[]{:S(2)}) collective-permute-start(bf16[256,512]{1,0:T(8,128)(2,1)S(1)} %add_convert_fusion.2), channel_id=1, source_target_pairs={{0,1},{1,2},{2,3},{3,0},{4,5},{5,6},{6,7},{7,4},{8,9},{9,10},{10,1... | collective-permute-start | bytes 786440 | tf_op jit(solution)/shard_map/ppermute | solution.py:245
  81.1 14.2 %collective-permute-start.6 = (bf16[256,512]{1,0:T(8,128)(2,1)S(1)}, bf16[256,512]{1,0:T(8,128)(2,1)S(1)}, u32[]{:S(2)}, u32[]{:S(2)}) collective-permute-start(bf16[256,512]{1,0:T(8,128)(2,1)S(1)} %add_convert_fusion.1), channel_id=1, source_target_pairs={{0,2},{1,3},{2,0},{3,1},{4,6},{5,7},{6,4},{7,5},{8,10},{9,11},{10,... | collective-permute-start | bytes 786440 | tf_op jit(solution)/shard_map/ppermute | solution.py:245
  82.7 13.0 %collective-permute-start.8 = (bf16[256,512]{1,0:T(8,128)(2,1)S(1)}, bf16[256,512]{1,0:T(8,128)(2,1)S(1)}, u32[]{:S(2)}, u32[]{:S(2)}) collective-permute-start(bf16[256,512]{1,0:T(8,128)(2,1)S(1)} %add_convert_fusion), channel_id=1, source_target_pairs={{0,3},{1,0},{2,1},{3,2},{4,7},{5,4},{6,5},{7,6},{8,11},{9,8},{10,9... | collective-permute-start | bytes 786440 | tf_op jit(solution)/shard_map/ppermute | solution.py:245
  121.4 4.1 %collective-permute-start.9 = (f32[4,4,256]{2,1,0:T(4,128)S(1)}, f32[4,4,256]{2,1,0:T(4,128)S(1)}, u32[]{:S(2)}, u32[]{:S(2)}) collective-permute-start(f32[4,4,256]{2,1,0:T(4,128)S(1)} %get-tuple-element.56), channel_id=1, source_target_pairs={{0,4},{4,0},{1,5},{5,1},{2,6},{6,2},{3,7},{7,3},{8,12},{12,8},{9,1... | collective-permute-start | bytes 49160 | tf_op jit(solution)/shard_map/ppermute | solution.py:241

commit v5 on v4

--- a/solution.py
+++ b/solution.py
@@ -12,9 +12,9 @@
 SEQ = ("x", "z", "core")
 ALL = ("x", "z", "core", "y")
 CHIPS = ("x", "z", "y")
-PLANE = ("x", "y")
 NX, NZ, NCORE, NY = 4, 8, 2, 4
-BLOCKS = NX * NY
+RING = 4
+assert NX == NY == RING
 F32, BF16 = jnp.float32, jnp.bfloat16
 NT = (((1,), (1,)), ((), ()))
 TN = (((0,), (0,)), ((), ()))
@@ -46,18 +46,26 @@
     return pl.ds(pl.multiple_of(block * width, width), width)
 
 
-def part_of(y, core):
-    return y * NCORE + core
+def place(core):
+    return jnp.where(core == 0, lax.axis_index("y"), lax.axis_index("x"))
+
+
+def part_at(side, steps):
+    core = lax.axis_index("core")
+    core = core if side == 0 else 1 - core
+    return core * RING + lax.rem(place(core) + steps + RING, RING)
 
 
 def pick_body(positions_hbm, counts_hbm, hidden, out, positions, counts, mine, sems):
     shards, capacity, width = out.shape
-    tokens = hidden.shape[0]
-    y = lax.axis_index("y")
+    tokens, depth = hidden.shape
     copies = [
         pltpu.make_async_copy(positions_hbm, positions, sems.at[0]),
         pltpu.make_async_copy(counts_hbm, counts, sems.at[1]),
-        pltpu.make_async_copy(hidden.at[:, columns(y, mine.shape[1])], mine, sems.at[2]),
+        pltpu.make_async_copy(
+            hidden.at[:, columns(lax.axis_index("y"), width)], mine.at[:, :width], sems.at[2]
+        ),
+        pltpu.make_async_copy(hidden.at[:, depth // 2 :], mine.at[:, width:], sems.at[3]),
     ]
     for copy in copies:
         copy.start()
@@ -72,7 +80,7 @@
     rank = lax.broadcasted_iota(jnp.int32, rows.shape, 0)
     rows = jnp.where(rank < counts[0, 0], rows, MARK).astype(BF16)
     for s in range(shards):
-        start = (s % NCORE * NX + s // (NZ * NCORE)) * width
+        start = s % NCORE * (1 + s // (NZ * NCORE)) * width
         out[s] = rows[:, start : start + width]
 
 
@@ -90,9 +98,7 @@
     target = lax.broadcasted_iota(jnp.int32, (MASKED, slots), 0)
     hot = (target == place).astype(F32).astype(BF16)
     chosen[...] = hot
-    mine = jnp.dot(hot, rows[...], preferred_element_type=F32).astype(BF16)
-    for i in range(picked.shape[0]):
-        picked[i] = mine
+    picked[...] = jnp.dot(hot, rows[...], preferred_element_type=F32).astype(BF16)
     totals = jnp.broadcast_to(total, (8, slots)).astype(BF16)
     count[...] = lax.dot_general(totals, hot, NT, preferred_element_type=F32)
 
@@ -122,32 +128,22 @@
     lse[...] = jnp.broadcast_to(logsumexp(rows), lse.shape)
 
 
-def lay_out(blocks, flat):
-    width = blocks.shape[2]
-    for x in range(NX):
-        for y in range(NY):
-            start = (y * NX + x) * width
-            flat[:, start : start + width] = blocks[x * NY + y]
-
-
-def student_part(blocks, weight, side, flat):
-    lay_out(blocks, flat)
-    width = flat.shape[1] // NY
+def student_part(blocks, weight, side):
     total = jnp.zeros((weight.shape[0], MASKED), F32)
-    for y in range(NY):
+    for k, block in enumerate(blocks):
         total += lax.dot_general(
-            weight[:, columns(part_of(y, side), width)], flat[:, y * width : (y + 1) * width],
+            weight[:, columns(part_at(side, -k), block.shape[1])], block[...],
             NT, preferred_element_type=F32,
         )
     return total
 
 
-def student_ours_body(blocks, weight, total, flat):
-    total[...] = student_part(blocks, weight, lax.axis_index("core"), flat)
-
-
-def student_theirs_body(blocks, weight, first, lse_teacher, out, stats, flat):
-    total = first[...] + student_part(blocks, weight, 1 - lax.axis_index("core"), flat)
+def student_ours_body(a, b, c, d, weight, total):
+    total[...] = student_part((a, b, c, d), weight, 0)
+
+
+def student_theirs_body(a, b, c, d, weight, first, lse_teacher, out, stats):
+    total = first[...] + student_part((a, b, c, d), weight, 1)
     out[...] = total
     both = jnp.concatenate([logsumexp(total), lse_teacher[0:1, :]], axis=0)
     stats[...] = jnp.broadcast_to(both[None], stats.shape)
@@ -160,11 +156,10 @@
 
 
 def products(grad, weight, side, parts):
-    y = lax.axis_index("y")
     for k, part in enumerate(parts):
-        owner = part_of(lax.rem(y + k, NY), side)
         part[...] = lax.dot_general(
-            grad, weight[:, columns(owner, part.shape[1])], TN, preferred_element_type=F32
+            grad, weight[:, columns(part_at(side, k), part.shape[1])], TN,
+            preferred_element_type=F32,
         ).astype(part.dtype)
 
 
@@ -176,26 +171,22 @@
     prob_teacher = jnp.exp(teacher[...].astype(F32) - lse[1:2, :])
     grad = (scale * (prob_student - prob_teacher)).astype(BF16)
     grad_logits[...] = grad
-    products(grad, weight, 1 - lax.axis_index("core"), parts)
+    products(grad, weight, 1, parts)
 
 
 def products_body(grad_logits, weight, *parts):
-    products(grad_logits[...], weight, lax.axis_index("core"), parts)
-
-
-def head_body(ours, theirs, grad_logits, out_hbm, flat_ours, flat_theirs, out, sems):
-    core = lax.axis_index("core")
-    width = flat_ours.shape[1] // NY
-    lay_out(ours, flat_ours)
-    lay_out(theirs, flat_theirs)
+    products(grad_logits[...], weight, 0, parts)
+
+
+def head_body(*refs):
+    blocks, (grad_logits, out_hbm, out, sems) = refs[: NCORE * RING], refs[NCORE * RING :]
     copies = []
-    for y in range(NY):
-        for flat, side in ((flat_ours, core), (flat_theirs, 1 - core)):
-            out[:, columns(part_of(y, side), width)] = jnp.dot(
-                grad_logits[...], flat[:, y * width : (y + 1) * width], preferred_element_type=F32
-            ).astype(BF16)
-        span = slice(y * NCORE * width, (y + 1) * NCORE * width)
-        copy = pltpu.make_async_copy(out.at[:, span], out_hbm.at[:, span], sems.at[y])
+    for i, block in enumerate(blocks):
+        span = columns(part_at(i // RING, -(i % RING)), block.shape[1])
+        out[i] = jnp.dot(
+            grad_logits[...], block[...], preferred_element_type=F32
+        ).astype(BF16)
+        copy = pltpu.make_async_copy(out.at[i], out_hbm.at[:, span], sems.at[i])
         copy.start()
         copies.append(copy)
     for copy in copies:
@@ -214,9 +205,10 @@
 
 def collect_body(parts, mine, other):
     chips, rows, half = parts.shape
-    total = jnp.sum(parts[...].astype(F32).reshape(NX * NZ, NY, rows, half), axis=0)
+    total = jnp.sum(parts[...].astype(F32).reshape(NX, NZ, NY, rows, half), axis=1)
+    first = lax.axis_index("core") == 0
+    total = jnp.where(first, jnp.sum(total, axis=0), jnp.sum(total, axis=1))
     low, high = total[:, : rows // 2], total[:, rows // 2 :]
-    first = lax.axis_index("core") == 0
     mine[...] = jnp.where(first, low, high)
     other[...] = jnp.where(first, high, low)
 
@@ -228,12 +220,12 @@
         jnp.where(first, mine[...], other[...]), jnp.where(first, other[...], mine[...]),
     )
     for i in range(out.shape[0]):
-        for y in range(NY):
-            for core in range(NCORE):
+        for core in range(NCORE):
+            for at in range(RING):
                 for h in range(2):
-                    start = (part_of(y, core) * 2 + h) * half
+                    start = ((core * RING + at) * 2 + h) * half
                     row = 2 * i + h
-                    whole[i : i + 1, start : start + half] = by_core[core][y, row : row + 1]
+                    whole[i : i + 1, start : start + half] = by_core[core][at, row : row + 1]
     out[...] = whole[...].astype(BF16)
 
 
@@ -241,8 +233,17 @@
     return lax.ppermute(x, "core", [(0, 1), (1, 0)])
 
 
-def shift_y(x, k):
-    return lax.ppermute(x, "y", [(i, (i + k) % NY) for i in range(NY)])
+def shift(v, k):
+    moves = []
+    for x in range(NX):
+        for z in range(NZ):
+            for y in range(NY):
+                for core, (to_x, to_y) in enumerate(((x, (y + k) % NY), ((x + k) % NX, y))):
+                    moves.append(
+                        (((x * NZ + z) * NCORE + core) * NY + y,
+                         ((to_x * NZ + z) * NCORE + core) * NY + to_y)
+                    )
+    return lax.ppermute(v, ALL, moves)
 
 
 def per_device(hidden, head_weight, teacher, positions, counts):
@@ -251,36 +252,31 @@
     shards = NX * NZ * NCORE
     slots = shards * capacity
     vocab = head_weight.shape[1]
-    part = depth // (NY * NCORE)
-    width = part // NX
+    part = depth // (RING * NCORE)
     own = capacity // NY
     chips = NX * NZ * NY
     weight = head_weight.T
     half_flops = vocab * depth * MASKED
     logits_shape = shape((vocab, MASKED), F32)
-    flat = pltpu.VMEM((MASKED, depth // NCORE), BF16)
 
     send = call(
-        pick_body, shape((shards, capacity, width), BF16),
+        pick_body, shape((shards, capacity, part), BF16),
         positions, counts.reshape(1, 1), hidden, specs=[HBM] * 3,
         scratch=[
             pltpu.SMEM(positions.shape, jnp.int32), pltpu.SMEM((1, 1), jnp.int32),
-            pltpu.VMEM((tokens, depth // NY), BF16), DMA((3,)),
+            pltpu.VMEM((tokens, part + depth // 2), BF16), DMA((4,)),
         ],
         limit=PICK_LIMIT,
     )
-    rows = lax.all_to_all(send, SEQ, 0, 0, tiled=True).reshape(slots, width)
+    rows = lax.all_to_all(send, SEQ, 0, 0, tiled=True).reshape(slots, part)
     picked, chosen, count = call(
         compact_body,
         (
-            shape((BLOCKS, MASKED, width), BF16), shape((MASKED, slots), BF16),
-            shape((8, MASKED), F32),
+            shape((MASKED, part), BF16), shape((MASKED, slots), BF16), shape((8, MASKED), F32),
         ),
-        rows, flops=2 * MASKED * slots * width,
-    )
-    blocks = lax.all_to_all(picked, PLANE, 0, 0, tiled=True)
-    swapped = swap_core(blocks)
-    blocks, chosen = lax.optimization_barrier((blocks, chosen))
+        rows, flops=2 * MASKED * slots * part,
+    )
+    blocks = [picked] + [shift(picked, k) for k in range(1, RING)]
     staged = call(
         teacher_body,
         (
@@ -291,30 +287,31 @@
         scratch=[pltpu.VMEM((vocab, slots), BF16), DMA(())],
         flops=2 * vocab * slots * MASKED + 4 * slots * slots * MASKED,
     )
-    total = call(
-        student_ours_body, logits_shape, blocks, weight, scratch=[flat], flops=half_flops
-    )
-    swapped, staged, total = lax.optimization_barrier((swapped, staged, total))
+    blocks[1], staged = lax.optimization_barrier((blocks[1], staged))
     teacher_rows, lse_teacher, back = staged
+    others = [swap_core(block) for block in blocks]
+    total = call(student_ours_body, logits_shape, *blocks, weight, flops=half_flops)
+    others[-1], total = lax.optimization_barrier((others[-1], total))
     student, stats = call(
         student_theirs_body, (logits_shape, shape((chips, 2, MASKED), F32)),
-        swapped, weight, total, lse_teacher, scratch=[flat], flops=half_flops,
+        *others, weight, total, lse_teacher, flops=half_flops,
     )
     stats = lax.all_to_all(stats, CHIPS, 0, 0, tiled=True)
     lse = call(combine_body, shape((2, MASKED), F32), stats)
     grad_logits, *theirs = call(
         logits_body,
-        (shape((vocab, MASKED), BF16),) + (shape((MASKED, part), BF16),) * NY,
+        (shape((vocab, MASKED), BF16),) + (shape((MASKED, part), BF16),) * RING,
         student, teacher_rows, lse, swap_core(lse), count, weight, flops=half_flops,
     )
     ours = call(
-        products_body, (shape((MASKED, part), F32),) * NY, grad_logits, weight, flops=half_flops
+        products_body, (shape((MASKED, part), F32),) * RING, grad_logits, weight,
+        flops=half_flops,
     )
     sums = [(a + swap_core(b).astype(F32)).astype(BF16) for a, b in zip(ours, theirs)]
-    sums = sums[:1] + [shift_y(sums[k], k) for k in range(1, NY)]
+    sums = sums[:1] + [shift(sums[k], k) for k in range(1, RING)]
     grad_head = call(
-        head_body, shape((vocab, depth), BF16), blocks, swapped, grad_logits, outs=HBM,
-        scratch=[flat, flat, pltpu.VMEM((vocab, depth), BF16), DMA((NY,))],
+        head_body, shape((vocab, depth), BF16), *blocks, *others, grad_logits, outs=HBM,
+        scratch=[pltpu.VMEM((NCORE * RING, vocab, part), BF16), DMA((NCORE * RING,))],
         flops=2 * half_flops,
     )
     sums[1], grad_head = lax.optimization_barrier((sums[1], grad_head))
@@ -323,7 +320,7 @@
         flops=4 * MASKED * slots * part,
     )
     partial = lax.all_to_all(partial.reshape(chips, 8, part // 2), CHIPS, 0, 0, tiled=True)
-    mine, other = call(collect_body, (shape((NY, 4, part // 2), F32),) * 2, partial)
+    mine, other = call(collect_body, (shape((RING, 4, part // 2), F32),) * 2, partial)
     grad_hidden = call(
         finish_body, shape((own, depth), BF16), mine, swap_core(other),
         scratch=[pltpu.VMEM((own, depth), F32)],

time: 126 us -> 118 us (0.937)
  blocking collectives: 89 us -> 73.8 us
  starting transfers between devices: 12 us -> 18.5 us
    all_to_all x2 -> x1, blocking collectives: 44.7 us -> 30.3 us  [per_device(): rows = lax.all_to_all(send, SEQ, 0, 0, tiled=True).reshape(slots, part)]
    ppermute x3 -> x6, starting transfers between devices: 3.37 us -> 7.61 us  [shift(): return lax.ppermute(v, ALL, moves)]
    ppermute x7 -> x10, starting transfers between devices: 8.6 us -> 10.9 us  [swap_core(): return lax.ppermute(x, 'core', [(0, 1), (1, 0)])]
    all_to_all x1, blocking collectives: 25.1 us -> 23.2 us  [per_device(): lax.all_to_all(partial.reshape(chips, 8, part // 2), CHIPS, 0, 0, tiled=T...]
    ppermute x3 -> x6, waiting for transfers between devices: 8.92 us -> 7.84 us  [shift(): return lax.ppermute(v, ALL, moves)]
    ppermute x7 -> x10, waiting for transfers between devices: 1.75 us -> 2.79 us  [swap_core(): return lax.ppermute(x, 'core', [(0, 1), (1, 0)])]
  transfers between devices with their start and end apart: 10 -> 16, of which waited for: 5 -> 8; matrix products, arithmetic and copies ran while one was open for 0% -> 0% of each run, Pallas kernels for 5% -> 5%
where the time goes in v5:
time: 118 us; the launch traced here: 117 us
  blocking collectives  73.8 us (63%)
  starting transfers between devices  18.5 us (16%)
  Pallas kernels  11.6 us (10%)
  waiting for transfers between devices  10.6 us (9%)
  between operations  1.6 us (1%)
    all_to_all x1, blocking collectives, per_device(): rows = lax.all_to_all(send, SEQ, 0, 0, tiled=True).reshape(slots, part)  30.3 us
    all_to_all x1, blocking collectives, per_device(): lax.all_to_all(partial.reshape(chips, 8, part // 2), CHIPS, 0, 0, tiled=T...  23.2 us
    all_to_all x1, blocking collectives, per_device(): stats = lax.all_to_all(stats, CHIPS, 0, 0, tiled=True)  20.2 us
    pallas_call x12, Pallas kernels, call(): pl.pallas_call(body, out_shape=out, in_specs=specs or [VMEM] * len(args),...  11.6 us
    ppermute x10, starting transfers between devices, swap_core(): return lax.ppermute(x, 'core', [(0, 1), (1, 0)])  10.9 us
    ppermute x6, waiting for transfers between devices, shift(): return lax.ppermute(v, ALL, moves)  7.84 us
    ppermute x6, starting transfers between devices, shift(): return lax.ppermute(v, ALL, moves)  7.61 us
    ppermute x10, waiting for transfers between devices, swap_core(): return lax.ppermute(x, 'core', [(0, 1), (1, 0)])  2.79 us
  transfers between devices with their start and end apart: 16, of which 8 were waited for; matrix products, arithmetic and copies ran while one was open for 0% of the time, Pallas kernels for 5%

profile of v5, /device:TPU:1, one launch (start us, length us, event | category | flops | bytes accessed | tf_op | source)
XLA Modules:
  0.0 117.5 jit_solution(5889197140312383185)
XLA Ops:
  1.4 2.2 %shard_map.68 = bf16[64,8,512]{2,1,0:T(8,128)(2,1)} custom-call(s32[1,8]{1,0:T(1,128)} %positions_hbm.1, s32[1,1]{1,0:T(1,128)} %bitcast.6.counts_hbm, bf16[64,4096]{1,0:T(8,128)(2,1)} %hidden.1), custom_call_target="tpu_custom_call" | custom-call | bytes 1048612 | tf_op jit(solution)/shard_map/pallas_call | solution.py:30
  3.6 30.3 %all_to_all.15 = bf16[64,8,512]{2,1,0:T(8,128)(2,1)S(1)} all-to-all(bf16[64,8,512]{2,1,0:T(8,128)(2,1)} %shard_map.68), channel_id=1, replica_groups=mesh['x'=4,'z'=8,'core'=2,'y'=4] {'x','z','core'}, dimensions={0} | all-to-all | bytes 1048576 | tf_op jit(solution)/shard_map/all_to_all | solution.py:271
  33.9 0.5 shard_map.69
  34.4 2.7 %collective-permute-start.5 = (bf16[256,512]{1,0:T(8,128)(2,1)S(1)}, bf16[256,512]{1,0:T(8,128)(2,1)S(1)}, u32[]{:S(2)}, u32[]{:S(2)}) collective-permute-start(bf16[256,512]{1,0:T(8,128)(2,1)S(1)} %get-tuple-element.29.a.refs_0_), channel_id=1, source_target_pairs={{0,3},{4,196},{1,0},{5,197},{2,1},{6,198},{3,2},{7,199},{8,11},{12... | collective-permute-start | bytes 786440 | tf_op jit(solution)/shard_map/ppermute | solution.py:246
  37.2 1.6 %collective-permute-start.3 = (bf16[256,512]{1,0:T(8,128)(2,1)S(1)}, bf16[256,512]{1,0:T(8,128)(2,1)S(1)}, u32[]{:S(2)}, u32[]{:S(2)}) collective-permute-start(bf16[256,512]{1,0:T(8,128)(2,1)S(1)} %get-tuple-element.29.a.refs_0_), channel_id=1, source_target_pairs={{0,2},{4,132},{1,3},{5,133},{2,0},{6,134},{3,1},{7,135},{8,10},{12... | collective-permute-start | bytes 786440 | tf_op jit(solution)/shard_map/ppermute | solution.py:246
  38.8 1.2 %collective-permute-start = (bf16[256,512]{1,0:T(8,128)(2,1)S(1)}, bf16[256,512]{1,0:T(8,128)(2,1)S(1)}, u32[]{:S(2)}, u32[]{:S(2)}) collective-permute-start(bf16[256,512]{1,0:T(8,128)(2,1)S(1)} %get-tuple-element.29.a.refs_0_), channel_id=1, source_target_pairs={{0,4},{4,0},{1,5},{5,1},{2,6},{6,2},{3,7},{7,3},{8,12},{12,8},{9,1... | collective-permute-start | bytes 786440 | tf_op jit(solution)/shard_map/ppermute | solution.py:233
  40.1 1.0 copy-done.1
  41.1 1.9 %shard_map.70 = (bf16[494,256]{1,0:T(8,128)(2,1)S(1)}, f32[8,256]{1,0:T(8,128)S(1)}, bf16[2,1024,256]{2,1,0:T(8,128)(2,1)S(1)}) custom-call(bf16[494,512]{1,0:T(8,128)(2,1)S(1)} %bitcast.13, bf16[256,512]{1,0:T(8,128)(2,1)S(1)} %get-tuple-element.30.chosen), custom_call_target="tpu_custom_call" | custom-call | flops 397934592 | bytes 2077696 | tf_op jit(solution)/shard_map/pallas_call | solution.py:30
  43.1 3.6 %collective-permute-done.1.b.refs_1_ = bf16[256,512]{1,0:T(8,128)(2,1)S(1)} collective-permute-done((bf16[256,512]{1,0:T(8,128)(2,1)S(1)}, bf16[256,512]{1,0:T(8,128)(2,1)S(1)}, u32[]{:S(2)}, u32[]{:S(2)}) %collective-permute-start.1) | collective-permute-done | bytes 262176 | tf_op jit(solution)/shard_map/ppermute | solution.py:246
  46.7 1.5 %collective-permute-start.4 = (bf16[256,512]{1,0:T(8,128)(2,1)S(1)}, bf16[256,512]{1,0:T(8,128)(2,1)S(1)}, u32[]{:S(2)}, u32[]{:S(2)}) collective-permute-start(bf16[256,512]{1,0:T(8,128)(2,1)S(1)} %collective-permute-done.3.c.refs_2_), channel_id=1, source_target_pairs={{0,4},{4,0},{1,5},{5,1},{2,6},{6,2},{3,7},{7,3},{8,12},{12,8},{9,1... | collective-permute-start | bytes 786440 | tf_op jit(solution)/shard_map/ppermute | solution.py:233
  48.3 0.7 shard_map.71.first
  49.0 0.4 collective-permute-done.4.c.refs_6_
  49.4 0.4 collective-permute-done.2.b.refs_5_
  49.8 0.9 shard_map.72
  50.7 20.2 %all_to_all.16.stats = f32[128,2,256]{2,1,0:T(2,128)S(1)} all-to-all(f32[128,2,256]{2,1,0:T(2,128)S(1)} %get-tuple-element.40), channel_id=1, replica_groups=mesh['x'=4,'z'=8,'core'=2,'y'=4] {'x','z','y'}, dimensions={0} | all-to-all | bytes 524288 | tf_op jit(solution)/shard_map/all_to_all | solution.py:299
  71.2 2.7 %collective-permute-start.7 = (f32[2,256]{1,0:T(2,128)S(1)}, f32[2,256]{1,0:T(2,128)S(1)}, u32[]{:S(2)}, u32[]{:S(2)}) collective-permute-start(f32[2,256]{1,0:T(2,128)S(1)} %shard_map.73.mine), channel_id=1, source_target_pairs={{0,4},{4,0},{1,5},{5,1},{2,6},{6,2},{3,7},{7,3},{8,12},{12,8},{9,1... | collective-permute-start | bytes 6152 | tf_op jit(solution)/shard_map/ppermute | solution.py:233
  73.9 0.8 collective-permute-done.7.other
  74.7 0.8 shard_map.74
  75.5 0.6 collective-permute-start.9
  76.3 0.3 collective-permute-start.11
  76.8 0.7 shard_map.75
  77.7 0.3 collective-permute-done.11
  78.1 1.4 %collective-permute-start.12 = (bf16[256,512]{1,0:T(8,128)(2,1)S(1)}, bf16[256,512]{1,0:T(8,128)(2,1)S(1)}, u32[]{:S(2)}, u32[]{:S(2)}) collective-permute-start(bf16[256,512]{1,0:T(8,128)(2,1)S(1)} %add_convert_fusion.1), channel_id=1, source_target_pairs={{0,2},{4,132},{1,3},{5,133},{2,0},{6,134},{3,1},{7,135},{8,10},{12... | collective-permute-start | bytes 786440 | tf_op jit(solution)/shard_map/ppermute | solution.py:246
  79.6 1.8 %collective-permute-start.14 = (bf16[256,512]{1,0:T(8,128)(2,1)S(1)}, bf16[256,512]{1,0:T(8,128)(2,1)S(1)}, u32[]{:S(2)}, u32[]{:S(2)}) collective-permute-start(bf16[256,512]{1,0:T(8,128)(2,1)S(1)} %add_convert_fusion), channel_id=1, source_target_pairs={{0,3},{4,196},{1,0},{5,197},{2,1},{6,198},{3,2},{7,199},{8,11},{12... | collective-permute-start | bytes 786440 | tf_op jit(solution)/shard_map/ppermute | solution.py:246
  81.4 2.3 %shard_map.76 = bf16[494,4096]{1,0:T(8,128)(2,1)} custom-call(bf16[256,512]{1,0:T(8,128)(2,1)S(1)} %get-tuple-element.29.a.refs_0_, bf16[256,512]{1,0:T(8,128)(2,1)S(1)} %collective-permute-done.1.b.refs_1_, bf16[256,512]{1,0:T(8,128)(2,1)S(1)} %collective-permute-done.3.c.refs_2_, bf16[256,512]{1,0:T(8,128)(2,1)S(1)} %collective-permute-done.5.d.refs_3_, ...), custom_call_target="tpu_custom_call" | custom-call | flops 1035993088 | bytes 6396928 | tf_op jit(solution)/shard_map/pallas_call | solution.py:30
  83.8 3.5 %collective-permute-done.10.b = bf16[256,512]{1,0:T(8,128)(2,1)S(1)} collective-permute-done((bf16[256,512]{1,0:T(8,128)(2,1)S(1)}, bf16[256,512]{1,0:T(8,128)(2,1)S(1)}, u32[]{:S(2)}, u32[]{:S(2)}) %collective-permute-start.10) | collective-permute-done | bytes 262176 | tf_op jit(solution)/shard_map/ppermute | solution.py:246
  87.3 0.8 collective-permute-done.14.d
  88.0 0.5 shard_map.77
  88.6 23.2 %all_to_all.17.parts = bf16[128,8,256]{2,1,0:T(8,128)(2,1)S(1)} all-to-all(bf16[128,8,256]{2,1,0:T(8,128)(2,1)S(1)} %bitcast.11), channel_id=1, replica_groups=mesh['x'=4,'z'=8,'core'=2,'y'=4] {'x','z','y'}, dimensions={0} | all-to-all | bytes 1048576 | tf_op jit(solution)/shard_map/all_to_all | solution.py:322
  111.9 4.1 %collective-permute-start.15 = (f32[4,4,256]{2,1,0:T(4,128)S(1)}, f32[4,4,256]{2,1,0:T(4,128)S(1)}, u32[]{:S(2)}, u32[]{:S(2)}) collective-permute-start(f32[4,4,256]{2,1,0:T(4,128)S(1)} %get-tuple-element.54), channel_id=1, source_target_pairs={{0,4},{4,0},{1,5},{5,1},{2,6},{6,2},{3,7},{7,3},{8,12},{12,8},{9,1... | collective-permute-start | bytes 49160 | tf_op jit(solution)/shard_map/ppermute | solution.py:233
  116.0 0.8 collective-permute-done.15.other
  116.8 0.6 shard_map.79
  (23 shorter events, 1.2 us)
Async XLA Ops:
  0.6 47.6 %copy-start = (bf16[4096,494]{0,1:T(8,128)(2,1)S(1)}, bf16[4096,494]{0,1:T(8,128)(2,1)}, u32[]{:S(2)}) copy-start(bf16[4096,494]{0,1:T(8,128)(2,1)} %param.6) | copy-start | bytes 12140548
  34.4 8.6 %collective-permute-start.5 = (bf16[256,512]{1,0:T(8,128)(2,1)S(1)}, bf16[256,512]{1,0:T(8,128)(2,1)S(1)}, u32[]{:S(2)}, u32[]{:S(2)}) collective-permute-start(bf16[256,512]{1,0:T(8,128)(2,1)S(1)} %get-tuple-element.29.a.refs_0_), channel_id=1, source_target_pairs={{0,3},{4,196},{1,0},{5,197},{2,1},{6,198},{3,2},{7,199},{8,11},{12... | collective-permute-start | bytes 786440 | tf_op jit(solution)/shard_map/ppermute | solution.py:246
  37.2 9.5 %collective-permute-start.1 = (bf16[256,512]{1,0:T(8,128)(2,1)S(1)}, bf16[256,512]{1,0:T(8,128)(2,1)S(1)}, u32[]{:S(2)}, u32[]{:S(2)}) collective-permute-start(bf16[256,512]{1,0:T(8,128)(2,1)S(1)} %get-tuple-element.29.a.refs_0_), channel_id=1, source_target_pairs={{0,1},{4,68},{1,2},{5,69},{2,3},{6,70},{3,0},{7,71},{8,9},{12,76},... | collective-permute-start | bytes 786440 | tf_op jit(solution)/shard_map/ppermute | solution.py:246
  37.2 9.5 %collective-permute-start.3 = (bf16[256,512]{1,0:T(8,128)(2,1)S(1)}, bf16[256,512]{1,0:T(8,128)(2,1)S(1)}, u32[]{:S(2)}, u32[]{:S(2)}) collective-permute-start(bf16[256,512]{1,0:T(8,128)(2,1)S(1)} %get-tuple-element.29.a.refs_0_), channel_id=1, source_target_pairs={{0,2},{4,132},{1,3},{5,133},{2,0},{6,134},{3,1},{7,135},{8,10},{12... | collective-permute-start | bytes 786440 | tf_op jit(solution)/shard_map/ppermute | solution.py:246
  38.8 10.2 %collective-permute-start = (bf16[256,512]{1,0:T(8,128)(2,1)S(1)}, bf16[256,512]{1,0:T(8,128)(2,1)S(1)}, u32[]{:S(2)}, u32[]{:S(2)}) collective-permute-start(bf16[256,512]{1,0:T(8,128)(2,1)S(1)} %get-tuple-element.29.a.refs_0_), channel_id=1, source_target_pairs={{0,4},{4,0},{1,5},{5,1},{2,6},{6,2},{3,7},{7,3},{8,12},{12,8},{9,1... | collective-permute-start | bytes 786440 | tf_op jit(solution)/shard_map/ppermute | solution.py:233
  40.1 1.0 copy-start.1
  43.0 6.0 %collective-permute-start.6 = (bf16[256,512]{1,0:T(8,128)(2,1)S(1)}, bf16[256,512]{1,0:T(8,128)(2,1)S(1)}, u32[]{:S(2)}, u32[]{:S(2)}) collective-permute-start(bf16[256,512]{1,0:T(8,128)(2,1)S(1)} %collective-permute-done.5.d.refs_3_), channel_id=1, source_target_pairs={{0,4},{4,0},{1,5},{5,1},{2,6},{6,2},{3,7},{7,3},{8,12},{12,8},{9,1... | collective-permute-start | bytes 786440 | tf_op jit(solution)/shard_map/ppermute | solution.py:233
  46.7 2.7 %collective-permute-start.4 = (bf16[256,512]{1,0:T(8,128)(2,1)S(1)}, bf16[256,512]{1,0:T(8,128)(2,1)S(1)}, u32[]{:S(2)}, u32[]{:S(2)}) collective-permute-start(bf16[256,512]{1,0:T(8,128)(2,1)S(1)} %collective-permute-done.3.c.refs_2_), channel_id=1, source_target_pairs={{0,4},{4,0},{1,5},{5,1},{2,6},{6,2},{3,7},{7,3},{8,12},{12,8},{9,1... | collective-permute-start | bytes 786440 | tf_op jit(solution)/shard_map/ppermute | solution.py:233
  48.3 1.5 %collective-permute-start.2 = (bf16[256,512]{1,0:T(8,128)(2,1)S(1)}, bf16[256,512]{1,0:T(8,128)(2,1)S(1)}, u32[]{:S(2)}, u32[]{:S(2)}) collective-permute-start(bf16[256,512]{1,0:T(8,128)(2,1)S(1)} %collective-permute-done.1.b.refs_1_), channel_id=1, source_target_pairs={{0,4},{4,0},{1,5},{5,1},{2,6},{6,2},{3,7},{7,3},{8,12},{12,8},{9,1... | collective-permute-start | bytes 786440 | tf_op jit(solution)/shard_map/ppermute | solution.py:233
  71.2 3.5 %collective-permute-start.7 = (f32[2,256]{1,0:T(2,128)S(1)}, f32[2,256]{1,0:T(2,128)S(1)}, u32[]{:S(2)}, u32[]{:S(2)}) collective-permute-start(f32[2,256]{1,0:T(2,128)S(1)} %shard_map.73.mine), channel_id=1, source_target_pairs={{0,4},{4,0},{1,5},{5,1},{2,6},{6,2},{3,7},{7,3},{8,12},{12,8},{9,1... | collective-permute-start | bytes 6152 | tf_op jit(solution)/shard_map/ppermute | solution.py:233
  75.5 2.0 %collective-permute-start.9 = (bf16[256,512]{1,0:T(8,128)(2,1)S(1)}, bf16[256,512]{1,0:T(8,128)(2,1)S(1)}, u32[]{:S(2)}, u32[]{:S(2)}) collective-permute-start(bf16[256,512]{1,0:T(8,128)(2,1)S(1)} %get-tuple-element.46), channel_id=1, source_target_pairs={{0,4},{4,0},{1,5},{5,1},{2,6},{6,2},{3,7},{7,3},{8,12},{12,8},{9,1... | collective-permute-start | bytes 786440 | tf_op jit(solution)/shard_map/ppermute | solution.py:233
  76.1 7.6 %collective-permute-start.8 = (bf16[256,512]{1,0:T(8,128)(2,1)S(1)}, bf16[256,512]{1,0:T(8,128)(2,1)S(1)}, u32[]{:S(2)}, u32[]{:S(2)}) collective-permute-start(bf16[256,512]{1,0:T(8,128)(2,1)S(1)} %get-tuple-element.44), channel_id=1, source_target_pairs={{0,4},{4,0},{1,5},{5,1},{2,6},{6,2},{3,7},{7,3},{8,12},{12,8},{9,1... | collective-permute-start | bytes 786440 | tf_op jit(solution)/shard_map/ppermute | solution.py:233
  76.3 1.8 %collective-permute-start.11 = (bf16[256,512]{1,0:T(8,128)(2,1)S(1)}, bf16[256,512]{1,0:T(8,128)(2,1)S(1)}, u32[]{:S(2)}, u32[]{:S(2)}) collective-permute-start(bf16[256,512]{1,0:T(8,128)(2,1)S(1)} %get-tuple-element.49), channel_id=1, source_target_pairs={{0,4},{4,0},{1,5},{5,1},{2,6},{6,2},{3,7},{7,3},{8,12},{12,8},{9,1... | collective-permute-start | bytes 786440 | tf_op jit(solution)/shard_map/ppermute | solution.py:233
  76.6 2.9 %collective-permute-start.13 = (bf16[256,512]{1,0:T(8,128)(2,1)S(1)}, bf16[256,512]{1,0:T(8,128)(2,1)S(1)}, u32[]{:S(2)}, u32[]{:S(2)}) collective-permute-start(bf16[256,512]{1,0:T(8,128)(2,1)S(1)} %get-tuple-element.51), channel_id=1, source_target_pairs={{0,4},{4,0},{1,5},{5,1},{2,6},{6,2},{3,7},{7,3},{8,12},{12,8},{9,1... | collective-permute-start | bytes 786440 | tf_op jit(solution)/shard_map/ppermute | solution.py:233
  77.6 9.6 %collective-permute-start.10 = (bf16[256,512]{1,0:T(8,128)(2,1)S(1)}, bf16[256,512]{1,0:T(8,128)(2,1)S(1)}, u32[]{:S(2)}, u32[]{:S(2)}) collective-permute-start(bf16[256,512]{1,0:T(8,128)(2,1)S(1)} %add_convert_fusion.2), channel_id=1, source_target_pairs={{0,1},{4,68},{1,2},{5,69},{2,3},{6,70},{3,0},{7,71},{8,9},{12,76},... | collective-permute-start | bytes 786440 | tf_op jit(solution)/shard_map/ppermute | solution.py:246
  78.1 9.1 %collective-permute-start.12 = (bf16[256,512]{1,0:T(8,128)(2,1)S(1)}, bf16[256,512]{1,0:T(8,128)(2,1)S(1)}, u32[]{:S(2)}, u32[]{:S(2)}) collective-permute-start(bf16[256,512]{1,0:T(8,128)(2,1)S(1)} %add_convert_fusion.1), channel_id=1, source_target_pairs={{0,2},{4,132},{1,3},{5,133},{2,0},{6,134},{3,1},{7,135},{8,10},{12... | collective-permute-start | bytes 786440 | tf_op jit(solution)/shard_map/ppermute | solution.py:246
  79.6 8.5 %collective-permute-start.14 = (bf16[256,512]{1,0:T(8,128)(2,1)S(1)}, bf16[256,512]{1,0:T(8,128)(2,1)S(1)}, u32[]{:S(2)}, u32[]{:S(2)}) collective-permute-start(bf16[256,512]{1,0:T(8,128)(2,1)S(1)} %add_convert_fusion), channel_id=1, source_target_pairs={{0,3},{4,196},{1,0},{5,197},{2,1},{6,198},{3,2},{7,199},{8,11},{12... | collective-permute-start | bytes 786440 | tf_op jit(solution)/shard_map/ppermute | solution.py:246
  111.9 4.9 %collective-permute-start.15 = (f32[4,4,256]{2,1,0:T(4,128)S(1)}, f32[4,4,256]{2,1,0:T(4,128)S(1)}, u32[]{:S(2)}, u32[]{:S(2)}) collective-permute-start(f32[4,4,256]{2,1,0:T(4,128)S(1)} %get-tuple-element.54), channel_id=1, source_target_pairs={{0,4},{4,0},{1,5},{5,1},{2,6},{6,2},{3,7},{7,3},{8,12},{12,8},{9,1... | collective-permute-start | bytes 49160 | tf_op jit(solution)/shard_map/ppermute | solution.py:233

commit v6 on v5

--- a/solution.py
+++ b/solution.py
@@ -1,3 +1,5 @@
+import functools
+
 import jax
 import jax.numpy as jnp
 from jax import lax
@@ -14,6 +16,8 @@
 CHIPS = ("x", "z", "y")
 NX, NZ, NCORE, NY = 4, 8, 2, 4
 RING = 4
+FIRST = ((0, 0), (0, 1), (0, 2), (0, 3), (1, 0), (1, 2))
+LAST = ((1, 3), (1, 1))
 assert NX == NY == RING
 F32, BF16 = jnp.float32, jnp.bfloat16
 NT = (((1,), (1,)), ((), ()))
@@ -128,9 +132,8 @@
     lse[...] = jnp.broadcast_to(logsumexp(rows), lse.shape)
 
 
-def student_part(blocks, weight, side):
-    total = jnp.zeros((weight.shape[0], MASKED), F32)
-    for k, block in enumerate(blocks):
+def student_part(blocks, which, weight, total):
+    for block, (side, k) in zip(blocks, which):
         total += lax.dot_general(
             weight[:, columns(part_at(side, -k), block.shape[1])], block[...],
             NT, preferred_element_type=F32,
@@ -138,12 +141,14 @@
     return total
 
 
-def student_ours_body(a, b, c, d, weight, total):
-    total[...] = student_part((a, b, c, d), weight, 0)
-
-
-def student_theirs_body(a, b, c, d, weight, first, lse_teacher, out, stats):
-    total = first[...] + student_part((a, b, c, d), weight, 1)
+def student_first_body(*refs):
+    blocks, (weight, total) = refs[: len(FIRST)], refs[len(FIRST) :]
+    total[...] = student_part(blocks, FIRST, weight, jnp.zeros(total.shape, F32))
+
+
+def student_last_body(*refs):
+    blocks, (weight, first, lse_teacher, out, stats) = refs[: len(LAST)], refs[len(LAST) :]
+    total = student_part(blocks, LAST, weight, first[...])
     out[...] = total
     both = jnp.concatenate([logsumexp(total), lse_teacher[0:1, :]], axis=0)
     stats[...] = jnp.broadcast_to(both[None], stats.shape)
@@ -155,15 +160,15 @@
     out[...] = top + jnp.log(jnp.sum(jnp.exp(x - top[None]), axis=0))
 
 
-def products(grad, weight, side, parts):
-    for k, part in enumerate(parts):
+def products(grad, weight, which, parts):
+    for part, (side, k) in zip(parts, which):
         part[...] = lax.dot_general(
             grad, weight[:, columns(part_at(side, k), part.shape[1])], TN,
             preferred_element_type=F32,
         ).astype(part.dtype)
 
 
-def logits_body(student, teacher, mine, other, count, weight, grad_logits, *parts):
+def logits_body(student, teacher, mine, other, count, weight, grad_logits, *parts, which):
     top = jnp.maximum(mine[...], other[...])
     lse = top + jnp.log(jnp.exp(mine[...] - top) + jnp.exp(other[...] - top))
     scale = LOSS_SCALE / count[0:1, :]
@@ -171,11 +176,11 @@
     prob_teacher = jnp.exp(teacher[...].astype(F32) - lse[1:2, :])
     grad = (scale * (prob_student - prob_teacher)).astype(BF16)
     grad_logits[...] = grad
-    products(grad, weight, 1, parts)
-
-
-def products_body(grad_logits, weight, *parts):
-    products(grad_logits[...], weight, 0, parts)
+    products(grad, weight, which, parts)
+
+
+def products_body(grad_logits, weight, *parts, which):
+    products(grad_logits[...], weight, which, parts)
 
 
 def head_body(*refs):
@@ -276,7 +281,7 @@
         ),
         rows, flops=2 * MASKED * slots * part,
     )
-    blocks = [picked] + [shift(picked, k) for k in range(1, RING)]
+    blocks = {(0, 0): picked} | {(0, k): shift(picked, k) for k in range(1, RING)}
     staged = call(
         teacher_body,
         (
@@ -287,30 +292,40 @@
         scratch=[pltpu.VMEM((vocab, slots), BF16), DMA(())],
         flops=2 * vocab * slots * MASKED + 4 * slots * slots * MASKED,
     )
-    blocks[1], staged = lax.optimization_barrier((blocks[1], staged))
+    blocks[0, 2], staged = lax.optimization_barrier((blocks[0, 2], staged))
     teacher_rows, lse_teacher, back = staged
-    others = [swap_core(block) for block in blocks]
-    total = call(student_ours_body, logits_shape, *blocks, weight, flops=half_flops)
-    others[-1], total = lax.optimization_barrier((others[-1], total))
+    blocks |= {(1, k): swap_core(blocks[0, k]) for k in range(RING)}
+    total = call(
+        student_first_body, logits_shape, *[blocks[at] for at in FIRST], weight, flops=half_flops
+    )
+    blocks[1, 1], total = lax.optimization_barrier((blocks[1, 1], total))
     student, stats = call(
-        student_theirs_body, (logits_shape, shape((chips, 2, MASKED), F32)),
-        *others, weight, total, lse_teacher, flops=half_flops,
+        student_last_body, (logits_shape, shape((chips, 2, MASKED), F32)),
+        *[blocks[at] for at in LAST], weight, total, lse_teacher, flops=half_flops,
     )
     stats = lax.all_to_all(stats, CHIPS, 0, 0, tiled=True)
     lse = call(combine_body, shape((2, MASKED), F32), stats)
-    grad_logits, *theirs = call(
-        logits_body,
-        (shape((vocab, MASKED), BF16),) + (shape((MASKED, part), BF16),) * RING,
-        student, teacher_rows, lse, swap_core(lse), count, weight, flops=half_flops,
-    )
-    ours = call(
-        products_body, (shape((MASKED, part), F32),) * RING, grad_logits, weight,
-        flops=half_flops,
-    )
-    sums = [(a + swap_core(b).astype(F32)).astype(BF16) for a, b in zip(ours, theirs)]
-    sums = sums[:1] + [shift(sums[k], k) for k in range(1, RING)]
+    parts = {}
+    which = ((1, 2),)
+    grad_logits, parts[1, 2] = call(
+        functools.partial(logits_body, which=which),
+        (shape((vocab, MASKED), BF16), shape((MASKED, part), BF16)),
+        student, teacher_rows, lse, swap_core(lse), count, weight, flops=half_flops // 4,
+    )
+    for which in (((0, 2), (1, 1), (1, 3)), ((0, 1), (0, 3)), ((1, 0), (0, 0))):
+        out = tuple(shape((MASKED, part), BF16 if side else F32) for side, k in which)
+        made = call(
+            functools.partial(products_body, which=which), out, grad_logits, weight,
+            flops=half_flops * len(which) // 4,
+        )
+        parts |= dict(zip(which, made))
+    both = {
+        k: (parts[0, k] + swap_core(parts[1, k]).astype(F32)).astype(BF16) for k in range(RING)
+    }
+    sums = [both[0]] + [shift(both[k], k) for k in range(1, RING)]
     grad_head = call(
-        head_body, shape((vocab, depth), BF16), *blocks, *others, grad_logits, outs=HBM,
+        head_body, shape((vocab, depth), BF16),
+        *[blocks[side, k] for side in range(NCORE) for k in range(RING)], grad_logits, outs=HBM,
         scratch=[pltpu.VMEM((NCORE * RING, vocab, part), BF16), DMA((NCORE * RING,))],
         flops=2 * half_flops,
     )

time: 118 us -> 116 us (0.983)
  waiting for transfers between devices: 10.6 us -> 6.33 us
    ppermute x6, waiting for transfers between devices: 7.84 us -> 4.38 us  [shift(): return lax.ppermute(v, ALL, moves)]
    all_to_all x1, blocking collectives: 20.2 us -> 22.4 us  [per_device(): stats = lax.all_to_all(stats, CHIPS, 0, 0, tiled=True)]
    pallas_call x12 -> x14, Pallas kernels: 11.6 us -> 12 us  [call(): pl.pallas_call(body, out_shape=out, in_specs=specs or [VMEM] * len(args),...]
  transfers between devices with their start and end apart: 16 -> 16, of which waited for: 8 -> 4; matrix products, arithmetic and copies ran while one was open for 0% -> 0% of each run, Pallas kernels for 5% -> 6%
where the time goes in v6:
time: 116 us
  blocking collectives  74.9 us (65%)
  starting transfers between devices  19.5 us (17%)
  Pallas kernels  12 us (10%)
  waiting for transfers between devices  6.33 us (5%)
  between operations  1.59 us (1%)
    all_to_all x1, blocking collectives, per_device(): rows = lax.all_to_all(send, SEQ, 0, 0, tiled=True).reshape(slots, part)  30.3 us
    all_to_all x1, blocking collectives, per_device(): stats = lax.all_to_all(stats, CHIPS, 0, 0, tiled=True)  22.4 us
    all_to_all x1, blocking collectives, per_device(): lax.all_to_all(partial.reshape(chips, 8, part // 2), CHIPS, 0, 0, tiled=T...  22.2 us
    pallas_call x14, Pallas kernels, call(): pl.pallas_call(body, out_shape=out, in_specs=specs or [VMEM] * len(args),...  12 us
    ppermute x10, starting transfers between devices, swap_core(): return lax.ppermute(x, 'core', [(0, 1), (1, 0)])  10.9 us
    ppermute x6, starting transfers between devices, shift(): return lax.ppermute(v, ALL, moves)  8.58 us
    ppermute x6, waiting for transfers between devices, shift(): return lax.ppermute(v, ALL, moves)  4.38 us
  transfers between devices with their start and end apart: 16, of which 4 were waited for; matrix products, arithmetic and copies ran while one was open for 0% of the time, Pallas kernels for 6%

profile of v6, /device:TPU:1, one launch (start us, length us, event | category | flops | bytes accessed | tf_op | source)
XLA Modules:
  0.0 115.6 jit_solution(9966038269821139985)
XLA Ops:
  1.4 2.2 %shard_map.68 = bf16[64,8,512]{2,1,0:T(8,128)(2,1)} custom-call(s32[1,8]{1,0:T(1,128)} %positions_hbm.1, s32[1,1]{1,0:T(1,128)} %bitcast.6.counts_hbm, bf16[64,4096]{1,0:T(8,128)(2,1)} %hidden.1), custom_call_target="tpu_custom_call" | custom-call | bytes 1048612 | tf_op jit(solution)/shard_map/pallas_call | solution.py:34
  3.6 30.3 %all_to_all.15 = bf16[64,8,512]{2,1,0:T(8,128)(2,1)S(1)} all-to-all(bf16[64,8,512]{2,1,0:T(8,128)(2,1)} %shard_map.68), channel_id=1, replica_groups=mesh['x'=4,'z'=8,'core'=2,'y'=4] {'x','z','core'}, dimensions={0} | all-to-all | bytes 1048576 | tf_op jit(solution)/shard_map/all_to_all | solution.py:276
  33.9 0.5 shard_map.69
  34.4 2.9 %collective-permute-start.4 = (bf16[256,512]{1,0:T(8,128)(2,1)S(1)}, bf16[256,512]{1,0:T(8,128)(2,1)S(1)}, u32[]{:S(2)}, u32[]{:S(2)}) collective-permute-start(bf16[256,512]{1,0:T(8,128)(2,1)S(1)} %get-tuple-element.29.refs_0_), channel_id=1, source_target_pairs={{0,2},{4,132},{1,3},{5,133},{2,0},{6,134},{3,1},{7,135},{8,10},{12... | collective-permute-start | bytes 786440 | tf_op jit(solution)/shard_map/ppermute | solution.py:251
  37.4 0.4 collective-permute-start.2
  37.8 2.3 %collective-permute-start = (bf16[256,512]{1,0:T(8,128)(2,1)S(1)}, bf16[256,512]{1,0:T(8,128)(2,1)S(1)}, u32[]{:S(2)}, u32[]{:S(2)}) collective-permute-start(bf16[256,512]{1,0:T(8,128)(2,1)S(1)} %get-tuple-element.29.refs_0_), channel_id=1, source_target_pairs={{0,3},{4,196},{1,0},{5,197},{2,1},{6,198},{3,2},{7,199},{8,11},{12... | collective-permute-start | bytes 786440 | tf_op jit(solution)/shard_map/ppermute | solution.py:251
  40.0 1.2 %collective-permute-start.5 = (bf16[256,512]{1,0:T(8,128)(2,1)S(1)}, bf16[256,512]{1,0:T(8,128)(2,1)S(1)}, u32[]{:S(2)}, u32[]{:S(2)}) collective-permute-start(bf16[256,512]{1,0:T(8,128)(2,1)S(1)} %get-tuple-element.29.refs_0_), channel_id=1, source_target_pairs={{0,4},{4,0},{1,5},{5,1},{2,6},{6,2},{3,7},{7,3},{8,12},{12,8},{9,1... | collective-permute-start | bytes 786440 | tf_op jit(solution)/shard_map/ppermute | solution.py:238
  41.3 1.0 copy-done.1
  42.3 1.9 %shard_map.70 = (bf16[494,256]{1,0:T(8,128)(2,1)S(1)}, f32[8,256]{1,0:T(8,128)S(1)}, bf16[2,1024,256]{2,1,0:T(8,128)(2,1)S(1)}) custom-call(bf16[494,512]{1,0:T(8,128)(2,1)S(1)} %bitcast.15, bf16[256,512]{1,0:T(8,128)(2,1)S(1)} %get-tuple-element.30.chosen), custom_call_target="tpu_custom_call" | custom-call | flops 397934592 | bytes 2077696 | tf_op jit(solution)/shard_map/pallas_call | solution.py:34
  44.4 1.3 %collective-permute-start.3 = (bf16[256,512]{1,0:T(8,128)(2,1)S(1)}, bf16[256,512]{1,0:T(8,128)(2,1)S(1)}, u32[]{:S(2)}, u32[]{:S(2)}) collective-permute-start(bf16[256,512]{1,0:T(8,128)(2,1)S(1)} %collective-permute-done.2.refs_1_), channel_id=1, source_target_pairs={{0,4},{4,0},{1,5},{5,1},{2,6},{6,2},{3,7},{7,3},{8,12},{12,8},{9,1... | collective-permute-start | bytes 786440 | tf_op jit(solution)/shard_map/ppermute | solution.py:238
  45.9 1.0 shard_map.71.refs_3_
  46.9 0.3 collective-permute-done.1.refs_0_.refs_7_
  47.2 0.7 shard_map.72
  47.8 22.4 %all_to_all.16.stats = f32[128,2,256]{2,1,0:T(2,128)S(1)} all-to-all(f32[128,2,256]{2,1,0:T(2,128)S(1)} %get-tuple-element.40), channel_id=1, replica_groups=mesh['x'=4,'z'=8,'core'=2,'y'=4] {'x','z','y'}, dimensions={0} | all-to-all | bytes 524288 | tf_op jit(solution)/shard_map/all_to_all | solution.py:306
  70.5 2.7 %collective-permute-start.7 = (f32[2,256]{1,0:T(2,128)S(1)}, f32[2,256]{1,0:T(2,128)S(1)}, u32[]{:S(2)}, u32[]{:S(2)}) collective-permute-start(f32[2,256]{1,0:T(2,128)S(1)} %shard_map.73.mine), channel_id=1, source_target_pairs={{0,4},{4,0},{1,5},{5,1},{2,6},{6,2},{3,7},{7,3},{8,12},{12,8},{9,1... | collective-permute-start | bytes 6152 | tf_op jit(solution)/shard_map/ppermute | solution.py:238
  73.1 0.8 collective-permute-done.7.other
  73.9 0.4 shard_map.74
  74.4 0.6 collective-permute-start.11
  75.0 0.6 shard_map.77
  75.8 0.5 shard_map.75
  76.3 0.5 shard_map.76
  76.8 0.4 collective-permute-start.8
  77.5 1.4 %collective-permute-start.12 = (bf16[256,512]{1,0:T(8,128)(2,1)S(1)}, bf16[256,512]{1,0:T(8,128)(2,1)S(1)}, u32[]{:S(2)}, u32[]{:S(2)}) collective-permute-start(bf16[256,512]{1,0:T(8,128)(2,1)S(1)} %add_convert_fusion.1), channel_id=1, source_target_pairs={{0,2},{4,132},{1,3},{5,133},{2,0},{6,134},{3,1},{7,135},{8,10},{12... | collective-permute-start | bytes 786440 | tf_op jit(solution)/shard_map/ppermute | solution.py:251
  78.9 1.0 collective-permute-start.14
  80.0 0.6 collective-permute-start.10
  80.6 2.3 %shard_map.78 = bf16[494,4096]{1,0:T(8,128)(2,1)} custom-call(bf16[256,512]{1,0:T(8,128)(2,1)S(1)} %get-tuple-element.29.refs_0_, bf16[256,512]{1,0:T(8,128)(2,1)S(1)} %collective-permute-done.2.refs_1_, bf16[256,512]{1,0:T(8,128)(2,1)S(1)} %collective-permute-done.4.refs_2_, bf16[256,512]{1,0:T(8,128)(2,1)S(1)} %collective-permute-done.refs_3_, ...), custom_call_target="tpu_custom_call" | custom-call | flops 1035993088 | bytes 6396928 | tf_op jit(solution)/shard_map/pallas_call | solution.py:34
  83.0 4.3 %collective-permute-done.10.b = bf16[256,512]{1,0:T(8,128)(2,1)S(1)} collective-permute-done((bf16[256,512]{1,0:T(8,128)(2,1)S(1)}, bf16[256,512]{1,0:T(8,128)(2,1)S(1)}, u32[]{:S(2)}, u32[]{:S(2)}) %collective-permute-start.10) | collective-permute-done | bytes 262176 | tf_op jit(solution)/shard_map/ppermute | solution.py:251
  87.4 0.5 shard_map.79
  87.9 22.2 %all_to_all.17.parts = bf16[128,8,256]{2,1,0:T(8,128)(2,1)S(1)} all-to-all(bf16[128,8,256]{2,1,0:T(8,128)(2,1)S(1)} %bitcast.13), channel_id=1, replica_groups=mesh['x'=4,'z'=8,'core'=2,'y'=4] {'x','z','y'}, dimensions={0} | all-to-all | bytes 1048576 | tf_op jit(solution)/shard_map/all_to_all | solution.py:337
  110.2 3.9 %collective-permute-start.15 = (f32[4,4,256]{2,1,0:T(4,128)S(1)}, f32[4,4,256]{2,1,0:T(4,128)S(1)}, u32[]{:S(2)}, u32[]{:S(2)}) collective-permute-start(f32[4,4,256]{2,1,0:T(4,128)S(1)} %get-tuple-element.54), channel_id=1, source_target_pairs={{0,4},{4,0},{1,5},{5,1},{2,6},{6,2},{3,7},{7,3},{8,12},{12,8},{9,1... | collective-permute-start | bytes 49160 | tf_op jit(solution)/shard_map/ppermute | solution.py:238
  114.2 0.8 collective-permute-done.15.other
  115.0 0.6 shard_map.81
  (25 shorter events, 1.5 us)
Async XLA Ops:
  0.6 45.3 %copy-start = (bf16[4096,494]{0,1:T(8,128)(2,1)S(1)}, bf16[4096,494]{0,1:T(8,128)(2,1)}, u32[]{:S(2)}) copy-start(bf16[4096,494]{0,1:T(8,128)(2,1)} %param.6) | copy-start | bytes 12140548
  34.4 9.8 %collective-permute-start.4 = (bf16[256,512]{1,0:T(8,128)(2,1)S(1)}, bf16[256,512]{1,0:T(8,128)(2,1)S(1)}, u32[]{:S(2)}, u32[]{:S(2)}) collective-permute-start(bf16[256,512]{1,0:T(8,128)(2,1)S(1)} %get-tuple-element.29.refs_0_), channel_id=1, source_target_pairs={{0,2},{4,132},{1,3},{5,133},{2,0},{6,134},{3,1},{7,135},{8,10},{12... | collective-permute-start | bytes 786440 | tf_op jit(solution)/shard_map/ppermute | solution.py:251
  37.4 7.0 %collective-permute-start.2 = (bf16[256,512]{1,0:T(8,128)(2,1)S(1)}, bf16[256,512]{1,0:T(8,128)(2,1)S(1)}, u32[]{:S(2)}, u32[]{:S(2)}) collective-permute-start(bf16[256,512]{1,0:T(8,128)(2,1)S(1)} %get-tuple-element.29.refs_0_), channel_id=1, source_target_pairs={{0,1},{4,68},{1,2},{5,69},{2,3},{6,70},{3,0},{7,71},{8,9},{12,76},... | collective-permute-start | bytes 786440 | tf_op jit(solution)/shard_map/ppermute | solution.py:251
  37.8 7.9 %collective-permute-start = (bf16[256,512]{1,0:T(8,128)(2,1)S(1)}, bf16[256,512]{1,0:T(8,128)(2,1)S(1)}, u32[]{:S(2)}, u32[]{:S(2)}) collective-permute-start(bf16[256,512]{1,0:T(8,128)(2,1)S(1)} %get-tuple-element.29.refs_0_), channel_id=1, source_target_pairs={{0,3},{4,196},{1,0},{5,197},{2,1},{6,198},{3,2},{7,199},{8,11},{12... | collective-permute-start | bytes 786440 | tf_op jit(solution)/shard_map/ppermute | solution.py:251
  40.0 5.8 %collective-permute-start.5 = (bf16[256,512]{1,0:T(8,128)(2,1)S(1)}, bf16[256,512]{1,0:T(8,128)(2,1)S(1)}, u32[]{:S(2)}, u32[]{:S(2)}) collective-permute-start(bf16[256,512]{1,0:T(8,128)(2,1)S(1)} %get-tuple-element.29.refs_0_), channel_id=1, source_target_pairs={{0,4},{4,0},{1,5},{5,1},{2,6},{6,2},{3,7},{7,3},{8,12},{12,8},{9,1... | collective-permute-start | bytes 786440 | tf_op jit(solution)/shard_map/ppermute | solution.py:238
  41.3 1.0 copy-start.1
  44.2 1.6 %collective-permute-start.6 = (bf16[256,512]{1,0:T(8,128)(2,1)S(1)}, bf16[256,512]{1,0:T(8,128)(2,1)S(1)}, u32[]{:S(2)}, u32[]{:S(2)}) collective-permute-start(bf16[256,512]{1,0:T(8,128)(2,1)S(1)} %collective-permute-done.4.refs_2_), channel_id=1, source_target_pairs={{0,4},{4,0},{1,5},{5,1},{2,6},{6,2},{3,7},{7,3},{8,12},{12,8},{9,1... | collective-permute-start | bytes 786440 | tf_op jit(solution)/shard_map/ppermute | solution.py:238
  44.4 2.5 %collective-permute-start.3 = (bf16[256,512]{1,0:T(8,128)(2,1)S(1)}, bf16[256,512]{1,0:T(8,128)(2,1)S(1)}, u32[]{:S(2)}, u32[]{:S(2)}) collective-permute-start(bf16[256,512]{1,0:T(8,128)(2,1)S(1)} %collective-permute-done.2.refs_1_), channel_id=1, source_target_pairs={{0,4},{4,0},{1,5},{5,1},{2,6},{6,2},{3,7},{7,3},{8,12},{12,8},{9,1... | collective-permute-start | bytes 786440 | tf_op jit(solution)/shard_map/ppermute | solution.py:238
  45.6 1.5 %collective-permute-start.1 = (bf16[256,512]{1,0:T(8,128)(2,1)S(1)}, bf16[256,512]{1,0:T(8,128)(2,1)S(1)}, u32[]{:S(2)}, u32[]{:S(2)}) collective-permute-start(bf16[256,512]{1,0:T(8,128)(2,1)S(1)} %collective-permute-done.refs_3_), channel_id=1, source_target_pairs={{0,4},{4,0},{1,5},{5,1},{2,6},{6,2},{3,7},{7,3},{8,12},{12,8},{9,1... | collective-permute-start | bytes 786440 | tf_op jit(solution)/shard_map/ppermute | solution.py:238
  70.5 3.5 %collective-permute-start.7 = (f32[2,256]{1,0:T(2,128)S(1)}, f32[2,256]{1,0:T(2,128)S(1)}, u32[]{:S(2)}, u32[]{:S(2)}) collective-permute-start(f32[2,256]{1,0:T(2,128)S(1)} %shard_map.73.mine), channel_id=1, source_target_pairs={{0,4},{4,0},{1,5},{5,1},{2,6},{6,2},{3,7},{7,3},{8,12},{12,8},{9,1... | collective-permute-start | bytes 6152 | tf_op jit(solution)/shard_map/ppermute | solution.py:238
  74.4 3.0 %collective-permute-start.11 = (bf16[256,512]{1,0:T(8,128)(2,1)S(1)}, bf16[256,512]{1,0:T(8,128)(2,1)S(1)}, u32[]{:S(2)}, u32[]{:S(2)}) collective-permute-start(bf16[256,512]{1,0:T(8,128)(2,1)S(1)} %get-tuple-element.49), channel_id=1, source_target_pairs={{0,4},{4,0},{1,5},{5,1},{2,6},{6,2},{3,7},{7,3},{8,12},{12,8},{9,1... | collective-permute-start | bytes 786440 | tf_op jit(solution)/shard_map/ppermute | solution.py:238
  75.6 3.2 %collective-permute-start.13 = (bf16[256,512]{1,0:T(8,128)(2,1)S(1)}, bf16[256,512]{1,0:T(8,128)(2,1)S(1)}, u32[]{:S(2)}, u32[]{:S(2)}) collective-permute-start(bf16[256,512]{1,0:T(8,128)(2,1)S(1)} %get-tuple-element.51), channel_id=1, source_target_pairs={{0,4},{4,0},{1,5},{5,1},{2,6},{6,2},{3,7},{7,3},{8,12},{12,8},{9,1... | collective-permute-start | bytes 786440 | tf_op jit(solution)/shard_map/ppermute | solution.py:238
  76.8 6.2 %collective-permute-start.8 = (bf16[256,512]{1,0:T(8,128)(2,1)S(1)}, bf16[256,512]{1,0:T(8,128)(2,1)S(1)}, u32[]{:S(2)}, u32[]{:S(2)}) collective-permute-start(bf16[256,512]{1,0:T(8,128)(2,1)S(1)} %get-tuple-element.44), channel_id=1, source_target_pairs={{0,4},{4,0},{1,5},{5,1},{2,6},{6,2},{3,7},{7,3},{8,12},{12,8},{9,1... | collective-permute-start | bytes 786440 | tf_op jit(solution)/shard_map/ppermute | solution.py:238
  77.2 2.8 %collective-permute-start.9 = (bf16[256,512]{1,0:T(8,128)(2,1)S(1)}, bf16[256,512]{1,0:T(8,128)(2,1)S(1)}, u32[]{:S(2)}, u32[]{:S(2)}) collective-permute-start(bf16[256,512]{1,0:T(8,128)(2,1)S(1)} %get-tuple-element.46), channel_id=1, source_target_pairs={{0,4},{4,0},{1,5},{5,1},{2,6},{6,2},{3,7},{7,3},{8,12},{12,8},{9,1... | collective-permute-start | bytes 786440 | tf_op jit(solution)/shard_map/ppermute | solution.py:238
  77.5 9.9 %collective-permute-start.12 = (bf16[256,512]{1,0:T(8,128)(2,1)S(1)}, bf16[256,512]{1,0:T(8,128)(2,1)S(1)}, u32[]{:S(2)}, u32[]{:S(2)}) collective-permute-start(bf16[256,512]{1,0:T(8,128)(2,1)S(1)} %add_convert_fusion.1), channel_id=1, source_target_pairs={{0,2},{4,132},{1,3},{5,133},{2,0},{6,134},{3,1},{7,135},{8,10},{12... | collective-permute-start | bytes 786440 | tf_op jit(solution)/shard_map/ppermute | solution.py:251
  78.9 8.5 %collective-permute-start.14 = (bf16[256,512]{1,0:T(8,128)(2,1)S(1)}, bf16[256,512]{1,0:T(8,128)(2,1)S(1)}, u32[]{:S(2)}, u32[]{:S(2)}) collective-permute-start(bf16[256,512]{1,0:T(8,128)(2,1)S(1)} %add_convert_fusion), channel_id=1, source_target_pairs={{0,3},{4,196},{1,0},{5,197},{2,1},{6,198},{3,2},{7,199},{8,11},{12... | collective-permute-start | bytes 786440 | tf_op jit(solution)/shard_map/ppermute | solution.py:251
  80.0 7.3 %collective-permute-start.10 = (bf16[256,512]{1,0:T(8,128)(2,1)S(1)}, bf16[256,512]{1,0:T(8,128)(2,1)S(1)}, u32[]{:S(2)}, u32[]{:S(2)}) collective-permute-start(bf16[256,512]{1,0:T(8,128)(2,1)S(1)} %add_convert_fusion.2), channel_id=1, source_target_pairs={{0,1},{4,68},{1,2},{5,69},{2,3},{6,70},{3,0},{7,71},{8,9},{12,76},... | collective-permute-start | bytes 786440 | tf_op jit(solution)/shard_map/ppermute | solution.py:251
  110.2 4.8 %collective-permute-start.15 = (f32[4,4,256]{2,1,0:T(4,128)S(1)}, f32[4,4,256]{2,1,0:T(4,128)S(1)}, u32[]{:S(2)}, u32[]{:S(2)}) collective-permute-start(f32[4,4,256]{2,1,0:T(4,128)S(1)} %get-tuple-element.54), channel_id=1, source_target_pairs={{0,4},{4,0},{1,5},{5,1},{2,6},{6,2},{3,7},{7,3},{8,12},{12,8},{9,1... | collective-permute-start | bytes 49160 | tf_op jit(solution)/shard_map/ppermute | solution.py:238

commit v7 on v6

--- a/solution.py
+++ b/solution.py
@@ -25,7 +25,7 @@
 VMEM = pl.BlockSpec(memory_space=pltpu.VMEM)
 HBM = pl.BlockSpec(memory_space=pltpu.HBM)
 DMA = pltpu.SemaphoreType.DMA
-LIMIT, PICK_LIMIT = 32 << 20, 62717952
+LIMIT, PICK_LIMIT = 32 << 20, 55996416
 
 
 def call(body, out, *args, specs=None, outs=VMEM, flops=0, scratch=(), limit=LIMIT):
@@ -60,29 +60,31 @@
     return core * RING + lax.rem(place(core) + steps + RING, RING)
 
 
-def pick_body(positions_hbm, counts_hbm, hidden, out, positions, counts, mine, sems):
+def pick_body(numbers, hidden, out, mine, sems):
     shards, capacity, width = out.shape
     tokens, depth = hidden.shape
     copies = [
-        pltpu.make_async_copy(positions_hbm, positions, sems.at[0]),
-        pltpu.make_async_copy(counts_hbm, counts, sems.at[1]),
         pltpu.make_async_copy(
-            hidden.at[:, columns(lax.axis_index("y"), width)], mine.at[:, :width], sems.at[2]
+            hidden.at[:, columns(lax.axis_index("y"), width)],
+            mine.at[:tokens, :width], sems.at[0],
         ),
-        pltpu.make_async_copy(hidden.at[:, depth // 2 :], mine.at[:, width:], sems.at[3]),
+        pltpu.make_async_copy(
+            hidden.at[:, depth // 2 :], mine.at[:tokens, width:], sems.at[1]
+        ),
     ]
     for copy in copies:
         copy.start()
+    more = (mine.shape[0] - tokens, mine.shape[1])
+    mine[tokens:, :] = (lax.broadcasted_iota(jnp.int32, more, 0) == 0).astype(F32).astype(BF16)
+    position, count = numbers[...] % tokens, numbers[...] // tokens
+    masked = lax.broadcasted_iota(jnp.int32, numbers.shape, 1) < count
+    row = lax.broadcasted_iota(jnp.int32, (mine.shape[0], capacity), 0)
+    source = jnp.where(masked, position, tokens)
+    hot = jnp.where(row == source, jnp.where(masked, 1.0, MARK), 0.0).astype(BF16)
     for copy in copies:
         copy.wait()
-    row = lax.broadcasted_iota(jnp.int32, (2 * capacity, tokens), 0)
-    column = lax.broadcasted_iota(jnp.int32, (2 * capacity, tokens), 1)
-    hot = jnp.zeros((2 * capacity, tokens), F32)
-    for k in range(capacity):
-        hot = jnp.where((row == k) & (column == positions[0, k]), 1.0, hot)
-    rows = jnp.dot(hot.astype(BF16), mine[...], preferred_element_type=F32)[:capacity]
-    rank = lax.broadcasted_iota(jnp.int32, rows.shape, 0)
-    rows = jnp.where(rank < counts[0, 0], rows, MARK).astype(BF16)
+    rows = lax.dot_general(hot, mine[...], TN, preferred_element_type=F32)
+    rows = rows.astype(BF16)
     for s in range(shards):
         start = s % NCORE * (1 + s // (NZ * NCORE)) * width
         out[s] = rows[:, start : start + width]
@@ -264,13 +266,10 @@
     half_flops = vocab * depth * MASKED
     logits_shape = shape((vocab, MASKED), F32)
 
+    numbers = positions + tokens * counts
     send = call(
-        pick_body, shape((shards, capacity, part), BF16),
-        positions, counts.reshape(1, 1), hidden, specs=[HBM] * 3,
-        scratch=[
-            pltpu.SMEM(positions.shape, jnp.int32), pltpu.SMEM((1, 1), jnp.int32),
-            pltpu.VMEM((tokens, part + depth // 2), BF16), DMA((4,)),
-        ],
+        pick_body, shape((shards, capacity, part), BF16), numbers, hidden, specs=[VMEM, HBM],
+        scratch=[pltpu.VMEM((tokens + 16, part + depth // 2), BF16), DMA((2,))],
         limit=PICK_LIMIT,
     )
     rows = lax.all_to_all(send, SEQ, 0, 0, tiled=True).reshape(slots, part)
@@ -312,17 +311,26 @@
         (shape((vocab, MASKED), BF16), shape((MASKED, part), BF16)),
         student, teacher_rows, lse, swap_core(lse), count, weight, flops=half_flops // 4,
     )
-    for which in (((0, 2), (1, 1), (1, 3)), ((0, 1), (0, 3)), ((1, 0), (0, 0))):
+    sums = {}
+
+    def make(which, tie):
+        grad, tie = lax.optimization_barrier((grad_logits, tie))
         out = tuple(shape((MASKED, part), BF16 if side else F32) for side, k in which)
         made = call(
-            functools.partial(products_body, which=which), out, grad_logits, weight,
+            functools.partial(products_body, which=which), out, grad, weight,
             flops=half_flops * len(which) // 4,
         )
-        parts |= dict(zip(which, made))
-    both = {
-        k: (parts[0, k] + swap_core(parts[1, k]).astype(F32)).astype(BF16) for k in range(RING)
-    }
-    sums = [both[0]] + [shift(both[k], k) for k in range(1, RING)]
+        parts.update(zip(which, made))
+        return tie
+
+    def add(k):
+        return (parts[0, k] + swap_core(parts[1, k]).astype(F32)).astype(BF16)
+
+    make(((0, 2), (1, 1)), lse)
+    make(((1, 3), (0, 1), (0, 3)), lse)
+    both = {k: add(k) for k in (2, 1, 3)}
+    both[1] = make(((1, 0), (0, 0)), both[1])
+    sums = [add(0)] + [shift(both[k], k) for k in range(1, RING)]
     grad_head = call(
         head_body, shape((vocab, depth), BF16),
         *[blocks[side, k] for side in range(NCORE) for k in range(RING)], grad_logits, outs=HBM,

time: 116 us -> 116 us (level)
  waiting for transfers between devices: 6.33 us -> 4.63 us
  starting transfers between devices: 19.5 us -> 20.7 us
    ppermute x6, waiting for transfers between devices: 4.38 us -> 2.68 us  [shift(): return lax.ppermute(v, ALL, moves)]
where the time goes in v7:
time: 116 us; the launch traced here: 115 us
  blocking collectives  75.3 us (65%)
  starting transfers between devices  20.7 us (18%)
  Pallas kernels  11.1 us (10%)
  waiting for transfers between devices  4.63 us (4%)
  between operations  1.6 us (1%)
    all_to_all x1, blocking collectives, per_device(): rows = lax.all_to_all(send, SEQ, 0, 0, tiled=True).reshape(slots, part)  30.1 us
    all_to_all x1, blocking collectives, per_device(): lax.all_to_all(partial.reshape(chips, 8, part // 2), CHIPS, 0, 0, tiled=T...  22.8 us
    all_to_all x1, blocking collectives, per_device(): stats = lax.all_to_all(stats, CHIPS, 0, 0, tiled=True)  22.4 us
    ppermute x10, starting transfers between devices, swap_core(): return lax.ppermute(x, 'core', [(0, 1), (1, 0)])  11.4 us
    pallas_call x14, Pallas kernels, call(): pl.pallas_call(body, out_shape=out, in_specs=specs or [VMEM] * len(args),...  11.1 us
    ppermute x6, starting transfers between devices, shift(): return lax.ppermute(v, ALL, moves)  9.33 us
    ppermute x6, waiting for transfers between devices, shift(): return lax.ppermute(v, ALL, moves)  2.68 us
  transfers between devices with their start and end apart: 16, of which 4 were waited for; matrix products, arithmetic and copies ran while one was open for 0% of the time, Pallas kernels for 6%

profile of v7, /device:TPU:1, one launch (start us, length us, event | category | flops | bytes accessed | tf_op | source)
XLA Modules:
  0.0 115.4 jit_solution(15728774259779760986)
XLA Ops:
  1.4 0.8 broadcast_add_fusion.numbers
  2.3 1.2 %shard_map.68 = bf16[64,8,512]{2,1,0:T(8,128)(2,1)S(1)} custom-call(s32[1,8]{1,0:T(1,128)S(1)} %broadcast_add_fusion.numbers, bf16[64,4096]{1,0:T(8,128)(2,1)} %hidden.1), custom_call_target="tpu_custom_call" | custom-call | bytes 1048608 | tf_op jit(solution)/shard_map/pallas_call | solution.py:34
  3.5 30.1 %all_to_all.15 = bf16[64,8,512]{2,1,0:T(8,128)(2,1)S(1)} all-to-all(bf16[64,8,512]{2,1,0:T(8,128)(2,1)S(1)} %shard_map.68), channel_id=1, replica_groups=mesh['x'=4,'z'=8,'core'=2,'y'=4] {'x','z','core'}, dimensions={0} | all-to-all | bytes 1048576 | tf_op jit(solution)/shard_map/all_to_all | solution.py:275
  33.6 0.5 shard_map.69
  34.1 2.9 %collective-permute-start.4 = (bf16[256,512]{1,0:T(8,128)(2,1)S(1)}, bf16[256,512]{1,0:T(8,128)(2,1)S(1)}, u32[]{:S(2)}, u32[]{:S(2)}) collective-permute-start(bf16[256,512]{1,0:T(8,128)(2,1)S(1)} %get-tuple-element.32.refs_0_), channel_id=1, source_target_pairs={{0,2},{4,132},{1,3},{5,133},{2,0},{6,134},{3,1},{7,135},{8,10},{12... | collective-permute-start | bytes 786440 | tf_op jit(solution)/shard_map/ppermute | solution.py:253
  37.1 0.4 collective-permute-start.2
  37.4 2.3 %collective-permute-start = (bf16[256,512]{1,0:T(8,128)(2,1)S(1)}, bf16[256,512]{1,0:T(8,128)(2,1)S(1)}, u32[]{:S(2)}, u32[]{:S(2)}) collective-permute-start(bf16[256,512]{1,0:T(8,128)(2,1)S(1)} %get-tuple-element.32.refs_0_), channel_id=1, source_target_pairs={{0,3},{4,196},{1,0},{5,197},{2,1},{6,198},{3,2},{7,199},{8,11},{12... | collective-permute-start | bytes 786440 | tf_op jit(solution)/shard_map/ppermute | solution.py:253
  39.7 1.2 %collective-permute-start.5 = (bf16[256,512]{1,0:T(8,128)(2,1)S(1)}, bf16[256,512]{1,0:T(8,128)(2,1)S(1)}, u32[]{:S(2)}, u32[]{:S(2)}) collective-permute-start(bf16[256,512]{1,0:T(8,128)(2,1)S(1)} %get-tuple-element.32.refs_0_), channel_id=1, source_target_pairs={{0,4},{4,0},{1,5},{5,1},{2,6},{6,2},{3,7},{7,3},{8,12},{12,8},{9,1... | collective-permute-start | bytes 786440 | tf_op jit(solution)/shard_map/ppermute | solution.py:240
  41.0 1.0 copy-done.1
  42.0 1.9 %shard_map.70 = (bf16[494,256]{1,0:T(8,128)(2,1)S(1)}, f32[8,256]{1,0:T(8,128)S(1)}, bf16[2,1024,256]{2,1,0:T(8,128)(2,1)S(1)}) custom-call(bf16[494,512]{1,0:T(8,128)(2,1)S(1)} %bitcast.14, bf16[256,512]{1,0:T(8,128)(2,1)S(1)} %get-tuple-element.33.chosen), custom_call_target="tpu_custom_call" | custom-call | flops 397934592 | bytes 2077696 | tf_op jit(solution)/shard_map/pallas_call | solution.py:34
  44.0 1.3 %collective-permute-start.3 = (bf16[256,512]{1,0:T(8,128)(2,1)S(1)}, bf16[256,512]{1,0:T(8,128)(2,1)S(1)}, u32[]{:S(2)}, u32[]{:S(2)}) collective-permute-start(bf16[256,512]{1,0:T(8,128)(2,1)S(1)} %collective-permute-done.2.refs_1_), channel_id=1, source_target_pairs={{0,4},{4,0},{1,5},{5,1},{2,6},{6,2},{3,7},{7,3},{8,12},{12,8},{9,1... | collective-permute-start | bytes 786440 | tf_op jit(solution)/shard_map/ppermute | solution.py:240
  45.6 1.0 shard_map.71.refs_3_
  46.9 0.7 shard_map.72
  47.5 22.4 %all_to_all.16.stats = f32[128,2,256]{2,1,0:T(2,128)S(1)} all-to-all(f32[128,2,256]{2,1,0:T(2,128)S(1)} %get-tuple-element.43), channel_id=1, replica_groups=mesh['x'=4,'z'=8,'core'=2,'y'=4] {'x','z','y'}, dimensions={0} | all-to-all | bytes 524288 | tf_op jit(solution)/shard_map/all_to_all | solution.py:305
  70.1 2.6 %collective-permute-start.7 = (f32[2,256]{1,0:T(2,128)S(1)}, f32[2,256]{1,0:T(2,128)S(1)}, u32[]{:S(2)}, u32[]{:S(2)}) collective-permute-start(f32[2,256]{1,0:T(2,128)S(1)} %shard_map.73.mine), channel_id=1, source_target_pairs={{0,4},{4,0},{1,5},{5,1},{2,6},{6,2},{3,7},{7,3},{8,12},{12,8},{9,1... | collective-permute-start | bytes 6152 | tf_op jit(solution)/shard_map/ppermute | solution.py:240
  72.8 0.8 collective-permute-done.7.other
  73.6 0.4 shard_map.74
  74.0 0.6 collective-permute-start.11
  74.7 0.5 shard_map.76
  75.4 0.6 shard_map.75
  76.0 0.4 collective-permute-start.13
  76.5 1.4 %collective-permute-start.12 = (bf16[256,512]{1,0:T(8,128)(2,1)S(1)}, bf16[256,512]{1,0:T(8,128)(2,1)S(1)}, u32[]{:S(2)}, u32[]{:S(2)}) collective-permute-start(bf16[256,512]{1,0:T(8,128)(2,1)S(1)} %add_convert_fusion.1), channel_id=1, source_target_pairs={{0,2},{4,132},{1,3},{5,133},{2,0},{6,134},{3,1},{7,135},{8,10},{12... | collective-permute-start | bytes 786440 | tf_op jit(solution)/shard_map/ppermute | solution.py:253
  78.0 0.5 shard_map.77
  78.5 0.6 collective-permute-start.9
  79.1 2.3 %collective-permute-start.14 = (bf16[256,512]{1,0:T(8,128)(2,1)S(1)}, bf16[256,512]{1,0:T(8,128)(2,1)S(1)}, u32[]{:S(2)}, u32[]{:S(2)}) collective-permute-start(bf16[256,512]{1,0:T(8,128)(2,1)S(1)} %add_convert_fusion), channel_id=1, source_target_pairs={{0,3},{4,196},{1,0},{5,197},{2,1},{6,198},{3,2},{7,199},{8,11},{12... | collective-permute-start | bytes 786440 | tf_op jit(solution)/shard_map/ppermute | solution.py:253
  81.4 2.3 %shard_map.78 = bf16[494,4096]{1,0:T(8,128)(2,1)} custom-call(bf16[256,512]{1,0:T(8,128)(2,1)S(1)} %get-tuple-element.32.refs_0_, bf16[256,512]{1,0:T(8,128)(2,1)S(1)} %collective-permute-done.2.refs_1_, bf16[256,512]{1,0:T(8,128)(2,1)S(1)} %collective-permute-done.4.refs_2_, bf16[256,512]{1,0:T(8,128)(2,1)S(1)} %collective-permute-done.refs_3_, ...), custom_call_target="tpu_custom_call" | custom-call | flops 1035993088 | bytes 6396928 | tf_op jit(solution)/shard_map/pallas_call | solution.py:34
  83.8 2.7 %collective-permute-done.10.b = bf16[256,512]{1,0:T(8,128)(2,1)S(1)} collective-permute-done((bf16[256,512]{1,0:T(8,128)(2,1)S(1)}, bf16[256,512]{1,0:T(8,128)(2,1)S(1)}, u32[]{:S(2)}, u32[]{:S(2)}) %collective-permute-start.10) | collective-permute-done | bytes 262176 | tf_op jit(solution)/shard_map/ppermute | solution.py:253
  86.5 0.5 shard_map.79
  87.0 22.8 %all_to_all.17.parts = bf16[128,8,256]{2,1,0:T(8,128)(2,1)S(1)} all-to-all(bf16[128,8,256]{2,1,0:T(8,128)(2,1)S(1)} %bitcast.12), channel_id=1, replica_groups=mesh['x'=4,'z'=8,'core'=2,'y'=4] {'x','z','y'}, dimensions={0} | all-to-all | bytes 1048576 | tf_op jit(solution)/shard_map/all_to_all | solution.py:345
  109.9 4.1 %collective-permute-start.15 = (f32[4,4,256]{2,1,0:T(4,128)S(1)}, f32[4,4,256]{2,1,0:T(4,128)S(1)}, u32[]{:S(2)}, u32[]{:S(2)}) collective-permute-start(f32[4,4,256]{2,1,0:T(4,128)S(1)} %get-tuple-element.60), channel_id=1, source_target_pairs={{0,4},{4,0},{1,5},{5,1},{2,6},{6,2},{3,7},{7,3},{8,12},{12,8},{9,1... | collective-permute-start | bytes 49160 | tf_op jit(solution)/shard_map/ppermute | solution.py:240
  114.0 0.8 collective-permute-done.15.other
  114.8 0.6 shard_map.81
  (26 shorter events, 1.6 us)
Async XLA Ops:
  0.6 44.9 %copy-start = (bf16[4096,494]{0,1:T(8,128)(2,1)S(1)}, bf16[4096,494]{0,1:T(8,128)(2,1)}, u32[]{:S(2)}) copy-start(bf16[4096,494]{0,1:T(8,128)(2,1)} %param.6) | copy-start | bytes 12140548
  34.1 9.8 %collective-permute-start.4 = (bf16[256,512]{1,0:T(8,128)(2,1)S(1)}, bf16[256,512]{1,0:T(8,128)(2,1)S(1)}, u32[]{:S(2)}, u32[]{:S(2)}) collective-permute-start(bf16[256,512]{1,0:T(8,128)(2,1)S(1)} %get-tuple-element.32.refs_0_), channel_id=1, source_target_pairs={{0,2},{4,132},{1,3},{5,133},{2,0},{6,134},{3,1},{7,135},{8,10},{12... | collective-permute-start | bytes 786440 | tf_op jit(solution)/shard_map/ppermute | solution.py:253
  37.1 7.0 %collective-permute-start.2 = (bf16[256,512]{1,0:T(8,128)(2,1)S(1)}, bf16[256,512]{1,0:T(8,128)(2,1)S(1)}, u32[]{:S(2)}, u32[]{:S(2)}) collective-permute-start(bf16[256,512]{1,0:T(8,128)(2,1)S(1)} %get-tuple-element.32.refs_0_), channel_id=1, source_target_pairs={{0,1},{4,68},{1,2},{5,69},{2,3},{6,70},{3,0},{7,71},{8,9},{12,76},... | collective-permute-start | bytes 786440 | tf_op jit(solution)/shard_map/ppermute | solution.py:253
  37.4 7.9 %collective-permute-start = (bf16[256,512]{1,0:T(8,128)(2,1)S(1)}, bf16[256,512]{1,0:T(8,128)(2,1)S(1)}, u32[]{:S(2)}, u32[]{:S(2)}) collective-permute-start(bf16[256,512]{1,0:T(8,128)(2,1)S(1)} %get-tuple-element.32.refs_0_), channel_id=1, source_target_pairs={{0,3},{4,196},{1,0},{5,197},{2,1},{6,198},{3,2},{7,199},{8,11},{12... | collective-permute-start | bytes 786440 | tf_op jit(solution)/shard_map/ppermute | solution.py:253
  39.7 5.8 %collective-permute-start.5 = (bf16[256,512]{1,0:T(8,128)(2,1)S(1)}, bf16[256,512]{1,0:T(8,128)(2,1)S(1)}, u32[]{:S(2)}, u32[]{:S(2)}) collective-permute-start(bf16[256,512]{1,0:T(8,128)(2,1)S(1)} %get-tuple-element.32.refs_0_), channel_id=1, source_target_pairs={{0,4},{4,0},{1,5},{5,1},{2,6},{6,2},{3,7},{7,3},{8,12},{12,8},{9,1... | collective-permute-start | bytes 786440 | tf_op jit(solution)/shard_map/ppermute | solution.py:240
  41.0 1.0 copy-start.1
  43.9 1.6 %collective-permute-start.6 = (bf16[256,512]{1,0:T(8,128)(2,1)S(1)}, bf16[256,512]{1,0:T(8,128)(2,1)S(1)}, u32[]{:S(2)}, u32[]{:S(2)}) collective-permute-start(bf16[256,512]{1,0:T(8,128)(2,1)S(1)} %collective-permute-done.4.refs_2_), channel_id=1, source_target_pairs={{0,4},{4,0},{1,5},{5,1},{2,6},{6,2},{3,7},{7,3},{8,12},{12,8},{9,1... | collective-permute-start | bytes 786440 | tf_op jit(solution)/shard_map/ppermute | solution.py:240
  44.0 2.5 %collective-permute-start.3 = (bf16[256,512]{1,0:T(8,128)(2,1)S(1)}, bf16[256,512]{1,0:T(8,128)(2,1)S(1)}, u32[]{:S(2)}, u32[]{:S(2)}) collective-permute-start(bf16[256,512]{1,0:T(8,128)(2,1)S(1)} %collective-permute-done.2.refs_1_), channel_id=1, source_target_pairs={{0,4},{4,0},{1,5},{5,1},{2,6},{6,2},{3,7},{7,3},{8,12},{12,8},{9,1... | collective-permute-start | bytes 786440 | tf_op jit(solution)/shard_map/ppermute | solution.py:240
  45.3 1.5 %collective-permute-start.1 = (bf16[256,512]{1,0:T(8,128)(2,1)S(1)}, bf16[256,512]{1,0:T(8,128)(2,1)S(1)}, u32[]{:S(2)}, u32[]{:S(2)}) collective-permute-start(bf16[256,512]{1,0:T(8,128)(2,1)S(1)} %collective-permute-done.refs_3_), channel_id=1, source_target_pairs={{0,4},{4,0},{1,5},{5,1},{2,6},{6,2},{3,7},{7,3},{8,12},{12,8},{9,1... | collective-permute-start | bytes 786440 | tf_op jit(solution)/shard_map/ppermute | solution.py:240
  70.1 3.5 %collective-permute-start.7 = (f32[2,256]{1,0:T(2,128)S(1)}, f32[2,256]{1,0:T(2,128)S(1)}, u32[]{:S(2)}, u32[]{:S(2)}) collective-permute-start(f32[2,256]{1,0:T(2,128)S(1)} %shard_map.73.mine), channel_id=1, source_target_pairs={{0,4},{4,0},{1,5},{5,1},{2,6},{6,2},{3,7},{7,3},{8,12},{12,8},{9,1... | collective-permute-start | bytes 6152 | tf_op jit(solution)/shard_map/ppermute | solution.py:240
  74.0 2.4 %collective-permute-start.11 = (bf16[256,512]{1,0:T(8,128)(2,1)S(1)}, bf16[256,512]{1,0:T(8,128)(2,1)S(1)}, u32[]{:S(2)}, u32[]{:S(2)}) collective-permute-start(bf16[256,512]{1,0:T(8,128)(2,1)S(1)} %get-tuple-element.55), channel_id=1, source_target_pairs={{0,4},{4,0},{1,5},{5,1},{2,6},{6,2},{3,7},{7,3},{8,12},{12,8},{9,1... | collective-permute-start | bytes 786440 | tf_op jit(solution)/shard_map/ppermute | solution.py:240
  75.1 2.7 %collective-permute-start.8 = (bf16[256,512]{1,0:T(8,128)(2,1)S(1)}, bf16[256,512]{1,0:T(8,128)(2,1)S(1)}, u32[]{:S(2)}, u32[]{:S(2)}) collective-permute-start(bf16[256,512]{1,0:T(8,128)(2,1)S(1)} %get-tuple-element.48), channel_id=1, source_target_pairs={{0,4},{4,0},{1,5},{5,1},{2,6},{6,2},{3,7},{7,3},{8,12},{12,8},{9,1... | collective-permute-start | bytes 786440 | tf_op jit(solution)/shard_map/ppermute | solution.py:240
  76.0 3.1 %collective-permute-start.13 = (bf16[256,512]{1,0:T(8,128)(2,1)S(1)}, bf16[256,512]{1,0:T(8,128)(2,1)S(1)}, u32[]{:S(2)}, u32[]{:S(2)}) collective-permute-start(bf16[256,512]{1,0:T(8,128)(2,1)S(1)} %get-tuple-element.57), channel_id=1, source_target_pairs={{0,4},{4,0},{1,5},{5,1},{2,6},{6,2},{3,7},{7,3},{8,12},{12,8},{9,1... | collective-permute-start | bytes 786440 | tf_op jit(solution)/shard_map/ppermute | solution.py:240
  76.5 10.0 %collective-permute-start.12 = (bf16[256,512]{1,0:T(8,128)(2,1)S(1)}, bf16[256,512]{1,0:T(8,128)(2,1)S(1)}, u32[]{:S(2)}, u32[]{:S(2)}) collective-permute-start(bf16[256,512]{1,0:T(8,128)(2,1)S(1)} %add_convert_fusion.1), channel_id=1, source_target_pairs={{0,2},{4,132},{1,3},{5,133},{2,0},{6,134},{3,1},{7,135},{8,10},{12... | collective-permute-start | bytes 786440 | tf_op jit(solution)/shard_map/ppermute | solution.py:253
  77.9 8.5 %collective-permute-start.10 = (bf16[256,512]{1,0:T(8,128)(2,1)S(1)}, bf16[256,512]{1,0:T(8,128)(2,1)S(1)}, u32[]{:S(2)}, u32[]{:S(2)}) collective-permute-start(bf16[256,512]{1,0:T(8,128)(2,1)S(1)} %add_convert_fusion.3), channel_id=1, source_target_pairs={{0,1},{4,68},{1,2},{5,69},{2,3},{6,70},{3,0},{7,71},{8,9},{12,76},... | collective-permute-start | bytes 786440 | tf_op jit(solution)/shard_map/ppermute | solution.py:253
  78.5 7.9 %collective-permute-start.9 = (bf16[256,512]{1,0:T(8,128)(2,1)S(1)}, bf16[256,512]{1,0:T(8,128)(2,1)S(1)}, u32[]{:S(2)}, u32[]{:S(2)}) collective-permute-start(bf16[256,512]{1,0:T(8,128)(2,1)S(1)} %get-tuple-element.51), channel_id=1, source_target_pairs={{0,4},{4,0},{1,5},{5,1},{2,6},{6,2},{3,7},{7,3},{8,12},{12,8},{9,1... | collective-permute-start | bytes 786440 | tf_op jit(solution)/shard_map/ppermute | solution.py:240
  79.1 7.4 %collective-permute-start.14 = (bf16[256,512]{1,0:T(8,128)(2,1)S(1)}, bf16[256,512]{1,0:T(8,128)(2,1)S(1)}, u32[]{:S(2)}, u32[]{:S(2)}) collective-permute-start(bf16[256,512]{1,0:T(8,128)(2,1)S(1)} %add_convert_fusion), channel_id=1, source_target_pairs={{0,3},{4,196},{1,0},{5,197},{2,1},{6,198},{3,2},{7,199},{8,11},{12... | collective-permute-start | bytes 786440 | tf_op jit(solution)/shard_map/ppermute | solution.py:253
  109.9 4.9 %collective-permute-start.15 = (f32[4,4,256]{2,1,0:T(4,128)S(1)}, f32[4,4,256]{2,1,0:T(4,128)S(1)}, u32[]{:S(2)}, u32[]{:S(2)}) collective-permute-start(f32[4,4,256]{2,1,0:T(4,128)S(1)} %get-tuple-element.60), channel_id=1, source_target_pairs={{0,4},{4,0},{1,5},{5,1},{2,6},{6,2},{3,7},{7,3},{8,12},{12,8},{9,1... | collective-permute-start | bytes 49160 | tf_op jit(solution)/shard_map/ppermute | solution.py:240

commit v8 on v7

--- a/solution.py
+++ b/solution.py
@@ -52,6 +52,10 @@
 
 def place(core):
     return jnp.where(core == 0, lax.axis_index("y"), lax.axis_index("x"))
+
+
+def second_place(core):
+    return jnp.where(core == 0, lax.axis_index("x"), lax.axis_index("y"))
 
 
 def part_at(side, steps):
@@ -120,8 +124,10 @@
     halves, sent, masked = back.shape
     slots = chosen.shape[1]
     row = lax.broadcasted_iota(jnp.int32, (sent, slots), 0)
-    chip, q = row // 8, row % 8
-    slot = chip // NY * 16 + q // 4 * 8 + chip % NY * 2 + q // 2 % 2
+    second, z, first, q = row // 256, row // 32 % NZ, row // 8 % RING, row % 8
+    straight = lax.axis_index("core") == 0
+    x, y = jnp.where(straight, second, first), jnp.where(straight, first, second)
+    slot = (x * NZ + z) * 16 + q // 4 * 8 + y * 2 + q // 2 % 2
     column = lax.broadcasted_iota(jnp.int32, (sent, slots), 1)
     pick = (column == slot).astype(F32).astype(BF16)
     placed = lax.dot_general(pick, chosen[...], NT, preferred_element_type=F32)
@@ -200,22 +206,24 @@
         copy.wait()
 
 
-def spread_body(a, b, c, d, back, out):
+def spread_body(a, b, c, d, back, *outs):
     total = a[...].astype(F32) + b[...].astype(F32) + c[...].astype(F32) + d[...].astype(F32)
     total = total.astype(BF16)
-    half = out.shape[1]
-    out[...] = (
-        jnp.dot(back[0], total[:, :half], preferred_element_type=F32)
-        + jnp.dot(back[1], total[:, half:], preferred_element_type=F32)
-    ).astype(BF16)
+    rows, half = outs[0].shape
+    here = second_place(lax.axis_index("core"))
+    for k, out in enumerate(outs):
+        span = columns(lax.rem(here + k, RING), rows)
+        out[...] = (
+            jnp.dot(back[0, span, :], total[:, :half], preferred_element_type=F32)
+            + jnp.dot(back[1, span, :], total[:, half:], preferred_element_type=F32)
+        ).astype(BF16)
 
 
 def collect_body(parts, mine, other):
-    chips, rows, half = parts.shape
-    total = jnp.sum(parts[...].astype(F32).reshape(NX, NZ, NY, rows, half), axis=1)
+    peers, rows, half = parts.shape
+    total = jnp.sum(parts[...].astype(F32).reshape(NZ, RING, rows, half), axis=0)
+    low, high = total[:, : rows // 2], total[:, rows // 2 :]
     first = lax.axis_index("core") == 0
-    total = jnp.where(first, jnp.sum(total, axis=0), jnp.sum(total, axis=1))
-    low, high = total[:, : rows // 2], total[:, rows // 2 :]
     mine[...] = jnp.where(first, low, high)
     other[...] = jnp.where(first, high, low)
 
@@ -240,17 +248,30 @@
     return lax.ppermute(x, "core", [(0, 1), (1, 0)])
 
 
-def shift(v, k):
+def index(x, z, core, y):
+    return ((x * NZ + z) * NCORE + core) * NY + y
+
+
+def shift(v, k, ring=1):
     moves = []
     for x in range(NX):
         for z in range(NZ):
             for y in range(NY):
-                for core, (to_x, to_y) in enumerate(((x, (y + k) % NY), ((x + k) % NX, y))):
-                    moves.append(
-                        (((x * NZ + z) * NCORE + core) * NY + y,
-                         ((to_x * NZ + z) * NCORE + core) * NY + to_y)
-                    )
+                for core in range(NCORE):
+                    if (core == 0) == (ring == 1):
+                        to = index(x, z, core, (y + k) % NY)
+                    else:
+                        to = index((x + k) % NX, z, core, y)
+                    moves.append((index(x, z, core, y), to))
     return lax.ppermute(v, ALL, moves)
+
+
+def peers():
+    groups = []
+    for second in range(RING):
+        groups.append([index(second, z, 0, y) for z in range(NZ) for y in range(NY)])
+        groups.append([index(x, z, 1, second) for z in range(NZ) for x in range(NX)])
+    return groups
 
 
 def per_device(hidden, head_weight, teacher, positions, counts):
@@ -338,11 +359,16 @@
         flops=2 * half_flops,
     )
     sums[1], grad_head = lax.optimization_barrier((sums[1], grad_head))
-    partial = call(
-        spread_body, shape((2 * slots, part // 2), BF16), *sums, back,
+    steps = call(
+        spread_body, (shape((2 * slots // RING, part // 2), BF16),) * RING, *sums, back,
         flops=4 * MASKED * slots * part,
     )
-    partial = lax.all_to_all(partial.reshape(chips, 8, part // 2), CHIPS, 0, 0, tiled=True)
+    steps = [steps[0]] + [shift(steps[k], k, ring=2) for k in (2, 1, 3)]
+    partial = sum(step.astype(F32) for step in steps).astype(BF16)
+    partial = lax.all_to_all(
+        partial.reshape(NZ * RING, 8, part // 2), ALL, 0, 0, tiled=True,
+        axis_index_groups=peers(),
+    )
     mine, other = call(collect_body, (shape((RING, 4, part // 2), F32),) * 2, partial)
     grad_hidden = call(
         finish_body, shape((own, depth), BF16), mine, swap_core(other),

time: 116 us -> 113 us (0.974)
  blocking collectives: 75.3 us -> 64.9 us
  starting transfers between devices: 20.7 us -> 24.7 us
  waiting for transfers between devices: 4.63 us -> 8.11 us
    all_to_all x1, blocking collectives: 22.8 us -> 12.4 us  [per_device(): lax.all_to_all(partial.reshape(NZ * RING, 8, part // 2), ALL, 0, 0, tiled...]
    ppermute x6 -> x9, starting transfers between devices: 9.33 us -> 12.9 us  [shift(): return lax.ppermute(v, ALL, moves)]
    ppermute x6 -> x9, waiting for transfers between devices: 2.68 us -> 6.17 us  [shift(): return lax.ppermute(v, ALL, moves)]
  transfers between devices with their start and end apart: 16 -> 19, of which waited for: 4 -> 7; matrix products, arithmetic and copies ran while one was open for 0% -> 0% of each run, Pallas kernels for 6% -> 6%
where the time goes in v8:
time: 113 us
  blocking collectives  64.9 us (57%)
  starting transfers between devices  24.7 us (22%)
  Pallas kernels  11.1 us (10%)
  waiting for transfers between devices  8.11 us (7%)
  between operations  1.62 us (1%)
  other arithmetic  1.19 us (1%)
    all_to_all x1, blocking collectives, per_device(): rows = lax.all_to_all(send, SEQ, 0, 0, tiled=True).reshape(slots, part)  30.1 us
    all_to_all x1, blocking collectives, per_device(): stats = lax.all_to_all(stats, CHIPS, 0, 0, tiled=True)  22.4 us
    ppermute x9, starting transfers between devices, shift(): return lax.ppermute(v, ALL, moves)  12.9 us
    all_to_all x1, blocking collectives, per_device(): lax.all_to_all(partial.reshape(NZ * RING, 8, part // 2), ALL, 0, 0, tiled...  12.4 us
    ppermute x10, starting transfers between devices, swap_core(): return lax.ppermute(x, 'core', [(0, 1), (1, 0)])  11.7 us
    pallas_call x14, Pallas kernels, call(): pl.pallas_call(body, out_shape=out, in_specs=specs or [VMEM] * len(args),...  11.1 us
    ppermute x9, waiting for transfers between devices, shift(): return lax.ppermute(v, ALL, moves)  6.17 us
  transfers between devices with their start and end apart: 19, of which 7 were waited for; matrix products, arithmetic and copies ran while one was open for 0% of the time, Pallas kernels for 6%

profile of v8, /device:TPU:1, one launch (start us, length us, event | category | flops | bytes accessed | tf_op | source)
XLA Modules:
  0.0 112.6 jit_solution(4724692547153988389)
XLA Ops:
  1.4 0.8 broadcast_add_fusion.numbers
  2.3 1.2 %shard_map.68 = bf16[64,8,512]{2,1,0:T(8,128)(2,1)S(1)} custom-call(s32[1,8]{1,0:T(1,128)S(1)} %broadcast_add_fusion.numbers, bf16[64,4096]{1,0:T(8,128)(2,1)} %hidden.1), custom_call_target="tpu_custom_call" | custom-call | bytes 1048608 | tf_op jit(solution)/shard_map/pallas_call | solution.py:34
  3.5 30.1 %all_to_all.15 = bf16[64,8,512]{2,1,0:T(8,128)(2,1)S(1)} all-to-all(bf16[64,8,512]{2,1,0:T(8,128)(2,1)S(1)} %shard_map.68), channel_id=1, replica_groups=mesh['x'=4,'z'=8,'core'=2,'y'=4] {'x','z','core'}, dimensions={0} | all-to-all | bytes 1048576 | tf_op jit(solution)/shard_map/all_to_all | solution.py:296
  33.6 0.5 shard_map.69
  34.1 2.9 %collective-permute-start.4 = (bf16[256,512]{1,0:T(8,128)(2,1)S(1)}, bf16[256,512]{1,0:T(8,128)(2,1)S(1)}, u32[]{:S(2)}, u32[]{:S(2)}) collective-permute-start(bf16[256,512]{1,0:T(8,128)(2,1)S(1)} %get-tuple-element.36.refs_0_), channel_id=1, source_target_pairs={{0,2},{4,132},{1,3},{5,133},{2,0},{6,134},{3,1},{7,135},{8,10},{12... | collective-permute-start | bytes 786440 | tf_op jit(solution)/shard_map/ppermute | solution.py:266
  37.4 2.3 %collective-permute-start = (bf16[256,512]{1,0:T(8,128)(2,1)S(1)}, bf16[256,512]{1,0:T(8,128)(2,1)S(1)}, u32[]{:S(2)}, u32[]{:S(2)}) collective-permute-start(bf16[256,512]{1,0:T(8,128)(2,1)S(1)} %get-tuple-element.36.refs_0_), channel_id=1, source_target_pairs={{0,3},{4,196},{1,0},{5,197},{2,1},{6,198},{3,2},{7,199},{8,11},{12... | collective-permute-start | bytes 786440 | tf_op jit(solution)/shard_map/ppermute | solution.py:266
  39.7 1.2 %collective-permute-start.5 = (bf16[256,512]{1,0:T(8,128)(2,1)S(1)}, bf16[256,512]{1,0:T(8,128)(2,1)S(1)}, u32[]{:S(2)}, u32[]{:S(2)}) collective-permute-start(bf16[256,512]{1,0:T(8,128)(2,1)S(1)} %get-tuple-element.36.refs_0_), channel_id=1, source_target_pairs={{0,4},{4,0},{1,5},{5,1},{2,6},{6,2},{3,7},{7,3},{8,12},{12,8},{9,1... | collective-permute-start | bytes 786440 | tf_op jit(solution)/shard_map/ppermute | solution.py:248
  41.0 1.0 copy-done.1
  42.0 2.0 %shard_map.70 = (bf16[494,256]{1,0:T(8,128)(2,1)S(1)}, f32[8,256]{1,0:T(8,128)S(1)}, bf16[2,1024,256]{2,1,0:T(8,128)(2,1)S(1)}) custom-call(bf16[494,512]{1,0:T(8,128)(2,1)S(1)} %bitcast.14, bf16[256,512]{1,0:T(8,128)(2,1)S(1)} %get-tuple-element.37.chosen), custom_call_target="tpu_custom_call" | custom-call | flops 397934592 | bytes 2077696 | tf_op jit(solution)/shard_map/pallas_call | solution.py:34
  44.1 1.2 %collective-permute-start.3 = (bf16[256,512]{1,0:T(8,128)(2,1)S(1)}, bf16[256,512]{1,0:T(8,128)(2,1)S(1)}, u32[]{:S(2)}, u32[]{:S(2)}) collective-permute-start(bf16[256,512]{1,0:T(8,128)(2,1)S(1)} %collective-permute-done.2.refs_1_), channel_id=1, source_target_pairs={{0,4},{4,0},{1,5},{5,1},{2,6},{6,2},{3,7},{7,3},{8,12},{12,8},{9,1... | collective-permute-start | bytes 786440 | tf_op jit(solution)/shard_map/ppermute | solution.py:248
  45.7 1.0 shard_map.71.refs_3_
  46.9 0.7 shard_map.72
  47.5 22.4 %all_to_all.16.stats = f32[128,2,256]{2,1,0:T(2,128)S(1)} all-to-all(f32[128,2,256]{2,1,0:T(2,128)S(1)} %get-tuple-element.47), channel_id=1, replica_groups=mesh['x'=4,'z'=8,'core'=2,'y'=4] {'x','z','y'}, dimensions={0} | all-to-all | bytes 524288 | tf_op jit(solution)/shard_map/all_to_all | solution.py:326
  70.1 2.6 %collective-permute-start.7 = (f32[2,256]{1,0:T(2,128)S(1)}, f32[2,256]{1,0:T(2,128)S(1)}, u32[]{:S(2)}, u32[]{:S(2)}) collective-permute-start(f32[2,256]{1,0:T(2,128)S(1)} %shard_map.73.mine), channel_id=1, source_target_pairs={{0,4},{4,0},{1,5},{5,1},{2,6},{6,2},{3,7},{7,3},{8,12},{12,8},{9,1... | collective-permute-start | bytes 6152 | tf_op jit(solution)/shard_map/ppermute | solution.py:248
  72.8 0.8 collective-permute-done.7.other
  74.0 0.6 collective-permute-start.11
  75.4 0.6 shard_map.75
  76.5 1.4 %collective-permute-start.12 = (bf16[256,512]{1,0:T(8,128)(2,1)S(1)}, bf16[256,512]{1,0:T(8,128)(2,1)S(1)}, u32[]{:S(2)}, u32[]{:S(2)}) collective-permute-start(bf16[256,512]{1,0:T(8,128)(2,1)S(1)} %add_convert_fusion.1), channel_id=1, source_target_pairs={{0,2},{4,132},{1,3},{5,133},{2,0},{6,134},{3,1},{7,135},{8,10},{12... | collective-permute-start | bytes 786440 | tf_op jit(solution)/shard_map/ppermute | solution.py:266
  78.5 0.6 collective-permute-start.9
  79.1 2.3 %collective-permute-start.14 = (bf16[256,512]{1,0:T(8,128)(2,1)S(1)}, bf16[256,512]{1,0:T(8,128)(2,1)S(1)}, u32[]{:S(2)}, u32[]{:S(2)}) collective-permute-start(bf16[256,512]{1,0:T(8,128)(2,1)S(1)} %add_convert_fusion), channel_id=1, source_target_pairs={{0,3},{4,196},{1,0},{5,197},{2,1},{6,198},{3,2},{7,199},{8,11},{12... | collective-permute-start | bytes 786440 | tf_op jit(solution)/shard_map/ppermute | solution.py:266
  81.4 2.3 %shard_map.78 = bf16[494,4096]{1,0:T(8,128)(2,1)} custom-call(bf16[256,512]{1,0:T(8,128)(2,1)S(1)} %get-tuple-element.36.refs_0_, bf16[256,512]{1,0:T(8,128)(2,1)S(1)} %collective-permute-done.2.refs_1_, bf16[256,512]{1,0:T(8,128)(2,1)S(1)} %collective-permute-done.4.refs_2_, bf16[256,512]{1,0:T(8,128)(2,1)S(1)} %collective-permute-done.refs_3_, ...), custom_call_target="tpu_custom_call" | custom-call | flops 1035993088 | bytes 6396928 | tf_op jit(solution)/shard_map/pallas_call | solution.py:34
  83.8 2.7 %collective-permute-done.10.b = bf16[256,512]{1,0:T(8,128)(2,1)S(1)} collective-permute-done((bf16[256,512]{1,0:T(8,128)(2,1)S(1)}, bf16[256,512]{1,0:T(8,128)(2,1)S(1)}, u32[]{:S(2)}, u32[]{:S(2)}) %collective-permute-start.10) | collective-permute-done | bytes 262176 | tf_op jit(solution)/shard_map/ppermute | solution.py:266
  86.5 0.5 shard_map.79
  87.0 0.9 collective-permute-start.15
  87.9 0.6 collective-permute-start.16
  88.5 2.1 %collective-permute-start.17 = (bf16[256,256]{1,0:T(8,128)(2,1)S(1)}, bf16[256,256]{1,0:T(8,128)(2,1)S(1)}, u32[]{:S(2)}, u32[]{:S(2)}) collective-permute-start(bf16[256,256]{1,0:T(8,128)(2,1)S(1)} %get-tuple-element.66), channel_id=1, source_target_pairs={{0,192},{4,7},{1,193},{5,4},{2,194},{6,5},{3,195},{7,6},{8,200},{1... | collective-permute-start | bytes 393224 | tf_op jit(solution)/shard_map/ppermute | solution.py:266
  90.6 1.9 %collective-permute-done.15 = bf16[256,256]{1,0:T(8,128)(2,1)S(1)} collective-permute-done((bf16[256,256]{1,0:T(8,128)(2,1)S(1)}, bf16[256,256]{1,0:T(8,128)(2,1)S(1)}, u32[]{:S(2)}, u32[]{:S(2)}) %collective-permute-start.15) | collective-permute-done | bytes 131104 | tf_op jit(solution)/shard_map/ppermute | solution.py:266
  92.5 1.6 %collective-permute-done.16 = bf16[256,256]{1,0:T(8,128)(2,1)S(1)} collective-permute-done((bf16[256,256]{1,0:T(8,128)(2,1)S(1)}, bf16[256,256]{1,0:T(8,128)(2,1)S(1)}, u32[]{:S(2)}, u32[]{:S(2)}) %collective-permute-start.16) | collective-permute-done | bytes 131104 | tf_op jit(solution)/shard_map/ppermute | solution.py:266
  94.2 12.4 %all_to_all.17.parts = bf16[32,8,256]{2,1,0:T(8,128)(2,1)S(1)} all-to-all(bf16[32,8,256]{2,1,0:T(8,128)(2,1)S(1)} %fusion), channel_id=1, replica_groups={{0,1,2,3,8,9,10,11,16,17,18,19,24,25,26,27,32,33,34,35,40,41,42,43,48,4..., dimensions={0} | all-to-all | bytes 262144 | tf_op jit(solution)/shard_map/all_to_all | solution.py:368
  106.6 4.5 %collective-permute-start.18 = (f32[4,4,256]{2,1,0:T(4,128)S(1)}, f32[4,4,256]{2,1,0:T(4,128)S(1)}, u32[]{:S(2)}, u32[]{:S(2)}) collective-permute-start(f32[4,4,256]{2,1,0:T(4,128)S(1)} %get-tuple-element.68), channel_id=1, source_target_pairs={{0,4},{4,0},{1,5},{5,1},{2,6},{6,2},{3,7},{7,3},{8,12},{12,8},{9,1... | collective-permute-start | bytes 49160 | tf_op jit(solution)/shard_map/ppermute | solution.py:248
  111.1 0.8 collective-permute-done.18.other
  112.0 0.6 shard_map.81
  (33 shorter events, 3.8 us)
Async XLA Ops:
  0.6 45.0 %copy-start = (bf16[4096,494]{0,1:T(8,128)(2,1)S(1)}, bf16[4096,494]{0,1:T(8,128)(2,1)}, u32[]{:S(2)}) copy-start(bf16[4096,494]{0,1:T(8,128)(2,1)} %param.6) | copy-start | bytes 12140548
  34.1 9.9 %collective-permute-start.4 = (bf16[256,512]{1,0:T(8,128)(2,1)S(1)}, bf16[256,512]{1,0:T(8,128)(2,1)S(1)}, u32[]{:S(2)}, u32[]{:S(2)}) collective-permute-start(bf16[256,512]{1,0:T(8,128)(2,1)S(1)} %get-tuple-element.36.refs_0_), channel_id=1, source_target_pairs={{0,2},{4,132},{1,3},{5,133},{2,0},{6,134},{3,1},{7,135},{8,10},{12... | collective-permute-start | bytes 786440 | tf_op jit(solution)/shard_map/ppermute | solution.py:266
  37.1 7.1 %collective-permute-start.2 = (bf16[256,512]{1,0:T(8,128)(2,1)S(1)}, bf16[256,512]{1,0:T(8,128)(2,1)S(1)}, u32[]{:S(2)}, u32[]{:S(2)}) collective-permute-start(bf16[256,512]{1,0:T(8,128)(2,1)S(1)} %get-tuple-element.36.refs_0_), channel_id=1, source_target_pairs={{0,1},{4,68},{1,2},{5,69},{2,3},{6,70},{3,0},{7,71},{8,9},{12,76},... | collective-permute-start | bytes 786440 | tf_op jit(solution)/shard_map/ppermute | solution.py:266
  37.4 7.9 %collective-permute-start = (bf16[256,512]{1,0:T(8,128)(2,1)S(1)}, bf16[256,512]{1,0:T(8,128)(2,1)S(1)}, u32[]{:S(2)}, u32[]{:S(2)}) collective-permute-start(bf16[256,512]{1,0:T(8,128)(2,1)S(1)} %get-tuple-element.36.refs_0_), channel_id=1, source_target_pairs={{0,3},{4,196},{1,0},{5,197},{2,1},{6,198},{3,2},{7,199},{8,11},{12... | collective-permute-start | bytes 786440 | tf_op jit(solution)/shard_map/ppermute | solution.py:266
  39.7 5.8 %collective-permute-start.5 = (bf16[256,512]{1,0:T(8,128)(2,1)S(1)}, bf16[256,512]{1,0:T(8,128)(2,1)S(1)}, u32[]{:S(2)}, u32[]{:S(2)}) collective-permute-start(bf16[256,512]{1,0:T(8,128)(2,1)S(1)} %get-tuple-element.36.refs_0_), channel_id=1, source_target_pairs={{0,4},{4,0},{1,5},{5,1},{2,6},{6,2},{3,7},{7,3},{8,12},{12,8},{9,1... | collective-permute-start | bytes 786440 | tf_op jit(solution)/shard_map/ppermute | solution.py:248
  41.0 1.0 copy-start.1
  44.0 1.6 %collective-permute-start.6 = (bf16[256,512]{1,0:T(8,128)(2,1)S(1)}, bf16[256,512]{1,0:T(8,128)(2,1)S(1)}, u32[]{:S(2)}, u32[]{:S(2)}) collective-permute-start(bf16[256,512]{1,0:T(8,128)(2,1)S(1)} %collective-permute-done.4.refs_2_), channel_id=1, source_target_pairs={{0,4},{4,0},{1,5},{5,1},{2,6},{6,2},{3,7},{7,3},{8,12},{12,8},{9,1... | collective-permute-start | bytes 786440 | tf_op jit(solution)/shard_map/ppermute | solution.py:248
  44.1 2.5 %collective-permute-start.3 = (bf16[256,512]{1,0:T(8,128)(2,1)S(1)}, bf16[256,512]{1,0:T(8,128)(2,1)S(1)}, u32[]{:S(2)}, u32[]{:S(2)}) collective-permute-start(bf16[256,512]{1,0:T(8,128)(2,1)S(1)} %collective-permute-done.2.refs_1_), channel_id=1, source_target_pairs={{0,4},{4,0},{1,5},{5,1},{2,6},{6,2},{3,7},{7,3},{8,12},{12,8},{9,1... | collective-permute-start | bytes 786440 | tf_op jit(solution)/shard_map/ppermute | solution.py:248
  45.3 1.5 %collective-permute-start.1 = (bf16[256,512]{1,0:T(8,128)(2,1)S(1)}, bf16[256,512]{1,0:T(8,128)(2,1)S(1)}, u32[]{:S(2)}, u32[]{:S(2)}) collective-permute-start(bf16[256,512]{1,0:T(8,128)(2,1)S(1)} %collective-permute-done.refs_3_), channel_id=1, source_target_pairs={{0,4},{4,0},{1,5},{5,1},{2,6},{6,2},{3,7},{7,3},{8,12},{12,8},{9,1... | collective-permute-start | bytes 786440 | tf_op jit(solution)/shard_map/ppermute | solution.py:248
  70.1 3.5 %collective-permute-start.7 = (f32[2,256]{1,0:T(2,128)S(1)}, f32[2,256]{1,0:T(2,128)S(1)}, u32[]{:S(2)}, u32[]{:S(2)}) collective-permute-start(f32[2,256]{1,0:T(2,128)S(1)} %shard_map.73.mine), channel_id=1, source_target_pairs={{0,4},{4,0},{1,5},{5,1},{2,6},{6,2},{3,7},{7,3},{8,12},{12,8},{9,1... | collective-permute-start | bytes 6152 | tf_op jit(solution)/shard_map/ppermute | solution.py:248
  74.0 2.4 %collective-permute-start.11 = (bf16[256,512]{1,0:T(8,128)(2,1)S(1)}, bf16[256,512]{1,0:T(8,128)(2,1)S(1)}, u32[]{:S(2)}, u32[]{:S(2)}) collective-permute-start(bf16[256,512]{1,0:T(8,128)(2,1)S(1)} %get-tuple-element.59), channel_id=1, source_target_pairs={{0,4},{4,0},{1,5},{5,1},{2,6},{6,2},{3,7},{7,3},{8,12},{12,8},{9,1... | collective-permute-start | bytes 786440 | tf_op jit(solution)/shard_map/ppermute | solution.py:248
  75.1 2.7 %collective-permute-start.8 = (bf16[256,512]{1,0:T(8,128)(2,1)S(1)}, bf16[256,512]{1,0:T(8,128)(2,1)S(1)}, u32[]{:S(2)}, u32[]{:S(2)}) collective-permute-start(bf16[256,512]{1,0:T(8,128)(2,1)S(1)} %get-tuple-element.52), channel_id=1, source_target_pairs={{0,4},{4,0},{1,5},{5,1},{2,6},{6,2},{3,7},{7,3},{8,12},{12,8},{9,1... | collective-permute-start | bytes 786440 | tf_op jit(solution)/shard_map/ppermute | solution.py:248
  76.0 3.1 %collective-permute-start.13 = (bf16[256,512]{1,0:T(8,128)(2,1)S(1)}, bf16[256,512]{1,0:T(8,128)(2,1)S(1)}, u32[]{:S(2)}, u32[]{:S(2)}) collective-permute-start(bf16[256,512]{1,0:T(8,128)(2,1)S(1)} %get-tuple-element.61), channel_id=1, source_target_pairs={{0,4},{4,0},{1,5},{5,1},{2,6},{6,2},{3,7},{7,3},{8,12},{12,8},{9,1... | collective-permute-start | bytes 786440 | tf_op jit(solution)/shard_map/ppermute | solution.py:248
  76.5 10.0 %collective-permute-start.12 = (bf16[256,512]{1,0:T(8,128)(2,1)S(1)}, bf16[256,512]{1,0:T(8,128)(2,1)S(1)}, u32[]{:S(2)}, u32[]{:S(2)}) collective-permute-start(bf16[256,512]{1,0:T(8,128)(2,1)S(1)} %add_convert_fusion.1), channel_id=1, source_target_pairs={{0,2},{4,132},{1,3},{5,133},{2,0},{6,134},{3,1},{7,135},{8,10},{12... | collective-permute-start | bytes 786440 | tf_op jit(solution)/shard_map/ppermute | solution.py:266
  77.9 8.5 %collective-permute-start.10 = (bf16[256,512]{1,0:T(8,128)(2,1)S(1)}, bf16[256,512]{1,0:T(8,128)(2,1)S(1)}, u32[]{:S(2)}, u32[]{:S(2)}) collective-permute-start(bf16[256,512]{1,0:T(8,128)(2,1)S(1)} %add_convert_fusion.3), channel_id=1, source_target_pairs={{0,1},{4,68},{1,2},{5,69},{2,3},{6,70},{3,0},{7,71},{8,9},{12,76},... | collective-permute-start | bytes 786440 | tf_op jit(solution)/shard_map/ppermute | solution.py:266
  78.5 7.9 %collective-permute-start.9 = (bf16[256,512]{1,0:T(8,128)(2,1)S(1)}, bf16[256,512]{1,0:T(8,128)(2,1)S(1)}, u32[]{:S(2)}, u32[]{:S(2)}) collective-permute-start(bf16[256,512]{1,0:T(8,128)(2,1)S(1)} %get-tuple-element.55), channel_id=1, source_target_pairs={{0,4},{4,0},{1,5},{5,1},{2,6},{6,2},{3,7},{7,3},{8,12},{12,8},{9,1... | collective-permute-start | bytes 786440 | tf_op jit(solution)/shard_map/ppermute | solution.py:248
  79.1 7.4 %collective-permute-start.14 = (bf16[256,512]{1,0:T(8,128)(2,1)S(1)}, bf16[256,512]{1,0:T(8,128)(2,1)S(1)}, u32[]{:S(2)}, u32[]{:S(2)}) collective-permute-start(bf16[256,512]{1,0:T(8,128)(2,1)S(1)} %add_convert_fusion), channel_id=1, source_target_pairs={{0,3},{4,196},{1,0},{5,197},{2,1},{6,198},{3,2},{7,199},{8,11},{12... | collective-permute-start | bytes 786440 | tf_op jit(solution)/shard_map/ppermute | solution.py:266
  87.0 5.5 %collective-permute-start.15 = (bf16[256,256]{1,0:T(8,128)(2,1)S(1)}, bf16[256,256]{1,0:T(8,128)(2,1)S(1)}, u32[]{:S(2)}, u32[]{:S(2)}) collective-permute-start(bf16[256,256]{1,0:T(8,128)(2,1)S(1)} %get-tuple-element.64), channel_id=1, source_target_pairs={{0,128},{4,6},{1,129},{5,7},{2,130},{6,4},{3,131},{7,5},{8,136},{1... | collective-permute-start | bytes 393224 | tf_op jit(solution)/shard_map/ppermute | solution.py:266
  87.9 6.2 %collective-permute-start.16 = (bf16[256,256]{1,0:T(8,128)(2,1)S(1)}, bf16[256,256]{1,0:T(8,128)(2,1)S(1)}, u32[]{:S(2)}, u32[]{:S(2)}) collective-permute-start(bf16[256,256]{1,0:T(8,128)(2,1)S(1)} %get-tuple-element.65), channel_id=1, source_target_pairs={{0,64},{4,5},{1,65},{5,6},{2,66},{6,7},{3,67},{7,4},{8,72},{12,13}... | collective-permute-start | bytes 393224 | tf_op jit(solution)/shard_map/ppermute | solution.py:266
  88.5 5.6 %collective-permute-start.17 = (bf16[256,256]{1,0:T(8,128)(2,1)S(1)}, bf16[256,256]{1,0:T(8,128)(2,1)S(1)}, u32[]{:S(2)}, u32[]{:S(2)}) collective-permute-start(bf16[256,256]{1,0:T(8,128)(2,1)S(1)} %get-tuple-element.66), channel_id=1, source_target_pairs={{0,192},{4,7},{1,193},{5,4},{2,194},{6,5},{3,195},{7,6},{8,200},{1... | collective-permute-start | bytes 393224 | tf_op jit(solution)/shard_map/ppermute | solution.py:266
  106.6 5.3 %collective-permute-start.18 = (f32[4,4,256]{2,1,0:T(4,128)S(1)}, f32[4,4,256]{2,1,0:T(4,128)S(1)}, u32[]{:S(2)}, u32[]{:S(2)}) collective-permute-start(f32[4,4,256]{2,1,0:T(4,128)S(1)} %get-tuple-element.68), channel_id=1, source_target_pairs={{0,4},{4,0},{1,5},{5,1},{2,6},{6,2},{3,7},{7,3},{8,12},{12,8},{9,1... | collective-permute-start | bytes 49160 | tf_op jit(solution)/shard_map/ppermute | solution.py:248

commit v9 on v8

--- a/solution.py
+++ b/solution.py
@@ -13,7 +13,6 @@
 
 SEQ = ("x", "z", "core")
 ALL = ("x", "z", "core", "y")
-CHIPS = ("x", "z", "y")
 NX, NZ, NCORE, NY = 4, 8, 2, 4
 RING = 4
 FIRST = ((0, 0), (0, 1), (0, 2), (0, 3), (1, 0), (1, 2))
@@ -168,6 +167,11 @@
     out[...] = top + jnp.log(jnp.sum(jnp.exp(x - top[None]), axis=0))
 
 
+def join_body(a, b, c, d, out):
+    top = jnp.maximum(jnp.maximum(a[...], b[...]), jnp.maximum(c[...], d[...]))
+    out[...] = top + jnp.log(sum(jnp.exp(x[...] - top) for x in (a, b, c, d)))
+
+
 def products(grad, weight, which, parts):
     for part, (side, k) in zip(parts, which):
         part[...] = lax.dot_general(
@@ -282,7 +286,6 @@
     vocab = head_weight.shape[1]
     part = depth // (RING * NCORE)
     own = capacity // NY
-    chips = NX * NZ * NY
     weight = head_weight.T
     half_flops = vocab * depth * MASKED
     logits_shape = shape((vocab, MASKED), F32)
@@ -320,11 +323,12 @@
     )
     blocks[1, 1], total = lax.optimization_barrier((blocks[1, 1], total))
     student, stats = call(
-        student_last_body, (logits_shape, shape((chips, 2, MASKED), F32)),
+        student_last_body, (logits_shape, shape((NZ * RING, 2, MASKED), F32)),
         *[blocks[at] for at in LAST], weight, total, lse_teacher, flops=half_flops,
     )
-    stats = lax.all_to_all(stats, CHIPS, 0, 0, tiled=True)
+    stats = lax.all_to_all(stats, ALL, 0, 0, tiled=True, axis_index_groups=peers())
     lse = call(combine_body, shape((2, MASKED), F32), stats)
+    lse = call(join_body, shape((2, MASKED), F32), lse, *[shift(lse, k, ring=2) for k in (2, 1, 3)])
     parts = {}
     which = ((1, 2),)
     grad_logits, parts[1, 2] = call(

time: 113 us -> 112 us (level)
  blocking collectives: 64.9 us -> 57.7 us
  starting transfers between devices: 24.7 us -> 29.3 us
  waiting for transfers between devices: 8.11 us -> 10.1 us
    all_to_all x1, blocking collectives: 22.4 us -> 14.2 us  [per_device(): lax.all_to_all(stats, ALL, 0, 0, tiled=True, axis_index_groups=peers())]
    ppermute x9 -> x12, starting transfers between devices: 12.9 us -> 18.2 us  [shift(): return lax.ppermute(v, ALL, moves)]
    ppermute x9 -> x12, waiting for transfers between devices: 6.17 us -> 8.18 us  [shift(): return lax.ppermute(v, ALL, moves)]
    pallas_call x14 -> x15, Pallas kernels: 11.1 us -> 10.9 us  [call(): pl.pallas_call(body, out_shape=out, in_specs=specs or [VMEM] * len(args),...]
  transfers between devices with their start and end apart: 19 -> 22, of which waited for: 7 -> 9; matrix products, arithmetic and copies ran while one was open for 0% -> 0% of each run, Pallas kernels for 6% -> 6%
where the time goes in v9:
time: 112 us
  blocking collectives  57.7 us (52%)
  starting transfers between devices  29.3 us (26%)
  Pallas kernels  10.9 us (10%)
  waiting for transfers between devices  10.1 us (9%)
  between operations  1.63 us (1%)
  other arithmetic  1.19 us (1%)
    all_to_all x1, blocking collectives, per_device(): rows = lax.all_to_all(send, SEQ, 0, 0, tiled=True).reshape(slots, part)  30.1 us
    ppermute x12, starting transfers between devices, shift(): return lax.ppermute(v, ALL, moves)  18.2 us
    all_to_all x1, blocking collectives, per_device(): lax.all_to_all(stats, ALL, 0, 0, tiled=True, axis_index_groups=peers())  14.2 us
    all_to_all x1, blocking collectives, per_device(): lax.all_to_all(partial.reshape(NZ * RING, 8, part // 2), ALL, 0, 0, tiled...  13.4 us
    ppermute x10, starting transfers between devices, swap_core(): return lax.ppermute(x, 'core', [(0, 1), (1, 0)])  11.2 us
    pallas_call x15, Pallas kernels, call(): pl.pallas_call(body, out_shape=out, in_specs=specs or [VMEM] * len(args),...  10.9 us
    ppermute x12, waiting for transfers between devices, shift(): return lax.ppermute(v, ALL, moves)  8.18 us
  transfers between devices with their start and end apart: 22, of which 9 were waited for; matrix products, arithmetic and copies ran while one was open for 0% of the time, Pallas kernels for 6%

profile of v9, /device:TPU:1, one launch (start us, length us, event | category | flops | bytes accessed | tf_op | source)
XLA Modules:
  0.0 111.8 jit_solution(14282916311504212567)
XLA Ops:
  1.4 0.8 broadcast_add_fusion.numbers
  2.3 1.2 %shard_map.68 = bf16[64,8,512]{2,1,0:T(8,128)(2,1)S(1)} custom-call(s32[1,8]{1,0:T(1,128)S(1)} %broadcast_add_fusion.numbers, bf16[64,4096]{1,0:T(8,128)(2,1)} %hidden.1), custom_call_target="tpu_custom_call" | custom-call | bytes 1048608 | tf_op jit(solution)/shard_map/pallas_call | solution.py:33
  3.5 30.1 %all_to_all.15 = bf16[64,8,512]{2,1,0:T(8,128)(2,1)S(1)} all-to-all(bf16[64,8,512]{2,1,0:T(8,128)(2,1)S(1)} %shard_map.68), channel_id=1, replica_groups=mesh['x'=4,'z'=8,'core'=2,'y'=4] {'x','z','core'}, dimensions={0} | all-to-all | bytes 1048576 | tf_op jit(solution)/shard_map/all_to_all | solution.py:299
  34.1 2.9 %collective-permute-start.4 = (bf16[256,512]{1,0:T(8,128)(2,1)S(1)}, bf16[256,512]{1,0:T(8,128)(2,1)S(1)}, u32[]{:S(2)}, u32[]{:S(2)}) collective-permute-start(bf16[256,512]{1,0:T(8,128)(2,1)S(1)} %get-tuple-element.36.refs_0_), channel_id=1, source_target_pairs={{0,2},{4,132},{1,3},{5,133},{2,0},{6,134},{3,1},{7,135},{8,10},{12... | collective-permute-start | bytes 786440 | tf_op jit(solution)/shard_map/ppermute | solution.py:270
  37.4 2.3 %collective-permute-start = (bf16[256,512]{1,0:T(8,128)(2,1)S(1)}, bf16[256,512]{1,0:T(8,128)(2,1)S(1)}, u32[]{:S(2)}, u32[]{:S(2)}) collective-permute-start(bf16[256,512]{1,0:T(8,128)(2,1)S(1)} %get-tuple-element.36.refs_0_), channel_id=1, source_target_pairs={{0,3},{4,196},{1,0},{5,197},{2,1},{6,198},{3,2},{7,199},{8,11},{12... | collective-permute-start | bytes 786440 | tf_op jit(solution)/shard_map/ppermute | solution.py:270
  39.7 1.2 %collective-permute-start.5 = (bf16[256,512]{1,0:T(8,128)(2,1)S(1)}, bf16[256,512]{1,0:T(8,128)(2,1)S(1)}, u32[]{:S(2)}, u32[]{:S(2)}) collective-permute-start(bf16[256,512]{1,0:T(8,128)(2,1)S(1)} %get-tuple-element.36.refs_0_), channel_id=1, source_target_pairs={{0,4},{4,0},{1,5},{5,1},{2,6},{6,2},{3,7},{7,3},{8,12},{12,8},{9,1... | collective-permute-start | bytes 786440 | tf_op jit(solution)/shard_map/ppermute | solution.py:252
  41.0 1.0 copy-done.1
  42.0 2.0 %shard_map.70 = (bf16[494,256]{1,0:T(8,128)(2,1)S(1)}, f32[8,256]{1,0:T(8,128)S(1)}, bf16[2,1024,256]{2,1,0:T(8,128)(2,1)S(1)}) custom-call(bf16[494,512]{1,0:T(8,128)(2,1)S(1)} %bitcast.14, bf16[256,512]{1,0:T(8,128)(2,1)S(1)} %get-tuple-element.37.chosen), custom_call_target="tpu_custom_call" | custom-call | flops 397934592 | bytes 2077696 | tf_op jit(solution)/shard_map/pallas_call | solution.py:33
  44.1 1.2 %collective-permute-start.3 = (bf16[256,512]{1,0:T(8,128)(2,1)S(1)}, bf16[256,512]{1,0:T(8,128)(2,1)S(1)}, u32[]{:S(2)}, u32[]{:S(2)}) collective-permute-start(bf16[256,512]{1,0:T(8,128)(2,1)S(1)} %collective-permute-done.2.refs_1_), channel_id=1, source_target_pairs={{0,4},{4,0},{1,5},{5,1},{2,6},{6,2},{3,7},{7,3},{8,12},{12,8},{9,1... | collective-permute-start | bytes 786440 | tf_op jit(solution)/shard_map/ppermute | solution.py:252
  45.7 1.0 shard_map.71.refs_3_
  46.9 0.6 shard_map.72
  47.5 14.2 %all_to_all.16.stats = f32[32,2,256]{2,1,0:T(2,128)S(1)} all-to-all(f32[32,2,256]{2,1,0:T(2,128)S(1)} %get-tuple-element.47), channel_id=1, replica_groups={{0,1,2,3,8,9,10,11,16,17,18,19,24,25,26,27,32,33,34,35,40,41,42,43,48,4..., dimensions={0} | all-to-all | bytes 131072 | tf_op jit(solution)/shard_map/all_to_all | solution.py:329
  61.8 2.8 %collective-permute-start.9 = (f32[2,256]{1,0:T(2,128)S(1)}, f32[2,256]{1,0:T(2,128)S(1)}, u32[]{:S(2)}, u32[]{:S(2)}) collective-permute-start(f32[2,256]{1,0:T(2,128)S(1)} %shard_map.73.a), channel_id=1, source_target_pairs={{0,192},{4,7},{1,193},{5,4},{2,194},{6,5},{3,195},{7,6},{8,200},{1... | collective-permute-start | bytes 6152 | tf_op jit(solution)/shard_map/ppermute | solution.py:270
  64.6 1.3 %collective-permute-start.7 = (f32[2,256]{1,0:T(2,128)S(1)}, f32[2,256]{1,0:T(2,128)S(1)}, u32[]{:S(2)}, u32[]{:S(2)}) collective-permute-start(f32[2,256]{1,0:T(2,128)S(1)} %shard_map.73.a), channel_id=1, source_target_pairs={{0,128},{4,6},{1,129},{5,7},{2,130},{6,4},{3,131},{7,5},{8,136},{1... | collective-permute-start | bytes 6152 | tf_op jit(solution)/shard_map/ppermute | solution.py:270
  65.9 2.4 %collective-permute-done.8.c = f32[2,256]{1,0:T(2,128)S(1)} collective-permute-done((f32[2,256]{1,0:T(2,128)S(1)}, f32[2,256]{1,0:T(2,128)S(1)}, u32[]{:S(2)}, u32[]{:S(2)}) %collective-permute-start.8) | collective-permute-done | bytes 2080 | tf_op jit(solution)/shard_map/ppermute | solution.py:270
  68.5 3.5 %collective-permute-start.10 = (f32[2,256]{1,0:T(2,128)S(1)}, f32[2,256]{1,0:T(2,128)S(1)}, u32[]{:S(2)}, u32[]{:S(2)}) collective-permute-start(f32[2,256]{1,0:T(2,128)S(1)} %shard_map.74.mine), channel_id=1, source_target_pairs={{0,4},{4,0},{1,5},{5,1},{2,6},{6,2},{3,7},{7,3},{8,12},{12,8},{9,1... | collective-permute-start | bytes 6152 | tf_op jit(solution)/shard_map/ppermute | solution.py:252
  72.0 0.8 collective-permute-done.10.other
  73.3 0.6 collective-permute-start.14
  75.7 1.4 %collective-permute-start.15 = (bf16[256,512]{1,0:T(8,128)(2,1)S(1)}, bf16[256,512]{1,0:T(8,128)(2,1)S(1)}, u32[]{:S(2)}, u32[]{:S(2)}) collective-permute-start(bf16[256,512]{1,0:T(8,128)(2,1)S(1)} %add_convert_fusion.1), channel_id=1, source_target_pairs={{0,2},{4,132},{1,3},{5,133},{2,0},{6,134},{3,1},{7,135},{8,10},{12... | collective-permute-start | bytes 786440 | tf_op jit(solution)/shard_map/ppermute | solution.py:270
  77.2 1.5 %collective-permute-start.13 = (bf16[256,512]{1,0:T(8,128)(2,1)S(1)}, bf16[256,512]{1,0:T(8,128)(2,1)S(1)}, u32[]{:S(2)}, u32[]{:S(2)}) collective-permute-start(bf16[256,512]{1,0:T(8,128)(2,1)S(1)} %add_convert_fusion.3), channel_id=1, source_target_pairs={{0,1},{4,68},{1,2},{5,69},{2,3},{6,70},{3,0},{7,71},{8,9},{12,76},... | collective-permute-start | bytes 786440 | tf_op jit(solution)/shard_map/ppermute | solution.py:270
  79.3 1.9 %collective-permute-start.17 = (bf16[256,512]{1,0:T(8,128)(2,1)S(1)}, bf16[256,512]{1,0:T(8,128)(2,1)S(1)}, u32[]{:S(2)}, u32[]{:S(2)}) collective-permute-start(bf16[256,512]{1,0:T(8,128)(2,1)S(1)} %add_convert_fusion), channel_id=1, source_target_pairs={{0,3},{4,196},{1,0},{5,197},{2,1},{6,198},{3,2},{7,199},{8,11},{12... | collective-permute-start | bytes 786440 | tf_op jit(solution)/shard_map/ppermute | solution.py:270
  81.3 2.3 %shard_map.79 = bf16[494,4096]{1,0:T(8,128)(2,1)} custom-call(bf16[256,512]{1,0:T(8,128)(2,1)S(1)} %get-tuple-element.36.refs_0_, bf16[256,512]{1,0:T(8,128)(2,1)S(1)} %collective-permute-done.2.refs_1_, bf16[256,512]{1,0:T(8,128)(2,1)S(1)} %collective-permute-done.4.refs_2_, bf16[256,512]{1,0:T(8,128)(2,1)S(1)} %collective-permute-done.refs_3_, ...), custom_call_target="tpu_custom_call" | custom-call | flops 1035993088 | bytes 6396928 | tf_op jit(solution)/shard_map/pallas_call | solution.py:33
  83.6 2.1 %collective-permute-done.13.b = bf16[256,512]{1,0:T(8,128)(2,1)S(1)} collective-permute-done((bf16[256,512]{1,0:T(8,128)(2,1)S(1)}, bf16[256,512]{1,0:T(8,128)(2,1)S(1)}, u32[]{:S(2)}, u32[]{:S(2)}) %collective-permute-start.13) | collective-permute-done | bytes 262176 | tf_op jit(solution)/shard_map/ppermute | solution.py:270
  86.3 1.0 collective-permute-start.18
  87.3 0.8 collective-permute-start.19
  88.1 1.9 %collective-permute-start.20 = (bf16[256,256]{1,0:T(8,128)(2,1)S(1)}, bf16[256,256]{1,0:T(8,128)(2,1)S(1)}, u32[]{:S(2)}, u32[]{:S(2)}) collective-permute-start(bf16[256,256]{1,0:T(8,128)(2,1)S(1)} %get-tuple-element.66), channel_id=1, source_target_pairs={{0,192},{4,7},{1,193},{5,4},{2,194},{6,5},{3,195},{7,6},{8,200},{1... | collective-permute-start | bytes 393224 | tf_op jit(solution)/shard_map/ppermute | solution.py:270
  89.9 1.8 %collective-permute-done.18 = bf16[256,256]{1,0:T(8,128)(2,1)S(1)} collective-permute-done((bf16[256,256]{1,0:T(8,128)(2,1)S(1)}, bf16[256,256]{1,0:T(8,128)(2,1)S(1)}, u32[]{:S(2)}, u32[]{:S(2)}) %collective-permute-start.18) | collective-permute-done | bytes 131104 | tf_op jit(solution)/shard_map/ppermute | solution.py:270
  91.8 1.6 %collective-permute-done.19 = bf16[256,256]{1,0:T(8,128)(2,1)S(1)} collective-permute-done((bf16[256,256]{1,0:T(8,128)(2,1)S(1)}, bf16[256,256]{1,0:T(8,128)(2,1)S(1)}, u32[]{:S(2)}, u32[]{:S(2)}) %collective-permute-start.19) | collective-permute-done | bytes 131104 | tf_op jit(solution)/shard_map/ppermute | solution.py:270
  93.4 13.4 %all_to_all.17.parts = bf16[32,8,256]{2,1,0:T(8,128)(2,1)S(1)} all-to-all(bf16[32,8,256]{2,1,0:T(8,128)(2,1)S(1)} %fusion), channel_id=1, replica_groups={{0,1,2,3,8,9,10,11,16,17,18,19,24,25,26,27,32,33,34,35,40,41,42,43,48,4..., dimensions={0} | all-to-all | bytes 262144 | tf_op jit(solution)/shard_map/all_to_all | solution.py:372
  106.8 3.5 %collective-permute-start.21 = (f32[4,4,256]{2,1,0:T(4,128)S(1)}, f32[4,4,256]{2,1,0:T(4,128)S(1)}, u32[]{:S(2)}, u32[]{:S(2)}) collective-permute-start(f32[4,4,256]{2,1,0:T(4,128)S(1)} %get-tuple-element.68), channel_id=1, source_target_pairs={{0,4},{4,0},{1,5},{5,1},{2,6},{6,2},{3,7},{7,3},{8,12},{12,8},{9,1... | collective-permute-start | bytes 49160 | tf_op jit(solution)/shard_map/ppermute | solution.py:252
  110.3 0.8 collective-permute-done.21.other
  111.2 0.6 shard_map.82
  (40 shorter events, 5.5 us)
Async XLA Ops:
  0.6 45.0 %copy-start = (bf16[4096,494]{0,1:T(8,128)(2,1)S(1)}, bf16[4096,494]{0,1:T(8,128)(2,1)}, u32[]{:S(2)}) copy-start(bf16[4096,494]{0,1:T(8,128)(2,1)} %param.6) | copy-start | bytes 12140548
  34.1 9.9 %collective-permute-start.4 = (bf16[256,512]{1,0:T(8,128)(2,1)S(1)}, bf16[256,512]{1,0:T(8,128)(2,1)S(1)}, u32[]{:S(2)}, u32[]{:S(2)}) collective-permute-start(bf16[256,512]{1,0:T(8,128)(2,1)S(1)} %get-tuple-element.36.refs_0_), channel_id=1, source_target_pairs={{0,2},{4,132},{1,3},{5,133},{2,0},{6,134},{3,1},{7,135},{8,10},{12... | collective-permute-start | bytes 786440 | tf_op jit(solution)/shard_map/ppermute | solution.py:270
  37.1 7.1 %collective-permute-start.2 = (bf16[256,512]{1,0:T(8,128)(2,1)S(1)}, bf16[256,512]{1,0:T(8,128)(2,1)S(1)}, u32[]{:S(2)}, u32[]{:S(2)}) collective-permute-start(bf16[256,512]{1,0:T(8,128)(2,1)S(1)} %get-tuple-element.36.refs_0_), channel_id=1, source_target_pairs={{0,1},{4,68},{1,2},{5,69},{2,3},{6,70},{3,0},{7,71},{8,9},{12,76},... | collective-permute-start | bytes 786440 | tf_op jit(solution)/shard_map/ppermute | solution.py:270
  37.4 7.9 %collective-permute-start = (bf16[256,512]{1,0:T(8,128)(2,1)S(1)}, bf16[256,512]{1,0:T(8,128)(2,1)S(1)}, u32[]{:S(2)}, u32[]{:S(2)}) collective-permute-start(bf16[256,512]{1,0:T(8,128)(2,1)S(1)} %get-tuple-element.36.refs_0_), channel_id=1, source_target_pairs={{0,3},{4,196},{1,0},{5,197},{2,1},{6,198},{3,2},{7,199},{8,11},{12... | collective-permute-start | bytes 786440 | tf_op jit(solution)/shard_map/ppermute | solution.py:270
  39.7 5.8 %collective-permute-start.5 = (bf16[256,512]{1,0:T(8,128)(2,1)S(1)}, bf16[256,512]{1,0:T(8,128)(2,1)S(1)}, u32[]{:S(2)}, u32[]{:S(2)}) collective-permute-start(bf16[256,512]{1,0:T(8,128)(2,1)S(1)} %get-tuple-element.36.refs_0_), channel_id=1, source_target_pairs={{0,4},{4,0},{1,5},{5,1},{2,6},{6,2},{3,7},{7,3},{8,12},{12,8},{9,1... | collective-permute-start | bytes 786440 | tf_op jit(solution)/shard_map/ppermute | solution.py:252
  41.0 1.0 copy-start.1
  44.0 1.6 %collective-permute-start.6 = (bf16[256,512]{1,0:T(8,128)(2,1)S(1)}, bf16[256,512]{1,0:T(8,128)(2,1)S(1)}, u32[]{:S(2)}, u32[]{:S(2)}) collective-permute-start(bf16[256,512]{1,0:T(8,128)(2,1)S(1)} %collective-permute-done.4.refs_2_), channel_id=1, source_target_pairs={{0,4},{4,0},{1,5},{5,1},{2,6},{6,2},{3,7},{7,3},{8,12},{12,8},{9,1... | collective-permute-start | bytes 786440 | tf_op jit(solution)/shard_map/ppermute | solution.py:252
  44.1 2.5 %collective-permute-start.3 = (bf16[256,512]{1,0:T(8,128)(2,1)S(1)}, bf16[256,512]{1,0:T(8,128)(2,1)S(1)}, u32[]{:S(2)}, u32[]{:S(2)}) collective-permute-start(bf16[256,512]{1,0:T(8,128)(2,1)S(1)} %collective-permute-done.2.refs_1_), channel_id=1, source_target_pairs={{0,4},{4,0},{1,5},{5,1},{2,6},{6,2},{3,7},{7,3},{8,12},{12,8},{9,1... | collective-permute-start | bytes 786440 | tf_op jit(solution)/shard_map/ppermute | solution.py:252
  45.3 1.5 %collective-permute-start.1 = (bf16[256,512]{1,0:T(8,128)(2,1)S(1)}, bf16[256,512]{1,0:T(8,128)(2,1)S(1)}, u32[]{:S(2)}, u32[]{:S(2)}) collective-permute-start(bf16[256,512]{1,0:T(8,128)(2,1)S(1)} %collective-permute-done.refs_3_), channel_id=1, source_target_pairs={{0,4},{4,0},{1,5},{5,1},{2,6},{6,2},{3,7},{7,3},{8,12},{12,8},{9,1... | collective-permute-start | bytes 786440 | tf_op jit(solution)/shard_map/ppermute | solution.py:252
  61.8 4.1 %collective-permute-start.9 = (f32[2,256]{1,0:T(2,128)S(1)}, f32[2,256]{1,0:T(2,128)S(1)}, u32[]{:S(2)}, u32[]{:S(2)}) collective-permute-start(f32[2,256]{1,0:T(2,128)S(1)} %shard_map.73.a), channel_id=1, source_target_pairs={{0,192},{4,7},{1,193},{5,4},{2,194},{6,5},{3,195},{7,6},{8,200},{1... | collective-permute-start | bytes 6152 | tf_op jit(solution)/shard_map/ppermute | solution.py:270
  64.6 3.6 %collective-permute-start.8 = (f32[2,256]{1,0:T(2,128)S(1)}, f32[2,256]{1,0:T(2,128)S(1)}, u32[]{:S(2)}, u32[]{:S(2)}) collective-permute-start(f32[2,256]{1,0:T(2,128)S(1)} %shard_map.73.a), channel_id=1, source_target_pairs={{0,64},{4,5},{1,65},{5,6},{2,66},{6,7},{3,67},{7,4},{8,72},{12,13}... | collective-permute-start | bytes 6152 | tf_op jit(solution)/shard_map/ppermute | solution.py:270
  64.6 3.9 %collective-permute-start.7 = (f32[2,256]{1,0:T(2,128)S(1)}, f32[2,256]{1,0:T(2,128)S(1)}, u32[]{:S(2)}, u32[]{:S(2)}) collective-permute-start(f32[2,256]{1,0:T(2,128)S(1)} %shard_map.73.a), channel_id=1, source_target_pairs={{0,128},{4,6},{1,129},{5,7},{2,130},{6,4},{3,131},{7,5},{8,136},{1... | collective-permute-start | bytes 6152 | tf_op jit(solution)/shard_map/ppermute | solution.py:270
  68.5 4.3 %collective-permute-start.10 = (f32[2,256]{1,0:T(2,128)S(1)}, f32[2,256]{1,0:T(2,128)S(1)}, u32[]{:S(2)}, u32[]{:S(2)}) collective-permute-start(f32[2,256]{1,0:T(2,128)S(1)} %shard_map.74.mine), channel_id=1, source_target_pairs={{0,4},{4,0},{1,5},{5,1},{2,6},{6,2},{3,7},{7,3},{8,12},{12,8},{9,1... | collective-permute-start | bytes 6152 | tf_op jit(solution)/shard_map/ppermute | solution.py:252
  73.3 2.4 %collective-permute-start.14 = (bf16[256,512]{1,0:T(8,128)(2,1)S(1)}, bf16[256,512]{1,0:T(8,128)(2,1)S(1)}, u32[]{:S(2)}, u32[]{:S(2)}) collective-permute-start(bf16[256,512]{1,0:T(8,128)(2,1)S(1)} %get-tuple-element.59), channel_id=1, source_target_pairs={{0,4},{4,0},{1,5},{5,1},{2,6},{6,2},{3,7},{7,3},{8,12},{12,8},{9,1... | collective-permute-start | bytes 786440 | tf_op jit(solution)/shard_map/ppermute | solution.py:252
  74.4 2.8 %collective-permute-start.11 = (bf16[256,512]{1,0:T(8,128)(2,1)S(1)}, bf16[256,512]{1,0:T(8,128)(2,1)S(1)}, u32[]{:S(2)}, u32[]{:S(2)}) collective-permute-start(bf16[256,512]{1,0:T(8,128)(2,1)S(1)} %get-tuple-element.52), channel_id=1, source_target_pairs={{0,4},{4,0},{1,5},{5,1},{2,6},{6,2},{3,7},{7,3},{8,12},{12,8},{9,1... | collective-permute-start | bytes 786440 | tf_op jit(solution)/shard_map/ppermute | solution.py:252
  75.2 4.0 %collective-permute-start.16 = (bf16[256,512]{1,0:T(8,128)(2,1)S(1)}, bf16[256,512]{1,0:T(8,128)(2,1)S(1)}, u32[]{:S(2)}, u32[]{:S(2)}) collective-permute-start(bf16[256,512]{1,0:T(8,128)(2,1)S(1)} %get-tuple-element.61), channel_id=1, source_target_pairs={{0,4},{4,0},{1,5},{5,1},{2,6},{6,2},{3,7},{7,3},{8,12},{12,8},{9,1... | collective-permute-start | bytes 786440 | tf_op jit(solution)/shard_map/ppermute | solution.py:252
  75.7 10.0 %collective-permute-start.15 = (bf16[256,512]{1,0:T(8,128)(2,1)S(1)}, bf16[256,512]{1,0:T(8,128)(2,1)S(1)}, u32[]{:S(2)}, u32[]{:S(2)}) collective-permute-start(bf16[256,512]{1,0:T(8,128)(2,1)S(1)} %add_convert_fusion.1), channel_id=1, source_target_pairs={{0,2},{4,132},{1,3},{5,133},{2,0},{6,134},{3,1},{7,135},{8,10},{12... | collective-permute-start | bytes 786440 | tf_op jit(solution)/shard_map/ppermute | solution.py:270
  77.2 8.4 %collective-permute-start.13 = (bf16[256,512]{1,0:T(8,128)(2,1)S(1)}, bf16[256,512]{1,0:T(8,128)(2,1)S(1)}, u32[]{:S(2)}, u32[]{:S(2)}) collective-permute-start(bf16[256,512]{1,0:T(8,128)(2,1)S(1)} %add_convert_fusion.3), channel_id=1, source_target_pairs={{0,1},{4,68},{1,2},{5,69},{2,3},{6,70},{3,0},{7,71},{8,9},{12,76},... | collective-permute-start | bytes 786440 | tf_op jit(solution)/shard_map/ppermute | solution.py:270
  79.1 6.5 %collective-permute-start.12 = (bf16[256,512]{1,0:T(8,128)(2,1)S(1)}, bf16[256,512]{1,0:T(8,128)(2,1)S(1)}, u32[]{:S(2)}, u32[]{:S(2)}) collective-permute-start(bf16[256,512]{1,0:T(8,128)(2,1)S(1)} %get-tuple-element.55), channel_id=1, source_target_pairs={{0,4},{4,0},{1,5},{5,1},{2,6},{6,2},{3,7},{7,3},{8,12},{12,8},{9,1... | collective-permute-start | bytes 786440 | tf_op jit(solution)/shard_map/ppermute | solution.py:252
  79.3 6.4 %collective-permute-start.17 = (bf16[256,512]{1,0:T(8,128)(2,1)S(1)}, bf16[256,512]{1,0:T(8,128)(2,1)S(1)}, u32[]{:S(2)}, u32[]{:S(2)}) collective-permute-start(bf16[256,512]{1,0:T(8,128)(2,1)S(1)} %add_convert_fusion), channel_id=1, source_target_pairs={{0,3},{4,196},{1,0},{5,197},{2,1},{6,198},{3,2},{7,199},{8,11},{12... | collective-permute-start | bytes 786440 | tf_op jit(solution)/shard_map/ppermute | solution.py:270
  86.3 5.5 %collective-permute-start.18 = (bf16[256,256]{1,0:T(8,128)(2,1)S(1)}, bf16[256,256]{1,0:T(8,128)(2,1)S(1)}, u32[]{:S(2)}, u32[]{:S(2)}) collective-permute-start(bf16[256,256]{1,0:T(8,128)(2,1)S(1)} %get-tuple-element.64), channel_id=1, source_target_pairs={{0,128},{4,6},{1,129},{5,7},{2,130},{6,4},{3,131},{7,5},{8,136},{1... | collective-permute-start | bytes 393224 | tf_op jit(solution)/shard_map/ppermute | solution.py:270
  87.3 6.1 %collective-permute-start.19 = (bf16[256,256]{1,0:T(8,128)(2,1)S(1)}, bf16[256,256]{1,0:T(8,128)(2,1)S(1)}, u32[]{:S(2)}, u32[]{:S(2)}) collective-permute-start(bf16[256,256]{1,0:T(8,128)(2,1)S(1)} %get-tuple-element.65), channel_id=1, source_target_pairs={{0,64},{4,5},{1,65},{5,6},{2,66},{6,7},{3,67},{7,4},{8,72},{12,13}... | collective-permute-start | bytes 393224 | tf_op jit(solution)/shard_map/ppermute | solution.py:270
  88.1 5.3 %collective-permute-start.20 = (bf16[256,256]{1,0:T(8,128)(2,1)S(1)}, bf16[256,256]{1,0:T(8,128)(2,1)S(1)}, u32[]{:S(2)}, u32[]{:S(2)}) collective-permute-start(bf16[256,256]{1,0:T(8,128)(2,1)S(1)} %get-tuple-element.66), channel_id=1, source_target_pairs={{0,192},{4,7},{1,193},{5,4},{2,194},{6,5},{3,195},{7,6},{8,200},{1... | collective-permute-start | bytes 393224 | tf_op jit(solution)/shard_map/ppermute | solution.py:270
  106.8 4.4 %collective-permute-start.21 = (f32[4,4,256]{2,1,0:T(4,128)S(1)}, f32[4,4,256]{2,1,0:T(4,128)S(1)}, u32[]{:S(2)}, u32[]{:S(2)}) collective-permute-start(f32[4,4,256]{2,1,0:T(4,128)S(1)} %get-tuple-element.68), channel_id=1, source_target_pairs={{0,4},{4,0},{1,5},{5,1},{2,6},{6,2},{3,7},{7,3},{8,12},{12,8},{9,1... | collective-permute-start | bytes 49160 | tf_op jit(solution)/shard_map/ppermute | solution.py:252

commit v10 on v9

--- a/solution.py
+++ b/solution.py
@@ -17,6 +17,7 @@
 RING = 4
 FIRST = ((0, 0), (0, 1), (0, 2), (0, 3), (1, 0), (1, 2))
 LAST = ((1, 3), (1, 1))
+Y_CORE = 1
 assert NX == NY == RING
 F32, BF16 = jnp.float32, jnp.bfloat16
 NT = (((1,), (1,)), ((), ()))
@@ -50,11 +51,11 @@
 
 
 def place(core):
-    return jnp.where(core == 0, lax.axis_index("y"), lax.axis_index("x"))
+    return jnp.where(core == Y_CORE, lax.axis_index("y"), lax.axis_index("x"))
 
 
 def second_place(core):
-    return jnp.where(core == 0, lax.axis_index("x"), lax.axis_index("y"))
+    return jnp.where(core == Y_CORE, lax.axis_index("x"), lax.axis_index("y"))
 
 
 def part_at(side, steps):
@@ -66,13 +67,13 @@
 def pick_body(numbers, hidden, out, mine, sems):
     shards, capacity, width = out.shape
     tokens, depth = hidden.shape
+    mine_y, x_half = Y_CORE * RING + lax.axis_index("y"), (1 - Y_CORE) * (depth // 2)
     copies = [
         pltpu.make_async_copy(
-            hidden.at[:, columns(lax.axis_index("y"), width)],
-            mine.at[:tokens, :width], sems.at[0],
+            hidden.at[:, columns(mine_y, width)], mine.at[:tokens, :width], sems.at[0]
         ),
         pltpu.make_async_copy(
-            hidden.at[:, depth // 2 :], mine.at[:tokens, width:], sems.at[1]
+            hidden.at[:, x_half : x_half + depth // 2], mine.at[:tokens, width:], sems.at[1]
         ),
     ]
     for copy in copies:
@@ -89,7 +90,7 @@
     rows = lax.dot_general(hot, mine[...], TN, preferred_element_type=F32)
     rows = rows.astype(BF16)
     for s in range(shards):
-        start = s % NCORE * (1 + s // (NZ * NCORE)) * width
+        start = 0 if s % NCORE == Y_CORE else (1 + s // (NZ * NCORE)) * width
         out[s] = rows[:, start : start + width]
 
 
@@ -124,7 +125,7 @@
     slots = chosen.shape[1]
     row = lax.broadcasted_iota(jnp.int32, (sent, slots), 0)
     second, z, first, q = row // 256, row // 32 % NZ, row // 8 % RING, row % 8
-    straight = lax.axis_index("core") == 0
+    straight = lax.axis_index("core") == Y_CORE
     x, y = jnp.where(straight, second, first), jnp.where(straight, first, second)
     slot = (x * NZ + z) * 16 + q // 4 * 8 + y * 2 + q // 2 % 2
     column = lax.broadcasted_iota(jnp.int32, (sent, slots), 1)
@@ -262,7 +263,7 @@
         for z in range(NZ):
             for y in range(NY):
                 for core in range(NCORE):
-                    if (core == 0) == (ring == 1):
+                    if (core == Y_CORE) == (ring == 1):
                         to = index(x, z, core, (y + k) % NY)
                     else:
                         to = index((x + k) % NX, z, core, y)
@@ -273,8 +274,8 @@
 def peers():
     groups = []
     for second in range(RING):
-        groups.append([index(second, z, 0, y) for z in range(NZ) for y in range(NY)])
-        groups.append([index(x, z, 1, second) for z in range(NZ) for x in range(NX)])
+        groups.append([index(second, z, Y_CORE, y) for z in range(NZ) for y in range(NY)])
+        groups.append([index(x, z, 1 - Y_CORE, second) for z in range(NZ) for x in range(NX)])
     return groups
 
 
@@ -328,7 +329,7 @@
     )
     stats = lax.all_to_all(stats, ALL, 0, 0, tiled=True, axis_index_groups=peers())
     lse = call(combine_body, shape((2, MASKED), F32), stats)
-    lse = call(join_body, shape((2, MASKED), F32), lse, *[shift(lse, k, ring=2) for k in (2, 1, 3)])
+    lse = call(join_body, shape((2, MASKED), F32), lse, *[shift(lse, k, ring=2) for k in (3, 1, 2)])
     parts = {}
     which = ((1, 2),)
     grad_logits, parts[1, 2] = call(

time: 112 us -> 112 us (level)
  blocking collectives: 57.7 us -> 60.4 us
  waiting for transfers between devices: 10.1 us -> 8.34 us
    all_to_all x1, blocking collectives: 14.2 us -> 16.3 us  [per_device(): lax.all_to_all(stats, ALL, 0, 0, tiled=True, axis_index_groups=peers())]
    ppermute x12, waiting for transfers between devices: 8.18 us -> 6.16 us  [shift(): return lax.ppermute(v, ALL, moves)]
    ppermute x10, starting transfers between devices: 11.2 us -> 9.86 us  [swap_core(): return lax.ppermute(x, 'core', [(0, 1), (1, 0)])]
  transfers between devices with their start and end apart: 22 -> 22, of which waited for: 9 -> 11; matrix products, arithmetic and copies ran while one was open for 0% -> 0% of each run, Pallas kernels for 6% -> 6%
where the time goes in v10:
time: 112 us
  blocking collectives  60.4 us (54%)
  starting transfers between devices  28.7 us (26%)
  Pallas kernels  10.9 us (10%)
  waiting for transfers between devices  8.34 us (7%)
  between operations  1.62 us (1%)
  other arithmetic  1.19 us (1%)
    all_to_all x1, blocking collectives, per_device(): rows = lax.all_to_all(send, SEQ, 0, 0, tiled=True).reshape(slots, part)  30.1 us
    ppermute x12, starting transfers between devices, shift(): return lax.ppermute(v, ALL, moves)  18.8 us
    all_to_all x1, blocking collectives, per_device(): lax.all_to_all(stats, ALL, 0, 0, tiled=True, axis_index_groups=peers())  16.3 us
    all_to_all x1, blocking collectives, per_device(): lax.all_to_all(partial.reshape(NZ * RING, 8, part // 2), ALL, 0, 0, tiled...  14 us
    pallas_call x15, Pallas kernels, call(): pl.pallas_call(body, out_shape=out, in_specs=specs or [VMEM] * len(args),...  10.9 us
    ppermute x10, starting transfers between devices, swap_core(): return lax.ppermute(x, 'core', [(0, 1), (1, 0)])  9.86 us
    ppermute x12, waiting for transfers between devices, shift(): return lax.ppermute(v, ALL, moves)  6.16 us
  transfers between devices with their start and end apart: 22, of which 11 were waited for; matrix products, arithmetic and copies ran while one was open for 0% of the time, Pallas kernels for 6%

profile of v10, /device:TPU:1, one launch (start us, length us, event | category | flops | bytes accessed | tf_op | source)
XLA Modules:
  0.0 112.1 jit_solution(17516516849656482808)
XLA Ops:
  1.4 0.8 broadcast_add_fusion.numbers
  2.3 1.2 %shard_map.68 = bf16[64,8,512]{2,1,0:T(8,128)(2,1)S(1)} custom-call(s32[1,8]{1,0:T(1,128)S(1)} %broadcast_add_fusion.numbers, bf16[64,4096]{1,0:T(8,128)(2,1)} %hidden.1), custom_call_target="tpu_custom_call" | custom-call | bytes 1048608 | tf_op jit(solution)/shard_map/pallas_call | solution.py:34
  3.5 30.1 %all_to_all.15 = bf16[64,8,512]{2,1,0:T(8,128)(2,1)S(1)} all-to-all(bf16[64,8,512]{2,1,0:T(8,128)(2,1)S(1)} %shard_map.68), channel_id=1, replica_groups=mesh['x'=4,'z'=8,'core'=2,'y'=4] {'x','z','core'}, dimensions={0} | all-to-all | bytes 1048576 | tf_op jit(solution)/shard_map/all_to_all | solution.py:300
  34.1 3.0 %collective-permute-start.4 = (bf16[256,512]{1,0:T(8,128)(2,1)S(1)}, bf16[256,512]{1,0:T(8,128)(2,1)S(1)}, u32[]{:S(2)}, u32[]{:S(2)}) collective-permute-start(bf16[256,512]{1,0:T(8,128)(2,1)S(1)} %get-tuple-element.36.refs_0_), channel_id=1, source_target_pairs={{0,128},{4,6},{1,129},{5,7},{2,130},{6,4},{3,131},{7,5},{8,136},{1... | collective-permute-start | bytes 786440 | tf_op jit(solution)/shard_map/ppermute | solution.py:271
  37.5 2.3 %collective-permute-start = (bf16[256,512]{1,0:T(8,128)(2,1)S(1)}, bf16[256,512]{1,0:T(8,128)(2,1)S(1)}, u32[]{:S(2)}, u32[]{:S(2)}) collective-permute-start(bf16[256,512]{1,0:T(8,128)(2,1)S(1)} %get-tuple-element.36.refs_0_), channel_id=1, source_target_pairs={{0,192},{4,7},{1,193},{5,4},{2,194},{6,5},{3,195},{7,6},{8,200},{1... | collective-permute-start | bytes 786440 | tf_op jit(solution)/shard_map/ppermute | solution.py:271
  39.8 0.7 collective-permute-start.5
  40.5 1.0 copy-done.1
  41.5 2.0 %shard_map.70 = (bf16[494,256]{1,0:T(8,128)(2,1)S(1)}, f32[8,256]{1,0:T(8,128)S(1)}, bf16[2,1024,256]{2,1,0:T(8,128)(2,1)S(1)}) custom-call(bf16[494,512]{1,0:T(8,128)(2,1)S(1)} %bitcast.14, bf16[256,512]{1,0:T(8,128)(2,1)S(1)} %get-tuple-element.37.chosen), custom_call_target="tpu_custom_call" | custom-call | flops 397934592 | bytes 2077696 | tf_op jit(solution)/shard_map/pallas_call | solution.py:34
  44.0 1.2 %collective-permute-start.3 = (bf16[256,512]{1,0:T(8,128)(2,1)S(1)}, bf16[256,512]{1,0:T(8,128)(2,1)S(1)}, u32[]{:S(2)}, u32[]{:S(2)}) collective-permute-start(bf16[256,512]{1,0:T(8,128)(2,1)S(1)} %collective-permute-done.2.refs_1_), channel_id=1, source_target_pairs={{0,4},{4,0},{1,5},{5,1},{2,6},{6,2},{3,7},{7,3},{8,12},{12,8},{9,1... | collective-permute-start | bytes 786440 | tf_op jit(solution)/shard_map/ppermute | solution.py:253
  45.3 1.0 shard_map.71.refs_3_
  46.8 0.6 shard_map.72
  47.4 16.3 %all_to_all.16.stats = f32[32,2,256]{2,1,0:T(2,128)S(1)} all-to-all(f32[32,2,256]{2,1,0:T(2,128)S(1)} %get-tuple-element.47), channel_id=1, replica_groups={{4,5,6,7,12,13,14,15,20,21,22,23,28,29,30,31,36,37,38,39,44,45,46,47,52..., dimensions={0} | all-to-all | bytes 131072 | tf_op jit(solution)/shard_map/all_to_all | solution.py:330
  63.8 0.8 collective-permute-start.9
  65.0 2.3 %collective-permute-start.7 = (f32[2,256]{1,0:T(2,128)S(1)}, f32[2,256]{1,0:T(2,128)S(1)}, u32[]{:S(2)}, u32[]{:S(2)}) collective-permute-start(f32[2,256]{1,0:T(2,128)S(1)} %shard_map.73.a), channel_id=1, source_target_pairs={{0,3},{4,196},{1,0},{5,197},{2,1},{6,198},{3,2},{7,199},{8,11},{12... | collective-permute-start | bytes 6152 | tf_op jit(solution)/shard_map/ppermute | solution.py:271
  67.2 0.8 collective-permute-done.9.d
  68.2 3.3 %collective-permute-start.10 = (f32[2,256]{1,0:T(2,128)S(1)}, f32[2,256]{1,0:T(2,128)S(1)}, u32[]{:S(2)}, u32[]{:S(2)}) collective-permute-start(f32[2,256]{1,0:T(2,128)S(1)} %shard_map.74.mine), channel_id=1, source_target_pairs={{0,4},{4,0},{1,5},{5,1},{2,6},{6,2},{3,7},{7,3},{8,12},{12,8},{9,1... | collective-permute-start | bytes 6152 | tf_op jit(solution)/shard_map/ppermute | solution.py:253
  71.5 0.8 collective-permute-done.10.other
  72.8 0.6 collective-permute-start.14
  74.1 0.6 shard_map.76
  75.2 1.3 %collective-permute-start.15 = (bf16[256,512]{1,0:T(8,128)(2,1)S(1)}, bf16[256,512]{1,0:T(8,128)(2,1)S(1)}, u32[]{:S(2)}, u32[]{:S(2)}) collective-permute-start(bf16[256,512]{1,0:T(8,128)(2,1)S(1)} %add_convert_fusion.1), channel_id=1, source_target_pairs={{0,128},{4,6},{1,129},{5,7},{2,130},{6,4},{3,131},{7,5},{8,136},{1... | collective-permute-start | bytes 786440 | tf_op jit(solution)/shard_map/ppermute | solution.py:271
  76.5 2.4 %collective-permute-start.13 = (bf16[256,512]{1,0:T(8,128)(2,1)S(1)}, bf16[256,512]{1,0:T(8,128)(2,1)S(1)}, u32[]{:S(2)}, u32[]{:S(2)}) collective-permute-start(bf16[256,512]{1,0:T(8,128)(2,1)S(1)} %add_convert_fusion.3), channel_id=1, source_target_pairs={{0,64},{4,5},{1,65},{5,6},{2,66},{6,7},{3,67},{7,4},{8,72},{12,13}... | collective-permute-start | bytes 786440 | tf_op jit(solution)/shard_map/ppermute | solution.py:271
  79.6 1.9 %collective-permute-start.17 = (bf16[256,512]{1,0:T(8,128)(2,1)S(1)}, bf16[256,512]{1,0:T(8,128)(2,1)S(1)}, u32[]{:S(2)}, u32[]{:S(2)}) collective-permute-start(bf16[256,512]{1,0:T(8,128)(2,1)S(1)} %add_convert_fusion), channel_id=1, source_target_pairs={{0,192},{4,7},{1,193},{5,4},{2,194},{6,5},{3,195},{7,6},{8,200},{1... | collective-permute-start | bytes 786440 | tf_op jit(solution)/shard_map/ppermute | solution.py:271
  81.6 2.3 %shard_map.79 = bf16[494,4096]{1,0:T(8,128)(2,1)} custom-call(bf16[256,512]{1,0:T(8,128)(2,1)S(1)} %get-tuple-element.36.refs_0_, bf16[256,512]{1,0:T(8,128)(2,1)S(1)} %collective-permute-done.2.refs_1_, bf16[256,512]{1,0:T(8,128)(2,1)S(1)} %collective-permute-done.4.refs_2_, bf16[256,512]{1,0:T(8,128)(2,1)S(1)} %collective-permute-done.refs_3_, ...), custom_call_target="tpu_custom_call" | custom-call | flops 1035993088 | bytes 6396928 | tf_op jit(solution)/shard_map/pallas_call | solution.py:34
  83.9 1.2 %collective-permute-done.13.b = bf16[256,512]{1,0:T(8,128)(2,1)S(1)} collective-permute-done((bf16[256,512]{1,0:T(8,128)(2,1)S(1)}, bf16[256,512]{1,0:T(8,128)(2,1)S(1)}, u32[]{:S(2)}, u32[]{:S(2)}) %collective-permute-start.13) | collective-permute-done | bytes 262176 | tf_op jit(solution)/shard_map/ppermute | solution.py:271
  86.2 1.4 %collective-permute-start.18 = (bf16[256,256]{1,0:T(8,128)(2,1)S(1)}, bf16[256,256]{1,0:T(8,128)(2,1)S(1)}, u32[]{:S(2)}, u32[]{:S(2)}) collective-permute-start(bf16[256,256]{1,0:T(8,128)(2,1)S(1)} %get-tuple-element.64), channel_id=1, source_target_pairs={{0,2},{4,132},{1,3},{5,133},{2,0},{6,134},{3,1},{7,135},{8,10},{12... | collective-permute-start | bytes 393224 | tf_op jit(solution)/shard_map/ppermute | solution.py:271
  88.0 2.2 %collective-permute-start.20 = (bf16[256,256]{1,0:T(8,128)(2,1)S(1)}, bf16[256,256]{1,0:T(8,128)(2,1)S(1)}, u32[]{:S(2)}, u32[]{:S(2)}) collective-permute-start(bf16[256,256]{1,0:T(8,128)(2,1)S(1)} %get-tuple-element.66), channel_id=1, source_target_pairs={{0,3},{4,196},{1,0},{5,197},{2,1},{6,198},{3,2},{7,199},{8,11},{12... | collective-permute-start | bytes 393224 | tf_op jit(solution)/shard_map/ppermute | solution.py:271
  90.2 1.7 %collective-permute-done.18 = bf16[256,256]{1,0:T(8,128)(2,1)S(1)} collective-permute-done((bf16[256,256]{1,0:T(8,128)(2,1)S(1)}, bf16[256,256]{1,0:T(8,128)(2,1)S(1)}, u32[]{:S(2)}, u32[]{:S(2)}) %collective-permute-start.18) | collective-permute-done | bytes 131104 | tf_op jit(solution)/shard_map/ppermute | solution.py:271
  91.9 1.4 %collective-permute-done.19 = bf16[256,256]{1,0:T(8,128)(2,1)S(1)} collective-permute-done((bf16[256,256]{1,0:T(8,128)(2,1)S(1)}, bf16[256,256]{1,0:T(8,128)(2,1)S(1)}, u32[]{:S(2)}, u32[]{:S(2)}) %collective-permute-start.19) | collective-permute-done | bytes 131104 | tf_op jit(solution)/shard_map/ppermute | solution.py:271
  93.4 14.0 %all_to_all.17.parts = bf16[32,8,256]{2,1,0:T(8,128)(2,1)S(1)} all-to-all(bf16[32,8,256]{2,1,0:T(8,128)(2,1)S(1)} %fusion), channel_id=1, replica_groups={{4,5,6,7,12,13,14,15,20,21,22,23,28,29,30,31,36,37,38,39,44,45,46,47,52..., dimensions={0} | all-to-all | bytes 262144 | tf_op jit(solution)/shard_map/all_to_all | solution.py:373
  107.4 3.3 %collective-permute-start.21 = (f32[4,4,256]{2,1,0:T(4,128)S(1)}, f32[4,4,256]{2,1,0:T(4,128)S(1)}, u32[]{:S(2)}, u32[]{:S(2)}) collective-permute-start(f32[4,4,256]{2,1,0:T(4,128)S(1)} %get-tuple-element.68), channel_id=1, source_target_pairs={{0,4},{4,0},{1,5},{5,1},{2,6},{6,2},{3,7},{7,3},{8,12},{12,8},{9,1... | collective-permute-start | bytes 49160 | tf_op jit(solution)/shard_map/ppermute | solution.py:253
  110.7 0.8 collective-permute-done.21.other
  111.5 0.6 shard_map.82
  (40 shorter events, 6.6 us)
Async XLA Ops:
  0.6 44.6 %copy-start = (bf16[4096,494]{0,1:T(8,128)(2,1)S(1)}, bf16[4096,494]{0,1:T(8,128)(2,1)}, u32[]{:S(2)}) copy-start(bf16[4096,494]{0,1:T(8,128)(2,1)} %param.6) | copy-start | bytes 12140548
  34.1 9.4 %collective-permute-start.4 = (bf16[256,512]{1,0:T(8,128)(2,1)S(1)}, bf16[256,512]{1,0:T(8,128)(2,1)S(1)}, u32[]{:S(2)}, u32[]{:S(2)}) collective-permute-start(bf16[256,512]{1,0:T(8,128)(2,1)S(1)} %get-tuple-element.36.refs_0_), channel_id=1, source_target_pairs={{0,128},{4,6},{1,129},{5,7},{2,130},{6,4},{3,131},{7,5},{8,136},{1... | collective-permute-start | bytes 786440 | tf_op jit(solution)/shard_map/ppermute | solution.py:271
  37.1 6.9 %collective-permute-start.2 = (bf16[256,512]{1,0:T(8,128)(2,1)S(1)}, bf16[256,512]{1,0:T(8,128)(2,1)S(1)}, u32[]{:S(2)}, u32[]{:S(2)}) collective-permute-start(bf16[256,512]{1,0:T(8,128)(2,1)S(1)} %get-tuple-element.36.refs_0_), channel_id=1, source_target_pairs={{0,64},{4,5},{1,65},{5,6},{2,66},{6,7},{3,67},{7,4},{8,72},{12,13}... | collective-permute-start | bytes 786440 | tf_op jit(solution)/shard_map/ppermute | solution.py:271
  37.5 7.7 %collective-permute-start = (bf16[256,512]{1,0:T(8,128)(2,1)S(1)}, bf16[256,512]{1,0:T(8,128)(2,1)S(1)}, u32[]{:S(2)}, u32[]{:S(2)}) collective-permute-start(bf16[256,512]{1,0:T(8,128)(2,1)S(1)} %get-tuple-element.36.refs_0_), channel_id=1, source_target_pairs={{0,192},{4,7},{1,193},{5,4},{2,194},{6,5},{3,195},{7,6},{8,200},{1... | collective-permute-start | bytes 786440 | tf_op jit(solution)/shard_map/ppermute | solution.py:271
  39.8 5.4 %collective-permute-start.5 = (bf16[256,512]{1,0:T(8,128)(2,1)S(1)}, bf16[256,512]{1,0:T(8,128)(2,1)S(1)}, u32[]{:S(2)}, u32[]{:S(2)}) collective-permute-start(bf16[256,512]{1,0:T(8,128)(2,1)S(1)} %get-tuple-element.36.refs_0_), channel_id=1, source_target_pairs={{0,4},{4,0},{1,5},{5,1},{2,6},{6,2},{3,7},{7,3},{8,12},{12,8},{9,1... | collective-permute-start | bytes 786440 | tf_op jit(solution)/shard_map/ppermute | solution.py:253
  40.5 1.0 copy-start.1
  43.5 1.7 %collective-permute-start.6 = (bf16[256,512]{1,0:T(8,128)(2,1)S(1)}, bf16[256,512]{1,0:T(8,128)(2,1)S(1)}, u32[]{:S(2)}, u32[]{:S(2)}) collective-permute-start(bf16[256,512]{1,0:T(8,128)(2,1)S(1)} %collective-permute-done.4.refs_2_), channel_id=1, source_target_pairs={{0,4},{4,0},{1,5},{5,1},{2,6},{6,2},{3,7},{7,3},{8,12},{12,8},{9,1... | collective-permute-start | bytes 786440 | tf_op jit(solution)/shard_map/ppermute | solution.py:253
  44.0 2.3 %collective-permute-start.3 = (bf16[256,512]{1,0:T(8,128)(2,1)S(1)}, bf16[256,512]{1,0:T(8,128)(2,1)S(1)}, u32[]{:S(2)}, u32[]{:S(2)}) collective-permute-start(bf16[256,512]{1,0:T(8,128)(2,1)S(1)} %collective-permute-done.2.refs_1_), channel_id=1, source_target_pairs={{0,4},{4,0},{1,5},{5,1},{2,6},{6,2},{3,7},{7,3},{8,12},{12,8},{9,1... | collective-permute-start | bytes 786440 | tf_op jit(solution)/shard_map/ppermute | solution.py:253
  45.2 1.5 %collective-permute-start.1 = (bf16[256,512]{1,0:T(8,128)(2,1)S(1)}, bf16[256,512]{1,0:T(8,128)(2,1)S(1)}, u32[]{:S(2)}, u32[]{:S(2)}) collective-permute-start(bf16[256,512]{1,0:T(8,128)(2,1)S(1)} %collective-permute-done.refs_3_), channel_id=1, source_target_pairs={{0,4},{4,0},{1,5},{5,1},{2,6},{6,2},{3,7},{7,3},{8,12},{12,8},{9,1... | collective-permute-start | bytes 786440 | tf_op jit(solution)/shard_map/ppermute | solution.py:253
  63.8 4.3 %collective-permute-start.9 = (f32[2,256]{1,0:T(2,128)S(1)}, f32[2,256]{1,0:T(2,128)S(1)}, u32[]{:S(2)}, u32[]{:S(2)}) collective-permute-start(f32[2,256]{1,0:T(2,128)S(1)} %shard_map.73.a), channel_id=1, source_target_pairs={{0,2},{4,132},{1,3},{5,133},{2,0},{6,134},{3,1},{7,135},{8,10},{12... | collective-permute-start | bytes 6152 | tf_op jit(solution)/shard_map/ppermute | solution.py:271
  64.6 3.6 %collective-permute-start.8 = (f32[2,256]{1,0:T(2,128)S(1)}, f32[2,256]{1,0:T(2,128)S(1)}, u32[]{:S(2)}, u32[]{:S(2)}) collective-permute-start(f32[2,256]{1,0:T(2,128)S(1)} %shard_map.73.a), channel_id=1, source_target_pairs={{0,1},{4,68},{1,2},{5,69},{2,3},{6,70},{3,0},{7,71},{8,9},{12,76},... | collective-permute-start | bytes 6152 | tf_op jit(solution)/shard_map/ppermute | solution.py:271
  65.0 3.2 %collective-permute-start.7 = (f32[2,256]{1,0:T(2,128)S(1)}, f32[2,256]{1,0:T(2,128)S(1)}, u32[]{:S(2)}, u32[]{:S(2)}) collective-permute-start(f32[2,256]{1,0:T(2,128)S(1)} %shard_map.73.a), channel_id=1, source_target_pairs={{0,3},{4,196},{1,0},{5,197},{2,1},{6,198},{3,2},{7,199},{8,11},{12... | collective-permute-start | bytes 6152 | tf_op jit(solution)/shard_map/ppermute | solution.py:271
  68.2 4.1 %collective-permute-start.10 = (f32[2,256]{1,0:T(2,128)S(1)}, f32[2,256]{1,0:T(2,128)S(1)}, u32[]{:S(2)}, u32[]{:S(2)}) collective-permute-start(f32[2,256]{1,0:T(2,128)S(1)} %shard_map.74.mine), channel_id=1, source_target_pairs={{0,4},{4,0},{1,5},{5,1},{2,6},{6,2},{3,7},{7,3},{8,12},{12,8},{9,1... | collective-permute-start | bytes 6152 | tf_op jit(solution)/shard_map/ppermute | solution.py:253
  72.8 2.4 %collective-permute-start.14 = (bf16[256,512]{1,0:T(8,128)(2,1)S(1)}, bf16[256,512]{1,0:T(8,128)(2,1)S(1)}, u32[]{:S(2)}, u32[]{:S(2)}) collective-permute-start(bf16[256,512]{1,0:T(8,128)(2,1)S(1)} %get-tuple-element.59), channel_id=1, source_target_pairs={{0,4},{4,0},{1,5},{5,1},{2,6},{6,2},{3,7},{7,3},{8,12},{12,8},{9,1... | collective-permute-start | bytes 786440 | tf_op jit(solution)/shard_map/ppermute | solution.py:253
  73.8 2.6 %collective-permute-start.11 = (bf16[256,512]{1,0:T(8,128)(2,1)S(1)}, bf16[256,512]{1,0:T(8,128)(2,1)S(1)}, u32[]{:S(2)}, u32[]{:S(2)}) collective-permute-start(bf16[256,512]{1,0:T(8,128)(2,1)S(1)} %get-tuple-element.52), channel_id=1, source_target_pairs={{0,4},{4,0},{1,5},{5,1},{2,6},{6,2},{3,7},{7,3},{8,12},{12,8},{9,1... | collective-permute-start | bytes 786440 | tf_op jit(solution)/shard_map/ppermute | solution.py:253
  74.7 4.9 %collective-permute-start.16 = (bf16[256,512]{1,0:T(8,128)(2,1)S(1)}, bf16[256,512]{1,0:T(8,128)(2,1)S(1)}, u32[]{:S(2)}, u32[]{:S(2)}) collective-permute-start(bf16[256,512]{1,0:T(8,128)(2,1)S(1)} %get-tuple-element.61), channel_id=1, source_target_pairs={{0,4},{4,0},{1,5},{5,1},{2,6},{6,2},{3,7},{7,3},{8,12},{12,8},{9,1... | collective-permute-start | bytes 786440 | tf_op jit(solution)/shard_map/ppermute | solution.py:253
  75.2 10.0 %collective-permute-start.15 = (bf16[256,512]{1,0:T(8,128)(2,1)S(1)}, bf16[256,512]{1,0:T(8,128)(2,1)S(1)}, u32[]{:S(2)}, u32[]{:S(2)}) collective-permute-start(bf16[256,512]{1,0:T(8,128)(2,1)S(1)} %add_convert_fusion.1), channel_id=1, source_target_pairs={{0,128},{4,6},{1,129},{5,7},{2,130},{6,4},{3,131},{7,5},{8,136},{1... | collective-permute-start | bytes 786440 | tf_op jit(solution)/shard_map/ppermute | solution.py:271
  76.5 8.6 %collective-permute-start.13 = (bf16[256,512]{1,0:T(8,128)(2,1)S(1)}, bf16[256,512]{1,0:T(8,128)(2,1)S(1)}, u32[]{:S(2)}, u32[]{:S(2)}) collective-permute-start(bf16[256,512]{1,0:T(8,128)(2,1)S(1)} %add_convert_fusion.3), channel_id=1, source_target_pairs={{0,64},{4,5},{1,65},{5,6},{2,66},{6,7},{3,67},{7,4},{8,72},{12,13}... | collective-permute-start | bytes 786440 | tf_op jit(solution)/shard_map/ppermute | solution.py:271
  79.4 5.7 %collective-permute-start.12 = (bf16[256,512]{1,0:T(8,128)(2,1)S(1)}, bf16[256,512]{1,0:T(8,128)(2,1)S(1)}, u32[]{:S(2)}, u32[]{:S(2)}) collective-permute-start(bf16[256,512]{1,0:T(8,128)(2,1)S(1)} %get-tuple-element.55), channel_id=1, source_target_pairs={{0,4},{4,0},{1,5},{5,1},{2,6},{6,2},{3,7},{7,3},{8,12},{12,8},{9,1... | collective-permute-start | bytes 786440 | tf_op jit(solution)/shard_map/ppermute | solution.py:253
  79.6 6.0 %collective-permute-start.17 = (bf16[256,512]{1,0:T(8,128)(2,1)S(1)}, bf16[256,512]{1,0:T(8,128)(2,1)S(1)}, u32[]{:S(2)}, u32[]{:S(2)}) collective-permute-start(bf16[256,512]{1,0:T(8,128)(2,1)S(1)} %add_convert_fusion), channel_id=1, source_target_pairs={{0,192},{4,7},{1,193},{5,4},{2,194},{6,5},{3,195},{7,6},{8,200},{1... | collective-permute-start | bytes 786440 | tf_op jit(solution)/shard_map/ppermute | solution.py:271
  86.2 5.7 %collective-permute-start.18 = (bf16[256,256]{1,0:T(8,128)(2,1)S(1)}, bf16[256,256]{1,0:T(8,128)(2,1)S(1)}, u32[]{:S(2)}, u32[]{:S(2)}) collective-permute-start(bf16[256,256]{1,0:T(8,128)(2,1)S(1)} %get-tuple-element.64), channel_id=1, source_target_pairs={{0,2},{4,132},{1,3},{5,133},{2,0},{6,134},{3,1},{7,135},{8,10},{12... | collective-permute-start | bytes 393224 | tf_op jit(solution)/shard_map/ppermute | solution.py:271
  87.5 5.7 %collective-permute-start.19 = (bf16[256,256]{1,0:T(8,128)(2,1)S(1)}, bf16[256,256]{1,0:T(8,128)(2,1)S(1)}, u32[]{:S(2)}, u32[]{:S(2)}) collective-permute-start(bf16[256,256]{1,0:T(8,128)(2,1)S(1)} %get-tuple-element.65), channel_id=1, source_target_pairs={{0,1},{4,68},{1,2},{5,69},{2,3},{6,70},{3,0},{7,71},{8,9},{12,76},... | collective-permute-start | bytes 393224 | tf_op jit(solution)/shard_map/ppermute | solution.py:271
  88.0 5.2 %collective-permute-start.20 = (bf16[256,256]{1,0:T(8,128)(2,1)S(1)}, bf16[256,256]{1,0:T(8,128)(2,1)S(1)}, u32[]{:S(2)}, u32[]{:S(2)}) collective-permute-start(bf16[256,256]{1,0:T(8,128)(2,1)S(1)} %get-tuple-element.66), channel_id=1, source_target_pairs={{0,3},{4,196},{1,0},{5,197},{2,1},{6,198},{3,2},{7,199},{8,11},{12... | collective-permute-start | bytes 393224 | tf_op jit(solution)/shard_map/ppermute | solution.py:271
  107.4 4.1 %collective-permute-start.21 = (f32[4,4,256]{2,1,0:T(4,128)S(1)}, f32[4,4,256]{2,1,0:T(4,128)S(1)}, u32[]{:S(2)}, u32[]{:S(2)}) collective-permute-start(f32[4,4,256]{2,1,0:T(4,128)S(1)} %get-tuple-element.68), channel_id=1, source_target_pairs={{0,4},{4,0},{1,5},{5,1},{2,6},{6,2},{3,7},{7,3},{8,12},{12,8},{9,1... | collective-permute-start | bytes 49160 | tf_op jit(solution)/shard_map/ppermute | solution.py:253

commit v11 on v10

--- a/solution.py
+++ b/solution.py
@@ -15,6 +15,7 @@
 ALL = ("x", "z", "core", "y")
 NX, NZ, NCORE, NY = 4, 8, 2, 4
 RING = 4
+ZS = tuple(reversed(range(NZ)))
 FIRST = ((0, 0), (0, 1), (0, 2), (0, 3), (1, 0), (1, 2))
 LAST = ((1, 3), (1, 1))
 Y_CORE = 1
@@ -124,7 +125,7 @@
     halves, sent, masked = back.shape
     slots = chosen.shape[1]
     row = lax.broadcasted_iota(jnp.int32, (sent, slots), 0)
-    second, z, first, q = row // 256, row // 32 % NZ, row // 8 % RING, row % 8
+    second, z, first, q = row // 256, NZ - 1 - row // 32 % NZ, row // 8 % RING, row % 8
     straight = lax.axis_index("core") == Y_CORE
     x, y = jnp.where(straight, second, first), jnp.where(straight, first, second)
     slot = (x * NZ + z) * 16 + q // 4 * 8 + y * 2 + q // 2 % 2
@@ -274,8 +275,8 @@
 def peers():
     groups = []
     for second in range(RING):
-        groups.append([index(second, z, Y_CORE, y) for z in range(NZ) for y in range(NY)])
-        groups.append([index(x, z, 1 - Y_CORE, second) for z in range(NZ) for x in range(NX)])
+        groups.append([index(second, z, Y_CORE, y) for z in ZS for y in range(NY)])
+        groups.append([index(x, z, 1 - Y_CORE, second) for z in ZS for x in range(NX)])
     return groups
 
 

time: 112 us -> 112 us (level)
    all_to_all x1, blocking collectives: 16.3 us -> 15.2 us  [per_device(): lax.all_to_all(stats, ALL, 0, 0, tiled=True, axis_index_groups=peers())]
  transfers between devices with their start and end apart: 22 -> 22, of which waited for: 11 -> 10; matrix products, arithmetic and copies ran while one was open for 0% -> 0% of each run, Pallas kernels for 6% -> 6%
where the time goes in v11:
time: 112 us
  blocking collectives  59.6 us (53%)
  starting transfers between devices  28.8 us (26%)
  Pallas kernels  10.9 us (10%)
  waiting for transfers between devices  8.94 us (8%)
  between operations  1.62 us (1%)
  other arithmetic  1.19 us (1%)
    all_to_all x1, blocking collectives, per_device(): rows = lax.all_to_all(send, SEQ, 0, 0, tiled=True).reshape(slots, part)  30.1 us
    ppermute x12, starting transfers between devices, shift(): return lax.ppermute(v, ALL, moves)  19.3 us
    all_to_all x1, blocking collectives, per_device(): lax.all_to_all(stats, ALL, 0, 0, tiled=True, axis_index_groups=peers())  15.2 us
    all_to_all x1, blocking collectives, per_device(): lax.all_to_all(partial.reshape(NZ * RING, 8, part // 2), ALL, 0, 0, tiled...  14.4 us
    pallas_call x15, Pallas kernels, call(): pl.pallas_call(body, out_shape=out, in_specs=specs or [VMEM] * len(args),...  10.9 us
    ppermute x10, starting transfers between devices, swap_core(): return lax.ppermute(x, 'core', [(0, 1), (1, 0)])  9.48 us
    ppermute x12, waiting for transfers between devices, shift(): return lax.ppermute(v, ALL, moves)  6.76 us
  transfers between devices with their start and end apart: 22, of which 10 were waited for; matrix products, arithmetic and copies ran while one was open for 0% of the time, Pallas kernels for 6%

profile of v11, /device:TPU:1, one launch (start us, length us, event | category | flops | bytes accessed | tf_op | source)
XLA Modules:
  0.0 112.0 jit_solution(2534846173645823125)
XLA Ops:
  1.4 0.8 broadcast_add_fusion.numbers
  2.3 1.2 %shard_map.68 = bf16[64,8,512]{2,1,0:T(8,128)(2,1)S(1)} custom-call(s32[1,8]{1,0:T(1,128)S(1)} %broadcast_add_fusion.numbers, bf16[64,4096]{1,0:T(8,128)(2,1)} %hidden.1), custom_call_target="tpu_custom_call" | custom-call | bytes 1048608 | tf_op jit(solution)/shard_map/pallas_call | solution.py:35
  3.5 30.1 %all_to_all.15 = bf16[64,8,512]{2,1,0:T(8,128)(2,1)S(1)} all-to-all(bf16[64,8,512]{2,1,0:T(8,128)(2,1)S(1)} %shard_map.68), channel_id=1, replica_groups=mesh['x'=4,'z'=8,'core'=2,'y'=4] {'x','z','core'}, dimensions={0} | all-to-all | bytes 1048576 | tf_op jit(solution)/shard_map/all_to_all | solution.py:301
  34.1 3.0 %collective-permute-start.4 = (bf16[256,512]{1,0:T(8,128)(2,1)S(1)}, bf16[256,512]{1,0:T(8,128)(2,1)S(1)}, u32[]{:S(2)}, u32[]{:S(2)}) collective-permute-start(bf16[256,512]{1,0:T(8,128)(2,1)S(1)} %get-tuple-element.36.refs_0_), channel_id=1, source_target_pairs={{0,128},{4,6},{1,129},{5,7},{2,130},{6,4},{3,131},{7,5},{8,136},{1... | collective-permute-start | bytes 786440 | tf_op jit(solution)/shard_map/ppermute | solution.py:272
  37.5 2.3 %collective-permute-start = (bf16[256,512]{1,0:T(8,128)(2,1)S(1)}, bf16[256,512]{1,0:T(8,128)(2,1)S(1)}, u32[]{:S(2)}, u32[]{:S(2)}) collective-permute-start(bf16[256,512]{1,0:T(8,128)(2,1)S(1)} %get-tuple-element.36.refs_0_), channel_id=1, source_target_pairs={{0,192},{4,7},{1,193},{5,4},{2,194},{6,5},{3,195},{7,6},{8,200},{1... | collective-permute-start | bytes 786440 | tf_op jit(solution)/shard_map/ppermute | solution.py:272
  39.8 0.7 collective-permute-start.5
  40.5 1.0 copy-done.1
  41.5 2.0 %shard_map.70 = (bf16[494,256]{1,0:T(8,128)(2,1)S(1)}, f32[8,256]{1,0:T(8,128)S(1)}, bf16[2,1024,256]{2,1,0:T(8,128)(2,1)S(1)}) custom-call(bf16[494,512]{1,0:T(8,128)(2,1)S(1)} %bitcast.14, bf16[256,512]{1,0:T(8,128)(2,1)S(1)} %get-tuple-element.37.chosen), custom_call_target="tpu_custom_call" | custom-call | flops 397934592 | bytes 2077696 | tf_op jit(solution)/shard_map/pallas_call | solution.py:35
  44.0 1.2 %collective-permute-start.3 = (bf16[256,512]{1,0:T(8,128)(2,1)S(1)}, bf16[256,512]{1,0:T(8,128)(2,1)S(1)}, u32[]{:S(2)}, u32[]{:S(2)}) collective-permute-start(bf16[256,512]{1,0:T(8,128)(2,1)S(1)} %collective-permute-done.2.refs_1_), channel_id=1, source_target_pairs={{0,4},{4,0},{1,5},{5,1},{2,6},{6,2},{3,7},{7,3},{8,12},{12,8},{9,1... | collective-permute-start | bytes 786440 | tf_op jit(solution)/shard_map/ppermute | solution.py:254
  45.3 1.0 shard_map.71.refs_3_
  46.8 0.6 shard_map.72
  47.4 15.2 %all_to_all.16.stats = f32[32,2,256]{2,1,0:T(2,128)S(1)} all-to-all(f32[32,2,256]{2,1,0:T(2,128)S(1)} %get-tuple-element.47), channel_id=1, replica_groups={{60,61,62,63,52,53,54,55,44,45,46,47,36,37,38,39,28,29,30,31,20,21,22,2..., dimensions={0} | all-to-all | bytes 131072 | tf_op jit(solution)/shard_map/all_to_all | solution.py:331
  62.6 1.6 %collective-permute-start.9 = (f32[2,256]{1,0:T(2,128)S(1)}, f32[2,256]{1,0:T(2,128)S(1)}, u32[]{:S(2)}, u32[]{:S(2)}) collective-permute-start(f32[2,256]{1,0:T(2,128)S(1)} %shard_map.73.a), channel_id=1, source_target_pairs={{0,2},{4,132},{1,3},{5,133},{2,0},{6,134},{3,1},{7,135},{8,10},{12... | collective-permute-start | bytes 6152 | tf_op jit(solution)/shard_map/ppermute | solution.py:272
  64.2 0.9 collective-permute-start.8
  65.1 1.8 %collective-permute-start.7 = (f32[2,256]{1,0:T(2,128)S(1)}, f32[2,256]{1,0:T(2,128)S(1)}, u32[]{:S(2)}, u32[]{:S(2)}) collective-permute-start(f32[2,256]{1,0:T(2,128)S(1)} %shard_map.73.a), channel_id=1, source_target_pairs={{0,3},{4,196},{1,0},{5,197},{2,1},{6,198},{3,2},{7,199},{8,11},{12... | collective-permute-start | bytes 6152 | tf_op jit(solution)/shard_map/ppermute | solution.py:272
  66.9 1.2 %collective-permute-done.8.c = f32[2,256]{1,0:T(2,128)S(1)} collective-permute-done((f32[2,256]{1,0:T(2,128)S(1)}, f32[2,256]{1,0:T(2,128)S(1)}, u32[]{:S(2)}, u32[]{:S(2)}) %collective-permute-start.8) | collective-permute-done | bytes 2080 | tf_op jit(solution)/shard_map/ppermute | solution.py:272
  68.1 3.4 %collective-permute-start.10 = (f32[2,256]{1,0:T(2,128)S(1)}, f32[2,256]{1,0:T(2,128)S(1)}, u32[]{:S(2)}, u32[]{:S(2)}) collective-permute-start(f32[2,256]{1,0:T(2,128)S(1)} %shard_map.74.mine), channel_id=1, source_target_pairs={{0,4},{4,0},{1,5},{5,1},{2,6},{6,2},{3,7},{7,3},{8,12},{12,8},{9,1... | collective-permute-start | bytes 6152 | tf_op jit(solution)/shard_map/ppermute | solution.py:254
  71.5 0.8 collective-permute-done.10.other
  72.8 0.6 collective-permute-start.14
  75.2 1.3 %collective-permute-start.15 = (bf16[256,512]{1,0:T(8,128)(2,1)S(1)}, bf16[256,512]{1,0:T(8,128)(2,1)S(1)}, u32[]{:S(2)}, u32[]{:S(2)}) collective-permute-start(bf16[256,512]{1,0:T(8,128)(2,1)S(1)} %add_convert_fusion.1), channel_id=1, source_target_pairs={{0,128},{4,6},{1,129},{5,7},{2,130},{6,4},{3,131},{7,5},{8,136},{1... | collective-permute-start | bytes 786440 | tf_op jit(solution)/shard_map/ppermute | solution.py:272
  76.6 2.4 %collective-permute-start.13 = (bf16[256,512]{1,0:T(8,128)(2,1)S(1)}, bf16[256,512]{1,0:T(8,128)(2,1)S(1)}, u32[]{:S(2)}, u32[]{:S(2)}) collective-permute-start(bf16[256,512]{1,0:T(8,128)(2,1)S(1)} %add_convert_fusion.3), channel_id=1, source_target_pairs={{0,64},{4,5},{1,65},{5,6},{2,66},{6,7},{3,67},{7,4},{8,72},{12,13}... | collective-permute-start | bytes 786440 | tf_op jit(solution)/shard_map/ppermute | solution.py:272
  79.7 1.5 %collective-permute-start.17 = (bf16[256,512]{1,0:T(8,128)(2,1)S(1)}, bf16[256,512]{1,0:T(8,128)(2,1)S(1)}, u32[]{:S(2)}, u32[]{:S(2)}) collective-permute-start(bf16[256,512]{1,0:T(8,128)(2,1)S(1)} %add_convert_fusion), channel_id=1, source_target_pairs={{0,192},{4,7},{1,193},{5,4},{2,194},{6,5},{3,195},{7,6},{8,200},{1... | collective-permute-start | bytes 786440 | tf_op jit(solution)/shard_map/ppermute | solution.py:272
  81.2 2.3 %shard_map.79 = bf16[494,4096]{1,0:T(8,128)(2,1)} custom-call(bf16[256,512]{1,0:T(8,128)(2,1)S(1)} %get-tuple-element.36.refs_0_, bf16[256,512]{1,0:T(8,128)(2,1)S(1)} %collective-permute-done.2.refs_1_, bf16[256,512]{1,0:T(8,128)(2,1)S(1)} %collective-permute-done.4.refs_2_, bf16[256,512]{1,0:T(8,128)(2,1)S(1)} %collective-permute-done.refs_3_, ...), custom_call_target="tpu_custom_call" | custom-call | flops 1035993088 | bytes 6396928 | tf_op jit(solution)/shard_map/pallas_call | solution.py:35
  83.5 1.6 %collective-permute-done.13.b = bf16[256,512]{1,0:T(8,128)(2,1)S(1)} collective-permute-done((bf16[256,512]{1,0:T(8,128)(2,1)S(1)}, bf16[256,512]{1,0:T(8,128)(2,1)S(1)}, u32[]{:S(2)}, u32[]{:S(2)}) %collective-permute-start.13) | collective-permute-done | bytes 262176 | tf_op jit(solution)/shard_map/ppermute | solution.py:272
  86.2 1.4 %collective-permute-start.18 = (bf16[256,256]{1,0:T(8,128)(2,1)S(1)}, bf16[256,256]{1,0:T(8,128)(2,1)S(1)}, u32[]{:S(2)}, u32[]{:S(2)}) collective-permute-start(bf16[256,256]{1,0:T(8,128)(2,1)S(1)} %get-tuple-element.64), channel_id=1, source_target_pairs={{0,2},{4,132},{1,3},{5,133},{2,0},{6,134},{3,1},{7,135},{8,10},{12... | collective-permute-start | bytes 393224 | tf_op jit(solution)/shard_map/ppermute | solution.py:272
  87.7 2.6 %collective-permute-start.20 = (bf16[256,256]{1,0:T(8,128)(2,1)S(1)}, bf16[256,256]{1,0:T(8,128)(2,1)S(1)}, u32[]{:S(2)}, u32[]{:S(2)}) collective-permute-start(bf16[256,256]{1,0:T(8,128)(2,1)S(1)} %get-tuple-element.66), channel_id=1, source_target_pairs={{0,3},{4,196},{1,0},{5,197},{2,1},{6,198},{3,2},{7,199},{8,11},{12... | collective-permute-start | bytes 393224 | tf_op jit(solution)/shard_map/ppermute | solution.py:272
  90.3 1.6 %collective-permute-done.18 = bf16[256,256]{1,0:T(8,128)(2,1)S(1)} collective-permute-done((bf16[256,256]{1,0:T(8,128)(2,1)S(1)}, bf16[256,256]{1,0:T(8,128)(2,1)S(1)}, u32[]{:S(2)}, u32[]{:S(2)}) %collective-permute-start.18) | collective-permute-done | bytes 131104 | tf_op jit(solution)/shard_map/ppermute | solution.py:272
  91.9 1.4 %collective-permute-done.19 = bf16[256,256]{1,0:T(8,128)(2,1)S(1)} collective-permute-done((bf16[256,256]{1,0:T(8,128)(2,1)S(1)}, bf16[256,256]{1,0:T(8,128)(2,1)S(1)}, u32[]{:S(2)}, u32[]{:S(2)}) %collective-permute-start.19) | collective-permute-done | bytes 131104 | tf_op jit(solution)/shard_map/ppermute | solution.py:272
  93.4 14.4 %all_to_all.17.parts = bf16[32,8,256]{2,1,0:T(8,128)(2,1)S(1)} all-to-all(bf16[32,8,256]{2,1,0:T(8,128)(2,1)S(1)} %fusion), channel_id=1, replica_groups={{60,61,62,63,52,53,54,55,44,45,46,47,36,37,38,39,28,29,30,31,20,21,22,2..., dimensions={0} | all-to-all | bytes 262144 | tf_op jit(solution)/shard_map/all_to_all | solution.py:374
  107.8 2.8 %collective-permute-start.21 = (f32[4,4,256]{2,1,0:T(4,128)S(1)}, f32[4,4,256]{2,1,0:T(4,128)S(1)}, u32[]{:S(2)}, u32[]{:S(2)}) collective-permute-start(f32[4,4,256]{2,1,0:T(4,128)S(1)} %get-tuple-element.68), channel_id=1, source_target_pairs={{0,4},{4,0},{1,5},{5,1},{2,6},{6,2},{3,7},{7,3},{8,12},{12,8},{9,1... | collective-permute-start | bytes 49160 | tf_op jit(solution)/shard_map/ppermute | solution.py:254
  110.5 0.8 collective-permute-done.21.other
  111.4 0.6 shard_map.82
  (40 shorter events, 6.2 us)
Async XLA Ops:
  0.6 44.6 %copy-start = (bf16[4096,494]{0,1:T(8,128)(2,1)S(1)}, bf16[4096,494]{0,1:T(8,128)(2,1)}, u32[]{:S(2)}) copy-start(bf16[4096,494]{0,1:T(8,128)(2,1)} %param.6) | copy-start | bytes 12140548
  34.1 9.4 %collective-permute-start.4 = (bf16[256,512]{1,0:T(8,128)(2,1)S(1)}, bf16[256,512]{1,0:T(8,128)(2,1)S(1)}, u32[]{:S(2)}, u32[]{:S(2)}) collective-permute-start(bf16[256,512]{1,0:T(8,128)(2,1)S(1)} %get-tuple-element.36.refs_0_), channel_id=1, source_target_pairs={{0,128},{4,6},{1,129},{5,7},{2,130},{6,4},{3,131},{7,5},{8,136},{1... | collective-permute-start | bytes 786440 | tf_op jit(solution)/shard_map/ppermute | solution.py:272
  37.1 6.9 %collective-permute-start.2 = (bf16[256,512]{1,0:T(8,128)(2,1)S(1)}, bf16[256,512]{1,0:T(8,128)(2,1)S(1)}, u32[]{:S(2)}, u32[]{:S(2)}) collective-permute-start(bf16[256,512]{1,0:T(8,128)(2,1)S(1)} %get-tuple-element.36.refs_0_), channel_id=1, source_target_pairs={{0,64},{4,5},{1,65},{5,6},{2,66},{6,7},{3,67},{7,4},{8,72},{12,13}... | collective-permute-start | bytes 786440 | tf_op jit(solution)/shard_map/ppermute | solution.py:272
  37.5 7.7 %collective-permute-start = (bf16[256,512]{1,0:T(8,128)(2,1)S(1)}, bf16[256,512]{1,0:T(8,128)(2,1)S(1)}, u32[]{:S(2)}, u32[]{:S(2)}) collective-permute-start(bf16[256,512]{1,0:T(8,128)(2,1)S(1)} %get-tuple-element.36.refs_0_), channel_id=1, source_target_pairs={{0,192},{4,7},{1,193},{5,4},{2,194},{6,5},{3,195},{7,6},{8,200},{1... | collective-permute-start | bytes 786440 | tf_op jit(solution)/shard_map/ppermute | solution.py:272
  39.8 5.4 %collective-permute-start.5 = (bf16[256,512]{1,0:T(8,128)(2,1)S(1)}, bf16[256,512]{1,0:T(8,128)(2,1)S(1)}, u32[]{:S(2)}, u32[]{:S(2)}) collective-permute-start(bf16[256,512]{1,0:T(8,128)(2,1)S(1)} %get-tuple-element.36.refs_0_), channel_id=1, source_target_pairs={{0,4},{4,0},{1,5},{5,1},{2,6},{6,2},{3,7},{7,3},{8,12},{12,8},{9,1... | collective-permute-start | bytes 786440 | tf_op jit(solution)/shard_map/ppermute | solution.py:254
  40.5 1.0 copy-start.1
  43.5 1.7 %collective-permute-start.6 = (bf16[256,512]{1,0:T(8,128)(2,1)S(1)}, bf16[256,512]{1,0:T(8,128)(2,1)S(1)}, u32[]{:S(2)}, u32[]{:S(2)}) collective-permute-start(bf16[256,512]{1,0:T(8,128)(2,1)S(1)} %collective-permute-done.4.refs_2_), channel_id=1, source_target_pairs={{0,4},{4,0},{1,5},{5,1},{2,6},{6,2},{3,7},{7,3},{8,12},{12,8},{9,1... | collective-permute-start | bytes 786440 | tf_op jit(solution)/shard_map/ppermute | solution.py:254
  44.0 2.3 %collective-permute-start.3 = (bf16[256,512]{1,0:T(8,128)(2,1)S(1)}, bf16[256,512]{1,0:T(8,128)(2,1)S(1)}, u32[]{:S(2)}, u32[]{:S(2)}) collective-permute-start(bf16[256,512]{1,0:T(8,128)(2,1)S(1)} %collective-permute-done.2.refs_1_), channel_id=1, source_target_pairs={{0,4},{4,0},{1,5},{5,1},{2,6},{6,2},{3,7},{7,3},{8,12},{12,8},{9,1... | collective-permute-start | bytes 786440 | tf_op jit(solution)/shard_map/ppermute | solution.py:254
  45.2 1.5 %collective-permute-start.1 = (bf16[256,512]{1,0:T(8,128)(2,1)S(1)}, bf16[256,512]{1,0:T(8,128)(2,1)S(1)}, u32[]{:S(2)}, u32[]{:S(2)}) collective-permute-start(bf16[256,512]{1,0:T(8,128)(2,1)S(1)} %collective-permute-done.refs_3_), channel_id=1, source_target_pairs={{0,4},{4,0},{1,5},{5,1},{2,6},{6,2},{3,7},{7,3},{8,12},{12,8},{9,1... | collective-permute-start | bytes 786440 | tf_op jit(solution)/shard_map/ppermute | solution.py:254
  62.6 4.3 %collective-permute-start.9 = (f32[2,256]{1,0:T(2,128)S(1)}, f32[2,256]{1,0:T(2,128)S(1)}, u32[]{:S(2)}, u32[]{:S(2)}) collective-permute-start(f32[2,256]{1,0:T(2,128)S(1)} %shard_map.73.a), channel_id=1, source_target_pairs={{0,2},{4,132},{1,3},{5,133},{2,0},{6,134},{3,1},{7,135},{8,10},{12... | collective-permute-start | bytes 6152 | tf_op jit(solution)/shard_map/ppermute | solution.py:272
  64.2 3.9 %collective-permute-start.8 = (f32[2,256]{1,0:T(2,128)S(1)}, f32[2,256]{1,0:T(2,128)S(1)}, u32[]{:S(2)}, u32[]{:S(2)}) collective-permute-start(f32[2,256]{1,0:T(2,128)S(1)} %shard_map.73.a), channel_id=1, source_target_pairs={{0,1},{4,68},{1,2},{5,69},{2,3},{6,70},{3,0},{7,71},{8,9},{12,76},... | collective-permute-start | bytes 6152 | tf_op jit(solution)/shard_map/ppermute | solution.py:272
  65.1 3.0 %collective-permute-start.7 = (f32[2,256]{1,0:T(2,128)S(1)}, f32[2,256]{1,0:T(2,128)S(1)}, u32[]{:S(2)}, u32[]{:S(2)}) collective-permute-start(f32[2,256]{1,0:T(2,128)S(1)} %shard_map.73.a), channel_id=1, source_target_pairs={{0,3},{4,196},{1,0},{5,197},{2,1},{6,198},{3,2},{7,199},{8,11},{12... | collective-permute-start | bytes 6152 | tf_op jit(solution)/shard_map/ppermute | solution.py:272
  68.1 4.2 %collective-permute-start.10 = (f32[2,256]{1,0:T(2,128)S(1)}, f32[2,256]{1,0:T(2,128)S(1)}, u32[]{:S(2)}, u32[]{:S(2)}) collective-permute-start(f32[2,256]{1,0:T(2,128)S(1)} %shard_map.74.mine), channel_id=1, source_target_pairs={{0,4},{4,0},{1,5},{5,1},{2,6},{6,2},{3,7},{7,3},{8,12},{12,8},{9,1... | collective-permute-start | bytes 6152 | tf_op jit(solution)/shard_map/ppermute | solution.py:254
  72.8 2.4 %collective-permute-start.14 = (bf16[256,512]{1,0:T(8,128)(2,1)S(1)}, bf16[256,512]{1,0:T(8,128)(2,1)S(1)}, u32[]{:S(2)}, u32[]{:S(2)}) collective-permute-start(bf16[256,512]{1,0:T(8,128)(2,1)S(1)} %get-tuple-element.59), channel_id=1, source_target_pairs={{0,4},{4,0},{1,5},{5,1},{2,6},{6,2},{3,7},{7,3},{8,12},{12,8},{9,1... | collective-permute-start | bytes 786440 | tf_op jit(solution)/shard_map/ppermute | solution.py:254
  73.9 2.6 %collective-permute-start.11 = (bf16[256,512]{1,0:T(8,128)(2,1)S(1)}, bf16[256,512]{1,0:T(8,128)(2,1)S(1)}, u32[]{:S(2)}, u32[]{:S(2)}) collective-permute-start(bf16[256,512]{1,0:T(8,128)(2,1)S(1)} %get-tuple-element.52), channel_id=1, source_target_pairs={{0,4},{4,0},{1,5},{5,1},{2,6},{6,2},{3,7},{7,3},{8,12},{12,8},{9,1... | collective-permute-start | bytes 786440 | tf_op jit(solution)/shard_map/ppermute | solution.py:254
  74.7 4.9 %collective-permute-start.16 = (bf16[256,512]{1,0:T(8,128)(2,1)S(1)}, bf16[256,512]{1,0:T(8,128)(2,1)S(1)}, u32[]{:S(2)}, u32[]{:S(2)}) collective-permute-start(bf16[256,512]{1,0:T(8,128)(2,1)S(1)} %get-tuple-element.61), channel_id=1, source_target_pairs={{0,4},{4,0},{1,5},{5,1},{2,6},{6,2},{3,7},{7,3},{8,12},{12,8},{9,1... | collective-permute-start | bytes 786440 | tf_op jit(solution)/shard_map/ppermute | solution.py:254
  75.2 10.0 %collective-permute-start.15 = (bf16[256,512]{1,0:T(8,128)(2,1)S(1)}, bf16[256,512]{1,0:T(8,128)(2,1)S(1)}, u32[]{:S(2)}, u32[]{:S(2)}) collective-permute-start(bf16[256,512]{1,0:T(8,128)(2,1)S(1)} %add_convert_fusion.1), channel_id=1, source_target_pairs={{0,128},{4,6},{1,129},{5,7},{2,130},{6,4},{3,131},{7,5},{8,136},{1... | collective-permute-start | bytes 786440 | tf_op jit(solution)/shard_map/ppermute | solution.py:272
  76.6 8.6 %collective-permute-start.13 = (bf16[256,512]{1,0:T(8,128)(2,1)S(1)}, bf16[256,512]{1,0:T(8,128)(2,1)S(1)}, u32[]{:S(2)}, u32[]{:S(2)}) collective-permute-start(bf16[256,512]{1,0:T(8,128)(2,1)S(1)} %add_convert_fusion.3), channel_id=1, source_target_pairs={{0,64},{4,5},{1,65},{5,6},{2,66},{6,7},{3,67},{7,4},{8,72},{12,13}... | collective-permute-start | bytes 786440 | tf_op jit(solution)/shard_map/ppermute | solution.py:272
  79.5 5.7 %collective-permute-start.12 = (bf16[256,512]{1,0:T(8,128)(2,1)S(1)}, bf16[256,512]{1,0:T(8,128)(2,1)S(1)}, u32[]{:S(2)}, u32[]{:S(2)}) collective-permute-start(bf16[256,512]{1,0:T(8,128)(2,1)S(1)} %get-tuple-element.55), channel_id=1, source_target_pairs={{0,4},{4,0},{1,5},{5,1},{2,6},{6,2},{3,7},{7,3},{8,12},{12,8},{9,1... | collective-permute-start | bytes 786440 | tf_op jit(solution)/shard_map/ppermute | solution.py:254
  79.7 6.0 %collective-permute-start.17 = (bf16[256,512]{1,0:T(8,128)(2,1)S(1)}, bf16[256,512]{1,0:T(8,128)(2,1)S(1)}, u32[]{:S(2)}, u32[]{:S(2)}) collective-permute-start(bf16[256,512]{1,0:T(8,128)(2,1)S(1)} %add_convert_fusion), channel_id=1, source_target_pairs={{0,192},{4,7},{1,193},{5,4},{2,194},{6,5},{3,195},{7,6},{8,200},{1... | collective-permute-start | bytes 786440 | tf_op jit(solution)/shard_map/ppermute | solution.py:272
  86.2 5.7 %collective-permute-start.18 = (bf16[256,256]{1,0:T(8,128)(2,1)S(1)}, bf16[256,256]{1,0:T(8,128)(2,1)S(1)}, u32[]{:S(2)}, u32[]{:S(2)}) collective-permute-start(bf16[256,256]{1,0:T(8,128)(2,1)S(1)} %get-tuple-element.64), channel_id=1, source_target_pairs={{0,2},{4,132},{1,3},{5,133},{2,0},{6,134},{3,1},{7,135},{8,10},{12... | collective-permute-start | bytes 393224 | tf_op jit(solution)/shard_map/ppermute | solution.py:272
  87.6 5.7 %collective-permute-start.19 = (bf16[256,256]{1,0:T(8,128)(2,1)S(1)}, bf16[256,256]{1,0:T(8,128)(2,1)S(1)}, u32[]{:S(2)}, u32[]{:S(2)}) collective-permute-start(bf16[256,256]{1,0:T(8,128)(2,1)S(1)} %get-tuple-element.65), channel_id=1, source_target_pairs={{0,1},{4,68},{1,2},{5,69},{2,3},{6,70},{3,0},{7,71},{8,9},{12,76},... | collective-permute-start | bytes 393224 | tf_op jit(solution)/shard_map/ppermute | solution.py:272
  87.7 5.6 %collective-permute-start.20 = (bf16[256,256]{1,0:T(8,128)(2,1)S(1)}, bf16[256,256]{1,0:T(8,128)(2,1)S(1)}, u32[]{:S(2)}, u32[]{:S(2)}) collective-permute-start(bf16[256,256]{1,0:T(8,128)(2,1)S(1)} %get-tuple-element.66), channel_id=1, source_target_pairs={{0,3},{4,196},{1,0},{5,197},{2,1},{6,198},{3,2},{7,199},{8,11},{12... | collective-permute-start | bytes 393224 | tf_op jit(solution)/shard_map/ppermute | solution.py:272
  107.8 3.6 %collective-permute-start.21 = (f32[4,4,256]{2,1,0:T(4,128)S(1)}, f32[4,4,256]{2,1,0:T(4,128)S(1)}, u32[]{:S(2)}, u32[]{:S(2)}) collective-permute-start(f32[4,4,256]{2,1,0:T(4,128)S(1)} %get-tuple-element.68), channel_id=1, source_target_pairs={{0,4},{4,0},{1,5},{5,1},{2,6},{6,2},{3,7},{7,3},{8,12},{12,8},{9,1... | collective-permute-start | bytes 49160 | tf_op jit(solution)/shard_map/ppermute | solution.py:254

commit v12 on v11

--- a/solution.py
+++ b/solution.py
@@ -15,7 +15,7 @@
 ALL = ("x", "z", "core", "y")
 NX, NZ, NCORE, NY = 4, 8, 2, 4
 RING = 4
-ZS = tuple(reversed(range(NZ)))
+ZS = tuple((z + NZ // 2) % NZ for z in range(NZ))
 FIRST = ((0, 0), (0, 1), (0, 2), (0, 3), (1, 0), (1, 2))
 LAST = ((1, 3), (1, 1))
 Y_CORE = 1
@@ -125,7 +125,7 @@
     halves, sent, masked = back.shape
     slots = chosen.shape[1]
     row = lax.broadcasted_iota(jnp.int32, (sent, slots), 0)
-    second, z, first, q = row // 256, NZ - 1 - row // 32 % NZ, row // 8 % RING, row % 8
+    second, z, first, q = row // 256, (row // 32 + NZ // 2) % NZ, row // 8 % RING, row % 8
     straight = lax.axis_index("core") == Y_CORE
     x, y = jnp.where(straight, second, first), jnp.where(straight, first, second)
     slot = (x * NZ + z) * 16 + q // 4 * 8 + y * 2 + q // 2 % 2

time: 112 us -> 111 us (level)
    all_to_all x1, blocking collectives: 15.2 us -> 14 us  [per_device(): lax.all_to_all(stats, ALL, 0, 0, tiled=True, axis_index_groups=peers())]
where the time goes in v12:
time: 111 us
  blocking collectives  59.5 us (54%)
  starting transfers between devices  27.9 us (25%)
  Pallas kernels  10.9 us (10%)
  waiting for transfers between devices  8.86 us (8%)
  between operations  1.62 us (1%)
  other arithmetic  1.19 us (1%)
    all_to_all x1, blocking collectives, per_device(): rows = lax.all_to_all(send, SEQ, 0, 0, tiled=True).reshape(slots, part)  30.1 us
    ppermute x12, starting transfers between devices, shift(): return lax.ppermute(v, ALL, moves)  19.2 us
    all_to_all x1, blocking collectives, per_device(): lax.all_to_all(partial.reshape(NZ * RING, 8, part // 2), ALL, 0, 0, tiled...  15.4 us
    all_to_all x1, blocking collectives, per_device(): lax.all_to_all(stats, ALL, 0, 0, tiled=True, axis_index_groups=peers())  14 us
    pallas_call x15, Pallas kernels, call(): pl.pallas_call(body, out_shape=out, in_specs=specs or [VMEM] * len(args),...  10.9 us
    ppermute x10, starting transfers between devices, swap_core(): return lax.ppermute(x, 'core', [(0, 1), (1, 0)])  8.71 us
    ppermute x12, waiting for transfers between devices, shift(): return lax.ppermute(v, ALL, moves)  6.68 us
  transfers between devices with their start and end apart: 22, of which 10 were waited for; matrix products, arithmetic and copies ran while one was open for 0% of the time, Pallas kernels for 6%

profile of v12, /device:TPU:1, one launch (start us, length us, event | category | flops | bytes accessed | tf_op | source)
XLA Modules:
  0.0 111.0 jit_solution(15762153590555953863)
XLA Ops:
  1.4 0.8 broadcast_add_fusion.numbers
  2.3 1.2 %shard_map.68 = bf16[64,8,512]{2,1,0:T(8,128)(2,1)S(1)} custom-call(s32[1,8]{1,0:T(1,128)S(1)} %broadcast_add_fusion.numbers, bf16[64,4096]{1,0:T(8,128)(2,1)} %hidden.1), custom_call_target="tpu_custom_call" | custom-call | bytes 1048608 | tf_op jit(solution)/shard_map/pallas_call | solution.py:35
  3.5 30.1 %all_to_all.15 = bf16[64,8,512]{2,1,0:T(8,128)(2,1)S(1)} all-to-all(bf16[64,8,512]{2,1,0:T(8,128)(2,1)S(1)} %shard_map.68), channel_id=1, replica_groups=mesh['x'=4,'z'=8,'core'=2,'y'=4] {'x','z','core'}, dimensions={0} | all-to-all | bytes 1048576 | tf_op jit(solution)/shard_map/all_to_all | solution.py:301
  34.1 3.0 %collective-permute-start.4 = (bf16[256,512]{1,0:T(8,128)(2,1)S(1)}, bf16[256,512]{1,0:T(8,128)(2,1)S(1)}, u32[]{:S(2)}, u32[]{:S(2)}) collective-permute-start(bf16[256,512]{1,0:T(8,128)(2,1)S(1)} %get-tuple-element.36.refs_0_), channel_id=1, source_target_pairs={{0,128},{4,6},{1,129},{5,7},{2,130},{6,4},{3,131},{7,5},{8,136},{1... | collective-permute-start | bytes 786440 | tf_op jit(solution)/shard_map/ppermute | solution.py:272
  37.5 2.3 %collective-permute-start = (bf16[256,512]{1,0:T(8,128)(2,1)S(1)}, bf16[256,512]{1,0:T(8,128)(2,1)S(1)}, u32[]{:S(2)}, u32[]{:S(2)}) collective-permute-start(bf16[256,512]{1,0:T(8,128)(2,1)S(1)} %get-tuple-element.36.refs_0_), channel_id=1, source_target_pairs={{0,192},{4,7},{1,193},{5,4},{2,194},{6,5},{3,195},{7,6},{8,200},{1... | collective-permute-start | bytes 786440 | tf_op jit(solution)/shard_map/ppermute | solution.py:272
  39.8 0.7 collective-permute-start.5
  40.5 1.0 copy-done.1
  41.5 2.1 %shard_map.70 = (bf16[494,256]{1,0:T(8,128)(2,1)S(1)}, f32[8,256]{1,0:T(8,128)S(1)}, bf16[2,1024,256]{2,1,0:T(8,128)(2,1)S(1)}) custom-call(bf16[494,512]{1,0:T(8,128)(2,1)S(1)} %bitcast.14, bf16[256,512]{1,0:T(8,128)(2,1)S(1)} %get-tuple-element.37.chosen), custom_call_target="tpu_custom_call" | custom-call | flops 397934592 | bytes 2077696 | tf_op jit(solution)/shard_map/pallas_call | solution.py:35
  44.0 1.2 %collective-permute-start.3 = (bf16[256,512]{1,0:T(8,128)(2,1)S(1)}, bf16[256,512]{1,0:T(8,128)(2,1)S(1)}, u32[]{:S(2)}, u32[]{:S(2)}) collective-permute-start(bf16[256,512]{1,0:T(8,128)(2,1)S(1)} %collective-permute-done.2.refs_1_), channel_id=1, source_target_pairs={{0,4},{4,0},{1,5},{5,1},{2,6},{6,2},{3,7},{7,3},{8,12},{12,8},{9,1... | collective-permute-start | bytes 786440 | tf_op jit(solution)/shard_map/ppermute | solution.py:254
  45.3 1.0 shard_map.71.refs_3_
  46.8 0.6 shard_map.72
  47.4 14.0 %all_to_all.16.stats = f32[32,2,256]{2,1,0:T(2,128)S(1)} all-to-all(f32[32,2,256]{2,1,0:T(2,128)S(1)} %get-tuple-element.47), channel_id=1, replica_groups={{36,37,38,39,44,45,46,47,52,53,54,55,60,61,62,63,4,5,6,7,12,13,14,15,20..., dimensions={0} | all-to-all | bytes 131072 | tf_op jit(solution)/shard_map/all_to_all | solution.py:331
  61.4 1.5 %collective-permute-start.9 = (f32[2,256]{1,0:T(2,128)S(1)}, f32[2,256]{1,0:T(2,128)S(1)}, u32[]{:S(2)}, u32[]{:S(2)}) collective-permute-start(f32[2,256]{1,0:T(2,128)S(1)} %shard_map.73.a), channel_id=1, source_target_pairs={{0,2},{4,132},{1,3},{5,133},{2,0},{6,134},{3,1},{7,135},{8,10},{12... | collective-permute-start | bytes 6152 | tf_op jit(solution)/shard_map/ppermute | solution.py:272
  63.0 1.0 collective-permute-start.8
  63.9 1.7 %collective-permute-start.7 = (f32[2,256]{1,0:T(2,128)S(1)}, f32[2,256]{1,0:T(2,128)S(1)}, u32[]{:S(2)}, u32[]{:S(2)}) collective-permute-start(f32[2,256]{1,0:T(2,128)S(1)} %shard_map.73.a), channel_id=1, source_target_pairs={{0,3},{4,196},{1,0},{5,197},{2,1},{6,198},{3,2},{7,199},{8,11},{12... | collective-permute-start | bytes 6152 | tf_op jit(solution)/shard_map/ppermute | solution.py:272
  65.6 1.3 %collective-permute-done.8.c = f32[2,256]{1,0:T(2,128)S(1)} collective-permute-done((f32[2,256]{1,0:T(2,128)S(1)}, f32[2,256]{1,0:T(2,128)S(1)}, u32[]{:S(2)}, u32[]{:S(2)}) %collective-permute-start.8) | collective-permute-done | bytes 2080 | tf_op jit(solution)/shard_map/ppermute | solution.py:272
  66.9 3.6 %collective-permute-start.10 = (f32[2,256]{1,0:T(2,128)S(1)}, f32[2,256]{1,0:T(2,128)S(1)}, u32[]{:S(2)}, u32[]{:S(2)}) collective-permute-start(f32[2,256]{1,0:T(2,128)S(1)} %shard_map.74.mine), channel_id=1, source_target_pairs={{0,4},{4,0},{1,5},{5,1},{2,6},{6,2},{3,7},{7,3},{8,12},{12,8},{9,1... | collective-permute-start | bytes 6152 | tf_op jit(solution)/shard_map/ppermute | solution.py:254
  70.5 0.8 collective-permute-done.10.other
  72.9 0.6 shard_map.76
  74.1 1.3 %collective-permute-start.15 = (bf16[256,512]{1,0:T(8,128)(2,1)S(1)}, bf16[256,512]{1,0:T(8,128)(2,1)S(1)}, u32[]{:S(2)}, u32[]{:S(2)}) collective-permute-start(bf16[256,512]{1,0:T(8,128)(2,1)S(1)} %add_convert_fusion.1), channel_id=1, source_target_pairs={{0,128},{4,6},{1,129},{5,7},{2,130},{6,4},{3,131},{7,5},{8,136},{1... | collective-permute-start | bytes 786440 | tf_op jit(solution)/shard_map/ppermute | solution.py:272
  75.4 2.4 %collective-permute-start.13 = (bf16[256,512]{1,0:T(8,128)(2,1)S(1)}, bf16[256,512]{1,0:T(8,128)(2,1)S(1)}, u32[]{:S(2)}, u32[]{:S(2)}) collective-permute-start(bf16[256,512]{1,0:T(8,128)(2,1)S(1)} %add_convert_fusion.3), channel_id=1, source_target_pairs={{0,64},{4,5},{1,65},{5,6},{2,66},{6,7},{3,67},{7,4},{8,72},{12,13}... | collective-permute-start | bytes 786440 | tf_op jit(solution)/shard_map/ppermute | solution.py:272
  78.5 1.6 %collective-permute-start.17 = (bf16[256,512]{1,0:T(8,128)(2,1)S(1)}, bf16[256,512]{1,0:T(8,128)(2,1)S(1)}, u32[]{:S(2)}, u32[]{:S(2)}) collective-permute-start(bf16[256,512]{1,0:T(8,128)(2,1)S(1)} %add_convert_fusion), channel_id=1, source_target_pairs={{0,192},{4,7},{1,193},{5,4},{2,194},{6,5},{3,195},{7,6},{8,200},{1... | collective-permute-start | bytes 786440 | tf_op jit(solution)/shard_map/ppermute | solution.py:272
  80.1 2.3 %shard_map.79 = bf16[494,4096]{1,0:T(8,128)(2,1)} custom-call(bf16[256,512]{1,0:T(8,128)(2,1)S(1)} %get-tuple-element.36.refs_0_, bf16[256,512]{1,0:T(8,128)(2,1)S(1)} %collective-permute-done.2.refs_1_, bf16[256,512]{1,0:T(8,128)(2,1)S(1)} %collective-permute-done.4.refs_2_, bf16[256,512]{1,0:T(8,128)(2,1)S(1)} %collective-permute-done.refs_3_, ...), custom_call_target="tpu_custom_call" | custom-call | flops 1035993088 | bytes 6396928 | tf_op jit(solution)/shard_map/pallas_call | solution.py:35
  82.4 1.6 %collective-permute-done.13.b = bf16[256,512]{1,0:T(8,128)(2,1)S(1)} collective-permute-done((bf16[256,512]{1,0:T(8,128)(2,1)S(1)}, bf16[256,512]{1,0:T(8,128)(2,1)S(1)}, u32[]{:S(2)}, u32[]{:S(2)}) %collective-permute-start.13) | collective-permute-done | bytes 262176 | tf_op jit(solution)/shard_map/ppermute | solution.py:272
  85.0 1.4 %collective-permute-start.18 = (bf16[256,256]{1,0:T(8,128)(2,1)S(1)}, bf16[256,256]{1,0:T(8,128)(2,1)S(1)}, u32[]{:S(2)}, u32[]{:S(2)}) collective-permute-start(bf16[256,256]{1,0:T(8,128)(2,1)S(1)} %get-tuple-element.64), channel_id=1, source_target_pairs={{0,2},{4,132},{1,3},{5,133},{2,0},{6,134},{3,1},{7,135},{8,10},{12... | collective-permute-start | bytes 393224 | tf_op jit(solution)/shard_map/ppermute | solution.py:272
  86.8 2.3 %collective-permute-start.20 = (bf16[256,256]{1,0:T(8,128)(2,1)S(1)}, bf16[256,256]{1,0:T(8,128)(2,1)S(1)}, u32[]{:S(2)}, u32[]{:S(2)}) collective-permute-start(bf16[256,256]{1,0:T(8,128)(2,1)S(1)} %get-tuple-element.66), channel_id=1, source_target_pairs={{0,3},{4,196},{1,0},{5,197},{2,1},{6,198},{3,2},{7,199},{8,11},{12... | collective-permute-start | bytes 393224 | tf_op jit(solution)/shard_map/ppermute | solution.py:272
  89.1 1.6 %collective-permute-done.18 = bf16[256,256]{1,0:T(8,128)(2,1)S(1)} collective-permute-done((bf16[256,256]{1,0:T(8,128)(2,1)S(1)}, bf16[256,256]{1,0:T(8,128)(2,1)S(1)}, u32[]{:S(2)}, u32[]{:S(2)}) %collective-permute-start.18) | collective-permute-done | bytes 131104 | tf_op jit(solution)/shard_map/ppermute | solution.py:272
  90.7 1.4 %collective-permute-done.19 = bf16[256,256]{1,0:T(8,128)(2,1)S(1)} collective-permute-done((bf16[256,256]{1,0:T(8,128)(2,1)S(1)}, bf16[256,256]{1,0:T(8,128)(2,1)S(1)}, u32[]{:S(2)}, u32[]{:S(2)}) %collective-permute-start.19) | collective-permute-done | bytes 131104 | tf_op jit(solution)/shard_map/ppermute | solution.py:272
  92.2 15.4 %all_to_all.17.parts = bf16[32,8,256]{2,1,0:T(8,128)(2,1)S(1)} all-to-all(bf16[32,8,256]{2,1,0:T(8,128)(2,1)S(1)} %fusion), channel_id=1, replica_groups={{36,37,38,39,44,45,46,47,52,53,54,55,60,61,62,63,4,5,6,7,12,13,14,15,20..., dimensions={0} | all-to-all | bytes 262144 | tf_op jit(solution)/shard_map/all_to_all | solution.py:374
  107.6 2.0 %collective-permute-start.21 = (f32[4,4,256]{2,1,0:T(4,128)S(1)}, f32[4,4,256]{2,1,0:T(4,128)S(1)}, u32[]{:S(2)}, u32[]{:S(2)}) collective-permute-start(f32[4,4,256]{2,1,0:T(4,128)S(1)} %get-tuple-element.68), channel_id=1, source_target_pairs={{0,4},{4,0},{1,5},{5,1},{2,6},{6,2},{3,7},{7,3},{8,12},{12,8},{9,1... | collective-permute-start | bytes 49160 | tf_op jit(solution)/shard_map/ppermute | solution.py:254
  109.6 0.8 collective-permute-done.21.other
  110.4 0.6 shard_map.82
  (40 shorter events, 6.2 us)
Async XLA Ops:
  0.6 44.6 %copy-start = (bf16[4096,494]{0,1:T(8,128)(2,1)S(1)}, bf16[4096,494]{0,1:T(8,128)(2,1)}, u32[]{:S(2)}) copy-start(bf16[4096,494]{0,1:T(8,128)(2,1)} %param.6) | copy-start | bytes 12140548
  34.1 9.5 %collective-permute-start.4 = (bf16[256,512]{1,0:T(8,128)(2,1)S(1)}, bf16[256,512]{1,0:T(8,128)(2,1)S(1)}, u32[]{:S(2)}, u32[]{:S(2)}) collective-permute-start(bf16[256,512]{1,0:T(8,128)(2,1)S(1)} %get-tuple-element.36.refs_0_), channel_id=1, source_target_pairs={{0,128},{4,6},{1,129},{5,7},{2,130},{6,4},{3,131},{7,5},{8,136},{1... | collective-permute-start | bytes 786440 | tf_op jit(solution)/shard_map/ppermute | solution.py:272
  37.1 6.9 %collective-permute-start.2 = (bf16[256,512]{1,0:T(8,128)(2,1)S(1)}, bf16[256,512]{1,0:T(8,128)(2,1)S(1)}, u32[]{:S(2)}, u32[]{:S(2)}) collective-permute-start(bf16[256,512]{1,0:T(8,128)(2,1)S(1)} %get-tuple-element.36.refs_0_), channel_id=1, source_target_pairs={{0,64},{4,5},{1,65},{5,6},{2,66},{6,7},{3,67},{7,4},{8,72},{12,13}... | collective-permute-start | bytes 786440 | tf_op jit(solution)/shard_map/ppermute | solution.py:272
  37.5 7.7 %collective-permute-start = (bf16[256,512]{1,0:T(8,128)(2,1)S(1)}, bf16[256,512]{1,0:T(8,128)(2,1)S(1)}, u32[]{:S(2)}, u32[]{:S(2)}) collective-permute-start(bf16[256,512]{1,0:T(8,128)(2,1)S(1)} %get-tuple-element.36.refs_0_), channel_id=1, source_target_pairs={{0,192},{4,7},{1,193},{5,4},{2,194},{6,5},{3,195},{7,6},{8,200},{1... | collective-permute-start | bytes 786440 | tf_op jit(solution)/shard_map/ppermute | solution.py:272
  39.8 5.4 %collective-permute-start.5 = (bf16[256,512]{1,0:T(8,128)(2,1)S(1)}, bf16[256,512]{1,0:T(8,128)(2,1)S(1)}, u32[]{:S(2)}, u32[]{:S(2)}) collective-permute-start(bf16[256,512]{1,0:T(8,128)(2,1)S(1)} %get-tuple-element.36.refs_0_), channel_id=1, source_target_pairs={{0,4},{4,0},{1,5},{5,1},{2,6},{6,2},{3,7},{7,3},{8,12},{12,8},{9,1... | collective-permute-start | bytes 786440 | tf_op jit(solution)/shard_map/ppermute | solution.py:254
  40.5 1.0 copy-start.1
  43.6 1.6 %collective-permute-start.6 = (bf16[256,512]{1,0:T(8,128)(2,1)S(1)}, bf16[256,512]{1,0:T(8,128)(2,1)S(1)}, u32[]{:S(2)}, u32[]{:S(2)}) collective-permute-start(bf16[256,512]{1,0:T(8,128)(2,1)S(1)} %collective-permute-done.4.refs_2_), channel_id=1, source_target_pairs={{0,4},{4,0},{1,5},{5,1},{2,6},{6,2},{3,7},{7,3},{8,12},{12,8},{9,1... | collective-permute-start | bytes 786440 | tf_op jit(solution)/shard_map/ppermute | solution.py:254
  44.0 2.3 %collective-permute-start.3 = (bf16[256,512]{1,0:T(8,128)(2,1)S(1)}, bf16[256,512]{1,0:T(8,128)(2,1)S(1)}, u32[]{:S(2)}, u32[]{:S(2)}) collective-permute-start(bf16[256,512]{1,0:T(8,128)(2,1)S(1)} %collective-permute-done.2.refs_1_), channel_id=1, source_target_pairs={{0,4},{4,0},{1,5},{5,1},{2,6},{6,2},{3,7},{7,3},{8,12},{12,8},{9,1... | collective-permute-start | bytes 786440 | tf_op jit(solution)/shard_map/ppermute | solution.py:254
  45.2 1.5 %collective-permute-start.1 = (bf16[256,512]{1,0:T(8,128)(2,1)S(1)}, bf16[256,512]{1,0:T(8,128)(2,1)S(1)}, u32[]{:S(2)}, u32[]{:S(2)}) collective-permute-start(bf16[256,512]{1,0:T(8,128)(2,1)S(1)} %collective-permute-done.refs_3_), channel_id=1, source_target_pairs={{0,4},{4,0},{1,5},{5,1},{2,6},{6,2},{3,7},{7,3},{8,12},{12,8},{9,1... | collective-permute-start | bytes 786440 | tf_op jit(solution)/shard_map/ppermute | solution.py:254
  61.4 4.2 %collective-permute-start.9 = (f32[2,256]{1,0:T(2,128)S(1)}, f32[2,256]{1,0:T(2,128)S(1)}, u32[]{:S(2)}, u32[]{:S(2)}) collective-permute-start(f32[2,256]{1,0:T(2,128)S(1)} %shard_map.73.a), channel_id=1, source_target_pairs={{0,2},{4,132},{1,3},{5,133},{2,0},{6,134},{3,1},{7,135},{8,10},{12... | collective-permute-start | bytes 6152 | tf_op jit(solution)/shard_map/ppermute | solution.py:272
  63.0 3.9 %collective-permute-start.8 = (f32[2,256]{1,0:T(2,128)S(1)}, f32[2,256]{1,0:T(2,128)S(1)}, u32[]{:S(2)}, u32[]{:S(2)}) collective-permute-start(f32[2,256]{1,0:T(2,128)S(1)} %shard_map.73.a), channel_id=1, source_target_pairs={{0,1},{4,68},{1,2},{5,69},{2,3},{6,70},{3,0},{7,71},{8,9},{12,76},... | collective-permute-start | bytes 6152 | tf_op jit(solution)/shard_map/ppermute | solution.py:272
  63.9 3.0 %collective-permute-start.7 = (f32[2,256]{1,0:T(2,128)S(1)}, f32[2,256]{1,0:T(2,128)S(1)}, u32[]{:S(2)}, u32[]{:S(2)}) collective-permute-start(f32[2,256]{1,0:T(2,128)S(1)} %shard_map.73.a), channel_id=1, source_target_pairs={{0,3},{4,196},{1,0},{5,197},{2,1},{6,198},{3,2},{7,199},{8,11},{12... | collective-permute-start | bytes 6152 | tf_op jit(solution)/shard_map/ppermute | solution.py:272
  66.9 4.4 %collective-permute-start.10 = (f32[2,256]{1,0:T(2,128)S(1)}, f32[2,256]{1,0:T(2,128)S(1)}, u32[]{:S(2)}, u32[]{:S(2)}) collective-permute-start(f32[2,256]{1,0:T(2,128)S(1)} %shard_map.74.mine), channel_id=1, source_target_pairs={{0,4},{4,0},{1,5},{5,1},{2,6},{6,2},{3,7},{7,3},{8,12},{12,8},{9,1... | collective-permute-start | bytes 6152 | tf_op jit(solution)/shard_map/ppermute | solution.py:254
  71.8 2.2 %collective-permute-start.14 = (bf16[256,512]{1,0:T(8,128)(2,1)S(1)}, bf16[256,512]{1,0:T(8,128)(2,1)S(1)}, u32[]{:S(2)}, u32[]{:S(2)}) collective-permute-start(bf16[256,512]{1,0:T(8,128)(2,1)S(1)} %get-tuple-element.59), channel_id=1, source_target_pairs={{0,4},{4,0},{1,5},{5,1},{2,6},{6,2},{3,7},{7,3},{8,12},{12,8},{9,1... | collective-permute-start | bytes 786440 | tf_op jit(solution)/shard_map/ppermute | solution.py:254
  72.7 2.6 %collective-permute-start.11 = (bf16[256,512]{1,0:T(8,128)(2,1)S(1)}, bf16[256,512]{1,0:T(8,128)(2,1)S(1)}, u32[]{:S(2)}, u32[]{:S(2)}) collective-permute-start(bf16[256,512]{1,0:T(8,128)(2,1)S(1)} %get-tuple-element.52), channel_id=1, source_target_pairs={{0,4},{4,0},{1,5},{5,1},{2,6},{6,2},{3,7},{7,3},{8,12},{12,8},{9,1... | collective-permute-start | bytes 786440 | tf_op jit(solution)/shard_map/ppermute | solution.py:254
  73.5 4.9 %collective-permute-start.16 = (bf16[256,512]{1,0:T(8,128)(2,1)S(1)}, bf16[256,512]{1,0:T(8,128)(2,1)S(1)}, u32[]{:S(2)}, u32[]{:S(2)}) collective-permute-start(bf16[256,512]{1,0:T(8,128)(2,1)S(1)} %get-tuple-element.61), channel_id=1, source_target_pairs={{0,4},{4,0},{1,5},{5,1},{2,6},{6,2},{3,7},{7,3},{8,12},{12,8},{9,1... | collective-permute-start | bytes 786440 | tf_op jit(solution)/shard_map/ppermute | solution.py:254
  74.1 10.0 %collective-permute-start.15 = (bf16[256,512]{1,0:T(8,128)(2,1)S(1)}, bf16[256,512]{1,0:T(8,128)(2,1)S(1)}, u32[]{:S(2)}, u32[]{:S(2)}) collective-permute-start(bf16[256,512]{1,0:T(8,128)(2,1)S(1)} %add_convert_fusion.1), channel_id=1, source_target_pairs={{0,128},{4,6},{1,129},{5,7},{2,130},{6,4},{3,131},{7,5},{8,136},{1... | collective-permute-start | bytes 786440 | tf_op jit(solution)/shard_map/ppermute | solution.py:272
  75.4 8.6 %collective-permute-start.13 = (bf16[256,512]{1,0:T(8,128)(2,1)S(1)}, bf16[256,512]{1,0:T(8,128)(2,1)S(1)}, u32[]{:S(2)}, u32[]{:S(2)}) collective-permute-start(bf16[256,512]{1,0:T(8,128)(2,1)S(1)} %add_convert_fusion.3), channel_id=1, source_target_pairs={{0,64},{4,5},{1,65},{5,6},{2,66},{6,7},{3,67},{7,4},{8,72},{12,13}... | collective-permute-start | bytes 786440 | tf_op jit(solution)/shard_map/ppermute | solution.py:272
  78.3 5.7 %collective-permute-start.12 = (bf16[256,512]{1,0:T(8,128)(2,1)S(1)}, bf16[256,512]{1,0:T(8,128)(2,1)S(1)}, u32[]{:S(2)}, u32[]{:S(2)}) collective-permute-start(bf16[256,512]{1,0:T(8,128)(2,1)S(1)} %get-tuple-element.55), channel_id=1, source_target_pairs={{0,4},{4,0},{1,5},{5,1},{2,6},{6,2},{3,7},{7,3},{8,12},{12,8},{9,1... | collective-permute-start | bytes 786440 | tf_op jit(solution)/shard_map/ppermute | solution.py:254
  78.5 6.0 %collective-permute-start.17 = (bf16[256,512]{1,0:T(8,128)(2,1)S(1)}, bf16[256,512]{1,0:T(8,128)(2,1)S(1)}, u32[]{:S(2)}, u32[]{:S(2)}) collective-permute-start(bf16[256,512]{1,0:T(8,128)(2,1)S(1)} %add_convert_fusion), channel_id=1, source_target_pairs={{0,192},{4,7},{1,193},{5,4},{2,194},{6,5},{3,195},{7,6},{8,200},{1... | collective-permute-start | bytes 786440 | tf_op jit(solution)/shard_map/ppermute | solution.py:272
  85.0 5.7 %collective-permute-start.18 = (bf16[256,256]{1,0:T(8,128)(2,1)S(1)}, bf16[256,256]{1,0:T(8,128)(2,1)S(1)}, u32[]{:S(2)}, u32[]{:S(2)}) collective-permute-start(bf16[256,256]{1,0:T(8,128)(2,1)S(1)} %get-tuple-element.64), channel_id=1, source_target_pairs={{0,2},{4,132},{1,3},{5,133},{2,0},{6,134},{3,1},{7,135},{8,10},{12... | collective-permute-start | bytes 393224 | tf_op jit(solution)/shard_map/ppermute | solution.py:272
  86.4 5.7 %collective-permute-start.19 = (bf16[256,256]{1,0:T(8,128)(2,1)S(1)}, bf16[256,256]{1,0:T(8,128)(2,1)S(1)}, u32[]{:S(2)}, u32[]{:S(2)}) collective-permute-start(bf16[256,256]{1,0:T(8,128)(2,1)S(1)} %get-tuple-element.65), channel_id=1, source_target_pairs={{0,1},{4,68},{1,2},{5,69},{2,3},{6,70},{3,0},{7,71},{8,9},{12,76},... | collective-permute-start | bytes 393224 | tf_op jit(solution)/shard_map/ppermute | solution.py:272
  86.8 5.4 %collective-permute-start.20 = (bf16[256,256]{1,0:T(8,128)(2,1)S(1)}, bf16[256,256]{1,0:T(8,128)(2,1)S(1)}, u32[]{:S(2)}, u32[]{:S(2)}) collective-permute-start(bf16[256,256]{1,0:T(8,128)(2,1)S(1)} %get-tuple-element.66), channel_id=1, source_target_pairs={{0,3},{4,196},{1,0},{5,197},{2,1},{6,198},{3,2},{7,199},{8,11},{12... | collective-permute-start | bytes 393224 | tf_op jit(solution)/shard_map/ppermute | solution.py:272
  107.6 2.8 %collective-permute-start.21 = (f32[4,4,256]{2,1,0:T(4,128)S(1)}, f32[4,4,256]{2,1,0:T(4,128)S(1)}, u32[]{:S(2)}, u32[]{:S(2)}) collective-permute-start(f32[4,4,256]{2,1,0:T(4,128)S(1)} %get-tuple-element.68), channel_id=1, source_target_pairs={{0,4},{4,0},{1,5},{5,1},{2,6},{6,2},{3,7},{7,3},{8,12},{12,8},{9,1... | collective-permute-start | bytes 49160 | tf_op jit(solution)/shard_map/ppermute | solution.py:254

commit v13 on v12

--- a/solution.py
+++ b/solution.py
@@ -16,6 +16,7 @@
 NX, NZ, NCORE, NY = 4, 8, 2, 4
 RING = 4
 ZS = tuple((z + NZ // 2) % NZ for z in range(NZ))
+PLACES = tuple((place + 1) % RING for place in range(RING))
 FIRST = ((0, 0), (0, 1), (0, 2), (0, 3), (1, 0), (1, 2))
 LAST = ((1, 3), (1, 1))
 Y_CORE = 1
@@ -125,7 +126,7 @@
     halves, sent, masked = back.shape
     slots = chosen.shape[1]
     row = lax.broadcasted_iota(jnp.int32, (sent, slots), 0)
-    second, z, first, q = row // 256, (row // 32 + NZ // 2) % NZ, row // 8 % RING, row % 8
+    second, z, first, q = row // 256, (row // 32 + NZ // 2) % NZ, (row // 8 + 1) % RING, row % 8
     straight = lax.axis_index("core") == Y_CORE
     x, y = jnp.where(straight, second, first), jnp.where(straight, first, second)
     slot = (x * NZ + z) * 16 + q // 4 * 8 + y * 2 + q // 2 % 2
@@ -246,7 +247,8 @@
                 for h in range(2):
                     start = ((core * RING + at) * 2 + h) * half
                     row = 2 * i + h
-                    whole[i : i + 1, start : start + half] = by_core[core][at, row : row + 1]
+                    near = PLACES.index(at)
+                    whole[i : i + 1, start : start + half] = by_core[core][near, row : row + 1]
     out[...] = whole[...].astype(BF16)
 
 
@@ -272,11 +274,11 @@
     return lax.ppermute(v, ALL, moves)
 
 
-def peers():
+def peers(places):
     groups = []
     for second in range(RING):
-        groups.append([index(second, z, Y_CORE, y) for z in ZS for y in range(NY)])
-        groups.append([index(x, z, 1 - Y_CORE, second) for z in ZS for x in range(NX)])
+        groups.append([index(second, z, Y_CORE, y) for z in ZS for y in places])
+        groups.append([index(x, z, 1 - Y_CORE, second) for z in ZS for x in places])
     return groups
 
 
@@ -328,7 +330,9 @@
         student_last_body, (logits_shape, shape((NZ * RING, 2, MASKED), F32)),
         *[blocks[at] for at in LAST], weight, total, lse_teacher, flops=half_flops,
     )
-    stats = lax.all_to_all(stats, ALL, 0, 0, tiled=True, axis_index_groups=peers())
+    stats = lax.all_to_all(
+        stats, ALL, 0, 0, tiled=True, axis_index_groups=peers(range(RING))
+    )
     lse = call(combine_body, shape((2, MASKED), F32), stats)
     lse = call(join_body, shape((2, MASKED), F32), lse, *[shift(lse, k, ring=2) for k in (3, 1, 2)])
     parts = {}
@@ -373,7 +377,7 @@
     partial = sum(step.astype(F32) for step in steps).astype(BF16)
     partial = lax.all_to_all(
         partial.reshape(NZ * RING, 8, part // 2), ALL, 0, 0, tiled=True,
-        axis_index_groups=peers(),
+        axis_index_groups=peers(PLACES),
     )
     mine, other = call(collect_body, (shape((RING, 4, part // 2), F32),) * 2, partial)
     grad_hidden = call(

time: 111 us -> 111 us (level)
  blocking collectives: 59.5 us -> 58.2 us
  starting transfers between devices: 27.9 us -> 29.1 us
    all_to_all x1, blocking collectives: 15.4 us -> 14.1 us  [per_device(): lax.all_to_all(partial.reshape(NZ * RING, 8, part // 2), ALL, 0, 0, tiled...]
    ppermute x10, starting transfers between devices: 8.71 us -> 9.84 us  [swap_core(): return lax.ppermute(x, 'core', [(0, 1), (1, 0)])]
where the time goes in v13:
time: 111 us
  blocking collectives  58.2 us (52%)
  starting transfers between devices  29.1 us (26%)
  Pallas kernels  11 us (10%)
  waiting for transfers between devices  8.77 us (8%)
  between operations  1.61 us (1%)
  other arithmetic  1.19 us (1%)
    all_to_all x1, blocking collectives, per_device(): rows = lax.all_to_all(send, SEQ, 0, 0, tiled=True).reshape(slots, part)  30.1 us
    ppermute x12, starting transfers between devices, shift(): return lax.ppermute(v, ALL, moves)  19.2 us
    all_to_all x1, blocking collectives, per_device(): lax.all_to_all(partial.reshape(NZ * RING, 8, part // 2), ALL, 0, 0, tiled...  14.1 us
    all_to_all x1, blocking collectives, per_device(): lax.all_to_all(stats, ALL, 0, 0, tiled=True, axis_index_groups=peers(rang...  14 us
    pallas_call x15, Pallas kernels, call(): pl.pallas_call(body, out_shape=out, in_specs=specs or [VMEM] * len(args),...  11 us
    ppermute x10, starting transfers between devices, swap_core(): return lax.ppermute(x, 'core', [(0, 1), (1, 0)])  9.84 us
    ppermute x12, waiting for transfers between devices, shift(): return lax.ppermute(v, ALL, moves)  6.58 us
  transfers between devices with their start and end apart: 22, of which 10 were waited for; matrix products, arithmetic and copies ran while one was open for 0% of the time, Pallas kernels for 6%

profile of v13, /device:TPU:1, one launch (start us, length us, event | category | flops | bytes accessed | tf_op | source)
XLA Modules:
  0.0 110.9 jit_solution(12822416066674542423)
XLA Ops:
  1.4 0.8 broadcast_add_fusion.numbers
  2.3 1.2 %shard_map.68 = bf16[64,8,512]{2,1,0:T(8,128)(2,1)S(1)} custom-call(s32[1,8]{1,0:T(1,128)S(1)} %broadcast_add_fusion.numbers, bf16[64,4096]{1,0:T(8,128)(2,1)} %hidden.1), custom_call_target="tpu_custom_call" | custom-call | bytes 1048608 | tf_op jit(solution)/shard_map/pallas_call | solution.py:36
  3.5 30.1 %all_to_all.15 = bf16[64,8,512]{2,1,0:T(8,128)(2,1)S(1)} all-to-all(bf16[64,8,512]{2,1,0:T(8,128)(2,1)S(1)} %shard_map.68), channel_id=1, replica_groups=mesh['x'=4,'z'=8,'core'=2,'y'=4] {'x','z','core'}, dimensions={0} | all-to-all | bytes 1048576 | tf_op jit(solution)/shard_map/all_to_all | solution.py:303
  34.1 3.0 %collective-permute-start.4 = (bf16[256,512]{1,0:T(8,128)(2,1)S(1)}, bf16[256,512]{1,0:T(8,128)(2,1)S(1)}, u32[]{:S(2)}, u32[]{:S(2)}) collective-permute-start(bf16[256,512]{1,0:T(8,128)(2,1)S(1)} %get-tuple-element.36.refs_0_), channel_id=1, source_target_pairs={{0,128},{4,6},{1,129},{5,7},{2,130},{6,4},{3,131},{7,5},{8,136},{1... | collective-permute-start | bytes 786440 | tf_op jit(solution)/shard_map/ppermute | solution.py:274
  37.5 2.3 %collective-permute-start = (bf16[256,512]{1,0:T(8,128)(2,1)S(1)}, bf16[256,512]{1,0:T(8,128)(2,1)S(1)}, u32[]{:S(2)}, u32[]{:S(2)}) collective-permute-start(bf16[256,512]{1,0:T(8,128)(2,1)S(1)} %get-tuple-element.36.refs_0_), channel_id=1, source_target_pairs={{0,192},{4,7},{1,193},{5,4},{2,194},{6,5},{3,195},{7,6},{8,200},{1... | collective-permute-start | bytes 786440 | tf_op jit(solution)/shard_map/ppermute | solution.py:274
  39.8 0.7 collective-permute-start.5
  40.5 1.0 copy-done.1
  41.5 2.2 %shard_map.70 = (bf16[494,256]{1,0:T(8,128)(2,1)S(1)}, f32[8,256]{1,0:T(8,128)S(1)}, bf16[2,1024,256]{2,1,0:T(8,128)(2,1)S(1)}) custom-call(bf16[494,512]{1,0:T(8,128)(2,1)S(1)} %bitcast.14, bf16[256,512]{1,0:T(8,128)(2,1)S(1)} %get-tuple-element.37.chosen), custom_call_target="tpu_custom_call" | custom-call | flops 397934592 | bytes 2077696 | tf_op jit(solution)/shard_map/pallas_call | solution.py:36
  44.0 1.2 %collective-permute-start.3 = (bf16[256,512]{1,0:T(8,128)(2,1)S(1)}, bf16[256,512]{1,0:T(8,128)(2,1)S(1)}, u32[]{:S(2)}, u32[]{:S(2)}) collective-permute-start(bf16[256,512]{1,0:T(8,128)(2,1)S(1)} %collective-permute-done.2.refs_1_), channel_id=1, source_target_pairs={{0,4},{4,0},{1,5},{5,1},{2,6},{6,2},{3,7},{7,3},{8,12},{12,8},{9,1... | collective-permute-start | bytes 786440 | tf_op jit(solution)/shard_map/ppermute | solution.py:256
  45.3 1.0 shard_map.71.refs_3_
  46.8 0.6 shard_map.72
  47.4 14.0 %all_to_all.16.stats = f32[32,2,256]{2,1,0:T(2,128)S(1)} all-to-all(f32[32,2,256]{2,1,0:T(2,128)S(1)} %get-tuple-element.47), channel_id=1, replica_groups={{36,37,38,39,44,45,46,47,52,53,54,55,60,61,62,63,4,5,6,7,12,13,14,15,20..., dimensions={0} | all-to-all | bytes 131072 | tf_op jit(solution)/shard_map/all_to_all | solution.py:333
  61.4 1.5 %collective-permute-start.9 = (f32[2,256]{1,0:T(2,128)S(1)}, f32[2,256]{1,0:T(2,128)S(1)}, u32[]{:S(2)}, u32[]{:S(2)}) collective-permute-start(f32[2,256]{1,0:T(2,128)S(1)} %shard_map.73.a), channel_id=1, source_target_pairs={{0,2},{4,132},{1,3},{5,133},{2,0},{6,134},{3,1},{7,135},{8,10},{12... | collective-permute-start | bytes 6152 | tf_op jit(solution)/shard_map/ppermute | solution.py:274
  63.0 1.0 collective-permute-start.8
  63.9 1.7 %collective-permute-start.7 = (f32[2,256]{1,0:T(2,128)S(1)}, f32[2,256]{1,0:T(2,128)S(1)}, u32[]{:S(2)}, u32[]{:S(2)}) collective-permute-start(f32[2,256]{1,0:T(2,128)S(1)} %shard_map.73.a), channel_id=1, source_target_pairs={{0,3},{4,196},{1,0},{5,197},{2,1},{6,198},{3,2},{7,199},{8,11},{12... | collective-permute-start | bytes 6152 | tf_op jit(solution)/shard_map/ppermute | solution.py:274
  65.6 1.3 %collective-permute-done.8.c = f32[2,256]{1,0:T(2,128)S(1)} collective-permute-done((f32[2,256]{1,0:T(2,128)S(1)}, f32[2,256]{1,0:T(2,128)S(1)}, u32[]{:S(2)}, u32[]{:S(2)}) %collective-permute-start.8) | collective-permute-done | bytes 2080 | tf_op jit(solution)/shard_map/ppermute | solution.py:274
  66.9 3.6 %collective-permute-start.10 = (f32[2,256]{1,0:T(2,128)S(1)}, f32[2,256]{1,0:T(2,128)S(1)}, u32[]{:S(2)}, u32[]{:S(2)}) collective-permute-start(f32[2,256]{1,0:T(2,128)S(1)} %shard_map.74.mine), channel_id=1, source_target_pairs={{0,4},{4,0},{1,5},{5,1},{2,6},{6,2},{3,7},{7,3},{8,12},{12,8},{9,1... | collective-permute-start | bytes 6152 | tf_op jit(solution)/shard_map/ppermute | solution.py:256
  70.5 0.8 collective-permute-done.10.other
  72.9 0.6 shard_map.76
  74.1 1.3 %collective-permute-start.15 = (bf16[256,512]{1,0:T(8,128)(2,1)S(1)}, bf16[256,512]{1,0:T(8,128)(2,1)S(1)}, u32[]{:S(2)}, u32[]{:S(2)}) collective-permute-start(bf16[256,512]{1,0:T(8,128)(2,1)S(1)} %add_convert_fusion.1), channel_id=1, source_target_pairs={{0,128},{4,6},{1,129},{5,7},{2,130},{6,4},{3,131},{7,5},{8,136},{1... | collective-permute-start | bytes 786440 | tf_op jit(solution)/shard_map/ppermute | solution.py:274
  75.4 2.4 %collective-permute-start.13 = (bf16[256,512]{1,0:T(8,128)(2,1)S(1)}, bf16[256,512]{1,0:T(8,128)(2,1)S(1)}, u32[]{:S(2)}, u32[]{:S(2)}) collective-permute-start(bf16[256,512]{1,0:T(8,128)(2,1)S(1)} %add_convert_fusion.3), channel_id=1, source_target_pairs={{0,64},{4,5},{1,65},{5,6},{2,66},{6,7},{3,67},{7,4},{8,72},{12,13}... | collective-permute-start | bytes 786440 | tf_op jit(solution)/shard_map/ppermute | solution.py:274
  78.5 1.6 %collective-permute-start.17 = (bf16[256,512]{1,0:T(8,128)(2,1)S(1)}, bf16[256,512]{1,0:T(8,128)(2,1)S(1)}, u32[]{:S(2)}, u32[]{:S(2)}) collective-permute-start(bf16[256,512]{1,0:T(8,128)(2,1)S(1)} %add_convert_fusion), channel_id=1, source_target_pairs={{0,192},{4,7},{1,193},{5,4},{2,194},{6,5},{3,195},{7,6},{8,200},{1... | collective-permute-start | bytes 786440 | tf_op jit(solution)/shard_map/ppermute | solution.py:274
  80.1 2.3 %shard_map.79 = bf16[494,4096]{1,0:T(8,128)(2,1)} custom-call(bf16[256,512]{1,0:T(8,128)(2,1)S(1)} %get-tuple-element.36.refs_0_, bf16[256,512]{1,0:T(8,128)(2,1)S(1)} %collective-permute-done.2.refs_1_, bf16[256,512]{1,0:T(8,128)(2,1)S(1)} %collective-permute-done.4.refs_2_, bf16[256,512]{1,0:T(8,128)(2,1)S(1)} %collective-permute-done.refs_3_, ...), custom_call_target="tpu_custom_call" | custom-call | flops 1035993088 | bytes 6396928 | tf_op jit(solution)/shard_map/pallas_call | solution.py:36
  82.4 1.6 %collective-permute-done.13.b = bf16[256,512]{1,0:T(8,128)(2,1)S(1)} collective-permute-done((bf16[256,512]{1,0:T(8,128)(2,1)S(1)}, bf16[256,512]{1,0:T(8,128)(2,1)S(1)}, u32[]{:S(2)}, u32[]{:S(2)}) %collective-permute-start.13) | collective-permute-done | bytes 262176 | tf_op jit(solution)/shard_map/ppermute | solution.py:274
  85.0 1.4 %collective-permute-start.18 = (bf16[256,256]{1,0:T(8,128)(2,1)S(1)}, bf16[256,256]{1,0:T(8,128)(2,1)S(1)}, u32[]{:S(2)}, u32[]{:S(2)}) collective-permute-start(bf16[256,256]{1,0:T(8,128)(2,1)S(1)} %get-tuple-element.64), channel_id=1, source_target_pairs={{0,2},{4,132},{1,3},{5,133},{2,0},{6,134},{3,1},{7,135},{8,10},{12... | collective-permute-start | bytes 393224 | tf_op jit(solution)/shard_map/ppermute | solution.py:274
  86.8 2.3 %collective-permute-start.20 = (bf16[256,256]{1,0:T(8,128)(2,1)S(1)}, bf16[256,256]{1,0:T(8,128)(2,1)S(1)}, u32[]{:S(2)}, u32[]{:S(2)}) collective-permute-start(bf16[256,256]{1,0:T(8,128)(2,1)S(1)} %get-tuple-element.66), channel_id=1, source_target_pairs={{0,3},{4,196},{1,0},{5,197},{2,1},{6,198},{3,2},{7,199},{8,11},{12... | collective-permute-start | bytes 393224 | tf_op jit(solution)/shard_map/ppermute | solution.py:274
  89.1 1.6 %collective-permute-done.18 = bf16[256,256]{1,0:T(8,128)(2,1)S(1)} collective-permute-done((bf16[256,256]{1,0:T(8,128)(2,1)S(1)}, bf16[256,256]{1,0:T(8,128)(2,1)S(1)}, u32[]{:S(2)}, u32[]{:S(2)}) %collective-permute-start.18) | collective-permute-done | bytes 131104 | tf_op jit(solution)/shard_map/ppermute | solution.py:274
  90.7 1.4 %collective-permute-done.19 = bf16[256,256]{1,0:T(8,128)(2,1)S(1)} collective-permute-done((bf16[256,256]{1,0:T(8,128)(2,1)S(1)}, bf16[256,256]{1,0:T(8,128)(2,1)S(1)}, u32[]{:S(2)}, u32[]{:S(2)}) %collective-permute-start.19) | collective-permute-done | bytes 131104 | tf_op jit(solution)/shard_map/ppermute | solution.py:274
  92.2 14.1 %all_to_all.17.parts = bf16[32,8,256]{2,1,0:T(8,128)(2,1)S(1)} all-to-all(bf16[32,8,256]{2,1,0:T(8,128)(2,1)S(1)} %fusion), channel_id=1, replica_groups={{37,38,39,36,45,46,47,44,53,54,55,52,61,62,63,60,5,6,7,4,13,14,15,12,21..., dimensions={0} | all-to-all | bytes 262144 | tf_op jit(solution)/shard_map/all_to_all | solution.py:378
  106.3 3.1 %collective-permute-start.21 = (f32[4,4,256]{2,1,0:T(4,128)S(1)}, f32[4,4,256]{2,1,0:T(4,128)S(1)}, u32[]{:S(2)}, u32[]{:S(2)}) collective-permute-start(f32[4,4,256]{2,1,0:T(4,128)S(1)} %get-tuple-element.68), channel_id=1, source_target_pairs={{0,4},{4,0},{1,5},{5,1},{2,6},{6,2},{3,7},{7,3},{8,12},{12,8},{9,1... | collective-permute-start | bytes 49160 | tf_op jit(solution)/shard_map/ppermute | solution.py:256
  109.4 0.8 collective-permute-done.21.other
  110.3 0.6 shard_map.82
  (40 shorter events, 6.1 us)
Async XLA Ops:
  0.6 44.7 %copy-start = (bf16[4096,494]{0,1:T(8,128)(2,1)S(1)}, bf16[4096,494]{0,1:T(8,128)(2,1)}, u32[]{:S(2)}) copy-start(bf16[4096,494]{0,1:T(8,128)(2,1)} %param.6) | copy-start | bytes 12140548
  34.1 9.6 %collective-permute-start.4 = (bf16[256,512]{1,0:T(8,128)(2,1)S(1)}, bf16[256,512]{1,0:T(8,128)(2,1)S(1)}, u32[]{:S(2)}, u32[]{:S(2)}) collective-permute-start(bf16[256,512]{1,0:T(8,128)(2,1)S(1)} %get-tuple-element.36.refs_0_), channel_id=1, source_target_pairs={{0,128},{4,6},{1,129},{5,7},{2,130},{6,4},{3,131},{7,5},{8,136},{1... | collective-permute-start | bytes 786440 | tf_op jit(solution)/shard_map/ppermute | solution.py:274
  37.1 6.9 %collective-permute-start.2 = (bf16[256,512]{1,0:T(8,128)(2,1)S(1)}, bf16[256,512]{1,0:T(8,128)(2,1)S(1)}, u32[]{:S(2)}, u32[]{:S(2)}) collective-permute-start(bf16[256,512]{1,0:T(8,128)(2,1)S(1)} %get-tuple-element.36.refs_0_), channel_id=1, source_target_pairs={{0,64},{4,5},{1,65},{5,6},{2,66},{6,7},{3,67},{7,4},{8,72},{12,13}... | collective-permute-start | bytes 786440 | tf_op jit(solution)/shard_map/ppermute | solution.py:274
  37.5 7.7 %collective-permute-start = (bf16[256,512]{1,0:T(8,128)(2,1)S(1)}, bf16[256,512]{1,0:T(8,128)(2,1)S(1)}, u32[]{:S(2)}, u32[]{:S(2)}) collective-permute-start(bf16[256,512]{1,0:T(8,128)(2,1)S(1)} %get-tuple-element.36.refs_0_), channel_id=1, source_target_pairs={{0,192},{4,7},{1,193},{5,4},{2,194},{6,5},{3,195},{7,6},{8,200},{1... | collective-permute-start | bytes 786440 | tf_op jit(solution)/shard_map/ppermute | solution.py:274
  39.8 5.4 %collective-permute-start.5 = (bf16[256,512]{1,0:T(8,128)(2,1)S(1)}, bf16[256,512]{1,0:T(8,128)(2,1)S(1)}, u32[]{:S(2)}, u32[]{:S(2)}) collective-permute-start(bf16[256,512]{1,0:T(8,128)(2,1)S(1)} %get-tuple-element.36.refs_0_), channel_id=1, source_target_pairs={{0,4},{4,0},{1,5},{5,1},{2,6},{6,2},{3,7},{7,3},{8,12},{12,8},{9,1... | collective-permute-start | bytes 786440 | tf_op jit(solution)/shard_map/ppermute | solution.py:256
  40.5 1.0 copy-start.1
  43.7 1.6 %collective-permute-start.6 = (bf16[256,512]{1,0:T(8,128)(2,1)S(1)}, bf16[256,512]{1,0:T(8,128)(2,1)S(1)}, u32[]{:S(2)}, u32[]{:S(2)}) collective-permute-start(bf16[256,512]{1,0:T(8,128)(2,1)S(1)} %collective-permute-done.4.refs_2_), channel_id=1, source_target_pairs={{0,4},{4,0},{1,5},{5,1},{2,6},{6,2},{3,7},{7,3},{8,12},{12,8},{9,1... | collective-permute-start | bytes 786440 | tf_op jit(solution)/shard_map/ppermute | solution.py:256
  44.0 2.3 %collective-permute-start.3 = (bf16[256,512]{1,0:T(8,128)(2,1)S(1)}, bf16[256,512]{1,0:T(8,128)(2,1)S(1)}, u32[]{:S(2)}, u32[]{:S(2)}) collective-permute-start(bf16[256,512]{1,0:T(8,128)(2,1)S(1)} %collective-permute-done.2.refs_1_), channel_id=1, source_target_pairs={{0,4},{4,0},{1,5},{5,1},{2,6},{6,2},{3,7},{7,3},{8,12},{12,8},{9,1... | collective-permute-start | bytes 786440 | tf_op jit(solution)/shard_map/ppermute | solution.py:256
  45.2 1.5 %collective-permute-start.1 = (bf16[256,512]{1,0:T(8,128)(2,1)S(1)}, bf16[256,512]{1,0:T(8,128)(2,1)S(1)}, u32[]{:S(2)}, u32[]{:S(2)}) collective-permute-start(bf16[256,512]{1,0:T(8,128)(2,1)S(1)} %collective-permute-done.refs_3_), channel_id=1, source_target_pairs={{0,4},{4,0},{1,5},{5,1},{2,6},{6,2},{3,7},{7,3},{8,12},{12,8},{9,1... | collective-permute-start | bytes 786440 | tf_op jit(solution)/shard_map/ppermute | solution.py:256
  61.4 4.2 %collective-permute-start.9 = (f32[2,256]{1,0:T(2,128)S(1)}, f32[2,256]{1,0:T(2,128)S(1)}, u32[]{:S(2)}, u32[]{:S(2)}) collective-permute-start(f32[2,256]{1,0:T(2,128)S(1)} %shard_map.73.a), channel_id=1, source_target_pairs={{0,2},{4,132},{1,3},{5,133},{2,0},{6,134},{3,1},{7,135},{8,10},{12... | collective-permute-start | bytes 6152 | tf_op jit(solution)/shard_map/ppermute | solution.py:274
  63.0 3.9 %collective-permute-start.8 = (f32[2,256]{1,0:T(2,128)S(1)}, f32[2,256]{1,0:T(2,128)S(1)}, u32[]{:S(2)}, u32[]{:S(2)}) collective-permute-start(f32[2,256]{1,0:T(2,128)S(1)} %shard_map.73.a), channel_id=1, source_target_pairs={{0,1},{4,68},{1,2},{5,69},{2,3},{6,70},{3,0},{7,71},{8,9},{12,76},... | collective-permute-start | bytes 6152 | tf_op jit(solution)/shard_map/ppermute | solution.py:274
  63.9 3.0 %collective-permute-start.7 = (f32[2,256]{1,0:T(2,128)S(1)}, f32[2,256]{1,0:T(2,128)S(1)}, u32[]{:S(2)}, u32[]{:S(2)}) collective-permute-start(f32[2,256]{1,0:T(2,128)S(1)} %shard_map.73.a), channel_id=1, source_target_pairs={{0,3},{4,196},{1,0},{5,197},{2,1},{6,198},{3,2},{7,199},{8,11},{12... | collective-permute-start | bytes 6152 | tf_op jit(solution)/shard_map/ppermute | solution.py:274
  66.9 4.4 %collective-permute-start.10 = (f32[2,256]{1,0:T(2,128)S(1)}, f32[2,256]{1,0:T(2,128)S(1)}, u32[]{:S(2)}, u32[]{:S(2)}) collective-permute-start(f32[2,256]{1,0:T(2,128)S(1)} %shard_map.74.mine), channel_id=1, source_target_pairs={{0,4},{4,0},{1,5},{5,1},{2,6},{6,2},{3,7},{7,3},{8,12},{12,8},{9,1... | collective-permute-start | bytes 6152 | tf_op jit(solution)/shard_map/ppermute | solution.py:256
  71.8 2.2 %collective-permute-start.14 = (bf16[256,512]{1,0:T(8,128)(2,1)S(1)}, bf16[256,512]{1,0:T(8,128)(2,1)S(1)}, u32[]{:S(2)}, u32[]{:S(2)}) collective-permute-start(bf16[256,512]{1,0:T(8,128)(2,1)S(1)} %get-tuple-element.59), channel_id=1, source_target_pairs={{0,4},{4,0},{1,5},{5,1},{2,6},{6,2},{3,7},{7,3},{8,12},{12,8},{9,1... | collective-permute-start | bytes 786440 | tf_op jit(solution)/shard_map/ppermute | solution.py:256
  72.7 2.6 %collective-permute-start.11 = (bf16[256,512]{1,0:T(8,128)(2,1)S(1)}, bf16[256,512]{1,0:T(8,128)(2,1)S(1)}, u32[]{:S(2)}, u32[]{:S(2)}) collective-permute-start(bf16[256,512]{1,0:T(8,128)(2,1)S(1)} %get-tuple-element.52), channel_id=1, source_target_pairs={{0,4},{4,0},{1,5},{5,1},{2,6},{6,2},{3,7},{7,3},{8,12},{12,8},{9,1... | collective-permute-start | bytes 786440 | tf_op jit(solution)/shard_map/ppermute | solution.py:256
  73.5 4.9 %collective-permute-start.16 = (bf16[256,512]{1,0:T(8,128)(2,1)S(1)}, bf16[256,512]{1,0:T(8,128)(2,1)S(1)}, u32[]{:S(2)}, u32[]{:S(2)}) collective-permute-start(bf16[256,512]{1,0:T(8,128)(2,1)S(1)} %get-tuple-element.61), channel_id=1, source_target_pairs={{0,4},{4,0},{1,5},{5,1},{2,6},{6,2},{3,7},{7,3},{8,12},{12,8},{9,1... | collective-permute-start | bytes 786440 | tf_op jit(solution)/shard_map/ppermute | solution.py:256
  74.1 10.0 %collective-permute-start.15 = (bf16[256,512]{1,0:T(8,128)(2,1)S(1)}, bf16[256,512]{1,0:T(8,128)(2,1)S(1)}, u32[]{:S(2)}, u32[]{:S(2)}) collective-permute-start(bf16[256,512]{1,0:T(8,128)(2,1)S(1)} %add_convert_fusion.1), channel_id=1, source_target_pairs={{0,128},{4,6},{1,129},{5,7},{2,130},{6,4},{3,131},{7,5},{8,136},{1... | collective-permute-start | bytes 786440 | tf_op jit(solution)/shard_map/ppermute | solution.py:274
  75.4 8.6 %collective-permute-start.13 = (bf16[256,512]{1,0:T(8,128)(2,1)S(1)}, bf16[256,512]{1,0:T(8,128)(2,1)S(1)}, u32[]{:S(2)}, u32[]{:S(2)}) collective-permute-start(bf16[256,512]{1,0:T(8,128)(2,1)S(1)} %add_convert_fusion.3), channel_id=1, source_target_pairs={{0,64},{4,5},{1,65},{5,6},{2,66},{6,7},{3,67},{7,4},{8,72},{12,13}... | collective-permute-start | bytes 786440 | tf_op jit(solution)/shard_map/ppermute | solution.py:274
  78.3 5.7 %collective-permute-start.12 = (bf16[256,512]{1,0:T(8,128)(2,1)S(1)}, bf16[256,512]{1,0:T(8,128)(2,1)S(1)}, u32[]{:S(2)}, u32[]{:S(2)}) collective-permute-start(bf16[256,512]{1,0:T(8,128)(2,1)S(1)} %get-tuple-element.55), channel_id=1, source_target_pairs={{0,4},{4,0},{1,5},{5,1},{2,6},{6,2},{3,7},{7,3},{8,12},{12,8},{9,1... | collective-permute-start | bytes 786440 | tf_op jit(solution)/shard_map/ppermute | solution.py:256
  78.5 6.0 %collective-permute-start.17 = (bf16[256,512]{1,0:T(8,128)(2,1)S(1)}, bf16[256,512]{1,0:T(8,128)(2,1)S(1)}, u32[]{:S(2)}, u32[]{:S(2)}) collective-permute-start(bf16[256,512]{1,0:T(8,128)(2,1)S(1)} %add_convert_fusion), channel_id=1, source_target_pairs={{0,192},{4,7},{1,193},{5,4},{2,194},{6,5},{3,195},{7,6},{8,200},{1... | collective-permute-start | bytes 786440 | tf_op jit(solution)/shard_map/ppermute | solution.py:274
  85.0 5.7 %collective-permute-start.18 = (bf16[256,256]{1,0:T(8,128)(2,1)S(1)}, bf16[256,256]{1,0:T(8,128)(2,1)S(1)}, u32[]{:S(2)}, u32[]{:S(2)}) collective-permute-start(bf16[256,256]{1,0:T(8,128)(2,1)S(1)} %get-tuple-element.64), channel_id=1, source_target_pairs={{0,2},{4,132},{1,3},{5,133},{2,0},{6,134},{3,1},{7,135},{8,10},{12... | collective-permute-start | bytes 393224 | tf_op jit(solution)/shard_map/ppermute | solution.py:274
  86.4 5.7 %collective-permute-start.19 = (bf16[256,256]{1,0:T(8,128)(2,1)S(1)}, bf16[256,256]{1,0:T(8,128)(2,1)S(1)}, u32[]{:S(2)}, u32[]{:S(2)}) collective-permute-start(bf16[256,256]{1,0:T(8,128)(2,1)S(1)} %get-tuple-element.65), channel_id=1, source_target_pairs={{0,1},{4,68},{1,2},{5,69},{2,3},{6,70},{3,0},{7,71},{8,9},{12,76},... | collective-permute-start | bytes 393224 | tf_op jit(solution)/shard_map/ppermute | solution.py:274
  86.8 5.4 %collective-permute-start.20 = (bf16[256,256]{1,0:T(8,128)(2,1)S(1)}, bf16[256,256]{1,0:T(8,128)(2,1)S(1)}, u32[]{:S(2)}, u32[]{:S(2)}) collective-permute-start(bf16[256,256]{1,0:T(8,128)(2,1)S(1)} %get-tuple-element.66), channel_id=1, source_target_pairs={{0,3},{4,196},{1,0},{5,197},{2,1},{6,198},{3,2},{7,199},{8,11},{12... | collective-permute-start | bytes 393224 | tf_op jit(solution)/shard_map/ppermute | solution.py:274
  106.3 3.9 %collective-permute-start.21 = (f32[4,4,256]{2,1,0:T(4,128)S(1)}, f32[4,4,256]{2,1,0:T(4,128)S(1)}, u32[]{:S(2)}, u32[]{:S(2)}) collective-permute-start(f32[4,4,256]{2,1,0:T(4,128)S(1)} %get-tuple-element.68), channel_id=1, source_target_pairs={{0,4},{4,0},{1,5},{5,1},{2,6},{6,2},{3,7},{7,3},{8,12},{12,8},{9,1... | collective-permute-start | bytes 49160 | tf_op jit(solution)/shard_map/ppermute | solution.py:256

commit v14 on v13

--- a/solution.py
+++ b/solution.py
@@ -274,11 +274,11 @@
     return lax.ppermute(v, ALL, moves)
 
 
-def peers(places):
+def peers():
     groups = []
     for second in range(RING):
-        groups.append([index(second, z, Y_CORE, y) for z in ZS for y in places])
-        groups.append([index(x, z, 1 - Y_CORE, second) for z in ZS for x in places])
+        groups.append([index(second, z, Y_CORE, y) for z in ZS for y in PLACES])
+        groups.append([index(x, z, 1 - Y_CORE, second) for z in ZS for x in PLACES])
     return groups
 
 
@@ -331,7 +331,7 @@
         *[blocks[at] for at in LAST], weight, total, lse_teacher, flops=half_flops,
     )
     stats = lax.all_to_all(
-        stats, ALL, 0, 0, tiled=True, axis_index_groups=peers(range(RING))
+        stats, ALL, 0, 0, tiled=True, axis_index_groups=peers()
     )
     lse = call(combine_body, shape((2, MASKED), F32), stats)
     lse = call(join_body, shape((2, MASKED), F32), lse, *[shift(lse, k, ring=2) for k in (3, 1, 2)])
@@ -377,7 +377,7 @@
     partial = sum(step.astype(F32) for step in steps).astype(BF16)
     partial = lax.all_to_all(
         partial.reshape(NZ * RING, 8, part // 2), ALL, 0, 0, tiled=True,
-        axis_index_groups=peers(PLACES),
+        axis_index_groups=peers(),
     )
     mine, other = call(collect_body, (shape((RING, 4, part // 2), F32),) * 2, partial)
     grad_hidden = call(

time: 111 us -> 111 us (level)
  no operation moved by 1% of the time
where the time goes in v14:
time: 111 us
  blocking collectives  58.3 us (53%)
  starting transfers between devices  29.3 us (26%)
  Pallas kernels  11 us (10%)
  waiting for transfers between devices  8.71 us (8%)
  between operations  1.61 us (1%)
  other arithmetic  1.19 us (1%)
    all_to_all x1, blocking collectives, per_device(): rows = lax.all_to_all(send, SEQ, 0, 0, tiled=True).reshape(slots, part)  30.1 us
    ppermute x12, starting transfers between devices, shift(): return lax.ppermute(v, ALL, moves)  19.4 us
    all_to_all x1, blocking collectives, per_device(): lax.all_to_all(partial.reshape(NZ * RING, 8, part // 2), ALL, 0, 0, tiled...  14.5 us
    all_to_all x1, blocking collectives, per_device(): lax.all_to_all(stats, ALL, 0, 0, tiled=True, axis_index_groups=peers())  13.6 us
    pallas_call x15, Pallas kernels, call(): pl.pallas_call(body, out_shape=out, in_specs=specs or [VMEM] * len(args),...  11 us
    ppermute x10, starting transfers between devices, swap_core(): return lax.ppermute(x, 'core', [(0, 1), (1, 0)])  9.95 us
    ppermute x12, waiting for transfers between devices, shift(): return lax.ppermute(v, ALL, moves)  6.51 us
  transfers between devices with their start and end apart: 22, of which 10 were waited for; matrix products, arithmetic and copies ran while one was open for 0% of the time, Pallas kernels for 6%

profile of v14, /device:TPU:1, one launch (start us, length us, event | category | flops | bytes accessed | tf_op | source)
XLA Modules:
  0.0 111.2 jit_solution(13030843197184407740)
XLA Ops:
  1.4 0.8 broadcast_add_fusion.numbers
  2.3 1.2 %shard_map.68 = bf16[64,8,512]{2,1,0:T(8,128)(2,1)S(1)} custom-call(s32[1,8]{1,0:T(1,128)S(1)} %broadcast_add_fusion.numbers, bf16[64,4096]{1,0:T(8,128)(2,1)} %hidden.1), custom_call_target="tpu_custom_call" | custom-call | bytes 1048608 | tf_op jit(solution)/shard_map/pallas_call | solution.py:36
  3.5 30.1 %all_to_all.15 = bf16[64,8,512]{2,1,0:T(8,128)(2,1)S(1)} all-to-all(bf16[64,8,512]{2,1,0:T(8,128)(2,1)S(1)} %shard_map.68), channel_id=1, replica_groups=mesh['x'=4,'z'=8,'core'=2,'y'=4] {'x','z','core'}, dimensions={0} | all-to-all | bytes 1048576 | tf_op jit(solution)/shard_map/all_to_all | solution.py:303
  34.1 3.0 %collective-permute-start.4 = (bf16[256,512]{1,0:T(8,128)(2,1)S(1)}, bf16[256,512]{1,0:T(8,128)(2,1)S(1)}, u32[]{:S(2)}, u32[]{:S(2)}) collective-permute-start(bf16[256,512]{1,0:T(8,128)(2,1)S(1)} %get-tuple-element.36.refs_0_), channel_id=1, source_target_pairs={{0,128},{4,6},{1,129},{5,7},{2,130},{6,4},{3,131},{7,5},{8,136},{1... | collective-permute-start | bytes 786440 | tf_op jit(solution)/shard_map/ppermute | solution.py:274
  37.5 2.3 %collective-permute-start = (bf16[256,512]{1,0:T(8,128)(2,1)S(1)}, bf16[256,512]{1,0:T(8,128)(2,1)S(1)}, u32[]{:S(2)}, u32[]{:S(2)}) collective-permute-start(bf16[256,512]{1,0:T(8,128)(2,1)S(1)} %get-tuple-element.36.refs_0_), channel_id=1, source_target_pairs={{0,192},{4,7},{1,193},{5,4},{2,194},{6,5},{3,195},{7,6},{8,200},{1... | collective-permute-start | bytes 786440 | tf_op jit(solution)/shard_map/ppermute | solution.py:274
  39.8 0.7 collective-permute-start.5
  40.5 1.0 copy-done.1
  41.5 2.2 %shard_map.70 = (bf16[494,256]{1,0:T(8,128)(2,1)S(1)}, f32[8,256]{1,0:T(8,128)S(1)}, bf16[2,1024,256]{2,1,0:T(8,128)(2,1)S(1)}) custom-call(bf16[494,512]{1,0:T(8,128)(2,1)S(1)} %bitcast.14, bf16[256,512]{1,0:T(8,128)(2,1)S(1)} %get-tuple-element.37.chosen), custom_call_target="tpu_custom_call" | custom-call | flops 397934592 | bytes 2077696 | tf_op jit(solution)/shard_map/pallas_call | solution.py:36
  44.0 1.2 %collective-permute-start.3 = (bf16[256,512]{1,0:T(8,128)(2,1)S(1)}, bf16[256,512]{1,0:T(8,128)(2,1)S(1)}, u32[]{:S(2)}, u32[]{:S(2)}) collective-permute-start(bf16[256,512]{1,0:T(8,128)(2,1)S(1)} %collective-permute-done.2.refs_1_), channel_id=1, source_target_pairs={{0,4},{4,0},{1,5},{5,1},{2,6},{6,2},{3,7},{7,3},{8,12},{12,8},{9,1... | collective-permute-start | bytes 786440 | tf_op jit(solution)/shard_map/ppermute | solution.py:256
  45.3 1.0 shard_map.71.refs_3_
  46.8 0.6 shard_map.72
  47.4 13.6 %all_to_all.16.stats = f32[32,2,256]{2,1,0:T(2,128)S(1)} all-to-all(f32[32,2,256]{2,1,0:T(2,128)S(1)} %get-tuple-element.47), channel_id=1, replica_groups={{37,38,39,36,45,46,47,44,53,54,55,52,61,62,63,60,5,6,7,4,13,14,15,12,21..., dimensions={0} | all-to-all | bytes 131072 | tf_op jit(solution)/shard_map/all_to_all | solution.py:333
  61.1 1.5 %collective-permute-start.9 = (f32[2,256]{1,0:T(2,128)S(1)}, f32[2,256]{1,0:T(2,128)S(1)}, u32[]{:S(2)}, u32[]{:S(2)}) collective-permute-start(f32[2,256]{1,0:T(2,128)S(1)} %shard_map.73.a), channel_id=1, source_target_pairs={{0,2},{4,132},{1,3},{5,133},{2,0},{6,134},{3,1},{7,135},{8,10},{12... | collective-permute-start | bytes 6152 | tf_op jit(solution)/shard_map/ppermute | solution.py:274
  62.6 1.0 collective-permute-start.8
  63.6 1.7 %collective-permute-start.7 = (f32[2,256]{1,0:T(2,128)S(1)}, f32[2,256]{1,0:T(2,128)S(1)}, u32[]{:S(2)}, u32[]{:S(2)}) collective-permute-start(f32[2,256]{1,0:T(2,128)S(1)} %shard_map.73.a), channel_id=1, source_target_pairs={{0,3},{4,196},{1,0},{5,197},{2,1},{6,198},{3,2},{7,199},{8,11},{12... | collective-permute-start | bytes 6152 | tf_op jit(solution)/shard_map/ppermute | solution.py:274
  65.3 1.3 %collective-permute-done.8.c = f32[2,256]{1,0:T(2,128)S(1)} collective-permute-done((f32[2,256]{1,0:T(2,128)S(1)}, f32[2,256]{1,0:T(2,128)S(1)}, u32[]{:S(2)}, u32[]{:S(2)}) %collective-permute-start.8) | collective-permute-done | bytes 2080 | tf_op jit(solution)/shard_map/ppermute | solution.py:274
  66.6 3.8 %collective-permute-start.10 = (f32[2,256]{1,0:T(2,128)S(1)}, f32[2,256]{1,0:T(2,128)S(1)}, u32[]{:S(2)}, u32[]{:S(2)}) collective-permute-start(f32[2,256]{1,0:T(2,128)S(1)} %shard_map.74.mine), channel_id=1, source_target_pairs={{0,4},{4,0},{1,5},{5,1},{2,6},{6,2},{3,7},{7,3},{8,12},{12,8},{9,1... | collective-permute-start | bytes 6152 | tf_op jit(solution)/shard_map/ppermute | solution.py:256
  70.4 0.8 collective-permute-done.10.other
  72.8 0.6 shard_map.76
  73.9 1.3 %collective-permute-start.15 = (bf16[256,512]{1,0:T(8,128)(2,1)S(1)}, bf16[256,512]{1,0:T(8,128)(2,1)S(1)}, u32[]{:S(2)}, u32[]{:S(2)}) collective-permute-start(bf16[256,512]{1,0:T(8,128)(2,1)S(1)} %add_convert_fusion.1), channel_id=1, source_target_pairs={{0,128},{4,6},{1,129},{5,7},{2,130},{6,4},{3,131},{7,5},{8,136},{1... | collective-permute-start | bytes 786440 | tf_op jit(solution)/shard_map/ppermute | solution.py:274
  75.3 2.4 %collective-permute-start.13 = (bf16[256,512]{1,0:T(8,128)(2,1)S(1)}, bf16[256,512]{1,0:T(8,128)(2,1)S(1)}, u32[]{:S(2)}, u32[]{:S(2)}) collective-permute-start(bf16[256,512]{1,0:T(8,128)(2,1)S(1)} %add_convert_fusion.3), channel_id=1, source_target_pairs={{0,64},{4,5},{1,65},{5,6},{2,66},{6,7},{3,67},{7,4},{8,72},{12,13}... | collective-permute-start | bytes 786440 | tf_op jit(solution)/shard_map/ppermute | solution.py:274
  78.4 1.3 %collective-permute-start.17 = (bf16[256,512]{1,0:T(8,128)(2,1)S(1)}, bf16[256,512]{1,0:T(8,128)(2,1)S(1)}, u32[]{:S(2)}, u32[]{:S(2)}) collective-permute-start(bf16[256,512]{1,0:T(8,128)(2,1)S(1)} %add_convert_fusion), channel_id=1, source_target_pairs={{0,192},{4,7},{1,193},{5,4},{2,194},{6,5},{3,195},{7,6},{8,200},{1... | collective-permute-start | bytes 786440 | tf_op jit(solution)/shard_map/ppermute | solution.py:274
  79.6 2.3 %shard_map.79 = bf16[494,4096]{1,0:T(8,128)(2,1)} custom-call(bf16[256,512]{1,0:T(8,128)(2,1)S(1)} %get-tuple-element.36.refs_0_, bf16[256,512]{1,0:T(8,128)(2,1)S(1)} %collective-permute-done.2.refs_1_, bf16[256,512]{1,0:T(8,128)(2,1)S(1)} %collective-permute-done.4.refs_2_, bf16[256,512]{1,0:T(8,128)(2,1)S(1)} %collective-permute-done.refs_3_, ...), custom_call_target="tpu_custom_call" | custom-call | flops 1035993088 | bytes 6396928 | tf_op jit(solution)/shard_map/pallas_call | solution.py:36
  82.0 1.9 %collective-permute-done.13.b = bf16[256,512]{1,0:T(8,128)(2,1)S(1)} collective-permute-done((bf16[256,512]{1,0:T(8,128)(2,1)S(1)}, bf16[256,512]{1,0:T(8,128)(2,1)S(1)}, u32[]{:S(2)}, u32[]{:S(2)}) %collective-permute-start.13) | collective-permute-done | bytes 262176 | tf_op jit(solution)/shard_map/ppermute | solution.py:274
  84.9 1.8 %collective-permute-start.18 = (bf16[256,256]{1,0:T(8,128)(2,1)S(1)}, bf16[256,256]{1,0:T(8,128)(2,1)S(1)}, u32[]{:S(2)}, u32[]{:S(2)}) collective-permute-start(bf16[256,256]{1,0:T(8,128)(2,1)S(1)} %get-tuple-element.64), channel_id=1, source_target_pairs={{0,2},{4,132},{1,3},{5,133},{2,0},{6,134},{3,1},{7,135},{8,10},{12... | collective-permute-start | bytes 393224 | tf_op jit(solution)/shard_map/ppermute | solution.py:274
  87.0 2.4 %collective-permute-start.20 = (bf16[256,256]{1,0:T(8,128)(2,1)S(1)}, bf16[256,256]{1,0:T(8,128)(2,1)S(1)}, u32[]{:S(2)}, u32[]{:S(2)}) collective-permute-start(bf16[256,256]{1,0:T(8,128)(2,1)S(1)} %get-tuple-element.66), channel_id=1, source_target_pairs={{0,3},{4,196},{1,0},{5,197},{2,1},{6,198},{3,2},{7,199},{8,11},{12... | collective-permute-start | bytes 393224 | tf_op jit(solution)/shard_map/ppermute | solution.py:274
  89.4 1.2 %collective-permute-done.18 = bf16[256,256]{1,0:T(8,128)(2,1)S(1)} collective-permute-done((bf16[256,256]{1,0:T(8,128)(2,1)S(1)}, bf16[256,256]{1,0:T(8,128)(2,1)S(1)}, u32[]{:S(2)}, u32[]{:S(2)}) %collective-permute-start.18) | collective-permute-done | bytes 131104 | tf_op jit(solution)/shard_map/ppermute | solution.py:274
  90.6 1.5 %collective-permute-done.19 = bf16[256,256]{1,0:T(8,128)(2,1)S(1)} collective-permute-done((bf16[256,256]{1,0:T(8,128)(2,1)S(1)}, bf16[256,256]{1,0:T(8,128)(2,1)S(1)}, u32[]{:S(2)}, u32[]{:S(2)}) %collective-permute-start.19) | collective-permute-done | bytes 131104 | tf_op jit(solution)/shard_map/ppermute | solution.py:274
  92.2 14.5 %all_to_all.17.parts = bf16[32,8,256]{2,1,0:T(8,128)(2,1)S(1)} all-to-all(bf16[32,8,256]{2,1,0:T(8,128)(2,1)S(1)} %fusion), channel_id=1, replica_groups={{37,38,39,36,45,46,47,44,53,54,55,52,61,62,63,60,5,6,7,4,13,14,15,12,21..., dimensions={0} | all-to-all | bytes 262144 | tf_op jit(solution)/shard_map/all_to_all | solution.py:378
  106.7 3.0 %collective-permute-start.21 = (f32[4,4,256]{2,1,0:T(4,128)S(1)}, f32[4,4,256]{2,1,0:T(4,128)S(1)}, u32[]{:S(2)}, u32[]{:S(2)}) collective-permute-start(f32[4,4,256]{2,1,0:T(4,128)S(1)} %get-tuple-element.68), channel_id=1, source_target_pairs={{0,4},{4,0},{1,5},{5,1},{2,6},{6,2},{3,7},{7,3},{8,12},{12,8},{9,1... | collective-permute-start | bytes 49160 | tf_op jit(solution)/shard_map/ppermute | solution.py:256
  109.7 0.8 collective-permute-done.21.other
  110.5 0.6 shard_map.82
  (40 shorter events, 6.1 us)
Async XLA Ops:
  0.6 44.7 %copy-start = (bf16[4096,494]{0,1:T(8,128)(2,1)S(1)}, bf16[4096,494]{0,1:T(8,128)(2,1)}, u32[]{:S(2)}) copy-start(bf16[4096,494]{0,1:T(8,128)(2,1)} %param.6) | copy-start | bytes 12140548
  34.1 9.6 %collective-permute-start.4 = (bf16[256,512]{1,0:T(8,128)(2,1)S(1)}, bf16[256,512]{1,0:T(8,128)(2,1)S(1)}, u32[]{:S(2)}, u32[]{:S(2)}) collective-permute-start(bf16[256,512]{1,0:T(8,128)(2,1)S(1)} %get-tuple-element.36.refs_0_), channel_id=1, source_target_pairs={{0,128},{4,6},{1,129},{5,7},{2,130},{6,4},{3,131},{7,5},{8,136},{1... | collective-permute-start | bytes 786440 | tf_op jit(solution)/shard_map/ppermute | solution.py:274
  37.1 6.9 %collective-permute-start.2 = (bf16[256,512]{1,0:T(8,128)(2,1)S(1)}, bf16[256,512]{1,0:T(8,128)(2,1)S(1)}, u32[]{:S(2)}, u32[]{:S(2)}) collective-permute-start(bf16[256,512]{1,0:T(8,128)(2,1)S(1)} %get-tuple-element.36.refs_0_), channel_id=1, source_target_pairs={{0,64},{4,5},{1,65},{5,6},{2,66},{6,7},{3,67},{7,4},{8,72},{12,13}... | collective-permute-start | bytes 786440 | tf_op jit(solution)/shard_map/ppermute | solution.py:274
  37.5 7.7 %collective-permute-start = (bf16[256,512]{1,0:T(8,128)(2,1)S(1)}, bf16[256,512]{1,0:T(8,128)(2,1)S(1)}, u32[]{:S(2)}, u32[]{:S(2)}) collective-permute-start(bf16[256,512]{1,0:T(8,128)(2,1)S(1)} %get-tuple-element.36.refs_0_), channel_id=1, source_target_pairs={{0,192},{4,7},{1,193},{5,4},{2,194},{6,5},{3,195},{7,6},{8,200},{1... | collective-permute-start | bytes 786440 | tf_op jit(solution)/shard_map/ppermute | solution.py:274
  39.8 5.4 %collective-permute-start.5 = (bf16[256,512]{1,0:T(8,128)(2,1)S(1)}, bf16[256,512]{1,0:T(8,128)(2,1)S(1)}, u32[]{:S(2)}, u32[]{:S(2)}) collective-permute-start(bf16[256,512]{1,0:T(8,128)(2,1)S(1)} %get-tuple-element.36.refs_0_), channel_id=1, source_target_pairs={{0,4},{4,0},{1,5},{5,1},{2,6},{6,2},{3,7},{7,3},{8,12},{12,8},{9,1... | collective-permute-start | bytes 786440 | tf_op jit(solution)/shard_map/ppermute | solution.py:256
  40.5 1.0 copy-start.1
  43.7 1.6 %collective-permute-start.6 = (bf16[256,512]{1,0:T(8,128)(2,1)S(1)}, bf16[256,512]{1,0:T(8,128)(2,1)S(1)}, u32[]{:S(2)}, u32[]{:S(2)}) collective-permute-start(bf16[256,512]{1,0:T(8,128)(2,1)S(1)} %collective-permute-done.4.refs_2_), channel_id=1, source_target_pairs={{0,4},{4,0},{1,5},{5,1},{2,6},{6,2},{3,7},{7,3},{8,12},{12,8},{9,1... | collective-permute-start | bytes 786440 | tf_op jit(solution)/shard_map/ppermute | solution.py:256
  44.0 2.3 %collective-permute-start.3 = (bf16[256,512]{1,0:T(8,128)(2,1)S(1)}, bf16[256,512]{1,0:T(8,128)(2,1)S(1)}, u32[]{:S(2)}, u32[]{:S(2)}) collective-permute-start(bf16[256,512]{1,0:T(8,128)(2,1)S(1)} %collective-permute-done.2.refs_1_), channel_id=1, source_target_pairs={{0,4},{4,0},{1,5},{5,1},{2,6},{6,2},{3,7},{7,3},{8,12},{12,8},{9,1... | collective-permute-start | bytes 786440 | tf_op jit(solution)/shard_map/ppermute | solution.py:256
  45.2 1.5 %collective-permute-start.1 = (bf16[256,512]{1,0:T(8,128)(2,1)S(1)}, bf16[256,512]{1,0:T(8,128)(2,1)S(1)}, u32[]{:S(2)}, u32[]{:S(2)}) collective-permute-start(bf16[256,512]{1,0:T(8,128)(2,1)S(1)} %collective-permute-done.refs_3_), channel_id=1, source_target_pairs={{0,4},{4,0},{1,5},{5,1},{2,6},{6,2},{3,7},{7,3},{8,12},{12,8},{9,1... | collective-permute-start | bytes 786440 | tf_op jit(solution)/shard_map/ppermute | solution.py:256
  61.1 4.2 %collective-permute-start.9 = (f32[2,256]{1,0:T(2,128)S(1)}, f32[2,256]{1,0:T(2,128)S(1)}, u32[]{:S(2)}, u32[]{:S(2)}) collective-permute-start(f32[2,256]{1,0:T(2,128)S(1)} %shard_map.73.a), channel_id=1, source_target_pairs={{0,2},{4,132},{1,3},{5,133},{2,0},{6,134},{3,1},{7,135},{8,10},{12... | collective-permute-start | bytes 6152 | tf_op jit(solution)/shard_map/ppermute | solution.py:274
  62.6 3.9 %collective-permute-start.8 = (f32[2,256]{1,0:T(2,128)S(1)}, f32[2,256]{1,0:T(2,128)S(1)}, u32[]{:S(2)}, u32[]{:S(2)}) collective-permute-start(f32[2,256]{1,0:T(2,128)S(1)} %shard_map.73.a), channel_id=1, source_target_pairs={{0,1},{4,68},{1,2},{5,69},{2,3},{6,70},{3,0},{7,71},{8,9},{12,76},... | collective-permute-start | bytes 6152 | tf_op jit(solution)/shard_map/ppermute | solution.py:274
  63.6 3.0 %collective-permute-start.7 = (f32[2,256]{1,0:T(2,128)S(1)}, f32[2,256]{1,0:T(2,128)S(1)}, u32[]{:S(2)}, u32[]{:S(2)}) collective-permute-start(f32[2,256]{1,0:T(2,128)S(1)} %shard_map.73.a), channel_id=1, source_target_pairs={{0,3},{4,196},{1,0},{5,197},{2,1},{6,198},{3,2},{7,199},{8,11},{12... | collective-permute-start | bytes 6152 | tf_op jit(solution)/shard_map/ppermute | solution.py:274
  66.6 4.6 %collective-permute-start.10 = (f32[2,256]{1,0:T(2,128)S(1)}, f32[2,256]{1,0:T(2,128)S(1)}, u32[]{:S(2)}, u32[]{:S(2)}) collective-permute-start(f32[2,256]{1,0:T(2,128)S(1)} %shard_map.74.mine), channel_id=1, source_target_pairs={{0,4},{4,0},{1,5},{5,1},{2,6},{6,2},{3,7},{7,3},{8,12},{12,8},{9,1... | collective-permute-start | bytes 6152 | tf_op jit(solution)/shard_map/ppermute | solution.py:256
  71.7 2.2 %collective-permute-start.14 = (bf16[256,512]{1,0:T(8,128)(2,1)S(1)}, bf16[256,512]{1,0:T(8,128)(2,1)S(1)}, u32[]{:S(2)}, u32[]{:S(2)}) collective-permute-start(bf16[256,512]{1,0:T(8,128)(2,1)S(1)} %get-tuple-element.59), channel_id=1, source_target_pairs={{0,4},{4,0},{1,5},{5,1},{2,6},{6,2},{3,7},{7,3},{8,12},{12,8},{9,1... | collective-permute-start | bytes 786440 | tf_op jit(solution)/shard_map/ppermute | solution.py:256
  72.6 2.6 %collective-permute-start.11 = (bf16[256,512]{1,0:T(8,128)(2,1)S(1)}, bf16[256,512]{1,0:T(8,128)(2,1)S(1)}, u32[]{:S(2)}, u32[]{:S(2)}) collective-permute-start(bf16[256,512]{1,0:T(8,128)(2,1)S(1)} %get-tuple-element.52), channel_id=1, source_target_pairs={{0,4},{4,0},{1,5},{5,1},{2,6},{6,2},{3,7},{7,3},{8,12},{12,8},{9,1... | collective-permute-start | bytes 786440 | tf_op jit(solution)/shard_map/ppermute | solution.py:256
  73.4 4.9 %collective-permute-start.16 = (bf16[256,512]{1,0:T(8,128)(2,1)S(1)}, bf16[256,512]{1,0:T(8,128)(2,1)S(1)}, u32[]{:S(2)}, u32[]{:S(2)}) collective-permute-start(bf16[256,512]{1,0:T(8,128)(2,1)S(1)} %get-tuple-element.61), channel_id=1, source_target_pairs={{0,4},{4,0},{1,5},{5,1},{2,6},{6,2},{3,7},{7,3},{8,12},{12,8},{9,1... | collective-permute-start | bytes 786440 | tf_op jit(solution)/shard_map/ppermute | solution.py:256
  73.9 10.0 %collective-permute-start.15 = (bf16[256,512]{1,0:T(8,128)(2,1)S(1)}, bf16[256,512]{1,0:T(8,128)(2,1)S(1)}, u32[]{:S(2)}, u32[]{:S(2)}) collective-permute-start(bf16[256,512]{1,0:T(8,128)(2,1)S(1)} %add_convert_fusion.1), channel_id=1, source_target_pairs={{0,128},{4,6},{1,129},{5,7},{2,130},{6,4},{3,131},{7,5},{8,136},{1... | collective-permute-start | bytes 786440 | tf_op jit(solution)/shard_map/ppermute | solution.py:274
  75.3 8.6 %collective-permute-start.13 = (bf16[256,512]{1,0:T(8,128)(2,1)S(1)}, bf16[256,512]{1,0:T(8,128)(2,1)S(1)}, u32[]{:S(2)}, u32[]{:S(2)}) collective-permute-start(bf16[256,512]{1,0:T(8,128)(2,1)S(1)} %add_convert_fusion.3), channel_id=1, source_target_pairs={{0,64},{4,5},{1,65},{5,6},{2,66},{6,7},{3,67},{7,4},{8,72},{12,13}... | collective-permute-start | bytes 786440 | tf_op jit(solution)/shard_map/ppermute | solution.py:274
  78.2 5.7 %collective-permute-start.12 = (bf16[256,512]{1,0:T(8,128)(2,1)S(1)}, bf16[256,512]{1,0:T(8,128)(2,1)S(1)}, u32[]{:S(2)}, u32[]{:S(2)}) collective-permute-start(bf16[256,512]{1,0:T(8,128)(2,1)S(1)} %get-tuple-element.55), channel_id=1, source_target_pairs={{0,4},{4,0},{1,5},{5,1},{2,6},{6,2},{3,7},{7,3},{8,12},{12,8},{9,1... | collective-permute-start | bytes 786440 | tf_op jit(solution)/shard_map/ppermute | solution.py:256
  78.4 6.0 %collective-permute-start.17 = (bf16[256,512]{1,0:T(8,128)(2,1)S(1)}, bf16[256,512]{1,0:T(8,128)(2,1)S(1)}, u32[]{:S(2)}, u32[]{:S(2)}) collective-permute-start(bf16[256,512]{1,0:T(8,128)(2,1)S(1)} %add_convert_fusion), channel_id=1, source_target_pairs={{0,192},{4,7},{1,193},{5,4},{2,194},{6,5},{3,195},{7,6},{8,200},{1... | collective-permute-start | bytes 786440 | tf_op jit(solution)/shard_map/ppermute | solution.py:274
  84.9 5.7 %collective-permute-start.18 = (bf16[256,256]{1,0:T(8,128)(2,1)S(1)}, bf16[256,256]{1,0:T(8,128)(2,1)S(1)}, u32[]{:S(2)}, u32[]{:S(2)}) collective-permute-start(bf16[256,256]{1,0:T(8,128)(2,1)S(1)} %get-tuple-element.64), channel_id=1, source_target_pairs={{0,2},{4,132},{1,3},{5,133},{2,0},{6,134},{3,1},{7,135},{8,10},{12... | collective-permute-start | bytes 393224 | tf_op jit(solution)/shard_map/ppermute | solution.py:274
  86.8 5.3 %collective-permute-start.19 = (bf16[256,256]{1,0:T(8,128)(2,1)S(1)}, bf16[256,256]{1,0:T(8,128)(2,1)S(1)}, u32[]{:S(2)}, u32[]{:S(2)}) collective-permute-start(bf16[256,256]{1,0:T(8,128)(2,1)S(1)} %get-tuple-element.65), channel_id=1, source_target_pairs={{0,1},{4,68},{1,2},{5,69},{2,3},{6,70},{3,0},{7,71},{8,9},{12,76},... | collective-permute-start | bytes 393224 | tf_op jit(solution)/shard_map/ppermute | solution.py:274
  87.0 5.0 %collective-permute-start.20 = (bf16[256,256]{1,0:T(8,128)(2,1)S(1)}, bf16[256,256]{1,0:T(8,128)(2,1)S(1)}, u32[]{:S(2)}, u32[]{:S(2)}) collective-permute-start(bf16[256,256]{1,0:T(8,128)(2,1)S(1)} %get-tuple-element.66), channel_id=1, source_target_pairs={{0,3},{4,196},{1,0},{5,197},{2,1},{6,198},{3,2},{7,199},{8,11},{12... | collective-permute-start | bytes 393224 | tf_op jit(solution)/shard_map/ppermute | solution.py:274
  106.7 3.8 %collective-permute-start.21 = (f32[4,4,256]{2,1,0:T(4,128)S(1)}, f32[4,4,256]{2,1,0:T(4,128)S(1)}, u32[]{:S(2)}, u32[]{:S(2)}) collective-permute-start(f32[4,4,256]{2,1,0:T(4,128)S(1)} %get-tuple-element.68), channel_id=1, source_target_pairs={{0,4},{4,0},{1,5},{5,1},{2,6},{6,2},{3,7},{7,3},{8,12},{12,8},{9,1... | collective-permute-start | bytes 49160 | tf_op jit(solution)/shard_map/ppermute | solution.py:256
